TPU v7x, 32 devices: a whole 2x2x4 slice. The times are simulated.
32 devices in a mesh: cascade: 2 (over y), coil: 4 (over z), readout: 4 (over x, core).
Axes of the slice: x: 2, y: 2, z: 4, core: 2. Of those that a mesh axis runs over, the one named last changes fastest.
Arguments:
- initial: bfloat16 [2, 4, 8, 128, 2, 128], P(None, None, 'readout'), may hold values from -6 to 6
- coil_maps: bfloat16 [2, 16, 8, 128, 2, 128], P(None, 'coil', 'readout'), may hold values from -1.5 to 1.5
- kspace: bfloat16 [2, 16, 4, 8, 128, 2, 128], P(None, 'coil', None, 'readout'), may hold values from -6 to 6
- sampled: int32 [16, 4, 128, 128], P('coil'), may hold values 0 or 1
- first_w: bfloat16 [2, 27, 2, 64], P('cascade'), may hold values from -0.875 to 0.875
- time_w: bfloat16 [2, 3, 64, 64], P('cascade'), may hold values from -0.4375 to 0.4375
- last_w: bfloat16 [2, 27, 64, 2], P('cascade'), may hold values from -0.15625 to 0.15625
Outputs:
- images: bfloat16 [2, 2, 4, 8, 128, 2, 128], P('cascade', None, None, 'readout', 'coil')
Inputs may be any that keep to these rules, and one draw needn't show every extreme that they name: `sampled`: 1 where the sample at that phase, line and partition was acquired for that coil, else 0.
All inputs are finite; a program needn't handle non-finite values. No bound on the sum of `sampled` on one device may be relied on, other than what follows from the above.
Results may differ from a plain program's by a relative error of at most 0.024.
Values may be sent and summed in bfloat16 or wider, within the bound.
No kernel may reach another device: no remote copies, remote signals or barrier semaphores. Data moves between devices by JAX's collectives and lax.ppermute only.
A program may use at most 128 MiB of HBM per device.

v0:
```python
import jax
import jax.numpy as jnp
from jax import lax
from jax.sharding import PartitionSpec as P


def extended(block, sides, width):
    for axis, dim in sides:
        count = lax.axis_size(axis)
        forward = [(i, i + 1) for i in range(count - 1)]
        backward = [(target, source) for source, target in forward]
        low = lax.ppermute(
            lax.slice_in_dim(block, block.shape[dim] - width, None, axis=dim), axis, forward
        )
        high = lax.ppermute(lax.slice_in_dim(block, 0, width, axis=dim), axis, backward)
        block = jnp.concatenate([low, block, high], axis=dim)
    return block


def fourier_table(length, direction):
    positions = jnp.arange(length, dtype=jnp.int32)
    products = positions[:, None] * positions[None, :] % length
    angles = products.astype(jnp.float32) * (2.0 * jnp.pi / length)
    factor = 1.0 / jnp.sqrt(jnp.float32(length))
    return (jnp.cos(angles) * factor, direction * jnp.sin(angles) * factor)


def row_matrix(length, direction):
    cosine_part, sine_part = fourier_table(length, direction)
    blocks = jnp.stack(
        [jnp.stack([cosine_part, -sine_part], -1), jnp.stack([sine_part, cosine_part], -1)], 1
    )
    return blocks.reshape(2 * length, 2 * length).astype(jnp.bfloat16)


def column_matrix(length, direction):
    cosine_part, sine_part = fourier_table(length, direction)
    blocks = jnp.stack(
        [jnp.stack([cosine_part, sine_part], 1), jnp.stack([-sine_part, cosine_part], 1)], 0
    )
    return blocks.reshape(2 * length, 2 * length).astype(jnp.bfloat16)


def multiply(coil_map, values, conjugate):
    coil_map = coil_map.astype(jnp.float32)
    values = values.astype(jnp.float32)
    map_real, map_imag = (coil_map[..., 0, :], coil_map[..., 1, :])
    value_real, value_imag = (values[..., 0, :], values[..., 1, :])
    if conjugate:
        return jnp.stack(
            [
                map_real * value_real + map_imag * value_imag,
                map_real * value_imag - map_imag * value_real,
            ],
            -2,
        )
    return jnp.stack(
        [
            map_real * value_real - map_imag * value_imag,
            map_real * value_imag + map_imag * value_real,
        ],
        -2,
    )


def along_columns(fields, matrix):
    layout = fields.shape
    flattened = fields.reshape(-1, 2 * layout[-1])
    return jnp.dot(flattened, matrix, preferred_element_type=jnp.float32).reshape(layout)


def along_rows(fields, matrix):
    layout = fields.shape
    flattened = fields.reshape(-1, 2 * layout[-3], layout[-1])
    result = jnp.einsum("ab,nbz->naz", matrix, flattened, preferred_element_type=jnp.float32)
    return result.reshape(layout)


def lift(padded, weights):
    row_count = padded.shape[1] - 2
    line_count = padded.shape[2] - 2
    part_count = padded.shape[4] - 2
    tap_views = [
        padded[
            :,
            row_shift : row_shift + row_count,
            line_shift : line_shift + line_count,
            :,
            part_shift : part_shift + part_count,
        ]
        for row_shift in range(3)
        for line_shift in range(3)
        for part_shift in range(3)
    ]
    stacked = jnp.stack(tap_views, 3)
    stacked = stacked.reshape(stacked.shape[0], row_count, line_count, -1, part_count)
    return jnp.einsum(
        "prlie,io->prloe",
        stacked,
        weights.reshape(-1, weights.shape[-1]),
        preferred_element_type=jnp.float32,
    )


def temporal(hidden, weights):
    phase_count = hidden.shape[0]
    padded = jnp.pad(hidden, ((2, 2), (0, 0), (0, 0), (0, 0), (0, 0)))
    total = hidden.astype(jnp.float32)
    for tap_index in range(3):
        total = total + jnp.einsum(
            "prlie,io->prloe",
            padded[2 * tap_index : 2 * tap_index + phase_count],
            weights[tap_index],
            preferred_element_type=jnp.float32,
        )
    return jax.nn.relu(total).astype(jnp.bfloat16)


def project(edged, weights, base):
    row_count = edged.shape[1] - 2
    line_count = edged.shape[2] - 2
    part_count = edged.shape[4]
    per_tap = jnp.einsum("prlie,tio->prltoe", edged, weights, preferred_element_type=jnp.float32)
    per_tap = jnp.pad(per_tap, ((0, 0), (0, 0), (0, 0), (0, 0), (0, 0), (1, 1)))
    total = base.astype(jnp.float32)
    for row_shift in range(3):
        for line_shift in range(3):
            for part_shift in range(3):
                tap_index = 9 * row_shift + 3 * line_shift + part_shift
                total = (
                    total
                    + per_tap[
                        :,
                        row_shift : row_shift + row_count,
                        line_shift : line_shift + line_count,
                        tap_index,
                        :,
                        part_shift : part_shift + part_count,
                    ]
                )
    return total.astype(jnp.bfloat16)


def cascade(image, coil_maps, measured, sampled, first_w, time_w, last_w, tables):
    forward_rows, forward_columns, inverse_rows, inverse_columns = tables
    coil_image = multiply(coil_maps[:, None], image[None], False).astype(jnp.bfloat16)
    half_done = along_columns(coil_image, forward_columns).astype(jnp.bfloat16)
    spectrum = along_rows(half_done, forward_rows)
    weight = sampled.astype(jnp.float32)[:, :, None, :, None, :]
    mixed = (spectrum + weight * (measured.astype(jnp.float32) - spectrum)).astype(jnp.bfloat16)
    back_half = along_rows(mixed, inverse_rows).astype(jnp.bfloat16)
    restored = along_columns(back_half, inverse_columns)
    terms = jnp.sum(multiply(coil_maps[:, None], restored, True), axis=0)
    summed = lax.psum(terms.astype(jnp.bfloat16), "coil").astype(jnp.float32)
    line_share = summed.shape[2] // lax.axis_size("coil")
    combined = lax.dynamic_slice_in_dim(summed, lax.axis_index("coil") * line_share, line_share, 2)
    combined = combined.astype(jnp.bfloat16)
    padded = extended(combined, (("coil", 2), ("readout", 1)), 1)
    padded = jnp.pad(padded, ((0, 0), (0, 0), (0, 0), (0, 0), (1, 1)))
    hidden = jax.nn.relu(lift(padded, first_w)).astype(jnp.bfloat16)
    mixed_time = temporal(hidden, time_w)
    edged = extended(mixed_time, (("coil", 2), ("readout", 1)), 1)
    return project(edged, last_w, combined)


def per_device(initial, coil_maps, kspace, sampled, first_w, time_w, last_w):
    section_no = lax.axis_index("cascade")
    line_total = kspace.shape[4]
    part_total = kspace.shape[6]
    tables = (
        row_matrix(line_total, -1.0),
        column_matrix(part_total, -1.0),
        row_matrix(line_total, 1.0),
        column_matrix(part_total, 1.0),
    )
    first_all, time_all, last_all = (
        lax.all_gather(first_w, "cascade", axis=0, tiled=True),
        lax.all_gather(time_w, "cascade", axis=0, tiled=True),
        lax.all_gather(last_w, "cascade", axis=0, tiled=True),
    )
    image = lax.dynamic_index_in_dim(initial, section_no, 0, False)
    block_maps = lax.dynamic_index_in_dim(coil_maps, section_no, 0, False)
    block_data = lax.dynamic_index_in_dim(kspace, section_no, 0, False)
    section_outputs = []
    for section_index in range(first_all.shape[0]):
        if section_index > 0:
            image = lax.all_gather(section_outputs[-1], "coil", axis=2, tiled=True)
        output = cascade(
            image,
            block_maps,
            block_data,
            sampled,
            first_all[section_index],
            time_all[section_index],
            last_all[section_index],
            tables,
        )
        section_outputs.append(output)
    stacked = jnp.stack(section_outputs)[:, None]
    return lax.all_to_all(stacked, "cascade", split_axis=0, concat_axis=1, tiled=True)


def solution(mesh):
    in_specs = (
        P(None, None, "readout", None, None, None),
        P(None, "coil", "readout", None, None, None),
        P(None, "coil", None, "readout", None, None, None),
        P("coil", None, None, None),
        P("cascade", None, None, None),
        P("cascade", None, None, None),
        P("cascade", None, None, None),
    )
    out_specs = P("cascade", None, None, "readout", "coil", None, None)
    return jax.shard_map(
        per_device, mesh=mesh, in_specs=in_specs, out_specs=out_specs, check_vma=False
    )
```

profile of v0, /device:TPU:1, one launch (start us, length us, event | category | flops | bytes accessed | tf_op | source)
XLA Modules:
  0.0 489.7 jit_solution(15871532507483083332)
XLA Ops:
  27.5 6.1 %copy.98 = bf16[128,2,128,2]{3,2,1,0:T(8,128)(2,1)} copy(bf16[128,2,128,2]{2,0,3,1:T(8,128)(2,1)S(1)} %get-tuple-element.53) | data formatting | bytes 262144 | tf_op jit(solution)/shard_map/stack | solution.py:30
  33.6 13.1 %reshape.369 = bf16[256,256,1]{1,0,2:T(8,128)(2,1)S(1)} reshape(bf16[128,2,128,2]{3,2,1,0:T(8,128)(2,1)} %copy.98) | data formatting | bytes 262144 | tf_op jit(solution)/shard_map/convert_element_type | solution.py:33
  46.7 6.1 %copy.102 = bf16[128,2,128,2]{3,2,1,0:T(8,128)(2,1)} copy(bf16[128,2,128,2]{2,0,3,1:T(8,128)(2,1)S(1)} %get-tuple-element.54) | data formatting | bytes 262144 | tf_op jit(solution)/shard_map/stack | solution.py:30
  52.9 13.1 %reshape.370 = bf16[256,256,1]{1,0,2:T(8,128)(2,1)S(1)} reshape(bf16[128,2,128,2]{3,2,1,0:T(8,128)(2,1)} %copy.102) | data formatting | bytes 262144 | tf_op jit(solution)/shard_map/convert_element_type | solution.py:33
  66.0 5.4 %constant_dynamic-slice_fusion = bf16[1,4,4,2,128,2,128]{6,5,4,3,2,1,0:T(2,128)(2,1)} fusion(bf16[2,4,4,2,128,2,128]{6,5,4,3,2,1,0:T(2,128)(2,1)} %param.9, s32[]{:T(128)S(6)} %select_n.100), kind=kLoop, calls=%fused_computation.425 | loop fusion | bytes 4194308 | tf_op jit(solution)/shard_map/jit(dynamic_index_in_dim)/dynamic_slice | solution.py:183
  80.9 5.6 %copy.101 = f32[32,256,128]{1,2,0:T(8,128)} copy(f32[32,256,128]{2,1,0:T(8,128)} %bitcast.993) | data formatting | bytes 8388608 | tf_op jit(solution)/shard_map/mul | solution.py:150
  86.6 6.2 %convert_bitcast_fusion.1 = bf16[32,256,128]{1,2,0:T(8,128)(2,1)} fusion(bf16[256,256,1]{1,0,2:T(8,128)(2,1)S(1)} %reshape.370, f32[32,256,128]{1,2,0:T(8,128)} %copy.101, f32[32,256,128]{1,2,0:T(8,128)} %copy.100, bf16[32,256,128]{2,1,0:T(8,128)(2,1)S(1)} %bitcast.1004, bf16[256,256,1]{1,0,2:T(8,128)(2,1)S(1)} %reshape.369), kind=kOutput, calls=%fused_computation.112 | convolution fusion | flops 1078984704 | bytes 12845056 | tf_op jit(solution)/shard_map/ab,nbz->naz/dot_general | solution.py:75
  105.2 39.4 %all-reduce.9.cloned.1.call-done = bf16[4,2,128,2,128]{4,3,2,1,0:T(2,128)(2,1)} async-done(((bf16[4,2,128,2,128]{4,3,2,1,0:T(2,128)(2,1)}), bf16[4,2,128,2,128]{4,3,2,1,0:T(2,128)(2,1)}) %all-reduce.9.cloned.1.call-update) | async-done | bytes 524304 | tf_op jit(solution)/shard_map/psum | solution.py:154
  153.4 6.2 %collective-permute-start.2 = (bf16[4,1,34,2,128]{4,3,2,1,0:T(2,128)(2,1)S(1)}, bf16[4,1,34,2,128]{4,3,2,1,0:T(2,128)(2,1)S(1)}, u32[]{:S(2)}, u32[]{:S(2)}) collective-permute-start(bf16[4,1,34,2,128]{4,3,2,1,0:T(2,128)(2,1)S(1)} %get-tuple-element.33), channel_id=1, source_target_pairs={{0,1},{1,2},{2,3},{4,5},{5,6},{6,7},{8,9},{9,10},{10,11},{12,13},{... | collective-permute-start | bytes 208904 | tf_op jit(solution)/shard_map/ppermute | solution.py:12
  180.5 6.0 %fusion.21 = bf16[4,2,32,64,128]{4,3,2,1,0:T(8,128)(2,1)} fusion(f32[4,2,32,128,64]{3,4,2,1,0:T(8,128)S(1)} %fusion.226, f32[4,2,32,128,64]{3,4,2,1,0:T(8,128)} %fusion.25, bf16[4,2,32,64,128]{4,3,2,1,0:T(8,128)(2,1)S(1)} %fusion.23, bf16[2,3,64,64]{3,2,1,0:T(8,128)(2,1)S(1)} %all_gather.13), kind=kOutput, calls=%fused_computation.68 | convolution fusion | flops 281018368 | bytes 29376512 | tf_op jit(solution)/shard_map/prlie,io->prloe/dot_general | solution.py:110
  202.3 5.4 %collective-permute-start.6 = (bf16[4,1,34,64,128]{4,3,2,1,0:T(8,128)(2,1)S(1)}, bf16[4,1,34,64,128]{4,3,2,1,0:T(8,128)(2,1)S(1)}, u32[]{:S(2)}, u32[]{:S(2)}) collective-permute-start(bf16[4,1,34,64,128]{4,3,2,1,0:T(8,128)(2,1)S(1)} %get-tuple-element.11), channel_id=1, source_target_pairs={{0,1},{1,2},{2,3},{4,5},{5,6},{6,7},{8,9},{9,10},{10,11},{12,13},{... | collective-permute-start | bytes 6684680 | tf_op jit(solution)/shard_map/ppermute | solution.py:12
  213.5 18.5 %collective-permute-done.6 = bf16[4,1,34,64,128]{4,3,2,1,0:T(8,128)(2,1)S(1)} collective-permute-done((bf16[4,1,34,64,128]{4,3,2,1,0:T(8,128)(2,1)S(1)}, bf16[4,1,34,64,128]{4,3,2,1,0:T(8,128)(2,1)S(1)}, u32[]{:S(2)}, u32[]{:S(2)}) %collective-permute-start.6) | collective-permute-done | bytes 2228256 | tf_op jit(solution)/shard_map/ppermute | solution.py:12
  236.4 7.0 %fusion.22 = f32[4,4,34,27,2,128]{5,3,4,2,1,0:T(8,128)} fusion(bf16[4,1,34,64,128]{4,3,2,1,0:T(8,128)(2,1)S(1)} %collective-permute-done.7, bf16[4,2,1,64,128]{4,3,2,1,0:T(8,128)(2,1)S(1)} %collective-permute-done.5, bf16[4,2,32,64,128]{4,3,2,1,0:T(8,128)(2,1)S(1)} %copy-done, bf16[4,2,1,64,128]{4,3,2,1,0:T(8,128)(2,1)S(1)} %collective-permute-done.4, ...), kind=kOutput, calls=%fused_computation.73 | convolution fusion | flops 525860864 | bytes 23960320 | tf_op jit(solution)/shard_map/prlie,tio->prltoe/dot_general | solution.py:123
  243.5 24.9 %copy.113 = f32[4,4,34,27,2,128]{5,4,2,1,0,3:T(2,128)S(1)} copy(f32[4,4,34,27,2,128]{5,3,4,2,1,0:T(8,128)} %fusion.22) | data formatting | bytes 30081024 | tf_op jit(solution)/shard_map/prlie,tio->prltoe/transpose | solution.py:123
  275.3 11.8 %all_gather.15 = bf16[4,2,128,2,128]{4,3,2,1,0:T(2,128)(2,1)S(1)} all-gather(bf16[4,2,32,2,128]{4,3,2,1,0:T(2,128)(2,1)S(1)} %fusion.145), channel_id=1, replica_groups=mesh['cascade'=2,'coil'=4,'readout'=4] {'coil'}, dimensions={2}, use_global_device_ids=true | all-gather | bytes 655360 | tf_op jit(solution)/shard_map/all_gather | solution.py:187
  296.4 6.2 %convert_bitcast_fusion = bf16[32,256,128]{1,2,0:T(8,128)(2,1)} fusion(bf16[256,256,1]{1,0,2:T(8,128)(2,1)S(1)} %reshape.370, f32[32,256,128]{1,2,0:T(8,128)} %copy.101, f32[32,256,128]{1,2,0:T(8,128)} %copy.100, bf16[32,256,128]{2,1,0:T(8,128)(2,1)S(1)} %bitcast.1005, bf16[256,256,1]{1,0,2:T(8,128)(2,1)S(1)} %reshape.369), kind=kOutput, calls=%fused_computation.107 | convolution fusion | flops 1078984704 | bytes 12845056 | tf_op jit(solution)/shard_map/ab,nbz->naz/dot_general | solution.py:75
  312.8 37.6 %all-reduce.11.cloned.1.call-done = bf16[4,2,128,2,128]{4,3,2,1,0:T(2,128)(2,1)} async-done(((bf16[4,2,128,2,128]{4,3,2,1,0:T(2,128)(2,1)}), bf16[4,2,128,2,128]{4,3,2,1,0:T(2,128)(2,1)}) %all-reduce.11.cloned.1.call-update) | async-done | bytes 524304 | tf_op jit(solution)/shard_map/psum | solution.py:154
  358.9 6.2 %collective-permute-start.10 = (bf16[4,1,34,2,128]{4,3,2,1,0:T(2,128)(2,1)S(1)}, bf16[4,1,34,2,128]{4,3,2,1,0:T(2,128)(2,1)S(1)}, u32[]{:S(2)}, u32[]{:S(2)}) collective-permute-start(bf16[4,1,34,2,128]{4,3,2,1,0:T(2,128)(2,1)S(1)} %get-tuple-element.29), channel_id=1, source_target_pairs={{0,1},{1,2},{2,3},{4,5},{5,6},{6,7},{8,9},{9,10},{10,11},{12,13},{... | collective-permute-start | bytes 208904 | tf_op jit(solution)/shard_map/ppermute | solution.py:12
  386.4 5.9 %fusion.19 = bf16[4,2,32,64,128]{4,3,2,1,0:T(8,128)(2,1)} fusion(f32[4,2,32,128,64]{3,4,2,1,0:T(8,128)} %fusion.225, f32[4,2,32,128,64]{3,4,2,1,0:T(8,128)S(1)} %fusion.27, bf16[4,2,32,64,128]{4,3,2,1,0:T(8,128)(2,1)S(1)} %fusion.24, bf16[2,3,64,64]{3,2,1,0:T(8,128)(2,1)S(1)} %copy-done.6), kind=kOutput, calls=%fused_computation.63 | convolution fusion | flops 281018368 | bytes 29376512 | tf_op jit(solution)/shard_map/prlie,io->prloe/dot_general | solution.py:110
  411.2 22.4 %collective-permute-done.14 = bf16[4,1,34,64,128]{4,3,2,1,0:T(8,128)(2,1)S(1)} collective-permute-done((bf16[4,1,34,64,128]{4,3,2,1,0:T(8,128)(2,1)S(1)}, bf16[4,1,34,64,128]{4,3,2,1,0:T(8,128)(2,1)S(1)}, u32[]{:S(2)}, u32[]{:S(2)}) %collective-permute-start.14) | collective-permute-done | bytes 2228256 | tf_op jit(solution)/shard_map/ppermute | solution.py:12
  438.0 7.0 %fusion.9 = f32[4,4,34,128,27,2]{3,4,5,2,1,0:T(8,128)} fusion(bf16[4,1,34,64,128]{4,3,2,1,0:T(8,128)(2,1)S(1)} %collective-permute-done.15, bf16[4,2,1,64,128]{4,3,2,1,0:T(8,128)(2,1)S(1)} %collective-permute-done.13, bf16[4,2,32,64,128]{4,3,2,1,0:T(8,128)(2,1)S(1)} %copy-done.1, bf16[4,2,1,64,128]{4,3,2,1,0:T(8,128)(2,1)S(1)} %collective-permute-done.12, ...), kind=kOutput, calls=%fused_computation.52 | convolution fusion | flops 525860864 | bytes 23960320 | tf_op jit(solution)/shard_map/prlie,tio->prltoe/dot_general | solution.py:123
  445.0 24.9 %copy.189 = f32[4,4,34,128,27,2]{3,5,2,1,0,4:T(2,128)S(1)} copy(f32[4,4,34,128,27,2]{3,4,5,2,1,0:T(8,128)} %fusion.9) | data formatting | bytes 30081024 | tf_op jit(solution)/shard_map/prlie,tio->prltoe/dot_general | solution.py:123
  470.0 5.2 %fusion.202 = bf16[1,4,2,32,2,128]{5,4,3,2,1,0:T(2,128)(2,1)S(1)} fusion(f32[4,4,34,27,2,128]{5,4,2,1,0,3:T(2,128)S(1)} %bitcast.992, bf16[4,2,128,2,128]{4,3,2,1,0:T(2,128)(2,1)S(1)} %copy-done.8, s32[]{:T(128)S(6)} %select_n.103), kind=kLoop, calls=%fused_computation.366 | loop fusion | flops 2031616 | bytes 17661956 | tf_op jit(solution)/shard_map/stack | solution.py:199
  475.5 6.4 %all_to_all.12 = bf16[2,1,4,2,32,2,128]{6,5,4,3,2,1,0:T(2,128)(2,1)S(1)} all-to-all(bf16[2,1,4,2,32,2,128]{6,5,4,3,2,1,0:T(2,128)(2,1)S(1)} %maximum_bitcast_fusion.6), channel_id=1, replica_groups=mesh['cascade'=2,'coil'=4,'readout'=4] {'cascade'}, dimensions={0} | all-to-all | bytes 524288 | tf_op jit(solution)/shard_map/all_to_all | solution.py:200
  (209 shorter events, 178.2 us)
Async XLA Ops:
  6.5 138.1 %all-reduce.9.cloned.1.call-start = ((), (), s32[]{:S(2)}) async-start(), calls=%async_computation.1 | async-start | bytes 1048576 | tf_op jit(solution)/shard_map/psum | solution.py:154
  103.4 46.4 %copy-start.16 = (bf16[1,27,2,64]{3,2,1,0:T(2,128)(2,1)S(1)}, bf16[1,27,2,64]{3,2,1,0:T(2,128)(2,1)}, u32[]{:S(2)}) copy-start(bf16[1,27,2,64]{3,2,1,0:T(2,128)(2,1)} %param.11) | copy-start | bytes 20740
  103.4 58.2 %copy-start.14 = (bf16[1,3,64,64]{3,2,1,0:T(8,128)(2,1)S(1)}, bf16[1,3,64,64]{3,2,1,0:T(8,128)(2,1)}, u32[]{:S(2)}) copy-start(bf16[1,3,64,64]{3,2,1,0:T(8,128)(2,1)} %param.12) | copy-start | bytes 73732
  105.1 245.2 %all-reduce.11.cloned.1.call-start = ((), (), s32[]{:S(2)}) async-start(), calls=%async_computation.2 | async-start | bytes 1048576 | tf_op jit(solution)/shard_map/psum | solution.py:154
  145.7 7.4 %collective-permute-start = (bf16[4,2,1,2,128]{4,3,2,1,0:T(2,128)(2,1)S(1)}, bf16[4,2,1,2,128]{4,3,2,1,0:T(2,128)(2,1)S(1)}, u32[]{:S(2)}, u32[]{:S(2)}) collective-permute-start(bf16[4,2,1,2,128]{4,3,2,1,0:T(2,128)(2,1)S(1)} %get-tuple-element.37), channel_id=1, source_target_pairs={{0,4},{4,8},{8,12},{1,5},{5,9},{9,13},{2,6},{6,10},{10,14},{3,7},{... | collective-permute-start | bytes 12296 | tf_op jit(solution)/shard_map/ppermute | solution.py:12
  148.5 4.6 collective-permute-start.1
  153.4 11.8 %collective-permute-start.2 = (bf16[4,1,34,2,128]{4,3,2,1,0:T(2,128)(2,1)S(1)}, bf16[4,1,34,2,128]{4,3,2,1,0:T(2,128)(2,1)S(1)}, u32[]{:S(2)}, u32[]{:S(2)}) collective-permute-start(bf16[4,1,34,2,128]{4,3,2,1,0:T(2,128)(2,1)S(1)} %get-tuple-element.33), channel_id=1, source_target_pairs={{0,1},{1,2},{2,3},{4,5},{5,6},{6,7},{8,9},{9,10},{10,11},{12,13},{... | collective-permute-start | bytes 208904 | tf_op jit(solution)/shard_map/ppermute | solution.py:12
  159.6 5.6 %collective-permute-start.3 = (bf16[4,1,34,2,128]{4,3,2,1,0:T(2,128)(2,1)S(1)}, bf16[4,1,34,2,128]{4,3,2,1,0:T(2,128)(2,1)S(1)}, u32[]{:S(2)}, u32[]{:S(2)}) collective-permute-start(bf16[4,1,34,2,128]{4,3,2,1,0:T(2,128)(2,1)S(1)} %get-tuple-element.34), channel_id=1, source_target_pairs={{1,0},{2,1},{3,2},{5,4},{6,5},{7,6},{9,8},{10,9},{11,10},{13,12},{... | collective-permute-start | bytes 208904 | tf_op jit(solution)/shard_map/ppermute | solution.py:15
  187.5 6.8 %collective-permute-start.4 = (bf16[4,2,1,64,128]{4,3,2,1,0:T(8,128)(2,1)S(1)}, bf16[4,2,1,64,128]{4,3,2,1,0:T(8,128)(2,1)S(1)}, u32[]{:S(2)}, u32[]{:S(2)}) collective-permute-start(bf16[4,2,1,64,128]{4,3,2,1,0:T(8,128)(2,1)S(1)} %get-tuple-element.15), channel_id=1, source_target_pairs={{0,4},{4,8},{8,12},{1,5},{5,9},{9,13},{2,6},{6,10},{10,14},{3,7},{... | collective-permute-start | bytes 393224 | tf_op jit(solution)/shard_map/ppermute | solution.py:12
  191.8 6.7 %collective-permute-start.5 = (bf16[4,2,1,64,128]{4,3,2,1,0:T(8,128)(2,1)S(1)}, bf16[4,2,1,64,128]{4,3,2,1,0:T(8,128)(2,1)S(1)}, u32[]{:S(2)}, u32[]{:S(2)}) collective-permute-start(bf16[4,2,1,64,128]{4,3,2,1,0:T(8,128)(2,1)S(1)} %get-tuple-element.16), channel_id=1, source_target_pairs={{4,0},{8,4},{12,8},{5,1},{9,5},{13,9},{6,2},{10,6},{14,10},{7,3},{... | collective-permute-start | bytes 393224 | tf_op jit(solution)/shard_map/ppermute | solution.py:15
  201.1 35.3 %copy-start = (bf16[4,2,32,64,128]{4,3,2,1,0:T(8,128)(2,1)S(1)}, bf16[4,2,32,64,128]{4,3,2,1,0:T(8,128)(2,1)}, u32[]{:S(2)}) copy-start(bf16[4,2,32,64,128]{4,3,2,1,0:T(8,128)(2,1)} %fusion.21) | copy-start | bytes 12582916
  202.3 29.7 %collective-permute-start.6 = (bf16[4,1,34,64,128]{4,3,2,1,0:T(8,128)(2,1)S(1)}, bf16[4,1,34,64,128]{4,3,2,1,0:T(8,128)(2,1)S(1)}, u32[]{:S(2)}, u32[]{:S(2)}) collective-permute-start(bf16[4,1,34,64,128]{4,3,2,1,0:T(8,128)(2,1)S(1)} %get-tuple-element.11), channel_id=1, source_target_pairs={{0,1},{1,2},{2,3},{4,5},{5,6},{6,7},{8,9},{9,10},{10,11},{12,13},{... | collective-permute-start | bytes 6684680 | tf_op jit(solution)/shard_map/ppermute | solution.py:12
  207.7 28.8 %collective-permute-start.7 = (bf16[4,1,34,64,128]{4,3,2,1,0:T(8,128)(2,1)S(1)}, bf16[4,1,34,64,128]{4,3,2,1,0:T(8,128)(2,1)S(1)}, u32[]{:S(2)}, u32[]{:S(2)}) collective-permute-start(bf16[4,1,34,64,128]{4,3,2,1,0:T(8,128)(2,1)S(1)} %get-tuple-element.12), channel_id=1, source_target_pairs={{1,0},{2,1},{3,2},{5,4},{6,5},{7,6},{9,8},{10,9},{11,10},{13,12},{... | collective-permute-start | bytes 6684680 | tf_op jit(solution)/shard_map/ppermute | solution.py:15
  350.4 25.3 %copy-start.8 = (bf16[4,2,128,2,128]{4,3,2,1,0:T(2,128)(2,1)S(1)}, bf16[4,2,128,2,128]{4,3,2,1,0:T(2,128)(2,1)}, u32[]{:S(2)}) copy-start(bf16[4,2,128,2,128]{4,3,2,1,0:T(2,128)(2,1)} %all-reduce.11.cloned.1.call-done) | copy-start | bytes 1572868
  351.4 4.1 collective-permute-start.8
  354.3 4.4 collective-permute-start.9
  358.9 8.1 %collective-permute-start.10 = (bf16[4,1,34,2,128]{4,3,2,1,0:T(2,128)(2,1)S(1)}, bf16[4,1,34,2,128]{4,3,2,1,0:T(2,128)(2,1)S(1)}, u32[]{:S(2)}, u32[]{:S(2)}) collective-permute-start(bf16[4,1,34,2,128]{4,3,2,1,0:T(2,128)(2,1)S(1)} %get-tuple-element.29), channel_id=1, source_target_pairs={{0,1},{1,2},{2,3},{4,5},{5,6},{6,7},{8,9},{9,10},{10,11},{12,13},{... | collective-permute-start | bytes 208904 | tf_op jit(solution)/shard_map/ppermute | solution.py:12
  365.1 5.6 %collective-permute-start.11 = (bf16[4,1,34,2,128]{4,3,2,1,0:T(2,128)(2,1)S(1)}, bf16[4,1,34,2,128]{4,3,2,1,0:T(2,128)(2,1)S(1)}, u32[]{:S(2)}, u32[]{:S(2)}) collective-permute-start(bf16[4,1,34,2,128]{4,3,2,1,0:T(2,128)(2,1)S(1)} %get-tuple-element.30), channel_id=1, source_target_pairs={{1,0},{2,1},{3,2},{5,4},{6,5},{7,6},{9,8},{10,9},{11,10},{13,12},{... | collective-permute-start | bytes 208904 | tf_op jit(solution)/shard_map/ppermute | solution.py:15
  393.3 4.9 %collective-permute-start.12 = (bf16[4,2,1,64,128]{4,3,2,1,0:T(8,128)(2,1)S(1)}, bf16[4,2,1,64,128]{4,3,2,1,0:T(8,128)(2,1)S(1)}, u32[]{:S(2)}, u32[]{:S(2)}) collective-permute-start(bf16[4,2,1,64,128]{4,3,2,1,0:T(8,128)(2,1)S(1)} %get-tuple-element.13), channel_id=1, source_target_pairs={{0,4},{4,8},{8,12},{1,5},{5,9},{9,13},{2,6},{6,10},{10,14},{3,7},{... | collective-permute-start | bytes 393224 | tf_op jit(solution)/shard_map/ppermute | solution.py:12
  396.3 5.7 %collective-permute-start.13 = (bf16[4,2,1,64,128]{4,3,2,1,0:T(8,128)(2,1)S(1)}, bf16[4,2,1,64,128]{4,3,2,1,0:T(8,128)(2,1)S(1)}, u32[]{:S(2)}, u32[]{:S(2)}) collective-permute-start(bf16[4,2,1,64,128]{4,3,2,1,0:T(8,128)(2,1)S(1)} %get-tuple-element.14), channel_id=1, source_target_pairs={{4,0},{8,4},{12,8},{5,1},{9,5},{13,9},{6,2},{10,6},{14,10},{7,3},{... | collective-permute-start | bytes 393224 | tf_op jit(solution)/shard_map/ppermute | solution.py:15
  404.7 33.4 %copy-start.1 = (bf16[4,2,32,64,128]{4,3,2,1,0:T(8,128)(2,1)S(1)}, bf16[4,2,32,64,128]{4,3,2,1,0:T(8,128)(2,1)}, u32[]{:S(2)}) copy-start(bf16[4,2,32,64,128]{4,3,2,1,0:T(8,128)(2,1)} %fusion.19) | copy-start | bytes 12582916
  404.7 33.3 %copy-start.15 = (bf16[1,27,64,2]{2,3,1,0:T(2,128)(2,1)S(1)}, bf16[1,27,64,2]{2,3,1,0:T(2,128)(2,1)}, u32[]{:S(2)}) copy-start(bf16[1,27,64,2]{2,3,1,0:T(2,128)(2,1)} %get-tuple-element.47) | copy-start | bytes 20740
  405.8 27.8 %collective-permute-start.14 = (bf16[4,1,34,64,128]{4,3,2,1,0:T(8,128)(2,1)S(1)}, bf16[4,1,34,64,128]{4,3,2,1,0:T(8,128)(2,1)S(1)}, u32[]{:S(2)}, u32[]{:S(2)}) collective-permute-start(bf16[4,1,34,64,128]{4,3,2,1,0:T(8,128)(2,1)S(1)} %get-tuple-element.9), channel_id=1, source_target_pairs={{0,1},{1,2},{2,3},{4,5},{5,6},{6,7},{8,9},{9,10},{10,11},{12,13},{... | collective-permute-start | bytes 6684680 | tf_op jit(solution)/shard_map/ppermute | solution.py:12
  409.3 28.8 %collective-permute-start.15 = (bf16[4,1,34,64,128]{4,3,2,1,0:T(8,128)(2,1)S(1)}, bf16[4,1,34,64,128]{4,3,2,1,0:T(8,128)(2,1)S(1)}, u32[]{:S(2)}, u32[]{:S(2)}) collective-permute-start(bf16[4,1,34,64,128]{4,3,2,1,0:T(8,128)(2,1)S(1)} %get-tuple-element.10), channel_id=1, source_target_pairs={{1,0},{2,1},{3,2},{5,4},{6,5},{7,6},{9,8},{10,9},{11,10},{13,12},{... | collective-permute-start | bytes 6684680 | tf_op jit(solution)/shard_map/ppermute | solution.py:15
  (12 other events, 77.1 us)
Sparse Core Ops, SparseCore 0:
  105.3 39.3 all-reduce.8
  312.9 37.3 all-reduce.10
where the time goes:
time: 497 us; the launch traced here: 490 us
  local copies, waits for them, and re-layouts  160 us (32%)
  waiting for transfers between devices  143 us (29%)
  matrix products  57.8 us (12%)
  starting transfers between devices  46.9 us (9%)
  other arithmetic  38.2 us (8%)
  blocking collectives  28.4 us (6%)
  between operations  14.7 us (3%)
    psum x2, waiting for transfers between devices, cascade(): summed = lax.psum(terms.astype(jnp.bfloat16), 'coil').astype(jnp.float32)  77 us
    ppermute x8, waiting for transfers between devices, extended(): lax.ppermute(lax.slice_in_dim(block, block.shape[dim] - width, None, axis...  42.9 us
    ppermute x8, starting transfers between devices, extended(): lax.ppermute(lax.slice_in_dim(block, block.shape[dim] - width, None, axis...  34 us
    convert_element_type x2, local copies, waits for them, and re-layouts, row_matrix(): return blocks.reshape(2 * length, 2 * length).astype(jnp.bfloat16)  26.2 us
    transpose x1, local copies, waits for them, and re-layouts, project(): jnp.einsum('prlie,tio->prltoe', edged, weights, preferred_element_type=jn...  24.9 us
    dot_general x1, local copies, waits for them, and re-layouts, project(): jnp.einsum('prlie,tio->prltoe', edged, weights, preferred_element_type=jn...  24.9 us
    ppermute x8, waiting for transfers between devices, extended(): lax.ppermute(lax.slice_in_dim(block, 0, width, axis=dim), axis, backward)  23.4 us
    dot_general x6, matrix products, temporal(): jnp.einsum('prlie,io->prloe', padded[2 * tap_index:2 * tap_index + phase_...  23.2 us
  transfers between devices with their start and end apart: 18, of which 12 were waited for; matrix products, arithmetic and copies ran while one was open for 0% of the time, Pallas kernels for 0%

commit v1 on v0

v1 whole, which is shorter than its diff:
```python
import functools

import jax
import jax.numpy as jnp
import numpy as np
from jax import lax
from jax.experimental import pallas as pl
from jax.experimental.pallas import tpu as pltpu
from jax.sharding import PartitionSpec as P

F32 = jnp.float32
BF16 = jnp.bfloat16
HALO = 2
VMEM_LIMIT = 48 * 1024 * 1024


def fourier_pair(length):
    positions = np.arange(length, dtype=np.int64)
    angles = (positions[:, None] * positions[None, :] % length) * (2.0 * np.pi / length)
    factor = 1.0 / np.sqrt(float(length))
    return np.cos(angles) * factor, np.sin(angles) * factor


def times_i(length):
    turn = np.zeros((2 * length, 2 * length))
    even = 2 * np.arange(length)
    turn[even, even + 1] = -1.0
    turn[even + 1, even] = 1.0
    return turn


def row_matrix(length, direction):
    cosine, sine = fourier_pair(length)
    sine = direction * sine
    return np.stack([np.stack([cosine, -sine], -1), np.stack([sine, cosine], -1)], 1).reshape(
        2 * length, 2 * length
    )


def bf16(values):
    return jnp.asarray(values.astype(jnp.bfloat16))


@functools.lru_cache(maxsize=None)
def consistency_tables(line_total, part_total, phases, share):
    cosine, sine = fourier_pair(part_total)
    turn = times_i(line_total)
    forward, inverse = row_matrix(line_total, -1.0), row_matrix(line_total, 1.0)
    duplicate = np.repeat(np.eye(line_total), 2, axis=0)
    even = np.zeros((line_total, 2 * line_total))
    even[np.arange(line_total), 2 * np.arange(line_total)] = 1.0
    odd = np.roll(even, 1, axis=1)
    return (
        np.concatenate([cosine, sine], 1),
        np.concatenate([forward, -forward @ turn], 1),
        np.concatenate([inverse, turn @ inverse], 0),
        np.block([[cosine, -sine], [sine, cosine]]),
        np.concatenate([duplicate @ even, duplicate @ odd], 0),
        turn,
        duplicate,
        phase_inside(phases, share),
    )


def phase_inside(phases, share):
    rows = np.arange(phases * share * 2).reshape(phases, share, 2).transpose(1, 0, 2).reshape(-1)
    return np.eye(phases * share * 2)[rows]


def dot(left, right):
    return jnp.dot(left, right, preferred_element_type=F32)


def consistency_kernel(info, *refs, pieces, shares, coils, phases, share_rows, edge):
    images, refs = refs[:pieces], refs[pieces:]
    maps, samples, mask, cs, af, gg, ww, dd, turn, dup, inside = refs[:11]
    outs = refs[11 : 11 + shares]
    image_now, image_turned, total, window = refs[11 + shares :]
    coil = pl.program_id(1)
    me = info[1]
    part = maps.shape[-1]
    rows = maps.shape[-2]
    lanes = [slice(p * part, (p + 1) * part) for p in range(phases)]

    @pl.when(coil == 0)
    def _():
        if pieces == 1:
            image = jnp.concatenate([images[0][0, p, 0] for p in range(phases)], 1)
        else:
            joined = total
            for k in range(pieces):
                start = pl.multiple_of(lax.rem(me + (pieces - k), pieces) * share_rows, share_rows)
                for p in range(phases):
                    joined[pl.ds(start, share_rows), lanes[p]] = images[k][p, 0].astype(F32)
            image = joined[...].astype(BF16)
        image_now[...] = image.astype(F32)
        image_turned[...] = dot(turn[...], image)
        total[...] = jnp.zeros_like(total)

    both = dot(dd[...], maps[0, 0, 0])
    map_real, map_imag = both[:rows], both[rows:]
    fields = [
        (map_real * image_now[:, lanes[p]] + map_imag * image_turned[:, lanes[p]]).astype(BF16)
        for p in range(phases)
    ]
    halves = dot(jnp.concatenate(fields, 0), cs[...]).astype(BF16)
    stacked = jnp.concatenate(
        [
            jnp.concatenate(
                [halves[p * rows : (p + 1) * rows, :part], halves[p * rows : (p + 1) * rows, part:]], 0
            )
            for p in range(phases)
        ],
        1,
    )
    spectrum = dot(af[...], stacked)
    acquired = dot(
        dup[...], jnp.concatenate([mask[0, p].astype(F32).astype(BF16) for p in range(phases)], 1)
    )
    measured = jnp.concatenate([samples[0, 0, p, 0] for p in range(phases)], 1).astype(F32)
    mixed = jnp.where(acquired > 0.5, measured, spectrum).astype(BF16)
    back = dot(gg[...], mixed).astype(BF16)
    paired = jnp.concatenate(
        [jnp.concatenate([back[:rows, lanes[p]], back[rows:, lanes[p]]], 1) for p in range(phases)], 0
    )
    restored = dot(paired, ww[...])
    for p in range(phases):
        field = restored[p * rows : (p + 1) * rows]
        total[:, lanes[p]] += map_real * field[:, :part] - map_imag * field[:, part:]

    @pl.when(coil == coils - 1)
    def _():
        summed = total[...].astype(BF16)
        blocks = jnp.concatenate(
            [
                jnp.concatenate(
                    [summed[k * share_rows : (k + 1) * share_rows, lanes[p]] for p in range(phases)], 0
                )
                for k in range(shares)
            ],
            1,
        )
        ordered = dot(inside[...], blocks).astype(BF16)
        width = phases * share_rows
        border = jnp.zeros((edge, part), BF16)
        window[0:edge] = border
        window[edge + shares * width : 2 * edge + shares * width] = border
        for k in range(shares):
            window[edge + k * width : edge + (k + 1) * width] = ordered[:, k * part : (k + 1) * part]
        for k in range(shares):
            start = pl.multiple_of(lax.rem(me + k, shares) * width, width)
            outs[k][0] = window[pl.ds(start, width + 2 * edge)]


def consistency(info, images, maps, samples, mask, shares):
    blocks, coils, phases, readouts, rows, part = samples.shape
    lines = rows // 2
    share_rows = rows // shares
    edge = HALO * phases * 2
    tables = tuple(bf16(t) for t in consistency_tables(lines, part, phases, lines // shares))
    pieces = len(images)
    if pieces == 1:
        image_specs = [
            pl.BlockSpec((1, phases, 1, rows, part), lambda r, j, info: (info[0], 0, r, 0, 0))
        ]
    else:
        image_specs = [
            pl.BlockSpec((phases, 1, share_rows, part), lambda r, j, info: (0, r, 0, 0))
        ] * pieces
    fixed = [pl.BlockSpec(t.shape, lambda r, j, info: (0, 0)) for t in tables]
    width = phases * share_rows + 2 * edge
    body = functools.partial(
        consistency_kernel,
        pieces=pieces,
        shares=shares,
        coils=coils,
        phases=phases,
        share_rows=share_rows,
        edge=edge,
    )
    return pl.pallas_call(
        body,
        grid_spec=pltpu.PrefetchScalarGridSpec(
            num_scalar_prefetch=1,
            grid=(readouts, coils),
            in_specs=image_specs
            + [
                pl.BlockSpec((1, 1, 1, rows, part), lambda r, j, info: (info[0], j, r, 0, 0)),
                pl.BlockSpec(
                    (1, 1, phases, 1, rows, part), lambda r, j, info: (info[0], j, 0, r, 0, 0)
                ),
                pl.BlockSpec((1, phases, lines, part), lambda r, j, info: (j, 0, 0, 0)),
            ]
            + fixed,
            out_specs=[pl.BlockSpec((1, width, part), lambda r, j, info: (r, 0, 0))] * shares,
            scratch_shapes=[
                pltpu.VMEM((rows, phases * part), F32),
                pltpu.VMEM((rows, phases * part), F32),
                pltpu.VMEM((rows, phases * part), F32),
                pltpu.VMEM((shares * phases * share_rows + 2 * edge, part), BF16),
            ],
        ),
        out_shape=[jax.ShapeDtypeStruct((readouts, width, part), BF16)] * shares,
        compiler_params=pltpu.CompilerParams(vmem_limit_bytes=VMEM_LIMIT),
        cost_estimate=pl.CostEstimate(
            flops=readouts * coils * phases * rows * part * rows * 20,
            bytes_accessed=8 * 1024 * 1024,
            transcendentals=0,
        ),
        name="consistency",
    )(info, *images, maps, samples, mask, *tables)


def tap_rows(phases, parts):
    rows = []
    for row_shift in range(3):
        for tap in range(9):
            for phase in range(phases):
                for piece in range(parts):
                    rows.append(((9 * row_shift + tap) * parts + piece, phase))
        rows += [(-1, -1)] * (-(9 * phases * parts) % 16)
    return rows


@functools.lru_cache(maxsize=None)
def weight_tables(phases, channels):
    rows = tap_rows(phases, 2)
    spread = np.zeros((len(rows), 64))
    own_phase = np.zeros((len(rows), phases * channels))
    for index, (source, phase) in enumerate(rows):
        if source >= 0:
            spread[index, source] = 1.0
            own_phase[index, phase * channels : (phase + 1) * channels] = 1.0
    tiled = np.tile(np.eye(channels), (1, phases))
    phase_of = np.repeat(np.arange(phases), channels)
    time_masks = np.stack(
        [phase_of[None, :] - phase_of[:, None] == 2 * (k - 1) for k in range(3)]
    ).astype(np.float64)
    return spread, own_phase, tiled, time_masks


def weights_kernel(info, *refs, pieces):
    packs = refs[:pieces]
    spread, spread_t, own_phase, own_phase_t, tiled, tiled_t, time_masks = refs[pieces : pieces + 7]
    first_out, time_out, last_out = refs[pieces + 7 :]
    channels = tiled.shape[0]
    pick = lax.rem(info[0] - pl.program_id(0) + pieces, pieces)
    pack = packs[0][...].astype(F32)
    for k in range(1, pieces):
        pack = jnp.where(pick == k, packs[k][...].astype(F32), pack)
    pack = pack.astype(BF16)

    def transposed(block):
        return lax.dot_general(
            tiled_t[...], block, (((1,), (1,)), ((), ())), preferred_element_type=F32
        ).astype(BF16)

    time = 0.0
    for k in range(3):
        block = transposed(pack[k * channels : (k + 1) * channels])
        time = time + dot(block, tiled[...]) * time_masks[k].astype(F32)
    time_out[0] = time.astype(BF16)
    first = transposed(pack[3 * channels : 3 * channels + 64])
    first_out[0] = (dot(first, spread_t[...]) * own_phase_t[...].astype(F32)).astype(BF16)
    last = dot(spread[...], pack[3 * channels + 64 :]).astype(BF16)
    last_out[0] = (dot(last, tiled[...]) * own_phase[...].astype(F32)).astype(BF16)


def weight_matrices(info, packs, phases):
    sections = len(packs)
    channels = packs[0].shape[1]
    spread, own_phase, tiled, time_masks = weight_tables(phases, channels)
    tables = [
        bf16(t) for t in (spread, spread.T, own_phase, own_phase.T, tiled, tiled.T, time_masks)
    ]
    wide = phases * channels
    taps = spread.shape[0]
    shapes = [(wide, taps), (wide, wide), (taps, wide)]
    return pl.pallas_call(
        functools.partial(weights_kernel, pieces=sections),
        grid_spec=pltpu.PrefetchScalarGridSpec(
            num_scalar_prefetch=1,
            grid=(sections,),
            in_specs=[pl.BlockSpec(p.shape, lambda s, info: (0, 0)) for p in packs]
            + [
                pl.BlockSpec(t.shape, functools.partial(lambda n, s, info: (0,) * n, t.ndim))
                for t in tables
            ],
            out_specs=[pl.BlockSpec((1,) + s, lambda s, info: (s, 0, 0)) for s in shapes],
        ),
        out_shape=[jax.ShapeDtypeStruct((sections,) + s, BF16) for s in shapes],
        compiler_params=pltpu.CompilerParams(vmem_limit_bytes=VMEM_LIMIT),
        cost_estimate=pl.CostEstimate(
            flops=sections * wide * wide * 1000, bytes_accessed=2 * 1024 * 1024, transcendentals=0
        ),
        name="weights",
    )(info, *packs, *tables)


def shifted(values, step):
    part = values.shape[1]
    lane = lax.broadcasted_iota(jnp.int32, values.shape, 1)
    if step > 0:
        return jnp.where(lane == 0, 0.0, pltpu.roll(values, 1, 1))
    return jnp.where(lane == part - 1, 0.0, pltpu.roll(values, part - 1, 1))


def denoise_kernel(info, own, low, high, first, time, last, apart, out, taps, sums, *, phases, chunk):
    step = pl.program_id(0)
    steps = pl.num_programs(0)
    readouts, span, part = own.shape
    cell = 2 * phases
    lines = span // cell
    group = taps.shape[2]
    used = 9 * cell

    @pl.when(step == 0)
    def _():
        slabs = (
            [low[readouts - HALO + k] for k in range(HALO)]
            + [own[k] for k in range(readouts)]
            + [high[k] for k in range(HALO)]
        )
        filler = [jnp.zeros((group - used, part), F32)] if group > used else []
        for index, slab in enumerate(slabs):
            slab = slab.astype(F32)
            views = [shifted(slab, 1), slab, shifted(slab, -1)]
            for line in range(1, lines - 1):
                around = [
                    views[e][cell * (line + c - 1) : cell * (line + c)]
                    for c in range(3)
                    for e in range(3)
                ]
                taps[index, line - 1] = jnp.concatenate(around + filler, 0).astype(BF16)
        sums[...] = jnp.zeros_like(sums)

    inside = jnp.where(step == 0, info[2], jnp.where(step == steps - 1, info[3], 1))

    @pl.when(inside == 1)
    def _():
        for begin in range(1, lines - 1, chunk):
            block = range(begin, min(begin + chunk, lines - 1))
            near = jnp.concatenate(
                [taps[pl.ds(step, 3), line - 1].reshape(3 * group, part) for line in block], 1
            )
            hidden = jnp.maximum(dot(first[0], near), 0.0).astype(BF16)
            mixed = jnp.maximum(hidden.astype(F32) + dot(time[0], hidden), 0.0).astype(BF16)
            pieces = [mixed[:, k * part : (k + 1) * part] for k in range(len(block))]
            if block[0] == 1:
                pieces[0] = pieces[0] * info[4].astype(F32).astype(BF16)
            if block[-1] == lines - 2:
                pieces[-1] = pieces[-1] * info[5].astype(F32).astype(BF16)
            mixed = jnp.concatenate(pieces, 1)
            result = dot(last[0], mixed)
            for a in range(3):
                target = step + 2 - a
                for e in range(3):
                    for line in range(block[0] - 1, block[-1] + 2):
                        terms = []
                        for c in range(3):
                            source = line + c - 1
                            if block[0] <= source <= block[-1]:
                                at = a * group + (3 * c + e) * cell
                                k = source - block[0]
                                terms.append(result[at : at + cell, k * part : (k + 1) * part])
                        sums[e, target, line * cell : (line + 1) * cell] += sum(terms[1:], terms[0])

    @pl.when(step == steps - 1)
    def _():
        body = slice(HALO * cell, span - HALO * cell)
        finals = []
        for r in range(readouts):
            value = own[r, body].astype(F32) + sums[1, r + HALO, body]
            value = value + shifted(sums[0, r + HALO, body], 1)
            value = value + shifted(sums[2, r + HALO, body], -1)
            finals.append(value.astype(BF16))
        ordered = dot(apart[...], jnp.concatenate(finals, 1)).astype(BF16)
        height = out.shape[2]
        for p in range(phases):
            for r in range(readouts):
                out[p, r] = ordered[p * height : (p + 1) * height, r * part : (r + 1) * part]


def denoise(info, own, low, high, matrices, section, phases):
    readouts, span, part = own.shape
    cell = 2 * phases
    lines = span // cell
    share = lines - 2 * HALO
    first, time, last = matrices
    apart = bf16(phase_inside(phases, share).T)
    group = first.shape[2] // 3
    whole = pl.BlockSpec((readouts, span, part), lambda s, info: (0, 0, 0))
    return pl.pallas_call(
        functools.partial(denoise_kernel, phases=phases, chunk=17),
        grid_spec=pltpu.PrefetchScalarGridSpec(
            num_scalar_prefetch=1,
            grid=(readouts + 2,),
            in_specs=[whole] * 3
            + [pl.BlockSpec((1,) + w.shape[1:], lambda s, info: (section, 0, 0)) for w in matrices]
            + [pl.BlockSpec(apart.shape, lambda s, info: (0, 0))],
            out_specs=pl.BlockSpec((phases, readouts, 2 * share, part), lambda s, info: (0, 0, 0, 0)),
            scratch_shapes=[
                pltpu.VMEM((readouts + 2 * HALO, lines - 2, group, part), BF16),
                pltpu.VMEM((3, readouts + 2 * HALO, span, part), F32),
            ],
        ),
        out_shape=jax.ShapeDtypeStruct((phases, readouts, 2 * share, part), BF16),
        compiler_params=pltpu.CompilerParams(vmem_limit_bytes=VMEM_LIMIT),
        cost_estimate=pl.CostEstimate(
            flops=6 * (readouts + 2) * lines * part * 256 * 256,
            bytes_accessed=2 * 1024 * 1024,
            transcendentals=0,
        ),
        name="denoise",
    )(info, own, low, high, first, time, last, apart)


def rotation(count, step):
    return [(i, (i + step) % count) for i in range(count)]


def per_device(initial, coil_maps, kspace, sampled, first_w, time_w, last_w):
    section_no = lax.axis_index("cascade")
    sections = lax.axis_size("cascade")
    coil_no = lax.axis_index("coil")
    shares = lax.axis_size("coil")
    readout_no = lax.axis_index("readout")
    readout_parts = lax.axis_size("readout")
    phases = kspace.shape[2]
    part = kspace.shape[-1]
    channels = first_w.shape[-1]

    def rows_of(array):
        return array.reshape(array.shape[:-3] + (2 * array.shape[-3], part))

    initial, coil_maps, kspace = rows_of(initial), rows_of(coil_maps), rows_of(kspace)
    info = jnp.stack(
        [
            section_no,
            coil_no,
            readout_no > 0,
            readout_no < readout_parts - 1,
            coil_no > 0,
            coil_no < shares - 1,
        ]
    ).astype(jnp.int32)

    def padded(block):
        return jnp.pad(block, ((0, -block.shape[0] % 64), (0, 0)))

    pack = jnp.concatenate(
        [
            time_w[0].reshape(-1, channels),
            padded(first_w[0].reshape(-1, channels)),
            padded(jnp.swapaxes(last_w[0], 1, 2).reshape(-1, channels)),
        ],
        0,
    )
    packs = [pack] + [
        lax.ppermute(pack, "cascade", rotation(sections, k)) for k in range(1, sections)
    ]
    matrices = None
    images = [initial]
    outputs = []
    for section in range(sections):
        shares_out = consistency(info, images, coil_maps, kspace, sampled, shares)
        if matrices is None:
            packs, shares_out = lax.optimization_barrier((packs, shares_out))
        parts = [shares_out[0]] + [
            lax.ppermute(shares_out[k], "coil", rotation(shares, k)) for k in range(1, shares)
        ]
        if matrices is None:
            matrices = weight_matrices(info, packs, phases)
        combined = sum(p.astype(F32) for p in parts).astype(BF16)
        forward = [(i, i + 1) for i in range(readout_parts - 1)]
        backward = [(target, source) for source, target in forward]
        low = lax.ppermute(combined, "readout", forward)
        high = lax.ppermute(combined, "readout", backward)
        output = denoise(info, combined, low, high, matrices, section, phases)
        outputs.append(output)
        if section < sections - 1:
            images = [output] + [
                lax.ppermute(output, "coil", rotation(shares, k)) for k in range(1, shares)
            ]

    stacked = jnp.stack(outputs)
    placed = [lax.dynamic_index_in_dim(stacked, section_no, 0, False)]
    for k in range(1, sections):
        piece = lax.dynamic_index_in_dim(stacked, (section_no + k) % sections, 0, False)
        placed.append(lax.ppermute(piece, "cascade", rotation(sections, k)))
    arrived = []
    for block in range(sections):
        value = placed[0]
        for k in range(1, sections):
            value = jnp.where((section_no - block) % sections == k, placed[k], value)
        arrived.append(value)
    result = jnp.stack(arrived)[None]
    return result.reshape(result.shape[:-2] + (result.shape[-2] // 2, 2, part))


def solution(mesh):
    in_specs = (
        P(None, None, "readout", None, None, None),
        P(None, "coil", "readout", None, None, None),
        P(None, "coil", None, "readout", None, None, None),
        P("coil", None, None, None),
        P("cascade", None, None, None),
        P("cascade", None, None, None),
        P("cascade", None, None, None),
    )
    out_specs = P("cascade", None, None, "readout", "coil", None, None)
    return jax.shard_map(
        per_device, mesh=mesh, in_specs=in_specs, out_specs=out_specs, check_vma=False
    )
```

time: 497 us -> 126 us (0.25); the launches traced: 490 us -> 125 us
  local copies, waits for them, and re-layouts: 160 us -> 12.6 us
  waiting for transfers between devices: 143 us -> 33.9 us
  matrix products: 57.8 us -> 0 us
  Pallas kernels: 0 us -> 49.5 us
  other arithmetic: 38.2 us -> 2.19 us
  blocking collectives: 28.4 us -> 0 us
  starting transfers between devices: 46.9 us -> 26.8 us
  between operations: 14.7 us -> 0.37 us
    psum x2 -> x0, waiting for transfers between devices: 77 us -> none  [cascade(): summed = lax.psum(terms.astype(jnp.bfloat16), 'coil').astype(jnp.float32)]
    dot_general x16 -> x0, matrix products: 57.8 us -> none  [the longest x6 23.2 us: temporal(): jnp.einsum('prlie,io->prloe', padded[2 * tap_index:2 * tap_index + phase_...]
    convert_element_type x10 -> x0, local copies, waits for them, and re-layouts: 52.2 us -> none  [the longest x2 26.2 us: row_matrix(): return blocks.reshape(2 * length, 2 * length).astype(jnp.bfloat16)]
    pallas_call x0 -> x5, Pallas kernels: none -> 49.5 us  [the longest x2 28.2 us: consistency(): pl.pallas_call(body, grid_spec=pltpu.PrefetchScalarGridSpec(num_scalar_pr...]
    ppermute x16 -> x15, waiting for transfers between devices: 66.3 us -> 33.9 us  [the longest x6 18.7 us: per_device(): lax.ppermute(shares_out[k], 'coil', rotation(shares, k))]
    dot_general x3 -> x0, local copies, waits for them, and re-layouts: 26 us -> none  [the longest x1 24.9 us: project(): jnp.einsum('prlie,tio->prltoe', edged, weights, preferred_element_type=jn...]
    transpose x1 -> x0, local copies, waits for them, and re-layouts: 24.9 us -> none  [project(): jnp.einsum('prlie,tio->prltoe', edged, weights, preferred_element_type=jn...]
    all_gather x4 -> x0, blocking collectives: 22 us -> none  [the longest x1 11.8 us: per_device(): image = lax.all_gather(section_outputs[-1], 'coil', axis=2, tiled=True)]
  transfers between devices with their start and end apart: 18 -> 15, of which waited for: 12 -> 10; matrix products, arithmetic and copies ran while one was open for 0% -> 0% of each run, Pallas kernels for 0% -> 13%
where the time goes in v1:
time: 126 us; the launch traced here: 125 us
  Pallas kernels  49.5 us (39%)
  waiting for transfers between devices  33.9 us (27%)
  starting transfers between devices  26.8 us (21%)
  local copies, waits for them, and re-layouts  12.6 us (10%)
  other arithmetic  2.19 us (2%)
    pallas_call x2, Pallas kernels, consistency(): pl.pallas_call(body, grid_spec=pltpu.PrefetchScalarGridSpec(num_scalar_pr...  28.2 us
    pallas_call x2, Pallas kernels, denoise(): pl.pallas_call(functools.partial(denoise_kernel, phases=phases, chunk=17)...  19.2 us
    ppermute x6, waiting for transfers between devices, per_device(): lax.ppermute(shares_out[k], 'coil', rotation(shares, k))  18.7 us
    unnamed x58, local copies, waits for them, and re-layouts  11 us
    ppermute x6, starting transfers between devices, per_device(): lax.ppermute(shares_out[k], 'coil', rotation(shares, k))  8.6 us
    ppermute x2, waiting for transfers between devices, per_device(): high = lax.ppermute(combined, 'readout', backward)  6.76 us
    ppermute x2, starting transfers between devices, per_device(): low = lax.ppermute(combined, 'readout', forward)  6.37 us
    ppermute x3, starting transfers between devices, per_device(): lax.ppermute(output, 'coil', rotation(shares, k))  5.56 us
  transfers between devices with their start and end apart: 15, of which 10 were waited for; matrix products, arithmetic and copies ran while one was open for 0% of the time, Pallas kernels for 13%

profile of v1, /device:TPU:1, one launch (start us, length us, event | category | flops | bytes accessed | tf_op | source)
XLA Modules:
  0.0 125.3 jit_solution(8185655551230650103)
XLA Ops:
  2.3 2.1 %collective-permute-start = (bf16[320,64]{1,0:T(8,128)(2,1)S(1)}, bf16[320,64]{1,0:T(8,128)(2,1)S(1)}, u32[]{:S(2)}, u32[]{:S(2)}) collective-permute-start(bf16[320,64]{1,0:T(8,128)(2,1)S(1)} %fusion.8.refs_0_), channel_id=1, source_target_pairs={{0,16},{16,0},{1,17},{17,1},{2,18},{18,2},{3,19},{19,3},{4,20},{20... | collective-permute-start | bytes 122888 | tf_op jit(solution)/shard_map/ppermute | solution.py:460
  15.5 14.0 %consistency.2 = (bf16[2,288,128]{2,1,0:T(8,128)(2,1)S(1)}, bf16[2,288,128]{2,1,0:T(8,128)(2,1)S(1)}, bf16[2,288,128]{2,1,0:T(8,128)(2,1)S(1)}, bf16[2,288,128]{2,1,0:T(8,128)(2,1)S(1)}) custom-call(s32[6]{0:T(128)S(1)} %stack.61.info, bf16[2,4,2,256,128]{4,3,2,1,0:T(8,128)(2,1)S(1)} %bitcast.29, bf16[2,4,2,256,128]{4,3,2,1,0:T(8,128)(2,1)S(1)} %bitcast.30, ...), custom_call_target="tpu_custom_call" | custom-call | flops 5368709120 | bytes 8388608 | tf_op jit(solution)/shard_map/consistency/pallas_call | solution.py:181
  29.5 1.4 %collective-permute-start.1 = (bf16[2,288,128]{2,1,0:T(8,128)(2,1)S(1)}, bf16[2,288,128]{2,1,0:T(8,128)(2,1)S(1)}, u32[]{:S(2)}, u32[]{:S(2)}) collective-permute-start(bf16[2,288,128]{2,1,0:T(8,128)(2,1)S(1)} %get-tuple-element.27), channel_id=1, source_target_pairs={{0,4},{4,8},{8,12},{12,0},{1,5},{5,9},{9,13},{13,1},{2,6},{6,10},{... | collective-permute-start | bytes 442376 | tf_op jit(solution)/shard_map/ppermute | solution.py:470
  30.9 2.3 %collective-permute-start.2 = (bf16[2,288,128]{2,1,0:T(8,128)(2,1)S(1)}, bf16[2,288,128]{2,1,0:T(8,128)(2,1)S(1)}, u32[]{:S(2)}, u32[]{:S(2)}) collective-permute-start(bf16[2,288,128]{2,1,0:T(8,128)(2,1)S(1)} %get-tuple-element.28), channel_id=1, source_target_pairs={{0,8},{4,12},{8,0},{12,4},{1,9},{5,13},{9,1},{13,5},{2,10},{6,14},... | collective-permute-start | bytes 442376 | tf_op jit(solution)/shard_map/ppermute | solution.py:470
  34.3 1.7 %collective-permute-done.1 = bf16[2,288,128]{2,1,0:T(8,128)(2,1)S(1)} collective-permute-done((bf16[2,288,128]{2,1,0:T(8,128)(2,1)S(1)}, bf16[2,288,128]{2,1,0:T(8,128)(2,1)S(1)}, u32[]{:S(2)}, u32[]{:S(2)}) %collective-permute-start.1) | collective-permute-done | bytes 147488 | tf_op jit(solution)/shard_map/ppermute | solution.py:470
  36.0 7.6 %collective-permute-done.2 = bf16[2,288,128]{2,1,0:T(8,128)(2,1)S(1)} collective-permute-done((bf16[2,288,128]{2,1,0:T(8,128)(2,1)S(1)}, bf16[2,288,128]{2,1,0:T(8,128)(2,1)S(1)}, u32[]{:S(2)}, u32[]{:S(2)}) %collective-permute-start.2) | collective-permute-done | bytes 147488 | tf_op jit(solution)/shard_map/ppermute | solution.py:470
  43.6 3.6 %collective-permute-start.4 = (bf16[2,288,128]{2,1,0:T(8,128)(2,1)S(1)}, bf16[2,288,128]{2,1,0:T(8,128)(2,1)S(1)}, u32[]{:S(2)}, u32[]{:S(2)}) collective-permute-start(bf16[2,288,128]{2,1,0:T(8,128)(2,1)S(1)} %add_convert_fusion.1.own), channel_id=1, source_target_pairs={{0,1},{1,2},{2,3},{4,5},{5,6},{6,7},{8,9},{9,10},{10,11},{12,13},{... | collective-permute-start | bytes 442376 | tf_op jit(solution)/shard_map/ppermute | solution.py:477
  47.2 1.9 %collective-permute-start.5 = (bf16[2,288,128]{2,1,0:T(8,128)(2,1)S(1)}, bf16[2,288,128]{2,1,0:T(8,128)(2,1)S(1)}, u32[]{:S(2)}, u32[]{:S(2)}) collective-permute-start(bf16[2,288,128]{2,1,0:T(8,128)(2,1)S(1)} %add_convert_fusion.1.own), channel_id=1, source_target_pairs={{1,0},{2,1},{3,2},{5,4},{6,5},{7,6},{9,8},{10,9},{11,10},{13,12},{... | collective-permute-start | bytes 442376 | tf_op jit(solution)/shard_map/ppermute | solution.py:478
  49.2 2.1 %weights.1 = (bf16[2,256,240]{2,1,0:T(8,128)(2,1)S(1)}, bf16[2,256,256]{2,1,0:T(8,128)(2,1)S(1)}, bf16[2,240,256]{2,1,0:T(8,128)(2,1)S(1)}) custom-call(s32[6]{0:T(128)S(1)} %stack.61.info, bf16[320,64]{1,0:T(8,128)(2,1)S(1)} %fusion.8.refs_0_, bf16[320,64]{1,0:T(8,128)(2,1)S(1)} %collective-permute-done.refs_1_, bf16[240,64]{1,0:T(8,128)(2,1)S(1)} %copy-done.4, ...), custom_call_target="tpu_custom_call" | custom-call | flops 131072000 | bytes 2097152 | tf_op jit(solution)/shard_map/weights/pallas_call | solution.py:279
  51.3 2.4 %collective-permute-done.5.high = bf16[2,288,128]{2,1,0:T(8,128)(2,1)S(1)} collective-permute-done((bf16[2,288,128]{2,1,0:T(8,128)(2,1)S(1)}, bf16[2,288,128]{2,1,0:T(8,128)(2,1)S(1)}, u32[]{:S(2)}, u32[]{:S(2)}) %collective-permute-start.5) | collective-permute-done | bytes 147488 | tf_op jit(solution)/shard_map/ppermute | solution.py:478
  53.8 9.6 %denoise.2.refs_0_ = bf16[4,2,64,128]{3,2,1,0:T(8,128)(2,1)S(1)} custom-call(s32[6]{0:T(128)S(1)} %stack.61.info, bf16[2,288,128]{2,1,0:T(8,128)(2,1)S(1)} %add_convert_fusion.1.own, bf16[2,288,128]{2,1,0:T(8,128)(2,1)S(1)} %collective-permute-done.4.low, bf16[2,288,128]{2,1,0:T(8,128)(2,1)S(1)} %collective-permute-done.5.high, ...), custom_call_target="tpu_custom_call" | custom-call | flops 7247757312 | bytes 2097152 | tf_op jit(solution)/shard_map/denoise/pallas_call | solution.py:393
  63.4 3.4 %collective-permute-start.6 = (bf16[4,2,64,128]{3,2,1,0:T(8,128)(2,1)S(1)}, bf16[4,2,64,128]{3,2,1,0:T(8,128)(2,1)S(1)}, u32[]{:S(2)}, u32[]{:S(2)}) collective-permute-start(bf16[4,2,64,128]{3,2,1,0:T(8,128)(2,1)S(1)} %denoise.2.refs_0_), channel_id=1, source_target_pairs={{0,4},{4,8},{8,12},{12,0},{1,5},{5,9},{9,13},{13,1},{2,6},{6,10},{... | collective-permute-start | bytes 393224 | tf_op jit(solution)/shard_map/ppermute | solution.py:483
  66.8 1.3 %collective-permute-start.7 = (bf16[4,2,64,128]{3,2,1,0:T(8,128)(2,1)S(1)}, bf16[4,2,64,128]{3,2,1,0:T(8,128)(2,1)S(1)}, u32[]{:S(2)}, u32[]{:S(2)}) collective-permute-start(bf16[4,2,64,128]{3,2,1,0:T(8,128)(2,1)S(1)} %denoise.2.refs_0_), channel_id=1, source_target_pairs={{0,8},{4,12},{8,0},{12,4},{1,9},{5,13},{9,1},{13,5},{2,10},{6,14},... | collective-permute-start | bytes 393224 | tf_op jit(solution)/shard_map/ppermute | solution.py:483
  69.0 1.4 %collective-permute-done.6.refs_1_ = bf16[4,2,64,128]{3,2,1,0:T(8,128)(2,1)S(1)} collective-permute-done((bf16[4,2,64,128]{3,2,1,0:T(8,128)(2,1)S(1)}, bf16[4,2,64,128]{3,2,1,0:T(8,128)(2,1)S(1)}, u32[]{:S(2)}, u32[]{:S(2)}) %collective-permute-start.6) | collective-permute-done | bytes 131104 | tf_op jit(solution)/shard_map/ppermute | solution.py:483
  70.4 3.3 %collective-permute-done.7.refs_2_ = bf16[4,2,64,128]{3,2,1,0:T(8,128)(2,1)S(1)} collective-permute-done((bf16[4,2,64,128]{3,2,1,0:T(8,128)(2,1)S(1)}, bf16[4,2,64,128]{3,2,1,0:T(8,128)(2,1)S(1)}, u32[]{:S(2)}, u32[]{:S(2)}) %collective-permute-start.7) | collective-permute-done | bytes 131104 | tf_op jit(solution)/shard_map/ppermute | solution.py:483
  73.8 14.2 %consistency.3 = (bf16[2,288,128]{2,1,0:T(8,128)(2,1)S(1)}, bf16[2,288,128]{2,1,0:T(8,128)(2,1)S(1)}, bf16[2,288,128]{2,1,0:T(8,128)(2,1)S(1)}, bf16[2,288,128]{2,1,0:T(8,128)(2,1)S(1)}) custom-call(s32[6]{0:T(128)S(1)} %stack.61.info, bf16[4,2,64,128]{3,2,1,0:T(8,128)(2,1)S(1)} %denoise.2.refs_0_, ...), custom_call_target="tpu_custom_call" | custom-call | flops 5368709120 | bytes 8388608 | tf_op jit(solution)/shard_map/consistency/pallas_call | solution.py:181
  89.1 2.8 %collective-permute-start.11 = (bf16[2,288,128]{2,1,0:T(8,128)(2,1)S(1)}, bf16[2,288,128]{2,1,0:T(8,128)(2,1)S(1)}, u32[]{:S(2)}, u32[]{:S(2)}) collective-permute-start(bf16[2,288,128]{2,1,0:T(8,128)(2,1)S(1)} %get-tuple-element.38), channel_id=1, source_target_pairs={{0,12},{4,0},{8,4},{12,8},{1,13},{5,1},{9,5},{13,9},{2,14},{6,2},{... | collective-permute-start | bytes 442376 | tf_op jit(solution)/shard_map/ppermute | solution.py:470
  91.9 6.2 %collective-permute-done.10 = bf16[2,288,128]{2,1,0:T(8,128)(2,1)S(1)} collective-permute-done((bf16[2,288,128]{2,1,0:T(8,128)(2,1)S(1)}, bf16[2,288,128]{2,1,0:T(8,128)(2,1)S(1)}, u32[]{:S(2)}, u32[]{:S(2)}) %collective-permute-start.10) | collective-permute-done | bytes 147488 | tf_op jit(solution)/shard_map/ppermute | solution.py:470
  98.1 3.2 %collective-permute-done.9 = bf16[2,288,128]{2,1,0:T(8,128)(2,1)S(1)} collective-permute-done((bf16[2,288,128]{2,1,0:T(8,128)(2,1)S(1)}, bf16[2,288,128]{2,1,0:T(8,128)(2,1)S(1)}, u32[]{:S(2)}, u32[]{:S(2)}) %collective-permute-start.9) | collective-permute-done | bytes 147488 | tf_op jit(solution)/shard_map/ppermute | solution.py:470
  101.4 2.8 %collective-permute-start.12 = (bf16[2,288,128]{2,1,0:T(8,128)(2,1)S(1)}, bf16[2,288,128]{2,1,0:T(8,128)(2,1)S(1)}, u32[]{:S(2)}, u32[]{:S(2)}) collective-permute-start(bf16[2,288,128]{2,1,0:T(8,128)(2,1)S(1)} %add_convert_fusion.own), channel_id=1, source_target_pairs={{0,1},{1,2},{2,3},{4,5},{5,6},{6,7},{8,9},{9,10},{10,11},{12,13},{... | collective-permute-start | bytes 442376 | tf_op jit(solution)/shard_map/ppermute | solution.py:477
  104.2 1.9 %collective-permute-start.13 = (bf16[2,288,128]{2,1,0:T(8,128)(2,1)S(1)}, bf16[2,288,128]{2,1,0:T(8,128)(2,1)S(1)}, u32[]{:S(2)}, u32[]{:S(2)}) collective-permute-start(bf16[2,288,128]{2,1,0:T(8,128)(2,1)S(1)} %add_convert_fusion.own), channel_id=1, source_target_pairs={{1,0},{2,1},{3,2},{5,4},{6,5},{7,6},{9,8},{10,9},{11,10},{13,12},{... | collective-permute-start | bytes 442376 | tf_op jit(solution)/shard_map/ppermute | solution.py:478
  106.2 4.4 %collective-permute-done.13.high = bf16[2,288,128]{2,1,0:T(8,128)(2,1)S(1)} collective-permute-done((bf16[2,288,128]{2,1,0:T(8,128)(2,1)S(1)}, bf16[2,288,128]{2,1,0:T(8,128)(2,1)S(1)}, u32[]{:S(2)}, u32[]{:S(2)}) %collective-permute-start.13) | collective-permute-done | bytes 147488 | tf_op jit(solution)/shard_map/ppermute | solution.py:478
  110.6 9.6 %denoise.3 = bf16[4,2,64,128]{3,2,1,0:T(8,128)(2,1)S(1)} custom-call(s32[6]{0:T(128)S(1)} %stack.61.info, bf16[2,288,128]{2,1,0:T(8,128)(2,1)S(1)} %add_convert_fusion.own, bf16[2,288,128]{2,1,0:T(8,128)(2,1)S(1)} %collective-permute-done.12.low, bf16[2,288,128]{2,1,0:T(8,128)(2,1)S(1)} %collective-permute-done.13.high, ...), custom_call_target="tpu_custom_call" | custom-call | flops 7247757312 | bytes 2097152 | tf_op jit(solution)/shard_map/denoise/pallas_call | solution.py:393
  120.6 3.6 %collective-permute-done.14 = bf16[4,2,64,128]{3,2,1,0:T(8,128)(2,1)S(1)} collective-permute-done((bf16[4,2,64,128]{3,2,1,0:T(8,128)(2,1)S(1)}, bf16[4,2,64,128]{3,2,1,0:T(8,128)(2,1)S(1)}, u32[]{:S(2)}, u32[]{:S(2)}) %collective-permute-start.14) | collective-permute-done | bytes 131104 | tf_op jit(solution)/shard_map/ppermute | solution.py:490
  (78 shorter events, 18.1 us)
Async XLA Ops:
  2.3 27.2 %collective-permute-start = (bf16[320,64]{1,0:T(8,128)(2,1)S(1)}, bf16[320,64]{1,0:T(8,128)(2,1)S(1)}, u32[]{:S(2)}, u32[]{:S(2)}) collective-permute-start(bf16[320,64]{1,0:T(8,128)(2,1)S(1)} %fusion.8.refs_0_), channel_id=1, source_target_pairs={{0,16},{16,0},{1,17},{17,1},{2,18},{18,2},{3,19},{19,3},{4,20},{20... | collective-permute-start | bytes 122888 | tf_op jit(solution)/shard_map/ppermute | solution.py:460
  15.4 33.7 %copy-start = (bf16[3,256,256]{2,1,0:T(8,128)(2,1)S(1)}, bf16[3,256,256]{2,1,0:T(8,128)(2,1)}, u32[]{:S(2)}) copy-start(bf16[3,256,256]{2,1,0:T(8,128)(2,1)} %constant.94.clone.refs_8_) | copy-start | bytes 1179652
  15.4 33.7 %copy-start.1 = (bf16[256,240]{1,0:T(8,128)(2,1)S(1)}, bf16[256,240]{1,0:T(8,128)(2,1)}, u32[]{:S(2)}) copy-start(bf16[256,240]{1,0:T(8,128)(2,1)} %constant.91.clone.refs_5_) | copy-start | bytes 368644
  15.4 33.7 %copy-start.2 = (bf16[240,256]{1,0:T(8,128)(2,1)S(1)}, bf16[240,256]{1,0:T(8,128)(2,1)}, u32[]{:S(2)}) copy-start(bf16[240,256]{1,0:T(8,128)(2,1)} %constant.90.clone.refs_4_) | copy-start | bytes 368644
  15.5 33.8 %copy-start.3 = (bf16[256,64]{1,0:T(8,128)(2,1)S(1)}, bf16[256,64]{1,0:T(8,128)(2,1)}, u32[]{:S(2)}) copy-start(bf16[256,64]{1,0:T(8,128)(2,1)} %constant.93.clone.refs_7_) | copy-start | bytes 98308
  15.5 33.8 %copy-start.4 = (bf16[240,64]{1,0:T(8,128)(2,1)S(1)}, bf16[240,64]{1,0:T(8,128)(2,1)}, u32[]{:S(2)}) copy-start(bf16[240,64]{1,0:T(8,128)(2,1)} %constant.88.clone.refs_2_) | copy-start | bytes 92164
  15.5 33.8 %copy-start.5 = (bf16[64,240]{1,0:T(8,128)(2,1)S(1)}, bf16[64,240]{1,0:T(8,128)(2,1)}, u32[]{:S(2)}) copy-start(bf16[64,240]{1,0:T(8,128)(2,1)} %constant.89.clone.refs_3_) | copy-start | bytes 92164
  15.5 33.8 %copy-start.6 = (bf16[64,256]{1,0:T(8,128)(2,1)S(1)}, bf16[64,256]{1,0:T(8,128)(2,1)}, u32[]{:S(2)}) copy-start(bf16[64,256]{1,0:T(8,128)(2,1)} %constant.92.clone.refs_6_) | copy-start | bytes 98308
  15.5 38.2 %copy-start.18 = (bf16[256,256]{1,0:T(8,128)(2,1)S(1)}, bf16[256,256]{1,0:T(8,128)(2,1)}, u32[]{:S(2)}) copy-start(bf16[256,256]{1,0:T(8,128)(2,1)} %constant.95.clone.apart) | copy-start | bytes 393220
  29.5 6.5 %collective-permute-start.1 = (bf16[2,288,128]{2,1,0:T(8,128)(2,1)S(1)}, bf16[2,288,128]{2,1,0:T(8,128)(2,1)S(1)}, u32[]{:S(2)}, u32[]{:S(2)}) collective-permute-start(bf16[2,288,128]{2,1,0:T(8,128)(2,1)S(1)} %get-tuple-element.27), channel_id=1, source_target_pairs={{0,4},{4,8},{8,12},{12,0},{1,5},{5,9},{9,13},{13,1},{2,6},{6,10},{... | collective-permute-start | bytes 442376 | tf_op jit(solution)/shard_map/ppermute | solution.py:470
  30.9 12.7 %collective-permute-start.2 = (bf16[2,288,128]{2,1,0:T(8,128)(2,1)S(1)}, bf16[2,288,128]{2,1,0:T(8,128)(2,1)S(1)}, u32[]{:S(2)}, u32[]{:S(2)}) collective-permute-start(bf16[2,288,128]{2,1,0:T(8,128)(2,1)S(1)} %get-tuple-element.28), channel_id=1, source_target_pairs={{0,8},{4,12},{8,0},{12,4},{1,9},{5,13},{9,1},{13,5},{2,10},{6,14},... | collective-permute-start | bytes 442376 | tf_op jit(solution)/shard_map/ppermute | solution.py:470
  33.2 10.3 %collective-permute-start.3 = (bf16[2,288,128]{2,1,0:T(8,128)(2,1)S(1)}, bf16[2,288,128]{2,1,0:T(8,128)(2,1)S(1)}, u32[]{:S(2)}, u32[]{:S(2)}) collective-permute-start(bf16[2,288,128]{2,1,0:T(8,128)(2,1)S(1)} %get-tuple-element.29), channel_id=1, source_target_pairs={{0,12},{4,0},{8,4},{12,8},{1,13},{5,1},{9,5},{13,9},{2,14},{6,2},{... | collective-permute-start | bytes 442376 | tf_op jit(solution)/shard_map/ppermute | solution.py:470
  43.6 7.7 %collective-permute-start.4 = (bf16[2,288,128]{2,1,0:T(8,128)(2,1)S(1)}, bf16[2,288,128]{2,1,0:T(8,128)(2,1)S(1)}, u32[]{:S(2)}, u32[]{:S(2)}) collective-permute-start(bf16[2,288,128]{2,1,0:T(8,128)(2,1)S(1)} %add_convert_fusion.1.own), channel_id=1, source_target_pairs={{0,1},{1,2},{2,3},{4,5},{5,6},{6,7},{8,9},{9,10},{10,11},{12,13},{... | collective-permute-start | bytes 442376 | tf_op jit(solution)/shard_map/ppermute | solution.py:477
  47.2 6.5 %collective-permute-start.5 = (bf16[2,288,128]{2,1,0:T(8,128)(2,1)S(1)}, bf16[2,288,128]{2,1,0:T(8,128)(2,1)S(1)}, u32[]{:S(2)}, u32[]{:S(2)}) collective-permute-start(bf16[2,288,128]{2,1,0:T(8,128)(2,1)S(1)} %add_convert_fusion.1.own), channel_id=1, source_target_pairs={{1,0},{2,1},{3,2},{5,4},{6,5},{7,6},{9,8},{10,9},{11,10},{13,12},{... | collective-permute-start | bytes 442376 | tf_op jit(solution)/shard_map/ppermute | solution.py:478
  53.7 20.0 %copy-start.15 = (bf16[512,256]{1,0:T(8,128)(2,1)S(1)}, bf16[512,256]{1,0:T(8,128)(2,1)}, u32[]{:S(2)}) copy-start(bf16[512,256]{1,0:T(8,128)(2,1)} %constant.82.clone.refs_6_.refs_9_) | copy-start | bytes 786436
  63.4 7.0 %collective-permute-start.6 = (bf16[4,2,64,128]{3,2,1,0:T(8,128)(2,1)S(1)}, bf16[4,2,64,128]{3,2,1,0:T(8,128)(2,1)S(1)}, u32[]{:S(2)}, u32[]{:S(2)}) collective-permute-start(bf16[4,2,64,128]{3,2,1,0:T(8,128)(2,1)S(1)} %denoise.2.refs_0_), channel_id=1, source_target_pairs={{0,4},{4,8},{8,12},{12,0},{1,5},{5,9},{9,13},{13,1},{2,6},{6,10},{... | collective-permute-start | bytes 393224 | tf_op jit(solution)/shard_map/ppermute | solution.py:483
  66.8 6.9 %collective-permute-start.7 = (bf16[4,2,64,128]{3,2,1,0:T(8,128)(2,1)S(1)}, bf16[4,2,64,128]{3,2,1,0:T(8,128)(2,1)S(1)}, u32[]{:S(2)}, u32[]{:S(2)}) collective-permute-start(bf16[4,2,64,128]{3,2,1,0:T(8,128)(2,1)S(1)} %denoise.2.refs_0_), channel_id=1, source_target_pairs={{0,8},{4,12},{8,0},{12,4},{1,9},{5,13},{9,1},{13,5},{2,10},{6,14},... | collective-permute-start | bytes 393224 | tf_op jit(solution)/shard_map/ppermute | solution.py:483
  68.2 5.5 %collective-permute-start.8 = (bf16[4,2,64,128]{3,2,1,0:T(8,128)(2,1)S(1)}, bf16[4,2,64,128]{3,2,1,0:T(8,128)(2,1)S(1)}, u32[]{:S(2)}, u32[]{:S(2)}) collective-permute-start(bf16[4,2,64,128]{3,2,1,0:T(8,128)(2,1)S(1)} %denoise.2.refs_0_), channel_id=1, source_target_pairs={{0,12},{4,0},{8,4},{12,8},{1,13},{5,1},{9,5},{13,9},{2,14},{6,2},{... | collective-permute-start | bytes 393224 | tf_op jit(solution)/shard_map/ppermute | solution.py:483
  88.1 10.0 %collective-permute-start.10 = (bf16[2,288,128]{2,1,0:T(8,128)(2,1)S(1)}, bf16[2,288,128]{2,1,0:T(8,128)(2,1)S(1)}, u32[]{:S(2)}, u32[]{:S(2)}) collective-permute-start(bf16[2,288,128]{2,1,0:T(8,128)(2,1)S(1)} %get-tuple-element.37), channel_id=1, source_target_pairs={{0,8},{4,12},{8,0},{12,4},{1,9},{5,13},{9,1},{13,5},{2,10},{6,14},... | collective-permute-start | bytes 442376 | tf_op jit(solution)/shard_map/ppermute | solution.py:470
  89.1 9.0 %collective-permute-start.11 = (bf16[2,288,128]{2,1,0:T(8,128)(2,1)S(1)}, bf16[2,288,128]{2,1,0:T(8,128)(2,1)S(1)}, u32[]{:S(2)}, u32[]{:S(2)}) collective-permute-start(bf16[2,288,128]{2,1,0:T(8,128)(2,1)S(1)} %get-tuple-element.38), channel_id=1, source_target_pairs={{0,12},{4,0},{8,4},{12,8},{1,13},{5,1},{9,5},{13,9},{2,14},{6,2},{... | collective-permute-start | bytes 442376 | tf_op jit(solution)/shard_map/ppermute | solution.py:470
  91.9 9.4 %collective-permute-start.9 = (bf16[2,288,128]{2,1,0:T(8,128)(2,1)S(1)}, bf16[2,288,128]{2,1,0:T(8,128)(2,1)S(1)}, u32[]{:S(2)}, u32[]{:S(2)}) collective-permute-start(bf16[2,288,128]{2,1,0:T(8,128)(2,1)S(1)} %get-tuple-element.36), channel_id=1, source_target_pairs={{0,4},{4,8},{8,12},{12,0},{1,5},{5,9},{9,13},{13,1},{2,6},{6,10},{... | collective-permute-start | bytes 442376 | tf_op jit(solution)/shard_map/ppermute | solution.py:470
  101.4 4.9 %collective-permute-start.12 = (bf16[2,288,128]{2,1,0:T(8,128)(2,1)S(1)}, bf16[2,288,128]{2,1,0:T(8,128)(2,1)S(1)}, u32[]{:S(2)}, u32[]{:S(2)}) collective-permute-start(bf16[2,288,128]{2,1,0:T(8,128)(2,1)S(1)} %add_convert_fusion.own), channel_id=1, source_target_pairs={{0,1},{1,2},{2,3},{4,5},{5,6},{6,7},{8,9},{9,10},{10,11},{12,13},{... | collective-permute-start | bytes 442376 | tf_op jit(solution)/shard_map/ppermute | solution.py:477
  104.2 6.5 %collective-permute-start.13 = (bf16[2,288,128]{2,1,0:T(8,128)(2,1)S(1)}, bf16[2,288,128]{2,1,0:T(8,128)(2,1)S(1)}, u32[]{:S(2)}, u32[]{:S(2)}) collective-permute-start(bf16[2,288,128]{2,1,0:T(8,128)(2,1)S(1)} %add_convert_fusion.own), channel_id=1, source_target_pairs={{1,0},{2,1},{3,2},{5,4},{6,5},{7,6},{9,8},{10,9},{11,10},{13,12},{... | collective-permute-start | bytes 442376 | tf_op jit(solution)/shard_map/ppermute | solution.py:478
  120.3 3.9 %collective-permute-start.14 = (bf16[4,2,64,128]{3,2,1,0:T(8,128)(2,1)S(1)}, bf16[4,2,64,128]{3,2,1,0:T(8,128)(2,1)S(1)}, u32[]{:S(2)}, u32[]{:S(2)}) collective-permute-start(bf16[4,2,64,128]{3,2,1,0:T(8,128)(2,1)S(1)} %fusion.6), channel_id=1, source_target_pairs={{0,16},{16,0},{1,17},{17,1},{2,18},{18,2},{3,19},{19,3},{4,20},{20... | collective-permute-start | bytes 393224 | tf_op jit(solution)/shard_map/ppermute | solution.py:490
  (20 other events, 190.9 us)

commit v2 on v1

--- a/solution.py
+++ b/solution.py
@@ -11,7 +11,9 @@
 F32 = jnp.float32
 BF16 = jnp.bfloat16
 HALO = 2
-VMEM_LIMIT = 48 * 1024 * 1024
+BATCH = 16
+WIDE_LIMIT = 62 * 1024 * 1024
+VMEM_LIMIT = 30 * 1024 * 1024
 
 
 def fourier_pair(length):
@@ -21,45 +23,40 @@
     return np.cos(angles) * factor, np.sin(angles) * factor
 
 
-def times_i(length):
-    turn = np.zeros((2 * length, 2 * length))
-    even = 2 * np.arange(length)
-    turn[even, even + 1] = -1.0
-    turn[even + 1, even] = 1.0
-    return turn
-
-
-def row_matrix(length, direction):
-    cosine, sine = fourier_pair(length)
-    sine = direction * sine
-    return np.stack([np.stack([cosine, -sine], -1), np.stack([sine, cosine], -1)], 1).reshape(
-        2 * length, 2 * length
-    )
-
-
 def bf16(values):
     return jnp.asarray(values.astype(jnp.bfloat16))
 
 
+def column_matrix(length, direction):
+    cosine, sine = fourier_pair(length)
+    return np.block([[cosine, direction * sine], [-direction * sine, cosine]])
+
+
+def parts_apart(length):
+    rows = np.arange(2 * length).reshape(length, 2).T.reshape(-1)
+    return np.eye(2 * length)[rows]
+
+
 @functools.lru_cache(maxsize=None)
 def consistency_tables(line_total, part_total, phases, share):
-    cosine, sine = fourier_pair(part_total)
-    turn = times_i(line_total)
-    forward, inverse = row_matrix(line_total, -1.0), row_matrix(line_total, 1.0)
-    duplicate = np.repeat(np.eye(line_total), 2, axis=0)
-    even = np.zeros((line_total, 2 * line_total))
-    even[np.arange(line_total), 2 * np.arange(line_total)] = 1.0
-    odd = np.roll(even, 1, axis=1)
-    return (
-        np.concatenate([cosine, sine], 1),
-        np.concatenate([forward, -forward @ turn], 1),
-        np.concatenate([inverse, turn @ inverse], 0),
-        np.block([[cosine, -sine], [sine, cosine]]),
-        np.concatenate([duplicate @ even, duplicate @ odd], 0),
-        turn,
-        duplicate,
-        phase_inside(phases, share),
-    )
+    tables = [
+        column_matrix(part_total, -1.0),
+        column_matrix(line_total, -1.0).T,
+        column_matrix(line_total, 1.0).T,
+        column_matrix(part_total, 1.0),
+        parts_apart(line_total),
+        line_major(phases, share),
+    ]
+    size = max(max(t.shape) for t in tables)
+    stacked = np.zeros((len(tables), size, size))
+    for index, table in enumerate(tables):
+        stacked[index, : table.shape[0], : table.shape[1]] = table
+    return stacked
+
+
+def line_major(phases, share):
+    rows = np.arange(phases * 2 * share).reshape(phases * 2, share).T.reshape(-1)
+    return np.eye(phases * 2 * share)[rows]
 
 
 def phase_inside(phases, share):
@@ -71,85 +68,128 @@
     return jnp.dot(left, right, preferred_element_type=F32)
 
 
-def consistency_kernel(info, *refs, pieces, shares, coils, phases, share_rows, edge):
+def consistency_kernel(info, *refs, pieces, shares, edge, batch, direct):
     images, refs = refs[:pieces], refs[pieces:]
-    maps, samples, mask, cs, af, gg, ww, dd, turn, dup, inside = refs[:11]
-    outs = refs[11 : 11 + shares]
-    image_now, image_turned, total, window = refs[11 + shares :]
-    coil = pl.program_id(1)
-    me = info[1]
-    part = maps.shape[-1]
-    rows = maps.shape[-2]
-    lanes = [slice(p * part, (p + 1) * part) for p in range(phases)]
-
-    @pl.when(coil == 0)
-    def _():
-        if pieces == 1:
-            image = jnp.concatenate([images[0][0, p, 0] for p in range(phases)], 1)
-        else:
-            joined = total
-            for k in range(pieces):
-                start = pl.multiple_of(lax.rem(me + (pieces - k), pieces) * share_rows, share_rows)
-                for p in range(phases):
-                    joined[pl.ds(start, share_rows), lanes[p]] = images[k][p, 0].astype(F32)
-            image = joined[...].astype(BF16)
-        image_now[...] = image.astype(F32)
-        image_turned[...] = dot(turn[...], image)
-        total[...] = jnp.zeros_like(total)
-
-    both = dot(dd[...], maps[0, 0, 0])
-    map_real, map_imag = both[:rows], both[rows:]
-    fields = [
-        (map_real * image_now[:, lanes[p]] + map_imag * image_turned[:, lanes[p]]).astype(BF16)
-        for p in range(phases)
-    ]
-    halves = dot(jnp.concatenate(fields, 0), cs[...]).astype(BF16)
-    stacked = jnp.concatenate(
-        [
-            jnp.concatenate(
-                [halves[p * rows : (p + 1) * rows, :part], halves[p * rows : (p + 1) * rows, part:]], 0
+    maps, samples, mask, tables = refs[:4]
+    outs = refs[4 : 4 + shares]
+    window, joined, refs = refs[4 + shares], refs[5 + shares], refs[6 + shares :]
+    block, me = info[0], info[1]
+    coils, phases, readouts, rows, part = samples.shape[1:]
+    count = rows // 2
+    share = count // shares
+
+    if direct:
+        waits = {}
+        maps, samples = maps.at[block], samples.at[block]
+    else:
+        sems = refs[-1]
+        sources = (tables, images[0].at[block], maps.at[block], mask, samples.at[block])
+        names = ("tables", "image", "maps", "mask", "samples")
+        waits = {}
+        for k, (name, source) in enumerate(zip(names, sources)):
+            waits[name] = pltpu.make_async_copy(source, refs[k], sems.at[k])
+            waits[name].start()
+        tables, image, maps, mask, samples = refs[:5]
+
+    def wait(name):
+        if name in waits:
+            waits.pop(name).wait()
+
+    wait("tables")
+    wait("image")
+    if pieces > 1:
+        image = joined
+        for k in range(pieces):
+            to = pl.multiple_of(lax.rem(me + (pieces - k), pieces) * 2 * share, 2 * share)
+            joined[:, :, pl.ds(to, 2 * share)] = images[k][...]
+
+    def apart(values):
+        return dot(tables[4, :rows, :rows], values)
+
+    def lane(n):
+        return slice(n * part, (n + 1) * part)
+
+    def band(n):
+        return slice(n * count, (n + 1) * count)
+
+    places = [(r, p) for r in range(readouts) for p in range(phases)]
+    image_now = apart(jnp.concatenate([image[p, r] for r, p in places], 1))
+    wait("maps")
+    maps_now = apart(
+        jnp.concatenate([maps[coil, r] for r in range(readouts) for coil in range(coils)], 1)
+    )
+
+    def map_parts(r, coil):
+        where = lane(r * coils + coil)
+        return maps_now[:count, where], maps_now[count:, where]
+
+    slabs = [(r, coil, p) for r in range(readouts) for coil in range(coils) for p in range(phases)]
+    real_sum = {place: 0.0 for place in places}
+    imag_sum = {place: 0.0 for place in places}
+    for begin in range(0, len(slabs), batch):
+        group = slabs[begin : begin + batch]
+        every = range(len(group))
+        fields = []
+        for r, coil, p in group:
+            map_real, map_imag = map_parts(r, coil)
+            where = lane(places.index((r, p)))
+            real, imag = image_now[:count, where], image_now[count:, where]
+            fields.append(
+                jnp.concatenate(
+                    [
+                        (map_real * real - map_imag * imag).astype(BF16),
+                        (map_real * imag + map_imag * real).astype(BF16),
+                    ],
+                    1,
+                )
             )
-            for p in range(phases)
-        ],
-        1,
-    )
-    spectrum = dot(af[...], stacked)
-    acquired = dot(
-        dup[...], jnp.concatenate([mask[0, p].astype(F32).astype(BF16) for p in range(phases)], 1)
-    )
-    measured = jnp.concatenate([samples[0, 0, p, 0] for p in range(phases)], 1).astype(F32)
-    mixed = jnp.where(acquired > 0.5, measured, spectrum).astype(BF16)
-    back = dot(gg[...], mixed).astype(BF16)
-    paired = jnp.concatenate(
-        [jnp.concatenate([back[:rows, lanes[p]], back[rows:, lanes[p]]], 1) for p in range(phases)], 0
-    )
-    restored = dot(paired, ww[...])
-    for p in range(phases):
-        field = restored[p * rows : (p + 1) * rows]
-        total[:, lanes[p]] += map_real * field[:, :part] - map_imag * field[:, part:]
-
-    @pl.when(coil == coils - 1)
-    def _():
-        summed = total[...].astype(BF16)
-        blocks = jnp.concatenate(
+        half = dot(jnp.concatenate(fields, 0), tables[0, : 2 * part, : 2 * part]).astype(BF16)
+        stacked = jnp.concatenate(
+            [jnp.concatenate([half[band(n), :part], half[band(n), part:]], 0) for n in every], 1
+        )
+        spectrum = dot(tables[1, :rows, :rows], stacked)
+        wait("mask")
+        wait("samples")
+        measured = apart(jnp.concatenate([samples[coil, p, r] for r, coil, p in group], 1))
+        acquired = jnp.concatenate([mask[coil, p] for r, coil, p in group], 1) != 0
+        mixed = jnp.concatenate(
             [
-                jnp.concatenate(
-                    [summed[k * share_rows : (k + 1) * share_rows, lanes[p]] for p in range(phases)], 0
-                )
-                for k in range(shares)
+                jnp.where(acquired, measured[:count], spectrum[:count]).astype(BF16),
+                jnp.where(acquired, measured[count:], spectrum[count:]).astype(BF16),
             ],
-            1,
+            0,
         )
-        ordered = dot(inside[...], blocks).astype(BF16)
-        width = phases * share_rows
-        border = jnp.zeros((edge, part), BF16)
-        window[0:edge] = border
-        window[edge + shares * width : 2 * edge + shares * width] = border
+        back = dot(tables[2, :rows, :rows], mixed).astype(BF16)
+        paired = jnp.concatenate(
+            [jnp.concatenate([back[:count, lane(n)], back[count:, lane(n)]], 1) for n in every], 0
+        )
+        restored = dot(paired, tables[3, : 2 * part, : 2 * part])
+        for n, (r, coil, p) in enumerate(group):
+            map_real, map_imag = map_parts(r, coil)
+            real, imag = restored[band(n), :part], restored[band(n), part:]
+            real_sum[r, p] = real_sum[r, p] + (map_real * real + map_imag * imag)
+            imag_sum[r, p] = imag_sum[r, p] + (map_real * imag - map_imag * real)
+
+    blocks = []
+    for r in range(readouts):
+        summed = [
+            v.astype(BF16) for p in range(phases) for v in (real_sum[r, p], imag_sum[r, p])
+        ]
+        blocks += [
+            jnp.concatenate([v[k * share : (k + 1) * share] for v in summed], 0)
+            for k in range(shares)
+        ]
+    width = phases * 2 * share
+    ordered = dot(tables[5, :width, :width], jnp.concatenate(blocks, 1)).astype(BF16)
+    border = jnp.zeros((edge, part), BF16)
+    for r in range(readouts):
+        window[r, 0:edge] = border
+        window[r, edge + shares * width : 2 * edge + shares * width] = border
         for k in range(shares):
-            window[edge + k * width : edge + (k + 1) * width] = ordered[:, k * part : (k + 1) * part]
-        for k in range(shares):
-            start = pl.multiple_of(lax.rem(me + k, shares) * width, width)
-            outs[k][0] = window[pl.ds(start, width + 2 * edge)]
+            window[r, edge + k * width : edge + (k + 1) * width] = ordered[:, lane(r * shares + k)]
+    for k in range(shares):
+        begin = pl.multiple_of(lax.rem(me + k, shares) * width, width)
+        outs[k][...] = window[:, pl.ds(begin, width + 2 * edge)]
 
 
 def consistency(info, images, maps, samples, mask, shares):
@@ -157,58 +197,43 @@
     lines = rows // 2
     share_rows = rows // shares
     edge = HALO * phases * 2
-    tables = tuple(bf16(t) for t in consistency_tables(lines, part, phases, lines // shares))
+    tables = bf16(consistency_tables(lines, part, phases, lines // shares))
     pieces = len(images)
-    if pieces == 1:
-        image_specs = [
-            pl.BlockSpec((1, phases, 1, rows, part), lambda r, j, info: (info[0], 0, r, 0, 0))
-        ]
-    else:
-        image_specs = [
-            pl.BlockSpec((phases, 1, share_rows, part), lambda r, j, info: (0, r, 0, 0))
-        ] * pieces
-    fixed = [pl.BlockSpec(t.shape, lambda r, j, info: (0, 0)) for t in tables]
+    direct = pieces > 1
     width = phases * share_rows + 2 * edge
     body = functools.partial(
-        consistency_kernel,
-        pieces=pieces,
-        shares=shares,
-        coils=coils,
-        phases=phases,
-        share_rows=share_rows,
-        edge=edge,
+        consistency_kernel, pieces=pieces, shares=shares, edge=edge, batch=BATCH, direct=direct
     )
+    image_shape = (phases, readouts, rows, part)
+    buffers = [
+        pltpu.VMEM(tables.shape, BF16),
+        pltpu.VMEM(image_shape, BF16),
+        pltpu.VMEM((coils, readouts, rows, part), BF16),
+        pltpu.VMEM((coils, phases, lines, part), jnp.int32),
+        pltpu.VMEM((coils, phases, readouts, rows, part), BF16),
+        pltpu.SemaphoreType.DMA((5,)),
+    ]
     return pl.pallas_call(
         body,
-        grid_spec=pltpu.PrefetchScalarGridSpec(
-            num_scalar_prefetch=1,
-            grid=(readouts, coils),
-            in_specs=image_specs
-            + [
-                pl.BlockSpec((1, 1, 1, rows, part), lambda r, j, info: (info[0], j, r, 0, 0)),
-                pl.BlockSpec(
-                    (1, 1, phases, 1, rows, part), lambda r, j, info: (info[0], j, 0, r, 0, 0)
-                ),
-                pl.BlockSpec((1, phases, lines, part), lambda r, j, info: (j, 0, 0, 0)),
-            ]
-            + fixed,
-            out_specs=[pl.BlockSpec((1, width, part), lambda r, j, info: (r, 0, 0))] * shares,
-            scratch_shapes=[
-                pltpu.VMEM((rows, phases * part), F32),
-                pltpu.VMEM((rows, phases * part), F32),
-                pltpu.VMEM((rows, phases * part), F32),
-                pltpu.VMEM((shares * phases * share_rows + 2 * edge, part), BF16),
-            ],
+        in_specs=[pl.BlockSpec(memory_space=pltpu.SMEM)]
+        + [pl.BlockSpec(memory_space=pltpu.VMEM if direct else pl.ANY)] * (pieces + 4),
+        out_specs=[pl.BlockSpec(memory_space=pltpu.VMEM)] * shares,
+        scratch_shapes=[
+            pltpu.VMEM((readouts, shares * phases * share_rows + 2 * edge, part), BF16),
+            pltpu.VMEM(image_shape if direct else (16, part), BF16),
+        ]
+        + ([] if direct else buffers),
+        out_shape=[jax.ShapeDtypeStruct((readouts, width, part), BF16)] * shares,
+        compiler_params=pltpu.CompilerParams(
+            vmem_limit_bytes=VMEM_LIMIT if direct else WIDE_LIMIT
         ),
-        out_shape=[jax.ShapeDtypeStruct((readouts, width, part), BF16)] * shares,
-        compiler_params=pltpu.CompilerParams(vmem_limit_bytes=VMEM_LIMIT),
         cost_estimate=pl.CostEstimate(
             flops=readouts * coils * phases * rows * part * rows * 20,
-            bytes_accessed=8 * 1024 * 1024,
+            bytes_accessed=4 * 1024 * 1024,
             transcendentals=0,
         ),
         name="consistency",
-    )(info, *images, maps, samples, mask, *tables)
+    )(info, *images, maps, samples, mask, tables)
 
 
 def tap_rows(phases, parts):
@@ -334,6 +359,8 @@
                 taps[index, line - 1] = jnp.concatenate(around + filler, 0).astype(BF16)
         sums[...] = jnp.zeros_like(sums)
 
+    used_taps = min(3, readouts)
+    begun = jnp.clip(step - readouts + 1, 0, 3 - used_taps)
     inside = jnp.where(step == 0, info[2], jnp.where(step == steps - 1, info[3], 1))
 
     @pl.when(inside == 1)
@@ -351,9 +378,9 @@
             if block[-1] == lines - 2:
                 pieces[-1] = pieces[-1] * info[5].astype(F32).astype(BF16)
             mixed = jnp.concatenate(pieces, 1)
-            result = dot(last[0], mixed)
-            for a in range(3):
-                target = step + 2 - a
+            result = dot(last[0, pl.ds(pl.multiple_of(begun * group, 16), used_taps * group)], mixed)
+            for a in range(used_taps):
+                target = step + 2 - begun - a
                 for e in range(3):
                     for line in range(block[0] - 1, block[-1] + 2):
                         terms = []
@@ -391,7 +418,7 @@
     group = first.shape[2] // 3
     whole = pl.BlockSpec((readouts, span, part), lambda s, info: (0, 0, 0))
     return pl.pallas_call(
-        functools.partial(denoise_kernel, phases=phases, chunk=17),
+        functools.partial(denoise_kernel, phases=phases, chunk=34),
         grid_spec=pltpu.PrefetchScalarGridSpec(
             num_scalar_prefetch=1,
             grid=(readouts + 2,),
@@ -448,51 +475,55 @@
     def padded(block):
         return jnp.pad(block, ((0, -block.shape[0] % 64), (0, 0)))
 
-    pack = jnp.concatenate(
-        [
-            time_w[0].reshape(-1, channels),
-            padded(first_w[0].reshape(-1, channels)),
-            padded(jnp.swapaxes(last_w[0], 1, 2).reshape(-1, channels)),
-        ],
-        0,
-    )
-    packs = [pack] + [
-        lax.ppermute(pack, "cascade", rotation(sections, k)) for k in range(1, sections)
-    ]
+    def exchanged(values, axis, count):
+        return [values[0]] + [
+            lax.ppermute(values[k], axis, rotation(count, k)) for k in range(1, count)
+        ]
+
+    forward = [(i, i + 1) for i in range(readout_parts - 1)]
+    backward = [(target, source) for source, target in forward]
+    images = [initial]
     matrices = None
-    images = [initial]
-    outputs = []
+    kept, sent = [], []
     for section in range(sections):
-        shares_out = consistency(info, images, coil_maps, kspace, sampled, shares)
+        partial = consistency(info, images, coil_maps, kspace, sampled, shares)
         if matrices is None:
-            packs, shares_out = lax.optimization_barrier((packs, shares_out))
-        parts = [shares_out[0]] + [
-            lax.ppermute(shares_out[k], "coil", rotation(shares, k)) for k in range(1, shares)
-        ]
+            partial, (first_w, time_w, last_w) = lax.optimization_barrier(
+                (partial, (first_w, time_w, last_w))
+            )
+        parts = exchanged(partial, "coil", shares)
         if matrices is None:
+            pack = jnp.concatenate(
+                [
+                    time_w[0].reshape(-1, channels),
+                    padded(first_w[0].reshape(-1, channels)),
+                    padded(jnp.swapaxes(last_w[0], 1, 2).reshape(-1, channels)),
+                ],
+                0,
+            )
+            packs = exchanged([pack] * sections, "cascade", sections)
             matrices = weight_matrices(info, packs, phases)
         combined = sum(p.astype(F32) for p in parts).astype(BF16)
-        forward = [(i, i + 1) for i in range(readout_parts - 1)]
-        backward = [(target, source) for source, target in forward]
         low = lax.ppermute(combined, "readout", forward)
         high = lax.ppermute(combined, "readout", backward)
         output = denoise(info, combined, low, high, matrices, section, phases)
-        outputs.append(output)
         if section < sections - 1:
-            images = [output] + [
-                lax.ppermute(output, "coil", rotation(shares, k)) for k in range(1, shares)
+            images = exchanged([output] * shares, "coil", shares)
+        kept.append(output)
+        sent.append(
+            [
+                lax.ppermute(output, "cascade", [((section + k) % sections, section)])
+                for k in range(1, sections)
             ]
-
-    stacked = jnp.stack(outputs)
-    placed = [lax.dynamic_index_in_dim(stacked, section_no, 0, False)]
-    for k in range(1, sections):
-        piece = lax.dynamic_index_in_dim(stacked, (section_no + k) % sections, 0, False)
-        placed.append(lax.ppermute(piece, "cascade", rotation(sections, k)))
+        )
+
     arrived = []
     for block in range(sections):
-        value = placed[0]
-        for k in range(1, sections):
-            value = jnp.where((section_no - block) % sections == k, placed[k], value)
+        value = None
+        for section in range(sections):
+            k = (block - section) % sections
+            piece = sent[section][k - 1] if k else kept[section]
+            value = piece if value is None else jnp.where(section_no == section, piece, value)
         arrived.append(value)
     result = jnp.stack(arrived)[None]
     return result.reshape(result.shape[:-2] + (result.shape[-2] // 2, 2, part))

time: 126 us -> 101 us (0.80)
  Pallas kernels: 49.5 us -> 31.6 us
  local copies, waits for them, and re-layouts: 12.6 us -> 0.83 us
  starting transfers between devices: 26.8 us -> 31.8 us
  waiting for transfers between devices: 33.9 us -> 32.6 us
    pallas_call x4, Pallas kernels: 47.5 us -> 29.6 us  [the longest x2 17.3 us: denoise(): pl.pallas_call(functools.partial(denoise_kernel, phases=phases, chunk=34)...]
    unnamed x58 -> x32, local copies, waits for them, and re-layouts: 11 us -> 0.09 us
    ppermute x11 -> x12, starting transfers between devices: 16.6 us -> 21.8 us  [the longest x10 17.4 us: exchanged(): lax.ppermute(values[k], axis, rotation(count, k))]
    ppermute x2, waiting for transfers between devices: 6.76 us -> 2.56 us  [per_device(): high = lax.ppermute(combined, 'readout', backward)]
    ppermute x11 -> x12, waiting for transfers between devices: 27 us -> 30 us  [the longest x10 28.1 us: exchanged(): lax.ppermute(values[k], axis, rotation(count, k))]
  transfers between devices with their start and end apart: 15 -> 16, of which waited for: 10 -> 11; matrix products, arithmetic and copies ran while one was open for 0% -> 0% of each run, Pallas kernels for 13% -> 11%
where the time goes in v2:
time: 101 us; the launch traced here: 99.4 us
  waiting for transfers between devices  32.6 us (32%)
  starting transfers between devices  31.8 us (31%)
  Pallas kernels  31.6 us (31%)
  other arithmetic  2.22 us (2%)
    ppermute x10, waiting for transfers between devices, exchanged(): lax.ppermute(values[k], axis, rotation(count, k))  28.1 us
    ppermute x10, starting transfers between devices, exchanged(): lax.ppermute(values[k], axis, rotation(count, k))  17.4 us
    pallas_call x2, Pallas kernels, denoise(): pl.pallas_call(functools.partial(denoise_kernel, phases=phases, chunk=34)...  17.3 us
    pallas_call x2, Pallas kernels, consistency(): pl.pallas_call(body, in_specs=[pl.BlockSpec(memory_space=pltpu.SMEM)] + [...  12.3 us
    ppermute x2, starting transfers between devices, per_device(): low = lax.ppermute(combined, 'readout', forward)  5.52 us
    ppermute x2, starting transfers between devices, per_device(): high = lax.ppermute(combined, 'readout', backward)  4.5 us
    ppermute x2, starting transfers between devices, per_device(): lax.ppermute(output, 'cascade', [((section + k) % sections, section)])  4.44 us
    ppermute x2, waiting for transfers between devices, per_device(): high = lax.ppermute(combined, 'readout', backward)  2.56 us
  transfers between devices with their start and end apart: 16, of which 11 were waited for; matrix products, arithmetic and copies ran while one was open for 0% of the time, Pallas kernels for 11%

profile of v2, /device:TPU:1, one launch (start us, length us, event | category | flops | bytes accessed | tf_op | source)
XLA Modules:
  0.0 99.4 jit_solution(16887412324992414149)
XLA Ops:
  0.8 7.5 %consistency.2 = (bf16[2,288,128]{2,1,0:T(8,128)(2,1)}, bf16[2,288,128]{2,1,0:T(8,128)(2,1)}, bf16[2,288,128]{2,1,0:T(8,128)(2,1)}, bf16[2,288,128]{2,1,0:T(8,128)(2,1)}) custom-call(s32[6]{0:T(128)} %stack.52.info, bf16[2,4,2,256,128]{4,3,2,1,0:T(8,128)(2,1)} %bitcast.23, bf16[2,4,2,256,128]{4,3,2,1,0:T(8,128)(2,1)} %bitcast.17, ...), custom_call_target="tpu_custom_call" | custom-call | flops 5368709120 | bytes 4194304 | tf_op jit(solution)/shard_map/consistency/pallas_call | solution.py:216
  8.3 2.2 %collective-permute-start = (bf16[2,288,128]{2,1,0:T(8,128)(2,1)}, bf16[2,288,128]{2,1,0:T(8,128)(2,1)S(1)}, u32[]{:S(2)}, u32[]{:S(2)}) collective-permute-start(bf16[2,288,128]{2,1,0:T(8,128)(2,1)} %get-tuple-element.28), channel_id=1, source_target_pairs={{0,4},{4,8},{8,12},{12,0},{1,5},{5,9},{9,13},{13,1},{2,6},{6,10},{... | collective-permute-start | bytes 442376 | tf_op jit(solution)/shard_map/ppermute | solution.py:480
  10.5 2.3 %collective-permute-start.1 = (bf16[2,288,128]{2,1,0:T(8,128)(2,1)}, bf16[2,288,128]{2,1,0:T(8,128)(2,1)S(1)}, u32[]{:S(2)}, u32[]{:S(2)}) collective-permute-start(bf16[2,288,128]{2,1,0:T(8,128)(2,1)} %get-tuple-element.29), channel_id=1, source_target_pairs={{0,8},{4,12},{8,0},{12,4},{1,9},{5,13},{9,1},{13,5},{2,10},{6,14},... | collective-permute-start | bytes 442376 | tf_op jit(solution)/shard_map/ppermute | solution.py:480
  13.9 2.4 %collective-permute-done = bf16[2,288,128]{2,1,0:T(8,128)(2,1)S(1)} collective-permute-done((bf16[2,288,128]{2,1,0:T(8,128)(2,1)}, bf16[2,288,128]{2,1,0:T(8,128)(2,1)S(1)}, u32[]{:S(2)}, u32[]{:S(2)}) %collective-permute-start) | collective-permute-done | bytes 147488 | tf_op jit(solution)/shard_map/ppermute | solution.py:480
  16.4 7.0 %collective-permute-done.1 = bf16[2,288,128]{2,1,0:T(8,128)(2,1)S(1)} collective-permute-done((bf16[2,288,128]{2,1,0:T(8,128)(2,1)}, bf16[2,288,128]{2,1,0:T(8,128)(2,1)S(1)}, u32[]{:S(2)}, u32[]{:S(2)}) %collective-permute-start.1) | collective-permute-done | bytes 147488 | tf_op jit(solution)/shard_map/ppermute | solution.py:480
  24.4 3.6 %collective-permute-start.3 = (bf16[2,288,128]{2,1,0:T(8,128)(2,1)S(1)}, bf16[2,288,128]{2,1,0:T(8,128)(2,1)S(1)}, u32[]{:S(2)}, u32[]{:S(2)}) collective-permute-start(bf16[2,288,128]{2,1,0:T(8,128)(2,1)S(1)} %add_convert_fusion.1.own), channel_id=1, source_target_pairs={{0,1},{1,2},{2,3},{4,5},{5,6},{6,7},{8,9},{9,10},{10,11},{12,13},{... | collective-permute-start | bytes 442376 | tf_op jit(solution)/shard_map/ppermute | solution.py:507
  28.0 1.9 %collective-permute-start.4 = (bf16[2,288,128]{2,1,0:T(8,128)(2,1)S(1)}, bf16[2,288,128]{2,1,0:T(8,128)(2,1)S(1)}, u32[]{:S(2)}, u32[]{:S(2)}) collective-permute-start(bf16[2,288,128]{2,1,0:T(8,128)(2,1)S(1)} %add_convert_fusion.1.own), channel_id=1, source_target_pairs={{1,0},{2,1},{3,2},{5,4},{6,5},{7,6},{9,8},{10,9},{11,10},{13,12},{... | collective-permute-start | bytes 442376 | tf_op jit(solution)/shard_map/ppermute | solution.py:508
  31.3 2.1 %collective-permute-done.5.refs_1_ = bf16[320,64]{1,0:T(8,128)(2,1)S(1)} collective-permute-done((bf16[320,64]{1,0:T(8,128)(2,1)S(1)}, bf16[320,64]{1,0:T(8,128)(2,1)S(1)}, u32[]{:S(2)}, u32[]{:S(2)}) %collective-permute-start.5) | collective-permute-done | bytes 40992 | tf_op jit(solution)/shard_map/ppermute | solution.py:480
  33.4 2.0 %weights.1 = (bf16[2,256,240]{2,1,0:T(8,128)(2,1)S(1)}, bf16[2,256,256]{2,1,0:T(8,128)(2,1)S(1)}, bf16[2,240,256]{2,1,0:T(8,128)(2,1)S(1)}) custom-call(s32[6]{0:T(128)S(1)} %copy-done.7, bf16[320,64]{1,0:T(8,128)(2,1)S(1)} %fusion.4.refs_0_, bf16[320,64]{1,0:T(8,128)(2,1)S(1)} %collective-permute-done.5.refs_1_, bf16[240,64]{1,0:T(8,128)(2,1)S(1)} %copy-done.4, ...), custom_call_target="tpu_custom_call" | custom-call | flops 131072000 | bytes 2097152 | tf_op jit(solution)/shard_map/weights/pallas_call | solution.py:304
  35.5 8.7 %denoise.2.refs_0_ = bf16[4,2,64,128]{3,2,1,0:T(8,128)(2,1)S(1)} custom-call(s32[6]{0:T(128)S(1)} %copy-done.7, bf16[2,288,128]{2,1,0:T(8,128)(2,1)S(1)} %add_convert_fusion.1.own, bf16[2,288,128]{2,1,0:T(8,128)(2,1)S(1)} %collective-permute-done.3.low, bf16[2,288,128]{2,1,0:T(8,128)(2,1)S(1)} %collective-permute-done.4.high, ...), custom_call_target="tpu_custom_call" | custom-call | flops 7247757312 | bytes 2097152 | tf_op jit(solution)/shard_map/denoise/pallas_call | solution.py:420
  44.2 3.4 %collective-permute-start.6 = (bf16[4,2,64,128]{3,2,1,0:T(8,128)(2,1)S(1)}, bf16[4,2,64,128]{3,2,1,0:T(8,128)(2,1)S(1)}, u32[]{:S(2)}, u32[]{:S(2)}) collective-permute-start(bf16[4,2,64,128]{3,2,1,0:T(8,128)(2,1)S(1)} %denoise.2.refs_0_), channel_id=1, source_target_pairs={{0,4},{4,8},{8,12},{12,0},{1,5},{5,9},{9,13},{13,1},{2,6},{6,10},{... | collective-permute-start | bytes 393224 | tf_op jit(solution)/shard_map/ppermute | solution.py:480
  49.8 2.7 %collective-permute-done.6.refs_1_ = bf16[4,2,64,128]{3,2,1,0:T(8,128)(2,1)S(1)} collective-permute-done((bf16[4,2,64,128]{3,2,1,0:T(8,128)(2,1)S(1)}, bf16[4,2,64,128]{3,2,1,0:T(8,128)(2,1)S(1)}, u32[]{:S(2)}, u32[]{:S(2)}) %collective-permute-start.6) | collective-permute-done | bytes 131104 | tf_op jit(solution)/shard_map/ppermute | solution.py:480
  52.4 3.6 %collective-permute-done.7.refs_2_ = bf16[4,2,64,128]{3,2,1,0:T(8,128)(2,1)S(1)} collective-permute-done((bf16[4,2,64,128]{3,2,1,0:T(8,128)(2,1)S(1)}, bf16[4,2,64,128]{3,2,1,0:T(8,128)(2,1)S(1)}, u32[]{:S(2)}, u32[]{:S(2)}) %collective-permute-start.7) | collective-permute-done | bytes 131104 | tf_op jit(solution)/shard_map/ppermute | solution.py:480
  56.4 4.8 %consistency.3 = (bf16[2,288,128]{2,1,0:T(8,128)(2,1)S(1)}, bf16[2,288,128]{2,1,0:T(8,128)(2,1)S(1)}, bf16[2,288,128]{2,1,0:T(8,128)(2,1)S(1)}, bf16[2,288,128]{2,1,0:T(8,128)(2,1)S(1)}) custom-call(s32[6]{0:T(128)S(1)} %copy-done.7, bf16[4,2,64,128]{3,2,1,0:T(8,128)(2,1)S(1)} %denoise.2.refs_0_, bf16[4,2,64,128]{3,2,1,0:T(8,128)(2,1)S(1)} %collective-permute-done.6.refs_1_, ...), custom_call_target="tpu_custom_call" | custom-call | flops 5368709120 | bytes 4194304 | tf_op jit(solution)/shard_map/consistency/pallas_call | solution.py:216
  61.2 2.0 %collective-permute-start.10 = (bf16[2,288,128]{2,1,0:T(8,128)(2,1)S(1)}, bf16[2,288,128]{2,1,0:T(8,128)(2,1)S(1)}, u32[]{:S(2)}, u32[]{:S(2)}) collective-permute-start(bf16[2,288,128]{2,1,0:T(8,128)(2,1)S(1)} %get-tuple-element.39), channel_id=1, source_target_pairs={{0,8},{4,12},{8,0},{12,4},{1,9},{5,13},{9,1},{13,5},{2,10},{6,14},... | collective-permute-start | bytes 442376 | tf_op jit(solution)/shard_map/ppermute | solution.py:480
  63.2 2.9 %collective-permute-start.11 = (bf16[2,288,128]{2,1,0:T(8,128)(2,1)S(1)}, bf16[2,288,128]{2,1,0:T(8,128)(2,1)S(1)}, u32[]{:S(2)}, u32[]{:S(2)}) collective-permute-start(bf16[2,288,128]{2,1,0:T(8,128)(2,1)S(1)} %get-tuple-element.40), channel_id=1, source_target_pairs={{0,12},{4,0},{8,4},{12,8},{1,13},{5,1},{9,5},{13,9},{2,14},{6,2},{... | collective-permute-start | bytes 442376 | tf_op jit(solution)/shard_map/ppermute | solution.py:480
  66.1 3.7 %collective-permute-done.10 = bf16[2,288,128]{2,1,0:T(8,128)(2,1)S(1)} collective-permute-done((bf16[2,288,128]{2,1,0:T(8,128)(2,1)S(1)}, bf16[2,288,128]{2,1,0:T(8,128)(2,1)S(1)}, u32[]{:S(2)}, u32[]{:S(2)}) %collective-permute-start.10) | collective-permute-done | bytes 147488 | tf_op jit(solution)/shard_map/ppermute | solution.py:480
  70.8 5.3 %collective-permute-done.9 = bf16[2,288,128]{2,1,0:T(8,128)(2,1)S(1)} collective-permute-done((bf16[2,288,128]{2,1,0:T(8,128)(2,1)S(1)}, bf16[2,288,128]{2,1,0:T(8,128)(2,1)S(1)}, u32[]{:S(2)}, u32[]{:S(2)}) %collective-permute-start.9) | collective-permute-done | bytes 147488 | tf_op jit(solution)/shard_map/ppermute | solution.py:480
  76.2 1.9 %collective-permute-start.12 = (bf16[2,288,128]{2,1,0:T(8,128)(2,1)S(1)}, bf16[2,288,128]{2,1,0:T(8,128)(2,1)S(1)}, u32[]{:S(2)}, u32[]{:S(2)}) collective-permute-start(bf16[2,288,128]{2,1,0:T(8,128)(2,1)S(1)} %add_convert_fusion.own), channel_id=1, source_target_pairs={{0,1},{1,2},{2,3},{4,5},{5,6},{6,7},{8,9},{9,10},{10,11},{12,13},{... | collective-permute-start | bytes 442376 | tf_op jit(solution)/shard_map/ppermute | solution.py:507
  78.1 2.6 %collective-permute-start.13 = (bf16[2,288,128]{2,1,0:T(8,128)(2,1)S(1)}, bf16[2,288,128]{2,1,0:T(8,128)(2,1)S(1)}, u32[]{:S(2)}, u32[]{:S(2)}) collective-permute-start(bf16[2,288,128]{2,1,0:T(8,128)(2,1)S(1)} %add_convert_fusion.own), channel_id=1, source_target_pairs={{1,0},{2,1},{3,2},{5,4},{6,5},{7,6},{9,8},{10,9},{11,10},{13,12},{... | collective-permute-start | bytes 442376 | tf_op jit(solution)/shard_map/ppermute | solution.py:508
  82.0 2.6 %collective-permute-done.13.high = bf16[2,288,128]{2,1,0:T(8,128)(2,1)S(1)} collective-permute-done((bf16[2,288,128]{2,1,0:T(8,128)(2,1)S(1)}, bf16[2,288,128]{2,1,0:T(8,128)(2,1)S(1)}, u32[]{:S(2)}, u32[]{:S(2)}) %collective-permute-start.13) | collective-permute-done | bytes 147488 | tf_op jit(solution)/shard_map/ppermute | solution.py:508
  84.6 8.7 %denoise.3 = bf16[4,2,64,128]{3,2,1,0:T(8,128)(2,1)S(1)} custom-call(s32[6]{0:T(128)S(1)} %copy-done.7, bf16[2,288,128]{2,1,0:T(8,128)(2,1)S(1)} %add_convert_fusion.own, bf16[2,288,128]{2,1,0:T(8,128)(2,1)S(1)} %collective-permute-done.12.low, bf16[2,288,128]{2,1,0:T(8,128)(2,1)S(1)} %collective-permute-done.13.high, ...), custom_call_target="tpu_custom_call" | custom-call | flops 7247757312 | bytes 2097152 | tf_op jit(solution)/shard_map/denoise/pallas_call | solution.py:420
  93.2 3.1 %collective-permute-start.14 = (bf16[4,2,64,128]{3,2,1,0:T(8,128)(2,1)S(1)}, bf16[4,2,64,128]{3,2,1,0:T(8,128)(2,1)S(1)}, u32[]{:S(2)}, u32[]{:S(2)}) collective-permute-start(bf16[4,2,64,128]{3,2,1,0:T(8,128)(2,1)S(1)} %denoise.3), channel_id=1, source_target_pairs={{0,16},{1,17},{2,18},{3,19},{4,20},{5,21},{6,22},{7,23},{8,24},{9,... | collective-permute-start | bytes 393224 | tf_op jit(solution)/shard_map/ppermute | solution.py:515
  96.4 1.9 %collective-permute-done.14 = bf16[4,2,64,128]{3,2,1,0:T(8,128)(2,1)S(1)} collective-permute-done((bf16[4,2,64,128]{3,2,1,0:T(8,128)(2,1)S(1)}, bf16[4,2,64,128]{3,2,1,0:T(8,128)(2,1)S(1)}, u32[]{:S(2)}, u32[]{:S(2)}) %collective-permute-start.14) | collective-permute-done | bytes 131104 | tf_op jit(solution)/shard_map/ppermute | solution.py:515
  (54 shorter events, 10.1 us)
Async XLA Ops:
  0.7 32.6 %copy-start = (bf16[3,256,256]{2,1,0:T(8,128)(2,1)S(1)}, bf16[3,256,256]{2,1,0:T(8,128)(2,1)}, u32[]{:S(2)}) copy-start(bf16[3,256,256]{2,1,0:T(8,128)(2,1)} %constant.46.clone.refs_8_) | copy-start | bytes 1179652
  0.7 32.6 %copy-start.1 = (bf16[256,240]{1,0:T(8,128)(2,1)S(1)}, bf16[256,240]{1,0:T(8,128)(2,1)}, u32[]{:S(2)}) copy-start(bf16[256,240]{1,0:T(8,128)(2,1)} %constant.43.clone.refs_5_) | copy-start | bytes 368644
  0.7 32.6 %copy-start.2 = (bf16[240,256]{1,0:T(8,128)(2,1)S(1)}, bf16[240,256]{1,0:T(8,128)(2,1)}, u32[]{:S(2)}) copy-start(bf16[240,256]{1,0:T(8,128)(2,1)} %constant.42.clone.refs_4_) | copy-start | bytes 368644
  0.7 32.6 %copy-start.3 = (bf16[256,64]{1,0:T(8,128)(2,1)S(1)}, bf16[256,64]{1,0:T(8,128)(2,1)}, u32[]{:S(2)}) copy-start(bf16[256,64]{1,0:T(8,128)(2,1)} %constant.45.clone.refs_7_) | copy-start | bytes 98308
  0.7 32.6 %copy-start.4 = (bf16[240,64]{1,0:T(8,128)(2,1)S(1)}, bf16[240,64]{1,0:T(8,128)(2,1)}, u32[]{:S(2)}) copy-start(bf16[240,64]{1,0:T(8,128)(2,1)} %constant.40.clone.refs_2_) | copy-start | bytes 92164
  0.7 32.6 %copy-start.5 = (bf16[64,240]{1,0:T(8,128)(2,1)S(1)}, bf16[64,240]{1,0:T(8,128)(2,1)}, u32[]{:S(2)}) copy-start(bf16[64,240]{1,0:T(8,128)(2,1)} %constant.41.clone.refs_3_) | copy-start | bytes 92164
  0.8 32.6 %copy-start.6 = (bf16[64,256]{1,0:T(8,128)(2,1)S(1)}, bf16[64,256]{1,0:T(8,128)(2,1)}, u32[]{:S(2)}) copy-start(bf16[64,256]{1,0:T(8,128)(2,1)} %constant.44.clone.refs_6_) | copy-start | bytes 98308
  0.8 34.7 %copy-start.12 = (bf16[256,256]{1,0:T(8,128)(2,1)S(1)}, bf16[256,256]{1,0:T(8,128)(2,1)}, u32[]{:S(2)}) copy-start(bf16[256,256]{1,0:T(8,128)(2,1)} %constant.47.clone.apart) | copy-start | bytes 393220
  8.3 8.1 %collective-permute-start = (bf16[2,288,128]{2,1,0:T(8,128)(2,1)}, bf16[2,288,128]{2,1,0:T(8,128)(2,1)S(1)}, u32[]{:S(2)}, u32[]{:S(2)}) collective-permute-start(bf16[2,288,128]{2,1,0:T(8,128)(2,1)} %get-tuple-element.28), channel_id=1, source_target_pairs={{0,4},{4,8},{8,12},{12,0},{1,5},{5,9},{9,13},{13,1},{2,6},{6,10},{... | collective-permute-start | bytes 442376 | tf_op jit(solution)/shard_map/ppermute | solution.py:480
  10.5 12.9 %collective-permute-start.1 = (bf16[2,288,128]{2,1,0:T(8,128)(2,1)}, bf16[2,288,128]{2,1,0:T(8,128)(2,1)S(1)}, u32[]{:S(2)}, u32[]{:S(2)}) collective-permute-start(bf16[2,288,128]{2,1,0:T(8,128)(2,1)} %get-tuple-element.29), channel_id=1, source_target_pairs={{0,8},{4,12},{8,0},{12,4},{1,9},{5,13},{9,1},{13,5},{2,10},{6,14},... | collective-permute-start | bytes 442376 | tf_op jit(solution)/shard_map/ppermute | solution.py:480
  12.8 10.6 %collective-permute-start.2 = (bf16[2,288,128]{2,1,0:T(8,128)(2,1)}, bf16[2,288,128]{2,1,0:T(8,128)(2,1)S(1)}, u32[]{:S(2)}, u32[]{:S(2)}) collective-permute-start(bf16[2,288,128]{2,1,0:T(8,128)(2,1)} %get-tuple-element.30), channel_id=1, source_target_pairs={{0,12},{4,0},{8,4},{12,8},{1,13},{5,1},{9,5},{13,9},{2,14},{6,2},{... | collective-permute-start | bytes 442376 | tf_op jit(solution)/shard_map/ppermute | solution.py:480
  24.4 11.1 %collective-permute-start.3 = (bf16[2,288,128]{2,1,0:T(8,128)(2,1)S(1)}, bf16[2,288,128]{2,1,0:T(8,128)(2,1)S(1)}, u32[]{:S(2)}, u32[]{:S(2)}) collective-permute-start(bf16[2,288,128]{2,1,0:T(8,128)(2,1)S(1)} %add_convert_fusion.1.own), channel_id=1, source_target_pairs={{0,1},{1,2},{2,3},{4,5},{5,6},{6,7},{8,9},{9,10},{10,11},{12,13},{... | collective-permute-start | bytes 442376 | tf_op jit(solution)/shard_map/ppermute | solution.py:507
  28.0 7.5 %collective-permute-start.4 = (bf16[2,288,128]{2,1,0:T(8,128)(2,1)S(1)}, bf16[2,288,128]{2,1,0:T(8,128)(2,1)S(1)}, u32[]{:S(2)}, u32[]{:S(2)}) collective-permute-start(bf16[2,288,128]{2,1,0:T(8,128)(2,1)S(1)} %add_convert_fusion.1.own), channel_id=1, source_target_pairs={{1,0},{2,1},{3,2},{5,4},{6,5},{7,6},{9,8},{10,9},{11,10},{13,12},{... | collective-permute-start | bytes 442376 | tf_op jit(solution)/shard_map/ppermute | solution.py:508
  30.0 3.4 %collective-permute-start.5 = (bf16[320,64]{1,0:T(8,128)(2,1)S(1)}, bf16[320,64]{1,0:T(8,128)(2,1)S(1)}, u32[]{:S(2)}, u32[]{:S(2)}) collective-permute-start(bf16[320,64]{1,0:T(8,128)(2,1)S(1)} %fusion.4.refs_0_), channel_id=1, source_target_pairs={{0,16},{16,0},{1,17},{17,1},{2,18},{18,2},{3,19},{19,3},{4,20},{20... | collective-permute-start | bytes 122888 | tf_op jit(solution)/shard_map/ppermute | solution.py:480
  44.2 8.2 %collective-permute-start.6 = (bf16[4,2,64,128]{3,2,1,0:T(8,128)(2,1)S(1)}, bf16[4,2,64,128]{3,2,1,0:T(8,128)(2,1)S(1)}, u32[]{:S(2)}, u32[]{:S(2)}) collective-permute-start(bf16[4,2,64,128]{3,2,1,0:T(8,128)(2,1)S(1)} %denoise.2.refs_0_), channel_id=1, source_target_pairs={{0,4},{4,8},{8,12},{12,0},{1,5},{5,9},{9,13},{13,1},{2,6},{6,10},{... | collective-permute-start | bytes 393224 | tf_op jit(solution)/shard_map/ppermute | solution.py:480
  47.6 8.5 %collective-permute-start.7 = (bf16[4,2,64,128]{3,2,1,0:T(8,128)(2,1)S(1)}, bf16[4,2,64,128]{3,2,1,0:T(8,128)(2,1)S(1)}, u32[]{:S(2)}, u32[]{:S(2)}) collective-permute-start(bf16[4,2,64,128]{3,2,1,0:T(8,128)(2,1)S(1)} %denoise.2.refs_0_), channel_id=1, source_target_pairs={{0,8},{4,12},{8,0},{12,4},{1,9},{5,13},{9,1},{13,5},{2,10},{6,14},... | collective-permute-start | bytes 393224 | tf_op jit(solution)/shard_map/ppermute | solution.py:480
  48.9 7.5 %collective-permute-start.8 = (bf16[4,2,64,128]{3,2,1,0:T(8,128)(2,1)S(1)}, bf16[4,2,64,128]{3,2,1,0:T(8,128)(2,1)S(1)}, u32[]{:S(2)}, u32[]{:S(2)}) collective-permute-start(bf16[4,2,64,128]{3,2,1,0:T(8,128)(2,1)S(1)} %denoise.2.refs_0_), channel_id=1, source_target_pairs={{0,12},{4,0},{8,4},{12,8},{1,13},{5,1},{9,5},{13,9},{2,14},{6,2},{... | collective-permute-start | bytes 393224 | tf_op jit(solution)/shard_map/ppermute | solution.py:480
  61.2 8.7 %collective-permute-start.10 = (bf16[2,288,128]{2,1,0:T(8,128)(2,1)S(1)}, bf16[2,288,128]{2,1,0:T(8,128)(2,1)S(1)}, u32[]{:S(2)}, u32[]{:S(2)}) collective-permute-start(bf16[2,288,128]{2,1,0:T(8,128)(2,1)S(1)} %get-tuple-element.39), channel_id=1, source_target_pairs={{0,8},{4,12},{8,0},{12,4},{1,9},{5,13},{9,1},{13,5},{2,10},{6,14},... | collective-permute-start | bytes 442376 | tf_op jit(solution)/shard_map/ppermute | solution.py:480
  63.2 7.6 %collective-permute-start.11 = (bf16[2,288,128]{2,1,0:T(8,128)(2,1)S(1)}, bf16[2,288,128]{2,1,0:T(8,128)(2,1)S(1)}, u32[]{:S(2)}, u32[]{:S(2)}) collective-permute-start(bf16[2,288,128]{2,1,0:T(8,128)(2,1)S(1)} %get-tuple-element.40), channel_id=1, source_target_pairs={{0,12},{4,0},{8,4},{12,8},{1,13},{5,1},{9,5},{13,9},{2,14},{6,2},{... | collective-permute-start | bytes 442376 | tf_op jit(solution)/shard_map/ppermute | solution.py:480
  66.1 10.0 %collective-permute-start.9 = (bf16[2,288,128]{2,1,0:T(8,128)(2,1)S(1)}, bf16[2,288,128]{2,1,0:T(8,128)(2,1)S(1)}, u32[]{:S(2)}, u32[]{:S(2)}) collective-permute-start(bf16[2,288,128]{2,1,0:T(8,128)(2,1)S(1)} %get-tuple-element.38), channel_id=1, source_target_pairs={{0,4},{4,8},{8,12},{12,0},{1,5},{5,9},{9,13},{13,1},{2,6},{6,10},{... | collective-permute-start | bytes 442376 | tf_op jit(solution)/shard_map/ppermute | solution.py:480
  76.2 5.8 %collective-permute-start.12 = (bf16[2,288,128]{2,1,0:T(8,128)(2,1)S(1)}, bf16[2,288,128]{2,1,0:T(8,128)(2,1)S(1)}, u32[]{:S(2)}, u32[]{:S(2)}) collective-permute-start(bf16[2,288,128]{2,1,0:T(8,128)(2,1)S(1)} %add_convert_fusion.own), channel_id=1, source_target_pairs={{0,1},{1,2},{2,3},{4,5},{5,6},{6,7},{8,9},{9,10},{10,11},{12,13},{... | collective-permute-start | bytes 442376 | tf_op jit(solution)/shard_map/ppermute | solution.py:507
  78.1 6.5 %collective-permute-start.13 = (bf16[2,288,128]{2,1,0:T(8,128)(2,1)S(1)}, bf16[2,288,128]{2,1,0:T(8,128)(2,1)S(1)}, u32[]{:S(2)}, u32[]{:S(2)}) collective-permute-start(bf16[2,288,128]{2,1,0:T(8,128)(2,1)S(1)} %add_convert_fusion.own), channel_id=1, source_target_pairs={{1,0},{2,1},{3,2},{5,4},{6,5},{7,6},{9,8},{10,9},{11,10},{13,12},{... | collective-permute-start | bytes 442376 | tf_op jit(solution)/shard_map/ppermute | solution.py:508
  80.7 15.7 %collective-permute-start.15 = (bf16[4,2,64,128]{3,2,1,0:T(8,128)(2,1)S(1)}, bf16[4,2,64,128]{3,2,1,0:T(8,128)(2,1)S(1)}, u32[]{:S(2)}, u32[]{:S(2)}) collective-permute-start(bf16[4,2,64,128]{3,2,1,0:T(8,128)(2,1)S(1)} %denoise.2.refs_0_), channel_id=1, source_target_pairs={{16,0},{17,1},{18,2},{19,3},{20,4},{21,5},{22,6},{23,7},{24,8},{25... | collective-permute-start | bytes 393224 | tf_op jit(solution)/shard_map/ppermute | solution.py:515
  93.2 5.1 %collective-permute-start.14 = (bf16[4,2,64,128]{3,2,1,0:T(8,128)(2,1)S(1)}, bf16[4,2,64,128]{3,2,1,0:T(8,128)(2,1)S(1)}, u32[]{:S(2)}, u32[]{:S(2)}) collective-permute-start(bf16[4,2,64,128]{3,2,1,0:T(8,128)(2,1)S(1)} %denoise.3), channel_id=1, source_target_pairs={{0,16},{1,17},{2,18},{3,19},{4,20},{5,21},{6,22},{7,23},{8,24},{9,... | collective-permute-start | bytes 393224 | tf_op jit(solution)/shard_map/ppermute | solution.py:515
  (8 other events, 171.9 us)

commit v3 on v2

--- a/solution.py
+++ b/solution.py
@@ -68,12 +68,12 @@
     return jnp.dot(left, right, preferred_element_type=F32)
 
 
-def consistency_kernel(info, *refs, pieces, shares, edge, batch, direct):
+def consistency_kernel(*refs, pieces, shares, edge, batch, direct):
     images, refs = refs[:pieces], refs[pieces:]
     maps, samples, mask, tables = refs[:4]
     outs = refs[4 : 4 + shares]
     window, joined, refs = refs[4 + shares], refs[5 + shares], refs[6 + shares :]
-    block, me = info[0], info[1]
+    block, me = lax.axis_index("cascade"), lax.axis_index("coil")
     coils, phases, readouts, rows, part = samples.shape[1:]
     count = rows // 2
     share = count // shares
@@ -192,7 +192,7 @@
         outs[k][...] = window[:, pl.ds(begin, width + 2 * edge)]
 
 
-def consistency(info, images, maps, samples, mask, shares):
+def consistency(images, maps, samples, mask, shares):
     blocks, coils, phases, readouts, rows, part = samples.shape
     lines = rows // 2
     share_rows = rows // shares
@@ -215,8 +215,7 @@
     ]
     return pl.pallas_call(
         body,
-        in_specs=[pl.BlockSpec(memory_space=pltpu.SMEM)]
-        + [pl.BlockSpec(memory_space=pltpu.VMEM if direct else pl.ANY)] * (pieces + 4),
+        in_specs=[pl.BlockSpec(memory_space=pltpu.VMEM if direct else pl.ANY)] * (pieces + 4),
         out_specs=[pl.BlockSpec(memory_space=pltpu.VMEM)] * shares,
         scratch_shapes=[
             pltpu.VMEM((readouts, shares * phases * share_rows + 2 * edge, part), BF16),
@@ -233,7 +232,7 @@
             transcendentals=0,
         ),
         name="consistency",
-    )(info, *images, maps, samples, mask, tables)
+    )(*images, maps, samples, mask, tables)
 
 
 def tap_rows(phases, parts):
@@ -264,34 +263,36 @@
     return spread, own_phase, tiled, time_masks
 
 
-def weights_kernel(info, *refs, pieces):
+def weights_kernel(*refs, pieces):
     packs = refs[:pieces]
     spread, spread_t, own_phase, own_phase_t, tiled, tiled_t, time_masks = refs[pieces : pieces + 7]
     first_out, time_out, last_out = refs[pieces + 7 :]
     channels = tiled.shape[0]
-    pick = lax.rem(info[0] - pl.program_id(0) + pieces, pieces)
-    pack = packs[0][...].astype(F32)
-    for k in range(1, pieces):
-        pack = jnp.where(pick == k, packs[k][...].astype(F32), pack)
-    pack = pack.astype(BF16)
+    me = lax.axis_index("cascade")
 
     def transposed(block):
         return lax.dot_general(
             tiled_t[...], block, (((1,), (1,)), ((), ())), preferred_element_type=F32
         ).astype(BF16)
 
-    time = 0.0
-    for k in range(3):
-        block = transposed(pack[k * channels : (k + 1) * channels])
-        time = time + dot(block, tiled[...]) * time_masks[k].astype(F32)
-    time_out[0] = time.astype(BF16)
-    first = transposed(pack[3 * channels : 3 * channels + 64])
-    first_out[0] = (dot(first, spread_t[...]) * own_phase_t[...].astype(F32)).astype(BF16)
-    last = dot(spread[...], pack[3 * channels + 64 :]).astype(BF16)
-    last_out[0] = (dot(last, tiled[...]) * own_phase[...].astype(F32)).astype(BF16)
-
-
-def weight_matrices(info, packs, phases):
+    for section in range(pieces):
+        pick = lax.rem(me - section + pieces, pieces)
+        pack = packs[0][...].astype(F32)
+        for k in range(1, pieces):
+            pack = jnp.where(pick == k, packs[k][...].astype(F32), pack)
+        pack = pack.astype(BF16)
+        time = 0.0
+        for k in range(3):
+            block = transposed(pack[k * channels : (k + 1) * channels])
+            time = time + dot(block, tiled[...]) * time_masks[k].astype(F32)
+        time_out[section] = time.astype(BF16)
+        first = transposed(pack[3 * channels : 3 * channels + 64])
+        first_out[section] = (dot(first, spread_t[...]) * own_phase_t[...].astype(F32)).astype(BF16)
+        last = dot(spread[...], pack[3 * channels + 64 :]).astype(BF16)
+        last_out[section] = (dot(last, tiled[...]) * own_phase[...].astype(F32)).astype(BF16)
+
+
+def weight_matrices(packs, phases):
     sections = len(packs)
     channels = packs[0].shape[1]
     spread, own_phase, tiled, time_masks = weight_tables(phases, channels)
@@ -303,23 +304,15 @@
     shapes = [(wide, taps), (wide, wide), (taps, wide)]
     return pl.pallas_call(
         functools.partial(weights_kernel, pieces=sections),
-        grid_spec=pltpu.PrefetchScalarGridSpec(
-            num_scalar_prefetch=1,
-            grid=(sections,),
-            in_specs=[pl.BlockSpec(p.shape, lambda s, info: (0, 0)) for p in packs]
-            + [
-                pl.BlockSpec(t.shape, functools.partial(lambda n, s, info: (0,) * n, t.ndim))
-                for t in tables
-            ],
-            out_specs=[pl.BlockSpec((1,) + s, lambda s, info: (s, 0, 0)) for s in shapes],
-        ),
+        in_specs=[pl.BlockSpec(memory_space=pltpu.VMEM)] * (sections + len(tables)),
+        out_specs=[pl.BlockSpec(memory_space=pltpu.VMEM)] * len(shapes),
         out_shape=[jax.ShapeDtypeStruct((sections,) + s, BF16) for s in shapes],
         compiler_params=pltpu.CompilerParams(vmem_limit_bytes=VMEM_LIMIT),
         cost_estimate=pl.CostEstimate(
             flops=sections * wide * wide * 1000, bytes_accessed=2 * 1024 * 1024, transcendentals=0
         ),
         name="weights",
-    )(info, *packs, *tables)
+    )(*packs, *tables)
 
 
 def shifted(values, step):
@@ -330,107 +323,104 @@
     return jnp.where(lane == part - 1, 0.0, pltpu.roll(values, part - 1, 1))
 
 
-def denoise_kernel(info, own, low, high, first, time, last, apart, out, taps, sums, *, phases, chunk):
-    step = pl.program_id(0)
-    steps = pl.num_programs(0)
+def denoise_kernel(own, even, odd, first, time, last, apart, out, taps, sums, *, phases, section):
     readouts, span, part = own.shape
     cell = 2 * phases
     lines = span // cell
     group = taps.shape[2]
     used = 9 * cell
-
-    @pl.when(step == 0)
-    def _():
-        slabs = (
-            [low[readouts - HALO + k] for k in range(HALO)]
-            + [own[k] for k in range(readouts)]
-            + [high[k] for k in range(HALO)]
-        )
-        filler = [jnp.zeros((group - used, part), F32)] if group > used else []
-        for index, slab in enumerate(slabs):
-            slab = slab.astype(F32)
-            views = [shifted(slab, 1), slab, shifted(slab, -1)]
-            for line in range(1, lines - 1):
-                around = [
-                    views[e][cell * (line + c - 1) : cell * (line + c)]
-                    for c in range(3)
-                    for e in range(3)
-                ]
-                taps[index, line - 1] = jnp.concatenate(around + filler, 0).astype(BF16)
-        sums[...] = jnp.zeros_like(sums)
-
+    steps = readouts + 2
+    readout_no, coil_no = lax.axis_index("readout"), lax.axis_index("coil")
+    low_inside = readout_no > 0
+    high_inside = readout_no < lax.axis_size("readout") - 1
+    first_line = (coil_no > 0).astype(F32).astype(BF16)
+    last_line = (coil_no < lax.axis_size("coil") - 1).astype(F32).astype(BF16)
+    swapped = lax.rem(readout_no, 2) == 1
+
+    def side(inside, here, there):
+        return jnp.where(inside, jnp.where(swapped, here.astype(F32), there.astype(F32)), 0.0)
+
+    slabs = (
+        [side(low_inside, even[readouts - HALO + k], odd[readouts - HALO + k]) for k in range(HALO)]
+        + [own[k].astype(F32) for k in range(readouts)]
+        + [side(high_inside, odd[k], even[k]) for k in range(HALO)]
+    )
+    filler = [jnp.zeros((group - used, part), F32)] if group > used else []
+    for index, slab in enumerate(slabs):
+        views = [shifted(slab, 1), slab, shifted(slab, -1)]
+        for line in range(1, lines - 1):
+            around = [
+                views[e][cell * (line + c - 1) : cell * (line + c)] for c in range(3) for e in range(3)
+            ]
+            taps[index, line - 1] = jnp.concatenate(around + filler, 0).astype(BF16)
+    sums[...] = jnp.zeros_like(sums)
     used_taps = min(3, readouts)
-    begun = jnp.clip(step - readouts + 1, 0, 3 - used_taps)
-    inside = jnp.where(step == 0, info[2], jnp.where(step == steps - 1, info[3], 1))
-
-    @pl.when(inside == 1)
-    def _():
-        for begin in range(1, lines - 1, chunk):
-            block = range(begin, min(begin + chunk, lines - 1))
+
+    def add_row(step, carry):
+        begun = jnp.clip(step - readouts + 1, 0, 3 - used_taps)
+        inside = ((step > 0) | low_inside) & ((step < steps - 1) | high_inside)
+
+        @pl.when(inside)
+        def _():
+            block = range(1, lines - 1)
             near = jnp.concatenate(
                 [taps[pl.ds(step, 3), line - 1].reshape(3 * group, part) for line in block], 1
             )
-            hidden = jnp.maximum(dot(first[0], near), 0.0).astype(BF16)
-            mixed = jnp.maximum(hidden.astype(F32) + dot(time[0], hidden), 0.0).astype(BF16)
-            pieces = [mixed[:, k * part : (k + 1) * part] for k in range(len(block))]
-            if block[0] == 1:
-                pieces[0] = pieces[0] * info[4].astype(F32).astype(BF16)
-            if block[-1] == lines - 2:
-                pieces[-1] = pieces[-1] * info[5].astype(F32).astype(BF16)
-            mixed = jnp.concatenate(pieces, 1)
-            result = dot(last[0, pl.ds(pl.multiple_of(begun * group, 16), used_taps * group)], mixed)
+            hidden = jnp.maximum(dot(first[section], near), 0.0).astype(BF16)
+            mixed = jnp.maximum(hidden.astype(F32) + dot(time[section], hidden), 0.0).astype(BF16)
+            edge = (len(block) - 1) * part
+            mixed = jnp.concatenate(
+                [mixed[:, :part] * first_line, mixed[:, part:edge], mixed[:, edge:] * last_line], 1
+            )
+            chosen = pl.ds(pl.multiple_of(begun * group, 16), used_taps * group)
+            result = dot(last[section, chosen], mixed)
             for a in range(used_taps):
                 target = step + 2 - begun - a
                 for e in range(3):
-                    for line in range(block[0] - 1, block[-1] + 2):
+                    for line in range(lines):
                         terms = []
                         for c in range(3):
-                            source = line + c - 1
-                            if block[0] <= source <= block[-1]:
+                            source = line + c - 2
+                            if 0 <= source < len(block):
                                 at = a * group + (3 * c + e) * cell
-                                k = source - block[0]
-                                terms.append(result[at : at + cell, k * part : (k + 1) * part])
+                                terms.append(
+                                    result[at : at + cell, source * part : (source + 1) * part]
+                                )
                         sums[e, target, line * cell : (line + 1) * cell] += sum(terms[1:], terms[0])
 
-    @pl.when(step == steps - 1)
-    def _():
-        body = slice(HALO * cell, span - HALO * cell)
-        finals = []
+        return carry
+
+    lax.fori_loop(0, steps, add_row, 0)
+
+    body = slice(HALO * cell, span - HALO * cell)
+    finals = []
+    for r in range(readouts):
+        value = own[r, body].astype(F32) + sums[1, r + HALO, body]
+        value = value + shifted(sums[0, r + HALO, body], 1)
+        value = value + shifted(sums[2, r + HALO, body], -1)
+        finals.append(value.astype(BF16))
+    ordered = dot(apart[...], jnp.concatenate(finals, 1)).astype(BF16)
+    height = out.shape[2]
+    for p in range(phases):
         for r in range(readouts):
-            value = own[r, body].astype(F32) + sums[1, r + HALO, body]
-            value = value + shifted(sums[0, r + HALO, body], 1)
-            value = value + shifted(sums[2, r + HALO, body], -1)
-            finals.append(value.astype(BF16))
-        ordered = dot(apart[...], jnp.concatenate(finals, 1)).astype(BF16)
-        height = out.shape[2]
-        for p in range(phases):
-            for r in range(readouts):
-                out[p, r] = ordered[p * height : (p + 1) * height, r * part : (r + 1) * part]
-
-
-def denoise(info, own, low, high, matrices, section, phases):
+            out[p, r] = ordered[p * height : (p + 1) * height, r * part : (r + 1) * part]
+
+
+def denoise(own, even, odd, matrices, section, phases):
     readouts, span, part = own.shape
     cell = 2 * phases
     lines = span // cell
     share = lines - 2 * HALO
-    first, time, last = matrices
     apart = bf16(phase_inside(phases, share).T)
-    group = first.shape[2] // 3
-    whole = pl.BlockSpec((readouts, span, part), lambda s, info: (0, 0, 0))
+    group = matrices[0].shape[2] // 3
     return pl.pallas_call(
-        functools.partial(denoise_kernel, phases=phases, chunk=34),
-        grid_spec=pltpu.PrefetchScalarGridSpec(
-            num_scalar_prefetch=1,
-            grid=(readouts + 2,),
-            in_specs=[whole] * 3
-            + [pl.BlockSpec((1,) + w.shape[1:], lambda s, info: (section, 0, 0)) for w in matrices]
-            + [pl.BlockSpec(apart.shape, lambda s, info: (0, 0))],
-            out_specs=pl.BlockSpec((phases, readouts, 2 * share, part), lambda s, info: (0, 0, 0, 0)),
-            scratch_shapes=[
-                pltpu.VMEM((readouts + 2 * HALO, lines - 2, group, part), BF16),
-                pltpu.VMEM((3, readouts + 2 * HALO, span, part), F32),
-            ],
-        ),
+        functools.partial(denoise_kernel, phases=phases, section=section),
+        in_specs=[pl.BlockSpec(memory_space=pltpu.VMEM)] * 7,
+        out_specs=pl.BlockSpec(memory_space=pltpu.VMEM),
+        scratch_shapes=[
+            pltpu.VMEM((readouts + 2 * HALO, lines - 2, group, part), BF16),
+            pltpu.VMEM((3, readouts + 2 * HALO, span, part), F32),
+        ],
         out_shape=jax.ShapeDtypeStruct((phases, readouts, 2 * share, part), BF16),
         compiler_params=pltpu.CompilerParams(vmem_limit_bytes=VMEM_LIMIT),
         cost_estimate=pl.CostEstimate(
@@ -439,19 +429,29 @@
             transcendentals=0,
         ),
         name="denoise",
-    )(info, own, low, high, first, time, last, apart)
+    )(own, even, odd, *matrices, apart)
 
 
 def rotation(count, step):
     return [(i, (i + step) % count) for i in range(count)]
+
+
+def swaps(count, first):
+    pairs = [(i, i + 1) for i in range(first, count - 1, 2)]
+    return pairs + [(target, source) for source, target in pairs]
+
+
+def exchanged(values, axis, count):
+    arrived = {0: values[0]}
+    for k in sorted(range(1, count), key=lambda k: abs(k - count / 2)):
+        arrived[k] = lax.ppermute(values[k], axis, rotation(count, k))
+    return [arrived[k] for k in range(count)]
 
 
 def per_device(initial, coil_maps, kspace, sampled, first_w, time_w, last_w):
     section_no = lax.axis_index("cascade")
     sections = lax.axis_size("cascade")
-    coil_no = lax.axis_index("coil")
     shares = lax.axis_size("coil")
-    readout_no = lax.axis_index("readout")
     readout_parts = lax.axis_size("readout")
     phases = kspace.shape[2]
     part = kspace.shape[-1]
@@ -460,33 +460,15 @@
     def rows_of(array):
         return array.reshape(array.shape[:-3] + (2 * array.shape[-3], part))
 
-    initial, coil_maps, kspace = rows_of(initial), rows_of(coil_maps), rows_of(kspace)
-    info = jnp.stack(
-        [
-            section_no,
-            coil_no,
-            readout_no > 0,
-            readout_no < readout_parts - 1,
-            coil_no > 0,
-            coil_no < shares - 1,
-        ]
-    ).astype(jnp.int32)
-
     def padded(block):
         return jnp.pad(block, ((0, -block.shape[0] % 64), (0, 0)))
 
-    def exchanged(values, axis, count):
-        return [values[0]] + [
-            lax.ppermute(values[k], axis, rotation(count, k)) for k in range(1, count)
-        ]
-
-    forward = [(i, i + 1) for i in range(readout_parts - 1)]
-    backward = [(target, source) for source, target in forward]
+    initial, coil_maps, kspace = rows_of(initial), rows_of(coil_maps), rows_of(kspace)
     images = [initial]
     matrices = None
     kept, sent = [], []
     for section in range(sections):
-        partial = consistency(info, images, coil_maps, kspace, sampled, shares)
+        partial = consistency(images, coil_maps, kspace, sampled, shares)
         if matrices is None:
             partial, (first_w, time_w, last_w) = lax.optimization_barrier(
                 (partial, (first_w, time_w, last_w))
@@ -502,11 +484,14 @@
                 0,
             )
             packs = exchanged([pack] * sections, "cascade", sections)
-            matrices = weight_matrices(info, packs, phases)
+            matrices = weight_matrices(packs, phases)
+            parts, matrices = lax.optimization_barrier((parts, matrices))
+        else:
+            parts, sent[-1] = lax.optimization_barrier((parts, sent[-1]))
         combined = sum(p.astype(F32) for p in parts).astype(BF16)
-        low = lax.ppermute(combined, "readout", forward)
-        high = lax.ppermute(combined, "readout", backward)
-        output = denoise(info, combined, low, high, matrices, section, phases)
+        even = lax.ppermute(combined, "readout", swaps(readout_parts, 0))
+        odd = lax.ppermute(combined, "readout", swaps(readout_parts, 1))
+        output = denoise(combined, even, odd, matrices, section, phases)
         if section < sections - 1:
             images = exchanged([output] * shares, "coil", shares)
         kept.append(output)

time: 101 us -> 88.4 us (0.88)
  waiting for transfers between devices: 32.6 us -> 24 us
  Pallas kernels: 31.6 us -> 27.9 us
    ppermute x14, waiting for transfers between devices: 30.7 us -> 17.6 us  [the longest x10 11.4 us: exchanged(): arrived[k] = lax.ppermute(values[k], axis, rotation(count, k))]
    ppermute x2, waiting for transfers between devices: 1.89 us -> 6.31 us  [per_device(): lax.ppermute(output, 'cascade', [((section + k) % sections, section)])]
    pallas_call x5, Pallas kernels: 31.6 us -> 27.9 us  [the longest x2 15.8 us: denoise(): pl.pallas_call(functools.partial(denoise_kernel, phases=phases, section=s...]
  transfers between devices with their start and end apart: 16 -> 16, of which waited for: 11 -> 10; matrix products, arithmetic and copies ran while one was open for 0% -> 0% of each run, Pallas kernels for 11% -> 1%
where the time goes in v3:
time: 88.4 us; the launch traced here: 87.3 us
  starting transfers between devices  32.7 us (37%)
  Pallas kernels  27.9 us (32%)
  waiting for transfers between devices  24 us (27%)
  other arithmetic  2.21 us (2%)
    ppermute x10, starting transfers between devices, exchanged(): arrived[k] = lax.ppermute(values[k], axis, rotation(count, k))  16 us
    pallas_call x2, Pallas kernels, denoise(): pl.pallas_call(functools.partial(denoise_kernel, phases=phases, section=s...  15.8 us
    ppermute x2, starting transfers between devices, per_device(): odd = lax.ppermute(combined, 'readout', swaps(readout_parts, 1))  11.5 us
    ppermute x10, waiting for transfers between devices, exchanged(): arrived[k] = lax.ppermute(values[k], axis, rotation(count, k))  11.4 us
    pallas_call x2, Pallas kernels, consistency(): pl.pallas_call(body, in_specs=[pl.BlockSpec(memory_space=pltpu.VMEM if di...  10.9 us
    ppermute x2, waiting for transfers between devices, per_device(): lax.ppermute(output, 'cascade', [((section + k) % sections, section)])  6.31 us
    ppermute x2, waiting for transfers between devices, per_device(): odd = lax.ppermute(combined, 'readout', swaps(readout_parts, 1))  6.21 us
    ppermute x2, starting transfers between devices, per_device(): lax.ppermute(output, 'cascade', [((section + k) % sections, section)])  4.43 us
  transfers between devices with their start and end apart: 16, of which 10 were waited for; matrix products, arithmetic and copies ran while one was open for 0% of the time, Pallas kernels for 1%

profile of v3, /device:TPU:1, one launch (start us, length us, event | category | flops | bytes accessed | tf_op | source)
XLA Modules:
  0.0 87.3 jit_solution(6646503881071519510)
XLA Ops:
  0.1 6.8 %consistency.2 = (bf16[2,288,128]{2,1,0:T(8,128)(2,1)}, bf16[2,288,128]{2,1,0:T(8,128)(2,1)}, bf16[2,288,128]{2,1,0:T(8,128)(2,1)}, bf16[2,288,128]{2,1,0:T(8,128)(2,1)}) custom-call(bf16[2,4,2,256,128]{4,3,2,1,0:T(8,128)(2,1)} %bitcast.17, bf16[2,4,2,256,128]{4,3,2,1,0:T(8,128)(2,1)} %bitcast.11, bf16[2,4,4,2,256,128]{5,4,3,2,1,0:T(8,128)(2,1)} %bitcast.9, ...), custom_call_target="tpu_custom_call" | custom-call | flops 5368709120 | bytes 4194304 | tf_op jit(solution)/shard_map/consistency/pallas_call | solution.py:216
  6.9 2.2 %collective-permute-start = (bf16[2,288,128]{2,1,0:T(8,128)(2,1)}, bf16[2,288,128]{2,1,0:T(8,128)(2,1)S(1)}, u32[]{:S(2)}, u32[]{:S(2)}) collective-permute-start(bf16[2,288,128]{2,1,0:T(8,128)(2,1)} %get-tuple-element.40), channel_id=1, source_target_pairs={{0,4},{4,8},{8,12},{12,0},{1,5},{5,9},{9,13},{13,1},{2,6},{6,10},{... | collective-permute-start | bytes 442376 | tf_op jit(solution)/shard_map/ppermute | solution.py:447
  9.1 2.3 %collective-permute-start.1 = (bf16[2,288,128]{2,1,0:T(8,128)(2,1)}, bf16[2,288,128]{2,1,0:T(8,128)(2,1)S(1)}, u32[]{:S(2)}, u32[]{:S(2)}) collective-permute-start(bf16[2,288,128]{2,1,0:T(8,128)(2,1)} %get-tuple-element.41), channel_id=1, source_target_pairs={{0,8},{4,12},{8,0},{12,4},{1,9},{5,13},{9,1},{13,5},{2,10},{6,14},... | collective-permute-start | bytes 442376 | tf_op jit(solution)/shard_map/ppermute | solution.py:447
  12.6 1.3 %collective-permute-start.3 = (bf16[320,64]{1,0:T(8,128)(2,1)S(1)}, bf16[320,64]{1,0:T(8,128)(2,1)S(1)}, u32[]{:S(2)}, u32[]{:S(2)}) collective-permute-start(bf16[320,64]{1,0:T(8,128)(2,1)S(1)} %fusion.4.refs_0_), channel_id=1, source_target_pairs={{0,16},{16,0},{1,17},{17,1},{2,18},{18,2},{3,19},{19,3},{4,20},{20... | collective-permute-start | bytes 122888 | tf_op jit(solution)/shard_map/ppermute | solution.py:447
  13.9 2.3 %collective-permute-done.3.refs_1_ = bf16[320,64]{1,0:T(8,128)(2,1)S(1)} collective-permute-done((bf16[320,64]{1,0:T(8,128)(2,1)S(1)}, bf16[320,64]{1,0:T(8,128)(2,1)S(1)}, u32[]{:S(2)}, u32[]{:S(2)}) %collective-permute-start.3) | collective-permute-done | bytes 40992 | tf_op jit(solution)/shard_map/ppermute | solution.py:447
  16.3 1.2 %weights.1 = (bf16[2,256,240]{2,1,0:T(8,128)(2,1)S(1)}, bf16[2,256,256]{2,1,0:T(8,128)(2,1)S(1)}, bf16[2,240,256]{2,1,0:T(8,128)(2,1)S(1)}) custom-call(bf16[320,64]{1,0:T(8,128)(2,1)S(1)} %fusion.4.refs_0_, bf16[320,64]{1,0:T(8,128)(2,1)S(1)} %collective-permute-done.3.refs_1_, bf16[240,64]{1,0:T(8,128)(2,1)S(1)} %copy-done.4, ...), custom_call_target="tpu_custom_call" | custom-call | flops 131072000 | bytes 2097152 | tf_op jit(solution)/shard_map/weights/pallas_call | solution.py:305
  17.5 4.5 %collective-permute-done.1 = bf16[2,288,128]{2,1,0:T(8,128)(2,1)S(1)} collective-permute-done((bf16[2,288,128]{2,1,0:T(8,128)(2,1)}, bf16[2,288,128]{2,1,0:T(8,128)(2,1)S(1)}, u32[]{:S(2)}, u32[]{:S(2)}) %collective-permute-start.1) | collective-permute-done | bytes 147488 | tf_op jit(solution)/shard_map/ppermute | solution.py:447
  23.7 3.3 %collective-permute-start.5 = (bf16[2,288,128]{2,1,0:T(8,128)(2,1)S(1)}, bf16[2,288,128]{2,1,0:T(8,128)(2,1)S(1)}, u32[]{:S(2)}, u32[]{:S(2)}) collective-permute-start(bf16[2,288,128]{2,1,0:T(8,128)(2,1)S(1)} %add_convert_fusion.1.own), channel_id=1, source_target_pairs={{1,2},{2,1},{5,6},{6,5},{9,10},{10,9},{13,14},{14,13},{17,18},{18,... | collective-permute-start | bytes 442376 | tf_op jit(solution)/shard_map/ppermute | solution.py:493
  27.0 3.4 %collective-permute-done.5.odd = bf16[2,288,128]{2,1,0:T(8,128)(2,1)S(1)} collective-permute-done((bf16[2,288,128]{2,1,0:T(8,128)(2,1)S(1)}, bf16[2,288,128]{2,1,0:T(8,128)(2,1)S(1)}, u32[]{:S(2)}, u32[]{:S(2)}) %collective-permute-start.5) | collective-permute-done | bytes 147488 | tf_op jit(solution)/shard_map/ppermute | solution.py:493
  30.4 7.9 %denoise.2.refs_0_ = bf16[4,2,64,128]{3,2,1,0:T(8,128)(2,1)S(1)} custom-call(bf16[2,288,128]{2,1,0:T(8,128)(2,1)S(1)} %add_convert_fusion.1.own, bf16[2,288,128]{2,1,0:T(8,128)(2,1)S(1)} %collective-permute-done.4.even, bf16[2,288,128]{2,1,0:T(8,128)(2,1)S(1)} %collective-permute-done.5.odd, bf16[2,256,240]{2,1,0:T(8,128)(2,1)S(1)} %get-tuple-element.53.first, ...), custom_call_target="tpu_custom_call" | custom-call | flops 7247757312 | bytes 2097152 | tf_op jit(solution)/shard_map/denoise/pallas_call | solution.py:416
  38.3 3.4 %collective-permute-start.6 = (bf16[4,2,64,128]{3,2,1,0:T(8,128)(2,1)S(1)}, bf16[4,2,64,128]{3,2,1,0:T(8,128)(2,1)S(1)}, u32[]{:S(2)}, u32[]{:S(2)}) collective-permute-start(bf16[4,2,64,128]{3,2,1,0:T(8,128)(2,1)S(1)} %denoise.2.refs_0_), channel_id=1, source_target_pairs={{0,4},{4,8},{8,12},{12,0},{1,5},{5,9},{9,13},{13,1},{2,6},{6,10},{... | collective-permute-start | bytes 393224 | tf_op jit(solution)/shard_map/ppermute | solution.py:447
  41.7 1.2 %collective-permute-start.7 = (bf16[4,2,64,128]{3,2,1,0:T(8,128)(2,1)S(1)}, bf16[4,2,64,128]{3,2,1,0:T(8,128)(2,1)S(1)}, u32[]{:S(2)}, u32[]{:S(2)}) collective-permute-start(bf16[4,2,64,128]{3,2,1,0:T(8,128)(2,1)S(1)} %denoise.2.refs_0_), channel_id=1, source_target_pairs={{0,8},{4,12},{8,0},{12,4},{1,9},{5,13},{9,1},{13,5},{2,10},{6,14},... | collective-permute-start | bytes 393224 | tf_op jit(solution)/shard_map/ppermute | solution.py:447
  43.9 1.1 %collective-permute-done.6.refs_1_ = bf16[4,2,64,128]{3,2,1,0:T(8,128)(2,1)S(1)} collective-permute-done((bf16[4,2,64,128]{3,2,1,0:T(8,128)(2,1)S(1)}, bf16[4,2,64,128]{3,2,1,0:T(8,128)(2,1)S(1)}, u32[]{:S(2)}, u32[]{:S(2)}) %collective-permute-start.6) | collective-permute-done | bytes 131104 | tf_op jit(solution)/shard_map/ppermute | solution.py:447
  45.0 2.9 %collective-permute-done.7.refs_2_ = bf16[4,2,64,128]{3,2,1,0:T(8,128)(2,1)S(1)} collective-permute-done((bf16[4,2,64,128]{3,2,1,0:T(8,128)(2,1)S(1)}, bf16[4,2,64,128]{3,2,1,0:T(8,128)(2,1)S(1)}, u32[]{:S(2)}, u32[]{:S(2)}) %collective-permute-start.7) | collective-permute-done | bytes 131104 | tf_op jit(solution)/shard_map/ppermute | solution.py:447
  48.2 4.1 %consistency.3 = (bf16[2,288,128]{2,1,0:T(8,128)(2,1)S(1)}, bf16[2,288,128]{2,1,0:T(8,128)(2,1)S(1)}, bf16[2,288,128]{2,1,0:T(8,128)(2,1)S(1)}, bf16[2,288,128]{2,1,0:T(8,128)(2,1)S(1)}) custom-call(bf16[4,2,64,128]{3,2,1,0:T(8,128)(2,1)S(1)} %denoise.2.refs_0_, bf16[4,2,64,128]{3,2,1,0:T(8,128)(2,1)S(1)} %collective-permute-done.6.refs_1_, ...), custom_call_target="tpu_custom_call" | custom-call | flops 5368709120 | bytes 4194304 | tf_op jit(solution)/shard_map/consistency/pallas_call | solution.py:216
  53.1 2.8 %collective-permute-start.11 = (bf16[2,288,128]{2,1,0:T(8,128)(2,1)S(1)}, bf16[2,288,128]{2,1,0:T(8,128)(2,1)S(1)}, u32[]{:S(2)}, u32[]{:S(2)}) collective-permute-start(bf16[2,288,128]{2,1,0:T(8,128)(2,1)S(1)} %get-tuple-element.59), channel_id=1, source_target_pairs={{0,12},{4,0},{8,4},{12,8},{1,13},{5,1},{9,5},{13,9},{2,14},{6,2},{... | collective-permute-start | bytes 442376 | tf_op jit(solution)/shard_map/ppermute | solution.py:447
  55.9 1.3 %collective-permute-start.12 = (bf16[4,2,64,128]{3,2,1,0:T(8,128)(2,1)S(1)}, bf16[4,2,64,128]{3,2,1,0:T(8,128)(2,1)S(1)}, u32[]{:S(2)}, u32[]{:S(2)}) collective-permute-start(bf16[4,2,64,128]{3,2,1,0:T(8,128)(2,1)S(1)} %denoise.2.refs_0_), channel_id=1, source_target_pairs={{16,0},{17,1},{18,2},{19,3},{20,4},{21,5},{22,6},{23,7},{24,8},{25... | collective-permute-start | bytes 393224 | tf_op jit(solution)/shard_map/ppermute | solution.py:500
  57.1 4.4 %collective-permute-done.12 = bf16[4,2,64,128]{3,2,1,0:T(8,128)(2,1)S(1)} collective-permute-done((bf16[4,2,64,128]{3,2,1,0:T(8,128)(2,1)S(1)}, bf16[4,2,64,128]{3,2,1,0:T(8,128)(2,1)S(1)}, u32[]{:S(2)}, u32[]{:S(2)}) %collective-permute-start.12) | collective-permute-done | bytes 131104 | tf_op jit(solution)/shard_map/ppermute | solution.py:500
  62.1 8.3 %collective-permute-start.14 = (bf16[2,288,128]{2,1,0:T(8,128)(2,1)S(1)}, bf16[2,288,128]{2,1,0:T(8,128)(2,1)S(1)}, u32[]{:S(2)}, u32[]{:S(2)}) collective-permute-start(bf16[2,288,128]{2,1,0:T(8,128)(2,1)S(1)} %add_convert_fusion.own), channel_id=1, source_target_pairs={{1,2},{2,1},{5,6},{6,5},{9,10},{10,9},{13,14},{14,13},{17,18},{18,... | collective-permute-start | bytes 442376 | tf_op jit(solution)/shard_map/ppermute | solution.py:493
  70.4 2.8 %collective-permute-done.14.odd = bf16[2,288,128]{2,1,0:T(8,128)(2,1)S(1)} collective-permute-done((bf16[2,288,128]{2,1,0:T(8,128)(2,1)S(1)}, bf16[2,288,128]{2,1,0:T(8,128)(2,1)S(1)}, u32[]{:S(2)}, u32[]{:S(2)}) %collective-permute-start.14) | collective-permute-done | bytes 147488 | tf_op jit(solution)/shard_map/ppermute | solution.py:493
  73.2 7.9 %denoise.3 = bf16[4,2,64,128]{3,2,1,0:T(8,128)(2,1)S(1)} custom-call(bf16[2,288,128]{2,1,0:T(8,128)(2,1)S(1)} %add_convert_fusion.own, bf16[2,288,128]{2,1,0:T(8,128)(2,1)S(1)} %collective-permute-done.13.even, bf16[2,288,128]{2,1,0:T(8,128)(2,1)S(1)} %collective-permute-done.14.odd, bf16[2,256,240]{2,1,0:T(8,128)(2,1)S(1)} %get-tuple-element.53.first, ...), custom_call_target="tpu_custom_call" | custom-call | flops 7247757312 | bytes 2097152 | tf_op jit(solution)/shard_map/denoise/pallas_call | solution.py:416
  81.1 3.1 %collective-permute-start.15 = (bf16[4,2,64,128]{3,2,1,0:T(8,128)(2,1)S(1)}, bf16[4,2,64,128]{3,2,1,0:T(8,128)(2,1)S(1)}, u32[]{:S(2)}, u32[]{:S(2)}) collective-permute-start(bf16[4,2,64,128]{3,2,1,0:T(8,128)(2,1)S(1)} %denoise.3), channel_id=1, source_target_pairs={{0,16},{1,17},{2,18},{3,19},{4,20},{5,21},{6,22},{7,23},{8,24},{9,... | collective-permute-start | bytes 393224 | tf_op jit(solution)/shard_map/ppermute | solution.py:500
  84.3 1.9 %collective-permute-done.15 = bf16[4,2,64,128]{3,2,1,0:T(8,128)(2,1)S(1)} collective-permute-done((bf16[4,2,64,128]{3,2,1,0:T(8,128)(2,1)S(1)}, bf16[4,2,64,128]{3,2,1,0:T(8,128)(2,1)S(1)}, u32[]{:S(2)}, u32[]{:S(2)}) %collective-permute-start.15) | collective-permute-done | bytes 131104 | tf_op jit(solution)/shard_map/ppermute | solution.py:500
  86.2 1.1 %pad_maximum_fusion = bf16[1,2,4,2,32,2,128]{6,5,4,3,2,1,0:T(2,128)(2,1)} fusion(bf16[1,1,4,2,32,2,128]{6,5,4,3,2,1,0:T(2,128)(2,1)S(1)} %bitcast.13, bf16[1,1,4,2,32,2,128]{6,5,4,3,2,1,0:T(2,128)(2,1)S(1)} %bitcast.14), kind=kLoop, calls=%fused_computation.2 | loop fusion | flops 131072 | bytes 524288 | tf_op jit(solution)/shard_map/stack | solution.py:513
  (51 shorter events, 5.4 us)
Async XLA Ops:
  0.0 16.3 %copy-start = (bf16[3,256,256]{2,1,0:T(8,128)(2,1)S(1)}, bf16[3,256,256]{2,1,0:T(8,128)(2,1)}, u32[]{:S(2)}) copy-start(bf16[3,256,256]{2,1,0:T(8,128)(2,1)} %constant.36.clone.refs_8_) | copy-start | bytes 1179652
  0.0 16.3 %copy-start.1 = (bf16[256,240]{1,0:T(8,128)(2,1)S(1)}, bf16[256,240]{1,0:T(8,128)(2,1)}, u32[]{:S(2)}) copy-start(bf16[256,240]{1,0:T(8,128)(2,1)} %constant.33.clone.refs_5_) | copy-start | bytes 368644
  0.0 16.2 %copy-start.2 = (bf16[240,256]{1,0:T(8,128)(2,1)S(1)}, bf16[240,256]{1,0:T(8,128)(2,1)}, u32[]{:S(2)}) copy-start(bf16[240,256]{1,0:T(8,128)(2,1)} %constant.32.clone.refs_4_) | copy-start | bytes 368644
  0.1 30.3 %copy-start.11 = (bf16[256,256]{1,0:T(8,128)(2,1)S(1)}, bf16[256,256]{1,0:T(8,128)(2,1)}, u32[]{:S(2)}) copy-start(bf16[256,256]{1,0:T(8,128)(2,1)} %constant.37.clone.apart) | copy-start | bytes 393220
  6.9 10.6 %collective-permute-start = (bf16[2,288,128]{2,1,0:T(8,128)(2,1)}, bf16[2,288,128]{2,1,0:T(8,128)(2,1)S(1)}, u32[]{:S(2)}, u32[]{:S(2)}) collective-permute-start(bf16[2,288,128]{2,1,0:T(8,128)(2,1)} %get-tuple-element.40), channel_id=1, source_target_pairs={{0,4},{4,8},{8,12},{12,0},{1,5},{5,9},{9,13},{13,1},{2,6},{6,10},{... | collective-permute-start | bytes 442376 | tf_op jit(solution)/shard_map/ppermute | solution.py:447
  9.1 12.9 %collective-permute-start.1 = (bf16[2,288,128]{2,1,0:T(8,128)(2,1)}, bf16[2,288,128]{2,1,0:T(8,128)(2,1)S(1)}, u32[]{:S(2)}, u32[]{:S(2)}) collective-permute-start(bf16[2,288,128]{2,1,0:T(8,128)(2,1)} %get-tuple-element.41), channel_id=1, source_target_pairs={{0,8},{4,12},{8,0},{12,4},{1,9},{5,13},{9,1},{13,5},{2,10},{6,14},... | collective-permute-start | bytes 442376 | tf_op jit(solution)/shard_map/ppermute | solution.py:447
  11.5 10.6 %collective-permute-start.2 = (bf16[2,288,128]{2,1,0:T(8,128)(2,1)}, bf16[2,288,128]{2,1,0:T(8,128)(2,1)S(1)}, u32[]{:S(2)}, u32[]{:S(2)}) collective-permute-start(bf16[2,288,128]{2,1,0:T(8,128)(2,1)} %get-tuple-element.42), channel_id=1, source_target_pairs={{0,12},{4,0},{8,4},{12,8},{1,13},{5,1},{9,5},{13,9},{2,14},{6,2},{... | collective-permute-start | bytes 442376 | tf_op jit(solution)/shard_map/ppermute | solution.py:447
  12.6 3.7 %collective-permute-start.3 = (bf16[320,64]{1,0:T(8,128)(2,1)S(1)}, bf16[320,64]{1,0:T(8,128)(2,1)S(1)}, u32[]{:S(2)}, u32[]{:S(2)}) collective-permute-start(bf16[320,64]{1,0:T(8,128)(2,1)S(1)} %fusion.4.refs_0_), channel_id=1, source_target_pairs={{0,16},{16,0},{1,17},{17,1},{2,18},{18,2},{3,19},{19,3},{4,20},{20... | collective-permute-start | bytes 122888 | tf_op jit(solution)/shard_map/ppermute | solution.py:447
  23.0 25.1 %copy-start.7 = (bf16[2,4,4,2,128,2,128]{6,5,4,3,2,1,0:T(2,128)(2,1)S(1)}, bf16[2,4,4,2,128,2,128]{6,5,4,3,2,1,0:T(2,128)(2,1)}, u32[]{:S(2)}) copy-start(bf16[2,4,4,2,128,2,128]{6,5,4,3,2,1,0:T(2,128)(2,1)} %param.20) | copy-start | bytes 12582916
  23.0 25.1 %copy-start.8 = (bf16[2,4,2,128,2,128]{5,4,3,2,1,0:T(2,128)(2,1)S(1)}, bf16[2,4,2,128,2,128]{5,4,3,2,1,0:T(2,128)(2,1)}, u32[]{:S(2)}) copy-start(bf16[2,4,2,128,2,128]{5,4,3,2,1,0:T(2,128)(2,1)} %param.19) | copy-start | bytes 3145732
  23.0 25.1 %copy-start.9 = (s32[4,4,128,128]{3,2,1,0:T(8,128)S(1)}, s32[4,4,128,128]{3,2,1,0:T(8,128)}, u32[]{:S(2)}) copy-start(s32[4,4,128,128]{3,2,1,0:T(8,128)} %refs_6_.2) | copy-start | bytes 3145732
  23.0 25.1 %copy-start.10 = (bf16[6,256,256]{2,1,0:T(8,128)(2,1)S(1)}, bf16[6,256,256]{2,1,0:T(8,128)(2,1)}, u32[]{:S(2)}) copy-start(bf16[6,256,256]{2,1,0:T(8,128)(2,1)} %constant.29.clone.refs_4_.refs_7_) | copy-start | bytes 2359300
  23.1 3.9 %collective-permute-start.4 = (bf16[2,288,128]{2,1,0:T(8,128)(2,1)S(1)}, bf16[2,288,128]{2,1,0:T(8,128)(2,1)S(1)}, u32[]{:S(2)}, u32[]{:S(2)}) collective-permute-start(bf16[2,288,128]{2,1,0:T(8,128)(2,1)S(1)} %add_convert_fusion.1.own), channel_id=1, source_target_pairs={{0,1},{2,3},{1,0},{3,2},{4,5},{6,7},{5,4},{7,6},{8,9},{10,11},{9,8... | collective-permute-start | bytes 442376 | tf_op jit(solution)/shard_map/ppermute | solution.py:492
  23.7 6.7 %collective-permute-start.5 = (bf16[2,288,128]{2,1,0:T(8,128)(2,1)S(1)}, bf16[2,288,128]{2,1,0:T(8,128)(2,1)S(1)}, u32[]{:S(2)}, u32[]{:S(2)}) collective-permute-start(bf16[2,288,128]{2,1,0:T(8,128)(2,1)S(1)} %add_convert_fusion.1.own), channel_id=1, source_target_pairs={{1,2},{2,1},{5,6},{6,5},{9,10},{10,9},{13,14},{14,13},{17,18},{18,... | collective-permute-start | bytes 442376 | tf_op jit(solution)/shard_map/ppermute | solution.py:493
  38.3 6.7 %collective-permute-start.6 = (bf16[4,2,64,128]{3,2,1,0:T(8,128)(2,1)S(1)}, bf16[4,2,64,128]{3,2,1,0:T(8,128)(2,1)S(1)}, u32[]{:S(2)}, u32[]{:S(2)}) collective-permute-start(bf16[4,2,64,128]{3,2,1,0:T(8,128)(2,1)S(1)} %denoise.2.refs_0_), channel_id=1, source_target_pairs={{0,4},{4,8},{8,12},{12,0},{1,5},{5,9},{9,13},{13,1},{2,6},{6,10},{... | collective-permute-start | bytes 393224 | tf_op jit(solution)/shard_map/ppermute | solution.py:447
  41.7 6.2 %collective-permute-start.7 = (bf16[4,2,64,128]{3,2,1,0:T(8,128)(2,1)S(1)}, bf16[4,2,64,128]{3,2,1,0:T(8,128)(2,1)S(1)}, u32[]{:S(2)}, u32[]{:S(2)}) collective-permute-start(bf16[4,2,64,128]{3,2,1,0:T(8,128)(2,1)S(1)} %denoise.2.refs_0_), channel_id=1, source_target_pairs={{0,8},{4,12},{8,0},{12,4},{1,9},{5,13},{9,1},{13,5},{2,10},{6,14},... | collective-permute-start | bytes 393224 | tf_op jit(solution)/shard_map/ppermute | solution.py:447
  42.9 5.2 %collective-permute-start.8 = (bf16[4,2,64,128]{3,2,1,0:T(8,128)(2,1)S(1)}, bf16[4,2,64,128]{3,2,1,0:T(8,128)(2,1)S(1)}, u32[]{:S(2)}, u32[]{:S(2)}) collective-permute-start(bf16[4,2,64,128]{3,2,1,0:T(8,128)(2,1)S(1)} %denoise.2.refs_0_), channel_id=1, source_target_pairs={{0,12},{4,0},{8,4},{12,8},{1,13},{5,1},{9,5},{13,9},{2,14},{6,2},{... | collective-permute-start | bytes 393224 | tf_op jit(solution)/shard_map/ppermute | solution.py:447
  52.3 9.6 %collective-permute-start.10 = (bf16[2,288,128]{2,1,0:T(8,128)(2,1)S(1)}, bf16[2,288,128]{2,1,0:T(8,128)(2,1)S(1)}, u32[]{:S(2)}, u32[]{:S(2)}) collective-permute-start(bf16[2,288,128]{2,1,0:T(8,128)(2,1)S(1)} %get-tuple-element.58), channel_id=1, source_target_pairs={{0,8},{4,12},{8,0},{12,4},{1,9},{5,13},{9,1},{13,5},{2,10},{6,14},... | collective-permute-start | bytes 442376 | tf_op jit(solution)/shard_map/ppermute | solution.py:447
  53.1 8.9 %collective-permute-start.11 = (bf16[2,288,128]{2,1,0:T(8,128)(2,1)S(1)}, bf16[2,288,128]{2,1,0:T(8,128)(2,1)S(1)}, u32[]{:S(2)}, u32[]{:S(2)}) collective-permute-start(bf16[2,288,128]{2,1,0:T(8,128)(2,1)S(1)} %get-tuple-element.59), channel_id=1, source_target_pairs={{0,12},{4,0},{8,4},{12,8},{1,13},{5,1},{9,5},{13,9},{2,14},{6,2},{... | collective-permute-start | bytes 442376 | tf_op jit(solution)/shard_map/ppermute | solution.py:447
  55.9 6.1 %collective-permute-start.9 = (bf16[2,288,128]{2,1,0:T(8,128)(2,1)S(1)}, bf16[2,288,128]{2,1,0:T(8,128)(2,1)S(1)}, u32[]{:S(2)}, u32[]{:S(2)}) collective-permute-start(bf16[2,288,128]{2,1,0:T(8,128)(2,1)S(1)} %get-tuple-element.57), channel_id=1, source_target_pairs={{0,4},{4,8},{8,12},{12,0},{1,5},{5,9},{9,13},{13,1},{2,6},{6,10},{... | collective-permute-start | bytes 442376 | tf_op jit(solution)/shard_map/ppermute | solution.py:447
  55.9 5.7 %collective-permute-start.12 = (bf16[4,2,64,128]{3,2,1,0:T(8,128)(2,1)S(1)}, bf16[4,2,64,128]{3,2,1,0:T(8,128)(2,1)S(1)}, u32[]{:S(2)}, u32[]{:S(2)}) collective-permute-start(bf16[4,2,64,128]{3,2,1,0:T(8,128)(2,1)S(1)} %denoise.2.refs_0_), channel_id=1, source_target_pairs={{16,0},{17,1},{18,2},{19,3},{20,4},{21,5},{22,6},{23,7},{24,8},{25... | collective-permute-start | bytes 393224 | tf_op jit(solution)/shard_map/ppermute | solution.py:500
  62.0 8.4 %collective-permute-start.13 = (bf16[2,288,128]{2,1,0:T(8,128)(2,1)S(1)}, bf16[2,288,128]{2,1,0:T(8,128)(2,1)S(1)}, u32[]{:S(2)}, u32[]{:S(2)}) collective-permute-start(bf16[2,288,128]{2,1,0:T(8,128)(2,1)S(1)} %add_convert_fusion.own), channel_id=1, source_target_pairs={{0,1},{2,3},{1,0},{3,2},{4,5},{6,7},{5,4},{7,6},{8,9},{10,11},{9,8... | collective-permute-start | bytes 442376 | tf_op jit(solution)/shard_map/ppermute | solution.py:492
  62.1 11.1 %collective-permute-start.14 = (bf16[2,288,128]{2,1,0:T(8,128)(2,1)S(1)}, bf16[2,288,128]{2,1,0:T(8,128)(2,1)S(1)}, u32[]{:S(2)}, u32[]{:S(2)}) collective-permute-start(bf16[2,288,128]{2,1,0:T(8,128)(2,1)S(1)} %add_convert_fusion.own), channel_id=1, source_target_pairs={{1,2},{2,1},{5,6},{6,5},{9,10},{10,9},{13,14},{14,13},{17,18},{18,... | collective-permute-start | bytes 442376 | tf_op jit(solution)/shard_map/ppermute | solution.py:493
  81.1 5.1 %collective-permute-start.15 = (bf16[4,2,64,128]{3,2,1,0:T(8,128)(2,1)S(1)}, bf16[4,2,64,128]{3,2,1,0:T(8,128)(2,1)S(1)}, u32[]{:S(2)}, u32[]{:S(2)}) collective-permute-start(bf16[4,2,64,128]{3,2,1,0:T(8,128)(2,1)S(1)} %denoise.3), channel_id=1, source_target_pairs={{0,16},{1,17},{2,18},{3,19},{4,20},{5,21},{6,22},{7,23},{8,24},{9,... | collective-permute-start | bytes 393224 | tf_op jit(solution)/shard_map/ppermute | solution.py:500
  (7 other events, 102.6 us)

commit v4 on v3

--- a/solution.py
+++ b/solution.py
@@ -88,6 +88,7 @@
         waits = {}
         for k, (name, source) in enumerate(zip(names, sources)):
             waits[name] = pltpu.make_async_copy(source, refs[k], sems.at[k])
+        for name in names:
             waits[name].start()
         tables, image, maps, mask, samples = refs[:5]
 
@@ -323,30 +324,31 @@
     return jnp.where(lane == part - 1, 0.0, pltpu.roll(values, part - 1, 1))
 
 
-def denoise_kernel(own, even, odd, first, time, last, apart, out, taps, sums, *, phases, section):
+def denoise_kernel(*refs, phases, section, second):
+    own, beside, first, time, last, *refs = refs
+    if second:
+        before, apart, out, taps, sums = refs
+    else:
+        sums, taps = refs
     readouts, span, part = own.shape
     cell = 2 * phases
     lines = span // cell
     group = taps.shape[2]
     used = 9 * cell
-    steps = readouts + 2
     readout_no, coil_no = lax.axis_index("readout"), lax.axis_index("coil")
-    low_inside = readout_no > 0
-    high_inside = readout_no < lax.axis_size("readout") - 1
+    upward = lax.rem(readout_no, 2) == (1 if second else 0)
+    there = jnp.where(upward, readout_no < lax.axis_size("readout") - 1, readout_no > 0)
     first_line = (coil_no > 0).astype(F32).astype(BF16)
     last_line = (coil_no < lax.axis_size("coil") - 1).astype(F32).astype(BF16)
-    swapped = lax.rem(readout_no, 2) == 1
-
-    def side(inside, here, there):
-        return jnp.where(inside, jnp.where(swapped, here.astype(F32), there.astype(F32)), 0.0)
-
-    slabs = (
-        [side(low_inside, even[readouts - HALO + k], odd[readouts - HALO + k]) for k in range(HALO)]
-        + [own[k].astype(F32) for k in range(readouts)]
-        + [side(high_inside, odd[k], even[k]) for k in range(HALO)]
-    )
+
+    own_at = jnp.where(upward, 0, HALO)
+    beside_at = jnp.where(upward, readouts, 0)
+    slabs = [(own_at + k, own[k].astype(F32)) for k in range(readouts)]
+    for k in range(HALO):
+        value = jnp.where(upward, beside[k].astype(F32), beside[readouts - HALO + k].astype(F32))
+        slabs.append((beside_at + k, jnp.where(there, value, 0.0)))
     filler = [jnp.zeros((group - used, part), F32)] if group > used else []
-    for index, slab in enumerate(slabs):
+    for index, slab in slabs:
         views = [shifted(slab, 1), slab, shifted(slab, -1)]
         for line in range(1, lines - 1):
             around = [
@@ -354,50 +356,50 @@
             ]
             taps[index, line - 1] = jnp.concatenate(around + filler, 0).astype(BF16)
     sums[...] = jnp.zeros_like(sums)
-    used_taps = min(3, readouts)
-
-    def add_row(step, carry):
-        begun = jnp.clip(step - readouts + 1, 0, 3 - used_taps)
-        inside = ((step > 0) | low_inside) & ((step < steps - 1) | high_inside)
-
-        @pl.when(inside)
-        def _():
-            block = range(1, lines - 1)
-            near = jnp.concatenate(
-                [taps[pl.ds(step, 3), line - 1].reshape(3 * group, part) for line in block], 1
-            )
-            hidden = jnp.maximum(dot(first[section], near), 0.0).astype(BF16)
-            mixed = jnp.maximum(hidden.astype(F32) + dot(time[section], hidden), 0.0).astype(BF16)
-            edge = (len(block) - 1) * part
-            mixed = jnp.concatenate(
-                [mixed[:, :part] * first_line, mixed[:, part:edge], mixed[:, edge:] * last_line], 1
-            )
-            chosen = pl.ds(pl.multiple_of(begun * group, 16), used_taps * group)
-            result = dot(last[section, chosen], mixed)
-            for a in range(used_taps):
-                target = step + 2 - begun - a
-                for e in range(3):
-                    for line in range(lines):
-                        terms = []
-                        for c in range(3):
-                            source = line + c - 2
-                            if 0 <= source < len(block):
-                                at = a * group + (3 * c + e) * cell
-                                terms.append(
-                                    result[at : at + cell, source * part : (source + 1) * part]
-                                )
-                        sums[e, target, line * cell : (line + 1) * cell] += sum(terms[1:], terms[0])
-
-        return carry
-
-    lax.fori_loop(0, steps, add_row, 0)
+
+    def add_row(row, begun, count):
+        start = row - 1 + own_at
+        block = range(1, lines - 1)
+        near = jnp.concatenate(
+            [taps[pl.ds(start, 3), line - 1].reshape(3 * group, part) for line in block], 1
+        )
+        hidden = jnp.maximum(dot(first[section], near), 0.0).astype(BF16)
+        mixed = jnp.maximum(hidden.astype(F32) + dot(time[section], hidden), 0.0).astype(BF16)
+        edge = (len(block) - 1) * part
+        mixed = jnp.concatenate(
+            [mixed[:, :part] * first_line, mixed[:, part:edge], mixed[:, edge:] * last_line], 1
+        )
+        chosen = pl.ds(pl.multiple_of(begun * group, 16), count * group)
+        result = dot(last[section, chosen], mixed)
+        for a in range(count):
+            target = row + 1 - begun - a
+            for e in range(3):
+                for line in range(lines):
+                    terms = []
+                    for c in range(3):
+                        source = line + c - 2
+                        if 0 <= source < len(block):
+                            at = a * group + (3 * c + e) * cell
+                            terms.append(
+                                result[at : at + cell, source * part : (source + 1) * part]
+                            )
+                    sums[e, target, line * cell : (line + 1) * cell] += sum(terms[1:], terms[0])
+
+    @pl.when(there)
+    def _():
+        add_row(jnp.where(upward, readouts, -1), jnp.where(upward, 2, 0), 1)
+
+    add_row(jnp.where(upward, readouts - 1, 0), jnp.where(upward, 1, 0), 2)
+    if not second:
+        for row in range(1, readouts - 1):
+            add_row(row, 0, 3)
+        return
 
     body = slice(HALO * cell, span - HALO * cell)
     finals = []
     for r in range(readouts):
-        value = own[r, body].astype(F32) + sums[1, r + HALO, body]
-        value = value + shifted(sums[0, r + HALO, body], 1)
-        value = value + shifted(sums[2, r + HALO, body], -1)
+        left, here, right = [sums[e, r, body] + before[e, r, body] for e in range(3)]
+        value = own[r, body].astype(F32) + here + shifted(left, 1) + shifted(right, -1)
         finals.append(value.astype(BF16))
     ordered = dot(apart[...], jnp.concatenate(finals, 1)).astype(BF16)
     height = out.shape[2]
@@ -406,30 +408,35 @@
             out[p, r] = ordered[p * height : (p + 1) * height, r * part : (r + 1) * part]
 
 
-def denoise(own, even, odd, matrices, section, phases):
+def denoise(own, beside, matrices, section, phases, before=None):
     readouts, span, part = own.shape
     cell = 2 * phases
     lines = span // cell
     share = lines - 2 * HALO
-    apart = bf16(phase_inside(phases, share).T)
     group = matrices[0].shape[2] // 3
+    second = before is not None
+    operands = [own, beside, *matrices]
+    sums_shape = (3, readouts, span, part)
+    scratch = [pltpu.VMEM((readouts + HALO, lines - 2, group, part), BF16)]
+    result = jax.ShapeDtypeStruct(sums_shape, F32)
+    if second:
+        operands += [before, bf16(phase_inside(phases, share).T)]
+        scratch.append(pltpu.VMEM(sums_shape, F32))
+        result = jax.ShapeDtypeStruct((phases, readouts, 2 * share, part), BF16)
     return pl.pallas_call(
-        functools.partial(denoise_kernel, phases=phases, section=section),
-        in_specs=[pl.BlockSpec(memory_space=pltpu.VMEM)] * 7,
+        functools.partial(denoise_kernel, phases=phases, section=section, second=second),
+        in_specs=[pl.BlockSpec(memory_space=pltpu.VMEM)] * len(operands),
         out_specs=pl.BlockSpec(memory_space=pltpu.VMEM),
-        scratch_shapes=[
-            pltpu.VMEM((readouts + 2 * HALO, lines - 2, group, part), BF16),
-            pltpu.VMEM((3, readouts + 2 * HALO, span, part), F32),
-        ],
-        out_shape=jax.ShapeDtypeStruct((phases, readouts, 2 * share, part), BF16),
+        scratch_shapes=scratch,
+        out_shape=result,
         compiler_params=pltpu.CompilerParams(vmem_limit_bytes=VMEM_LIMIT),
         cost_estimate=pl.CostEstimate(
-            flops=6 * (readouts + 2) * lines * part * 256 * 256,
+            flops=6 * readouts * lines * part * 256 * 256,
             bytes_accessed=2 * 1024 * 1024,
             transcendentals=0,
         ),
         name="denoise",
-    )(own, even, odd, *matrices, apart)
+    )(*operands)
 
 
 def rotation(count, step):
@@ -466,7 +473,7 @@
     initial, coil_maps, kspace = rows_of(initial), rows_of(coil_maps), rows_of(kspace)
     images = [initial]
     matrices = None
-    kept, sent = [], []
+    sent = []
     for section in range(sections):
         partial = consistency(images, coil_maps, kspace, sampled, shares)
         if matrices is None:
@@ -491,23 +498,18 @@
         combined = sum(p.astype(F32) for p in parts).astype(BF16)
         even = lax.ppermute(combined, "readout", swaps(readout_parts, 0))
         odd = lax.ppermute(combined, "readout", swaps(readout_parts, 1))
-        output = denoise(combined, even, odd, matrices, section, phases)
+        reached = denoise(combined, even, matrices, section, phases)
+        output = denoise(combined, odd, matrices, section, phases, reached)
         if section < sections - 1:
             images = exchanged([output] * shares, "coil", shares)
-        kept.append(output)
-        sent.append(
-            [
-                lax.ppermute(output, "cascade", [((section + k) % sections, section)])
-                for k in range(1, sections)
-            ]
-        )
+        sent.append(exchanged([output] * sections, "cascade", sections))
 
     arrived = []
     for block in range(sections):
         value = None
         for section in range(sections):
-            k = (block - section) % sections
-            piece = sent[section][k - 1] if k else kept[section]
+            k = (section - block) % sections
+            piece = sent[section][k]
             value = piece if value is None else jnp.where(section_no == section, piece, value)
         arrived.append(value)
     result = jnp.stack(arrived)[None]

time: 88.4 us -> 81.9 us (0.926); the launches traced: 87.3 us -> 81.8 us
  starting transfers between devices: 32.7 us -> 25.5 us
  waiting for transfers between devices: 24 us -> 25.8 us
    ppermute x10 -> x12, waiting for transfers between devices: 11.4 us -> 25 us  [exchanged(): arrived[k] = lax.ppermute(values[k], axis, rotation(count, k))]
    ppermute x2, starting transfers between devices: 11.5 us -> 4.92 us  [per_device(): odd = lax.ppermute(combined, 'readout', swaps(readout_parts, 1))]
    ppermute x2 -> x0, waiting for transfers between devices: 6.31 us -> none  [per_device(): lax.ppermute(output, 'cascade', [((section + k) % sections, section)])]
    ppermute x2, waiting for transfers between devices: 6.21 us -> 0.81 us  [per_device(): odd = lax.ppermute(combined, 'readout', swaps(readout_parts, 1))]
    ppermute x2 -> x0, starting transfers between devices: 4.43 us -> none  [per_device(): lax.ppermute(output, 'cascade', [((section + k) % sections, section)])]
    ppermute x10 -> x12, starting transfers between devices: 16 us -> 19.2 us  [exchanged(): arrived[k] = lax.ppermute(values[k], axis, rotation(count, k))]
    pallas_call x2 -> x4, Pallas kernels: 15.8 us -> 15.8 us  [denoise(): pl.pallas_call(functools.partial(denoise_kernel, phases=phases, section=s...]
  transfers between devices with their start and end apart: 16 -> 16, of which waited for: 10 -> 10; matrix products, arithmetic and copies ran while one was open for 0% -> 0% of each run, Pallas kernels for 1% -> 11%
where the time goes in v4:
time: 81.9 us; the launch traced here: 81.8 us
  Pallas kernels  27.9 us (34%)
  waiting for transfers between devices  25.8 us (32%)
  starting transfers between devices  25.5 us (31%)
  other arithmetic  2.2 us (3%)
    ppermute x12, waiting for transfers between devices, exchanged(): arrived[k] = lax.ppermute(values[k], axis, rotation(count, k))  25 us
    ppermute x12, starting transfers between devices, exchanged(): arrived[k] = lax.ppermute(values[k], axis, rotation(count, k))  19.2 us
    pallas_call x4, Pallas kernels, denoise(): pl.pallas_call(functools.partial(denoise_kernel, phases=phases, section=s...  15.8 us
    pallas_call x2, Pallas kernels, consistency(): pl.pallas_call(body, in_specs=[pl.BlockSpec(memory_space=pltpu.VMEM if di...  10.9 us
    ppermute x2, starting transfers between devices, per_device(): odd = lax.ppermute(combined, 'readout', swaps(readout_parts, 1))  4.92 us
  transfers between devices with their start and end apart: 16, of which 10 were waited for; matrix products, arithmetic and copies ran while one was open for 0% of the time, Pallas kernels for 11%

profile of v4, /device:TPU:1, one launch (start us, length us, event | category | flops | bytes accessed | tf_op | source)
XLA Modules:
  0.0 81.8 jit_solution(9752311996932321326)
XLA Ops:
  0.1 6.8 %consistency.2 = (bf16[2,288,128]{2,1,0:T(8,128)(2,1)}, bf16[2,288,128]{2,1,0:T(8,128)(2,1)}, bf16[2,288,128]{2,1,0:T(8,128)(2,1)}, bf16[2,288,128]{2,1,0:T(8,128)(2,1)}) custom-call(bf16[2,4,2,256,128]{4,3,2,1,0:T(8,128)(2,1)} %bitcast.17, bf16[2,4,2,256,128]{4,3,2,1,0:T(8,128)(2,1)} %bitcast.11, bf16[2,4,4,2,256,128]{5,4,3,2,1,0:T(8,128)(2,1)} %bitcast.9, ...), custom_call_target="tpu_custom_call" | custom-call | flops 5368709120 | bytes 4194304 | tf_op jit(solution)/shard_map/consistency/pallas_call | solution.py:217
  6.9 2.2 %collective-permute-start = (bf16[2,288,128]{2,1,0:T(8,128)(2,1)}, bf16[2,288,128]{2,1,0:T(8,128)(2,1)S(1)}, u32[]{:S(2)}, u32[]{:S(2)}) collective-permute-start(bf16[2,288,128]{2,1,0:T(8,128)(2,1)} %get-tuple-element.41), channel_id=1, source_target_pairs={{0,4},{4,8},{8,12},{12,0},{1,5},{5,9},{9,13},{13,1},{2,6},{6,10},{... | collective-permute-start | bytes 442376 | tf_op jit(solution)/shard_map/ppermute | solution.py:454
  9.1 2.3 %collective-permute-start.1 = (bf16[2,288,128]{2,1,0:T(8,128)(2,1)}, bf16[2,288,128]{2,1,0:T(8,128)(2,1)S(1)}, u32[]{:S(2)}, u32[]{:S(2)}) collective-permute-start(bf16[2,288,128]{2,1,0:T(8,128)(2,1)} %get-tuple-element.42), channel_id=1, source_target_pairs={{0,8},{4,12},{8,0},{12,4},{1,9},{5,13},{9,1},{13,5},{2,10},{6,14},... | collective-permute-start | bytes 442376 | tf_op jit(solution)/shard_map/ppermute | solution.py:454
  12.6 1.3 %collective-permute-start.3 = (bf16[320,64]{1,0:T(8,128)(2,1)S(1)}, bf16[320,64]{1,0:T(8,128)(2,1)S(1)}, u32[]{:S(2)}, u32[]{:S(2)}) collective-permute-start(bf16[320,64]{1,0:T(8,128)(2,1)S(1)} %fusion.4.refs_0_), channel_id=1, source_target_pairs={{0,16},{16,0},{1,17},{17,1},{2,18},{18,2},{3,19},{19,3},{4,20},{20... | collective-permute-start | bytes 122888 | tf_op jit(solution)/shard_map/ppermute | solution.py:454
  13.9 2.3 %collective-permute-done.3.refs_1_ = bf16[320,64]{1,0:T(8,128)(2,1)S(1)} collective-permute-done((bf16[320,64]{1,0:T(8,128)(2,1)S(1)}, bf16[320,64]{1,0:T(8,128)(2,1)S(1)}, u32[]{:S(2)}, u32[]{:S(2)}) %collective-permute-start.3) | collective-permute-done | bytes 40992 | tf_op jit(solution)/shard_map/ppermute | solution.py:454
  17.5 4.5 %collective-permute-done.1 = bf16[2,288,128]{2,1,0:T(8,128)(2,1)S(1)} collective-permute-done((bf16[2,288,128]{2,1,0:T(8,128)(2,1)}, bf16[2,288,128]{2,1,0:T(8,128)(2,1)S(1)}, u32[]{:S(2)}, u32[]{:S(2)}) %collective-permute-start.1) | collective-permute-done | bytes 147488 | tf_op jit(solution)/shard_map/ppermute | solution.py:454
  23.6 3.0 %collective-permute-start.4 = (bf16[2,288,128]{2,1,0:T(8,128)(2,1)S(1)}, bf16[2,288,128]{2,1,0:T(8,128)(2,1)S(1)}, u32[]{:S(2)}, u32[]{:S(2)}) collective-permute-start(bf16[2,288,128]{2,1,0:T(8,128)(2,1)S(1)} %add_convert_fusion.1.refs_0_), channel_id=1, source_target_pairs={{1,2},{2,1},{5,6},{6,5},{9,10},{10,9},{13,14},{14,13},{17,18},{18,... | collective-permute-start | bytes 442376 | tf_op jit(solution)/shard_map/ppermute | solution.py:500
  26.7 3.7 %denoise.4.refs_5_ = f32[3,2,288,128]{3,2,1,0:T(8,128)S(1)} custom-call(bf16[2,288,128]{2,1,0:T(8,128)(2,1)S(1)} %add_convert_fusion.1.refs_0_, bf16[2,288,128]{2,1,0:T(8,128)(2,1)S(1)} %collective-permute-done.5.refs_1_, bf16[2,256,240]{2,1,0:T(8,128)(2,1)S(1)} %get-tuple-element.54.refs_2_, bf16[2,256,256]{2,1,0:T(8,128)(2,1)S(1)} %get-tuple-element.55.refs_3_, ...), custom_call_target="tpu_custom_call" | custom-call | flops 3623878656 | bytes 2097152 | tf_op jit(solution)/shard_map/denoise/pallas_call | solution.py:426
  30.5 4.2 %denoise.5.refs_0_ = bf16[4,2,64,128]{3,2,1,0:T(8,128)(2,1)S(1)} custom-call(bf16[2,288,128]{2,1,0:T(8,128)(2,1)S(1)} %add_convert_fusion.1.refs_0_, bf16[2,288,128]{2,1,0:T(8,128)(2,1)S(1)} %collective-permute-done.4.refs_1_, bf16[2,256,240]{2,1,0:T(8,128)(2,1)S(1)} %get-tuple-element.54.refs_2_, bf16[2,256,256]{2,1,0:T(8,128)(2,1)S(1)} %get-tuple-element.55.refs_3_, ...), custom_call_target="tpu_custom_call" | custom-call | flops 3623878656 | bytes 2097152 | tf_op jit(solution)/shard_map/denoise/pallas_call | solution.py:426
  34.6 3.4 %collective-permute-start.6 = (bf16[4,2,64,128]{3,2,1,0:T(8,128)(2,1)S(1)}, bf16[4,2,64,128]{3,2,1,0:T(8,128)(2,1)S(1)}, u32[]{:S(2)}, u32[]{:S(2)}) collective-permute-start(bf16[4,2,64,128]{3,2,1,0:T(8,128)(2,1)S(1)} %denoise.5.refs_0_), channel_id=1, source_target_pairs={{0,4},{4,8},{8,12},{12,0},{1,5},{5,9},{9,13},{13,1},{2,6},{6,10},{... | collective-permute-start | bytes 393224 | tf_op jit(solution)/shard_map/ppermute | solution.py:454
  38.0 1.3 %collective-permute-start.7 = (bf16[4,2,64,128]{3,2,1,0:T(8,128)(2,1)S(1)}, bf16[4,2,64,128]{3,2,1,0:T(8,128)(2,1)S(1)}, u32[]{:S(2)}, u32[]{:S(2)}) collective-permute-start(bf16[4,2,64,128]{3,2,1,0:T(8,128)(2,1)S(1)} %denoise.5.refs_0_), channel_id=1, source_target_pairs={{0,8},{4,12},{8,0},{12,4},{1,9},{5,13},{9,1},{13,5},{2,10},{6,14},... | collective-permute-start | bytes 393224 | tf_op jit(solution)/shard_map/ppermute | solution.py:454
  40.2 2.6 %collective-permute-done.6.refs_1_ = bf16[4,2,64,128]{3,2,1,0:T(8,128)(2,1)S(1)} collective-permute-done((bf16[4,2,64,128]{3,2,1,0:T(8,128)(2,1)S(1)}, bf16[4,2,64,128]{3,2,1,0:T(8,128)(2,1)S(1)}, u32[]{:S(2)}, u32[]{:S(2)}) %collective-permute-start.6) | collective-permute-done | bytes 131104 | tf_op jit(solution)/shard_map/ppermute | solution.py:454
  42.8 3.5 %collective-permute-done.7.refs_2_ = bf16[4,2,64,128]{3,2,1,0:T(8,128)(2,1)S(1)} collective-permute-done((bf16[4,2,64,128]{3,2,1,0:T(8,128)(2,1)S(1)}, bf16[4,2,64,128]{3,2,1,0:T(8,128)(2,1)S(1)}, u32[]{:S(2)}, u32[]{:S(2)}) %collective-permute-start.7) | collective-permute-done | bytes 131104 | tf_op jit(solution)/shard_map/ppermute | solution.py:454
  46.4 4.1 %consistency.3 = (bf16[2,288,128]{2,1,0:T(8,128)(2,1)S(1)}, bf16[2,288,128]{2,1,0:T(8,128)(2,1)S(1)}, bf16[2,288,128]{2,1,0:T(8,128)(2,1)S(1)}, bf16[2,288,128]{2,1,0:T(8,128)(2,1)S(1)}) custom-call(bf16[4,2,64,128]{3,2,1,0:T(8,128)(2,1)S(1)} %denoise.5.refs_0_, bf16[4,2,64,128]{3,2,1,0:T(8,128)(2,1)S(1)} %collective-permute-done.6.refs_1_, ...), custom_call_target="tpu_custom_call" | custom-call | flops 5368709120 | bytes 4194304 | tf_op jit(solution)/shard_map/consistency/pallas_call | solution.py:217
  50.5 1.4 %collective-permute-start.10 = (bf16[2,288,128]{2,1,0:T(8,128)(2,1)S(1)}, bf16[2,288,128]{2,1,0:T(8,128)(2,1)S(1)}, u32[]{:S(2)}, u32[]{:S(2)}) collective-permute-start(bf16[2,288,128]{2,1,0:T(8,128)(2,1)S(1)} %get-tuple-element.59), channel_id=1, source_target_pairs={{0,8},{4,12},{8,0},{12,4},{1,9},{5,13},{9,1},{13,5},{2,10},{6,14},... | collective-permute-start | bytes 442376 | tf_op jit(solution)/shard_map/ppermute | solution.py:454
  51.9 2.8 %collective-permute-start.11 = (bf16[2,288,128]{2,1,0:T(8,128)(2,1)S(1)}, bf16[2,288,128]{2,1,0:T(8,128)(2,1)S(1)}, u32[]{:S(2)}, u32[]{:S(2)}) collective-permute-start(bf16[2,288,128]{2,1,0:T(8,128)(2,1)S(1)} %get-tuple-element.60), channel_id=1, source_target_pairs={{0,12},{4,0},{8,4},{12,8},{1,13},{5,1},{9,5},{13,9},{2,14},{6,2},{... | collective-permute-start | bytes 442376 | tf_op jit(solution)/shard_map/ppermute | solution.py:454
  54.7 1.2 %collective-permute-start.12 = (bf16[4,2,64,128]{3,2,1,0:T(8,128)(2,1)S(1)}, bf16[4,2,64,128]{3,2,1,0:T(8,128)(2,1)S(1)}, u32[]{:S(2)}, u32[]{:S(2)}) collective-permute-start(bf16[4,2,64,128]{3,2,1,0:T(8,128)(2,1)S(1)} %denoise.5.refs_0_), channel_id=1, source_target_pairs={{0,16},{16,0},{1,17},{17,1},{2,18},{18,2},{3,19},{19,3},{4,20},{20... | collective-permute-start | bytes 393224 | tf_op jit(solution)/shard_map/ppermute | solution.py:454
  56.0 3.6 %collective-permute-done.12 = bf16[4,2,64,128]{3,2,1,0:T(8,128)(2,1)S(1)} collective-permute-done((bf16[4,2,64,128]{3,2,1,0:T(8,128)(2,1)S(1)}, bf16[4,2,64,128]{3,2,1,0:T(8,128)(2,1)S(1)}, u32[]{:S(2)}, u32[]{:S(2)}) %collective-permute-start.12) | collective-permute-done | bytes 131104 | tf_op jit(solution)/shard_map/ppermute | solution.py:454
  60.2 5.2 %collective-permute-done.9 = bf16[2,288,128]{2,1,0:T(8,128)(2,1)S(1)} collective-permute-done((bf16[2,288,128]{2,1,0:T(8,128)(2,1)S(1)}, bf16[2,288,128]{2,1,0:T(8,128)(2,1)S(1)}, u32[]{:S(2)}, u32[]{:S(2)}) %collective-permute-start.9) | collective-permute-done | bytes 147488 | tf_op jit(solution)/shard_map/ppermute | solution.py:454
  66.1 1.9 %collective-permute-start.13 = (bf16[2,288,128]{2,1,0:T(8,128)(2,1)S(1)}, bf16[2,288,128]{2,1,0:T(8,128)(2,1)S(1)}, u32[]{:S(2)}, u32[]{:S(2)}) collective-permute-start(bf16[2,288,128]{2,1,0:T(8,128)(2,1)S(1)} %add_convert_fusion.refs_0_), channel_id=1, source_target_pairs={{1,2},{2,1},{5,6},{6,5},{9,10},{10,9},{13,14},{14,13},{17,18},{18,... | collective-permute-start | bytes 442376 | tf_op jit(solution)/shard_map/ppermute | solution.py:500
  68.1 3.7 %denoise.6.refs_5_ = f32[3,2,288,128]{3,2,1,0:T(8,128)S(1)} custom-call(bf16[2,288,128]{2,1,0:T(8,128)(2,1)S(1)} %add_convert_fusion.refs_0_, bf16[2,288,128]{2,1,0:T(8,128)(2,1)S(1)} %collective-permute-done.14.refs_1_, bf16[2,256,240]{2,1,0:T(8,128)(2,1)S(1)} %get-tuple-element.54.refs_2_, bf16[2,256,256]{2,1,0:T(8,128)(2,1)S(1)} %get-tuple-element.55.refs_3_, ...), custom_call_target="tpu_custom_call" | custom-call | flops 3623878656 | bytes 2097152 | tf_op jit(solution)/shard_map/denoise/pallas_call | solution.py:426
  72.6 4.2 %denoise.7 = bf16[4,2,64,128]{3,2,1,0:T(8,128)(2,1)S(1)} custom-call(bf16[2,288,128]{2,1,0:T(8,128)(2,1)S(1)} %add_convert_fusion.refs_0_, bf16[2,288,128]{2,1,0:T(8,128)(2,1)S(1)} %collective-permute-done.13.refs_1_, bf16[2,256,240]{2,1,0:T(8,128)(2,1)S(1)} %get-tuple-element.54.refs_2_, bf16[2,256,256]{2,1,0:T(8,128)(2,1)S(1)} %get-tuple-element.55.refs_3_, ...), custom_call_target="tpu_custom_call" | custom-call | flops 3623878656 | bytes 2097152 | tf_op jit(solution)/shard_map/denoise/pallas_call | solution.py:426
  76.8 1.3 %collective-permute-start.15 = (bf16[4,2,64,128]{3,2,1,0:T(8,128)(2,1)S(1)}, bf16[4,2,64,128]{3,2,1,0:T(8,128)(2,1)S(1)}, u32[]{:S(2)}, u32[]{:S(2)}) collective-permute-start(bf16[4,2,64,128]{3,2,1,0:T(8,128)(2,1)S(1)} %denoise.7), channel_id=1, source_target_pairs={{0,16},{16,0},{1,17},{17,1},{2,18},{18,2},{3,19},{19,3},{4,20},{20... | collective-permute-start | bytes 393224 | tf_op jit(solution)/shard_map/ppermute | solution.py:454
  78.1 2.6 %collective-permute-done.15 = bf16[4,2,64,128]{3,2,1,0:T(8,128)(2,1)S(1)} collective-permute-done((bf16[4,2,64,128]{3,2,1,0:T(8,128)(2,1)S(1)}, bf16[4,2,64,128]{3,2,1,0:T(8,128)(2,1)S(1)}, u32[]{:S(2)}, u32[]{:S(2)}) %collective-permute-start.15) | collective-permute-done | bytes 131104 | tf_op jit(solution)/shard_map/ppermute | solution.py:454
  (53 shorter events, 8.3 us)
Async XLA Ops:
  0.0 16.2 %copy-start = (bf16[3,256,256]{2,1,0:T(8,128)(2,1)S(1)}, bf16[3,256,256]{2,1,0:T(8,128)(2,1)}, u32[]{:S(2)}) copy-start(bf16[3,256,256]{2,1,0:T(8,128)(2,1)} %constant.36.clone.refs_8_) | copy-start | bytes 1179652
  0.0 16.2 %copy-start.1 = (bf16[256,240]{1,0:T(8,128)(2,1)S(1)}, bf16[256,240]{1,0:T(8,128)(2,1)}, u32[]{:S(2)}) copy-start(bf16[256,240]{1,0:T(8,128)(2,1)} %constant.33.clone.refs_5_) | copy-start | bytes 368644
  0.0 16.2 %copy-start.2 = (bf16[240,256]{1,0:T(8,128)(2,1)S(1)}, bf16[240,256]{1,0:T(8,128)(2,1)}, u32[]{:S(2)}) copy-start(bf16[240,256]{1,0:T(8,128)(2,1)} %constant.32.clone.refs_4_) | copy-start | bytes 368644
  0.0 16.2 %copy-start.3 = (bf16[256,64]{1,0:T(8,128)(2,1)S(1)}, bf16[256,64]{1,0:T(8,128)(2,1)}, u32[]{:S(2)}) copy-start(bf16[256,64]{1,0:T(8,128)(2,1)} %constant.35.clone.refs_7_) | copy-start | bytes 98308
  0.1 16.2 %copy-start.4 = (bf16[240,64]{1,0:T(8,128)(2,1)S(1)}, bf16[240,64]{1,0:T(8,128)(2,1)}, u32[]{:S(2)}) copy-start(bf16[240,64]{1,0:T(8,128)(2,1)} %constant.30.clone.refs_2_) | copy-start | bytes 92164
  0.1 16.2 %copy-start.5 = (bf16[64,240]{1,0:T(8,128)(2,1)S(1)}, bf16[64,240]{1,0:T(8,128)(2,1)}, u32[]{:S(2)}) copy-start(bf16[64,240]{1,0:T(8,128)(2,1)} %constant.31.clone.refs_3_) | copy-start | bytes 92164
  0.1 16.2 %copy-start.6 = (bf16[64,256]{1,0:T(8,128)(2,1)S(1)}, bf16[64,256]{1,0:T(8,128)(2,1)}, u32[]{:S(2)}) copy-start(bf16[64,256]{1,0:T(8,128)(2,1)} %constant.34.clone.refs_6_) | copy-start | bytes 98308
  6.9 10.6 %collective-permute-start = (bf16[2,288,128]{2,1,0:T(8,128)(2,1)}, bf16[2,288,128]{2,1,0:T(8,128)(2,1)S(1)}, u32[]{:S(2)}, u32[]{:S(2)}) collective-permute-start(bf16[2,288,128]{2,1,0:T(8,128)(2,1)} %get-tuple-element.41), channel_id=1, source_target_pairs={{0,4},{4,8},{8,12},{12,0},{1,5},{5,9},{9,13},{13,1},{2,6},{6,10},{... | collective-permute-start | bytes 442376 | tf_op jit(solution)/shard_map/ppermute | solution.py:454
  9.1 12.9 %collective-permute-start.1 = (bf16[2,288,128]{2,1,0:T(8,128)(2,1)}, bf16[2,288,128]{2,1,0:T(8,128)(2,1)S(1)}, u32[]{:S(2)}, u32[]{:S(2)}) collective-permute-start(bf16[2,288,128]{2,1,0:T(8,128)(2,1)} %get-tuple-element.42), channel_id=1, source_target_pairs={{0,8},{4,12},{8,0},{12,4},{1,9},{5,13},{9,1},{13,5},{2,10},{6,14},... | collective-permute-start | bytes 442376 | tf_op jit(solution)/shard_map/ppermute | solution.py:454
  11.4 10.6 %collective-permute-start.2 = (bf16[2,288,128]{2,1,0:T(8,128)(2,1)}, bf16[2,288,128]{2,1,0:T(8,128)(2,1)S(1)}, u32[]{:S(2)}, u32[]{:S(2)}) collective-permute-start(bf16[2,288,128]{2,1,0:T(8,128)(2,1)} %get-tuple-element.43), channel_id=1, source_target_pairs={{0,12},{4,0},{8,4},{12,8},{1,13},{5,1},{9,5},{13,9},{2,14},{6,2},{... | collective-permute-start | bytes 442376 | tf_op jit(solution)/shard_map/ppermute | solution.py:454
  12.6 3.7 %collective-permute-start.3 = (bf16[320,64]{1,0:T(8,128)(2,1)S(1)}, bf16[320,64]{1,0:T(8,128)(2,1)S(1)}, u32[]{:S(2)}, u32[]{:S(2)}) collective-permute-start(bf16[320,64]{1,0:T(8,128)(2,1)S(1)} %fusion.4.refs_0_), channel_id=1, source_target_pairs={{0,16},{16,0},{1,17},{17,1},{2,18},{18,2},{3,19},{19,3},{4,20},{20... | collective-permute-start | bytes 122888 | tf_op jit(solution)/shard_map/ppermute | solution.py:454
  23.0 3.7 %collective-permute-start.5 = (bf16[2,288,128]{2,1,0:T(8,128)(2,1)S(1)}, bf16[2,288,128]{2,1,0:T(8,128)(2,1)S(1)}, u32[]{:S(2)}, u32[]{:S(2)}) collective-permute-start(bf16[2,288,128]{2,1,0:T(8,128)(2,1)S(1)} %add_convert_fusion.1.refs_0_), channel_id=1, source_target_pairs={{0,1},{2,3},{1,0},{3,2},{4,5},{6,7},{5,4},{7,6},{8,9},{10,11},{9,8... | collective-permute-start | bytes 442376 | tf_op jit(solution)/shard_map/ppermute | solution.py:499
  23.6 6.8 %collective-permute-start.4 = (bf16[2,288,128]{2,1,0:T(8,128)(2,1)S(1)}, bf16[2,288,128]{2,1,0:T(8,128)(2,1)S(1)}, u32[]{:S(2)}, u32[]{:S(2)}) collective-permute-start(bf16[2,288,128]{2,1,0:T(8,128)(2,1)S(1)} %add_convert_fusion.1.refs_0_), channel_id=1, source_target_pairs={{1,2},{2,1},{5,6},{6,5},{9,10},{10,9},{13,14},{14,13},{17,18},{18,... | collective-permute-start | bytes 442376 | tf_op jit(solution)/shard_map/ppermute | solution.py:500
  30.4 16.0 %copy-start.7 = (bf16[2,4,4,2,128,2,128]{6,5,4,3,2,1,0:T(2,128)(2,1)S(1)}, bf16[2,4,4,2,128,2,128]{6,5,4,3,2,1,0:T(2,128)(2,1)}, u32[]{:S(2)}) copy-start(bf16[2,4,4,2,128,2,128]{6,5,4,3,2,1,0:T(2,128)(2,1)} %param.20) | copy-start | bytes 12582916
  34.6 8.1 %collective-permute-start.6 = (bf16[4,2,64,128]{3,2,1,0:T(8,128)(2,1)S(1)}, bf16[4,2,64,128]{3,2,1,0:T(8,128)(2,1)S(1)}, u32[]{:S(2)}, u32[]{:S(2)}) collective-permute-start(bf16[4,2,64,128]{3,2,1,0:T(8,128)(2,1)S(1)} %denoise.5.refs_0_), channel_id=1, source_target_pairs={{0,4},{4,8},{8,12},{12,0},{1,5},{5,9},{9,13},{13,1},{2,6},{6,10},{... | collective-permute-start | bytes 393224 | tf_op jit(solution)/shard_map/ppermute | solution.py:454
  38.0 8.3 %collective-permute-start.7 = (bf16[4,2,64,128]{3,2,1,0:T(8,128)(2,1)S(1)}, bf16[4,2,64,128]{3,2,1,0:T(8,128)(2,1)S(1)}, u32[]{:S(2)}, u32[]{:S(2)}) collective-permute-start(bf16[4,2,64,128]{3,2,1,0:T(8,128)(2,1)S(1)} %denoise.5.refs_0_), channel_id=1, source_target_pairs={{0,8},{4,12},{8,0},{12,4},{1,9},{5,13},{9,1},{13,5},{2,10},{6,14},... | collective-permute-start | bytes 393224 | tf_op jit(solution)/shard_map/ppermute | solution.py:454
  39.4 7.0 %collective-permute-start.8 = (bf16[4,2,64,128]{3,2,1,0:T(8,128)(2,1)S(1)}, bf16[4,2,64,128]{3,2,1,0:T(8,128)(2,1)S(1)}, u32[]{:S(2)}, u32[]{:S(2)}) collective-permute-start(bf16[4,2,64,128]{3,2,1,0:T(8,128)(2,1)S(1)} %denoise.5.refs_0_), channel_id=1, source_target_pairs={{0,12},{4,0},{8,4},{12,8},{1,13},{5,1},{9,5},{13,9},{2,14},{6,2},{... | collective-permute-start | bytes 393224 | tf_op jit(solution)/shard_map/ppermute | solution.py:454
  50.5 9.7 %collective-permute-start.10 = (bf16[2,288,128]{2,1,0:T(8,128)(2,1)S(1)}, bf16[2,288,128]{2,1,0:T(8,128)(2,1)S(1)}, u32[]{:S(2)}, u32[]{:S(2)}) collective-permute-start(bf16[2,288,128]{2,1,0:T(8,128)(2,1)S(1)} %get-tuple-element.59), channel_id=1, source_target_pairs={{0,8},{4,12},{8,0},{12,4},{1,9},{5,13},{9,1},{13,5},{2,10},{6,14},... | collective-permute-start | bytes 442376 | tf_op jit(solution)/shard_map/ppermute | solution.py:454
  51.9 8.3 %collective-permute-start.11 = (bf16[2,288,128]{2,1,0:T(8,128)(2,1)S(1)}, bf16[2,288,128]{2,1,0:T(8,128)(2,1)S(1)}, u32[]{:S(2)}, u32[]{:S(2)}) collective-permute-start(bf16[2,288,128]{2,1,0:T(8,128)(2,1)S(1)} %get-tuple-element.60), channel_id=1, source_target_pairs={{0,12},{4,0},{8,4},{12,8},{1,13},{5,1},{9,5},{13,9},{2,14},{6,2},{... | collective-permute-start | bytes 442376 | tf_op jit(solution)/shard_map/ppermute | solution.py:454
  54.7 10.6 %collective-permute-start.9 = (bf16[2,288,128]{2,1,0:T(8,128)(2,1)S(1)}, bf16[2,288,128]{2,1,0:T(8,128)(2,1)S(1)}, u32[]{:S(2)}, u32[]{:S(2)}) collective-permute-start(bf16[2,288,128]{2,1,0:T(8,128)(2,1)S(1)} %get-tuple-element.58), channel_id=1, source_target_pairs={{0,4},{4,8},{8,12},{12,0},{1,5},{5,9},{9,13},{13,1},{2,6},{6,10},{... | collective-permute-start | bytes 442376 | tf_op jit(solution)/shard_map/ppermute | solution.py:454
  54.7 4.8 %collective-permute-start.12 = (bf16[4,2,64,128]{3,2,1,0:T(8,128)(2,1)S(1)}, bf16[4,2,64,128]{3,2,1,0:T(8,128)(2,1)S(1)}, u32[]{:S(2)}, u32[]{:S(2)}) collective-permute-start(bf16[4,2,64,128]{3,2,1,0:T(8,128)(2,1)S(1)} %denoise.5.refs_0_), channel_id=1, source_target_pairs={{0,16},{16,0},{1,17},{17,1},{2,18},{18,2},{3,19},{19,3},{4,20},{20... | collective-permute-start | bytes 393224 | tf_op jit(solution)/shard_map/ppermute | solution.py:454
  65.4 2.6 %collective-permute-start.14 = (bf16[2,288,128]{2,1,0:T(8,128)(2,1)S(1)}, bf16[2,288,128]{2,1,0:T(8,128)(2,1)S(1)}, u32[]{:S(2)}, u32[]{:S(2)}) collective-permute-start(bf16[2,288,128]{2,1,0:T(8,128)(2,1)S(1)} %add_convert_fusion.refs_0_), channel_id=1, source_target_pairs={{0,1},{2,3},{1,0},{3,2},{4,5},{6,7},{5,4},{7,6},{8,9},{10,11},{9,8... | collective-permute-start | bytes 442376 | tf_op jit(solution)/shard_map/ppermute | solution.py:499
  66.1 6.5 %collective-permute-start.13 = (bf16[2,288,128]{2,1,0:T(8,128)(2,1)S(1)}, bf16[2,288,128]{2,1,0:T(8,128)(2,1)S(1)}, u32[]{:S(2)}, u32[]{:S(2)}) collective-permute-start(bf16[2,288,128]{2,1,0:T(8,128)(2,1)S(1)} %add_convert_fusion.refs_0_), channel_id=1, source_target_pairs={{1,2},{2,1},{5,6},{6,5},{9,10},{10,9},{13,14},{14,13},{17,18},{18,... | collective-permute-start | bytes 442376 | tf_op jit(solution)/shard_map/ppermute | solution.py:500
  76.8 3.9 %collective-permute-start.15 = (bf16[4,2,64,128]{3,2,1,0:T(8,128)(2,1)S(1)}, bf16[4,2,64,128]{3,2,1,0:T(8,128)(2,1)S(1)}, u32[]{:S(2)}, u32[]{:S(2)}) collective-permute-start(bf16[4,2,64,128]{3,2,1,0:T(8,128)(2,1)S(1)} %denoise.7), channel_id=1, source_target_pairs={{0,16},{16,0},{1,17},{17,1},{2,18},{18,2},{3,19},{19,3},{4,20},{20... | collective-permute-start | bytes 393224 | tf_op jit(solution)/shard_map/ppermute | solution.py:454
  (7 other events, 93.0 us)

commit v5 on v4

--- a/solution.py
+++ b/solution.py
@@ -12,7 +12,6 @@
 BF16 = jnp.bfloat16
 HALO = 2
 BATCH = 16
-WIDE_LIMIT = 62 * 1024 * 1024
 VMEM_LIMIT = 30 * 1024 * 1024
 
 
@@ -68,13 +67,14 @@
     return jnp.dot(left, right, preferred_element_type=F32)
 
 
-def consistency_kernel(*refs, pieces, shares, edge, batch, direct):
+def consistency_kernel(*refs, pieces, shares, edge, batch, direct, chosen):
     images, refs = refs[:pieces], refs[pieces:]
     maps, samples, mask, tables = refs[:4]
     outs = refs[4 : 4 + shares]
     window, joined, refs = refs[4 + shares], refs[5 + shares], refs[6 + shares :]
     block, me = lax.axis_index("cascade"), lax.axis_index("coil")
-    coils, phases, readouts, rows, part = samples.shape[1:]
+    coils, phases, _, rows, part = samples.shape[1:]
+    readouts = len(chosen)
     count = rows // 2
     share = count // shares
 
@@ -117,7 +117,7 @@
     image_now = apart(jnp.concatenate([image[p, r] for r, p in places], 1))
     wait("maps")
     maps_now = apart(
-        jnp.concatenate([maps[coil, r] for r in range(readouts) for coil in range(coils)], 1)
+        jnp.concatenate([maps[coil, r] for r in chosen for coil in range(coils)], 1)
     )
 
     def map_parts(r, coil):
@@ -151,7 +151,9 @@
         spectrum = dot(tables[1, :rows, :rows], stacked)
         wait("mask")
         wait("samples")
-        measured = apart(jnp.concatenate([samples[coil, p, r] for r, coil, p in group], 1))
+        measured = apart(
+            jnp.concatenate([samples[coil, p, chosen[r]] for r, coil, p in group], 1)
+        )
         acquired = jnp.concatenate([mask[coil, p] for r, coil, p in group], 1) != 0
         mixed = jnp.concatenate(
             [
@@ -193,8 +195,9 @@
         outs[k][...] = window[:, pl.ds(begin, width + 2 * edge)]
 
 
-def consistency(images, maps, samples, mask, shares):
-    blocks, coils, phases, readouts, rows, part = samples.shape
+def consistency(images, maps, samples, mask, shares, chosen):
+    blocks, coils, phases, every, rows, part = samples.shape
+    readouts = len(chosen)
     lines = rows // 2
     share_rows = rows // shares
     edge = HALO * phases * 2
@@ -203,15 +206,15 @@
     direct = pieces > 1
     width = phases * share_rows + 2 * edge
     body = functools.partial(
-        consistency_kernel, pieces=pieces, shares=shares, edge=edge, batch=BATCH, direct=direct
+        consistency_kernel, pieces=pieces, shares=shares, edge=edge, batch=BATCH, direct=direct, chosen=chosen
     )
     image_shape = (phases, readouts, rows, part)
     buffers = [
         pltpu.VMEM(tables.shape, BF16),
         pltpu.VMEM(image_shape, BF16),
-        pltpu.VMEM((coils, readouts, rows, part), BF16),
+        pltpu.VMEM((coils, every, rows, part), BF16),
         pltpu.VMEM((coils, phases, lines, part), jnp.int32),
-        pltpu.VMEM((coils, phases, readouts, rows, part), BF16),
+        pltpu.VMEM((coils, phases, every, rows, part), BF16),
         pltpu.SemaphoreType.DMA((5,)),
     ]
     return pl.pallas_call(
@@ -225,7 +228,7 @@
         + ([] if direct else buffers),
         out_shape=[jax.ShapeDtypeStruct((readouts, width, part), BF16)] * shares,
         compiler_params=pltpu.CompilerParams(
-            vmem_limit_bytes=VMEM_LIMIT if direct else WIDE_LIMIT
+            vmem_limit_bytes=VMEM_LIMIT
         ),
         cost_estimate=pl.CostEstimate(
             flops=readouts * coils * phases * rows * part * rows * 20,
@@ -233,7 +236,7 @@
             transcendentals=0,
         ),
         name="consistency",
-    )(*images, maps, samples, mask, tables)
+    )(*[x if direct else pltpu.with_memory_space_constraint(x, pltpu.HBM) for x in (*images, maps, samples, mask, tables)])
 
 
 def tap_rows(phases, parts):
@@ -324,10 +327,15 @@
     return jnp.where(lane == part - 1, 0.0, pltpu.roll(values, part - 1, 1))
 
 
-def denoise_kernel(*refs, phases, section, second):
-    own, beside, first, time, last, *refs = refs
-    if second:
-        before, apart, out, taps, sums = refs
+def denoise_kernel(*refs, phases, section, stage):
+    refs = list(refs)
+    own = refs.pop(0)
+    beside = None if stage == "alone" else refs.pop(0)
+    first, time, last = refs[:3]
+    refs = refs[3:]
+    before = None if stage == "alone" else refs.pop(0)
+    if stage == "far":
+        apart, *outs, taps, sums = refs
     else:
         sums, taps = refs
     readouts, span, part = own.shape
@@ -336,26 +344,31 @@
     group = taps.shape[2]
     used = 9 * cell
     readout_no, coil_no = lax.axis_index("readout"), lax.axis_index("coil")
-    upward = lax.rem(readout_no, 2) == (1 if second else 0)
+    upward = lax.rem(readout_no, 2) == (0 if stage == "near" else 1)
     there = jnp.where(upward, readout_no < lax.axis_size("readout") - 1, readout_no > 0)
     first_line = (coil_no > 0).astype(F32).astype(BF16)
     last_line = (coil_no < lax.axis_size("coil") - 1).astype(F32).astype(BF16)
-
     own_at = jnp.where(upward, 0, HALO)
     beside_at = jnp.where(upward, readouts, 0)
-    slabs = [(own_at + k, own[k].astype(F32)) for k in range(readouts)]
-    for k in range(HALO):
-        value = jnp.where(upward, beside[k].astype(F32), beside[readouts - HALO + k].astype(F32))
-        slabs.append((beside_at + k, jnp.where(there, value, 0.0)))
-    filler = [jnp.zeros((group - used, part), F32)] if group > used else []
-    for index, slab in slabs:
-        views = [shifted(slab, 1), slab, shifted(slab, -1)]
-        for line in range(1, lines - 1):
-            around = [
-                views[e][cell * (line + c - 1) : cell * (line + c)] for c in range(3) for e in range(3)
-            ]
-            taps[index, line - 1] = jnp.concatenate(around + filler, 0).astype(BF16)
-    sums[...] = jnp.zeros_like(sums)
+
+    def fill_taps():
+        slabs = [(own_at + k, own[k].astype(F32)) for k in range(readouts)]
+        for k in range(HALO):
+            value = jnp.zeros((span, part), F32)
+            if beside is not None:
+                low = beside[readouts - HALO + k].astype(F32)
+                value = jnp.where(there, jnp.where(upward, beside[k].astype(F32), low), value)
+            slabs.append((beside_at + k, value))
+        filler = [jnp.zeros((group - used, part), F32)] if group > used else []
+        for index, slab in slabs:
+            views = [shifted(slab, 1), slab, shifted(slab, -1)]
+            for line in range(1, lines - 1):
+                around = [
+                    views[e][cell * (line + c - 1) : cell * (line + c)]
+                    for c in range(3)
+                    for e in range(3)
+                ]
+                taps[index, line - 1] = jnp.concatenate(around + filler, 0).astype(BF16)
 
     def add_row(row, begun, count):
         start = row - 1 + own_at
@@ -385,57 +398,75 @@
                             )
                     sums[e, target, line * cell : (line + 1) * cell] += sum(terms[1:], terms[0])
 
-    @pl.when(there)
-    def _():
+    def add_outer():
         add_row(jnp.where(upward, readouts, -1), jnp.where(upward, 2, 0), 1)
 
-    add_row(jnp.where(upward, readouts - 1, 0), jnp.where(upward, 1, 0), 2)
-    if not second:
+    def add_inner():
+        add_row(jnp.where(upward, readouts - 1, 0), jnp.where(upward, 1, 0), 2)
+
+    sums[...] = jnp.zeros_like(sums) if before is None else before[...]
+    if stage == "near":
+        fill_taps()
+        pl.when(there)(add_outer)
+        add_inner()
         for row in range(1, readouts - 1):
             add_row(row, 0, 3)
         return
 
+    @pl.when(there if stage == "far" else jnp.logical_not(there))
+    def _():
+        fill_taps()
+        if stage == "far":
+            add_outer()
+        add_inner()
+
+    if stage == "alone":
+        return
     body = slice(HALO * cell, span - HALO * cell)
     finals = []
     for r in range(readouts):
-        left, here, right = [sums[e, r, body] + before[e, r, body] for e in range(3)]
+        left, here, right = [sums[e, r, body] for e in range(3)]
         value = own[r, body].astype(F32) + here + shifted(left, 1) + shifted(right, -1)
         finals.append(value.astype(BF16))
     ordered = dot(apart[...], jnp.concatenate(finals, 1)).astype(BF16)
-    height = out.shape[2]
+    height = outs[0].shape[2]
     for p in range(phases):
         for r in range(readouts):
-            out[p, r] = ordered[p * height : (p + 1) * height, r * part : (r + 1) * part]
-
-
-def denoise(own, beside, matrices, section, phases, before=None):
+            piece = ordered[p * height : (p + 1) * height, r * part : (r + 1) * part]
+            outs[0][p, r] = piece
+            if len(outs) > 1:
+                outs[1 + r][p, 0] = piece
+
+
+def denoise(stage, own, matrices, section, phases, beside=None, before=None, split=False):
     readouts, span, part = own.shape
     cell = 2 * phases
     lines = span // cell
     share = lines - 2 * HALO
     group = matrices[0].shape[2] // 3
-    second = before is not None
-    operands = [own, beside, *matrices]
+    operands = [own] + [beside] * (stage != "alone") + list(matrices) + [before] * (stage != "alone")
     sums_shape = (3, readouts, span, part)
     scratch = [pltpu.VMEM((readouts + HALO, lines - 2, group, part), BF16)]
-    result = jax.ShapeDtypeStruct(sums_shape, F32)
-    if second:
-        operands += [before, bf16(phase_inside(phases, share).T)]
+    result = [jax.ShapeDtypeStruct(sums_shape, F32)]
+    if stage == "far":
+        operands.append(bf16(phase_inside(phases, share).T))
         scratch.append(pltpu.VMEM(sums_shape, F32))
-        result = jax.ShapeDtypeStruct((phases, readouts, 2 * share, part), BF16)
+        result = [jax.ShapeDtypeStruct((phases, readouts, 2 * share, part), BF16)]
+        if split:
+            result += [jax.ShapeDtypeStruct((phases, 1, 2 * share, part), BF16)] * readouts
     return pl.pallas_call(
-        functools.partial(denoise_kernel, phases=phases, section=section, second=second),
+        functools.partial(denoise_kernel, phases=phases, section=section, stage=stage),
         in_specs=[pl.BlockSpec(memory_space=pltpu.VMEM)] * len(operands),
-        out_specs=pl.BlockSpec(memory_space=pltpu.VMEM),
+        out_specs=[pl.BlockSpec(memory_space=pltpu.VMEM)] * len(result),
         scratch_shapes=scratch,
         out_shape=result,
         compiler_params=pltpu.CompilerParams(vmem_limit_bytes=VMEM_LIMIT),
         cost_estimate=pl.CostEstimate(
-            flops=6 * readouts * lines * part * 256 * 256,
+            flops=(1 if stage == "alone" else 6) * readouts * lines * part * 256 * 256,
             bytes_accessed=2 * 1024 * 1024,
             transcendentals=0,
         ),
-        name="denoise",
+        name="denoise_" + stage,
     )(*operands)
 
 
@@ -444,7 +475,7 @@
 
 
 def swaps(count, first):
-    pairs = [(i, i + 1) for i in range(first, count - 1, 2)]
+    pairs = [(i, (i + 1) % count) for i in range(first, count, 2)]
     return pairs + [(target, source) for source, target in pairs]
 
 
@@ -471,16 +502,26 @@
         return jnp.pad(block, ((0, -block.shape[0] % 64), (0, 0)))
 
     initial, coil_maps, kspace = rows_of(initial), rows_of(coil_maps), rows_of(kspace)
-    images = [initial]
+    readouts = kspace.shape[3]
+    images = [[initial]]
     matrices = None
     sent = []
     for section in range(sections):
-        partial = consistency(images, coil_maps, kspace, sampled, shares)
-        if matrices is None:
-            partial, (first_w, time_w, last_w) = lax.optimization_barrier(
-                (partial, (first_w, time_w, last_w))
-            )
-        parts = exchanged(partial, "coil", shares)
+        if section == 0:
+            choices = [tuple(range(readouts))]
+        else:
+            choices = [(r,) for r in range(readouts)]
+        parts = []
+        for image, chosen in zip(images, choices):
+            partial = consistency(image, coil_maps, kspace, sampled, shares, chosen)
+            if matrices is None:
+                partial, (first_w, time_w, last_w) = lax.optimization_barrier(
+                    (partial, (first_w, time_w, last_w))
+                )
+            if section > 0 and chosen[-1] == readouts - 1:
+                partial, waiting = lax.optimization_barrier((partial, waiting))
+                sent.append(exchanged([waiting] * sections, "cascade", sections))
+            parts.append(exchanged(partial, "coil", shares))
         if matrices is None:
             pack = jnp.concatenate(
                 [
@@ -495,14 +536,20 @@
             parts, matrices = lax.optimization_barrier((parts, matrices))
         else:
             parts, sent[-1] = lax.optimization_barrier((parts, sent[-1]))
-        combined = sum(p.astype(F32) for p in parts).astype(BF16)
+        combined = jnp.concatenate(
+            [sum(p.astype(F32) for p in pieces).astype(BF16) for pieces in parts], 0
+        )
         even = lax.ppermute(combined, "readout", swaps(readout_parts, 0))
         odd = lax.ppermute(combined, "readout", swaps(readout_parts, 1))
-        reached = denoise(combined, even, matrices, section, phases)
-        output = denoise(combined, odd, matrices, section, phases, reached)
-        if section < sections - 1:
-            images = exchanged([output] * shares, "coil", shares)
-        sent.append(exchanged([output] * sections, "cascade", sections))
+        (sums,) = denoise("alone", combined, matrices, section, phases)
+        (sums,) = denoise("near", combined, matrices, section, phases, even, sums)
+        more = section < sections - 1
+        output, *split = denoise("far", combined, matrices, section, phases, odd, sums, more)
+        images = [exchanged([value] * shares, "coil", shares) for value in split]
+        if more:
+            waiting = output
+        else:
+            sent.append(exchanged([output] * sections, "cascade", sections))
 
     arrived = []
     for block in range(sections):

time: 81.9 us -> 78.8 us (0.962)
  waiting for transfers between devices: 25.8 us -> 18.2 us
  starting transfers between devices: 25.5 us -> 30 us
  other arithmetic: 2.2 us -> 1.32 us
    ppermute x12 -> x18, waiting for transfers between devices: 25 us -> 17.6 us  [exchanged(): arrived[k] = lax.ppermute(values[k], axis, rotation(count, k))]
    ppermute x12 -> x18, starting transfers between devices: 19.2 us -> 23.8 us  [exchanged(): arrived[k] = lax.ppermute(values[k], axis, rotation(count, k))]
    ppermute x2, starting transfers between devices: 4.92 us -> 2.6 us  [per_device(): odd = lax.ppermute(combined, 'readout', swaps(readout_parts, 1))]
    ppermute x2, starting transfers between devices: 1.35 us -> 3.62 us  [per_device(): even = lax.ppermute(combined, 'readout', swaps(readout_parts, 0))]
    convert_element_type x2, other arithmetic: 1.07 us -> 0.16 us  [per_device(): sum((p.astype(F32) for p in pieces)).astype(BF16)]
    pallas_call x4 -> x6, Pallas kernels: 15.8 us -> 16.5 us  [denoise(): pl.pallas_call(functools.partial(denoise_kernel, phases=phases, section=s...]
    pallas_call x2 -> x3, Pallas kernels: 10.9 us -> 11 us  [consistency(): pl.pallas_call(body, in_specs=[pl.BlockSpec(memory_space=pltpu.VMEM if di...]
  transfers between devices with their start and end apart: 16 -> 22, of which waited for: 10 -> 9; matrix products, arithmetic and copies ran while one was open for 0% -> 0% of each run, Pallas kernels for 11% -> 18%
where the time goes in v5:
time: 78.8 us; the launch traced here: 78.7 us
  starting transfers between devices  30 us (38%)
  Pallas kernels  28.7 us (36%)
  waiting for transfers between devices  18.2 us (23%)
  other arithmetic  1.32 us (2%)
    ppermute x18, starting transfers between devices, exchanged(): arrived[k] = lax.ppermute(values[k], axis, rotation(count, k))  23.8 us
    ppermute x18, waiting for transfers between devices, exchanged(): arrived[k] = lax.ppermute(values[k], axis, rotation(count, k))  17.6 us
    pallas_call x6, Pallas kernels, denoise(): pl.pallas_call(functools.partial(denoise_kernel, phases=phases, section=s...  16.5 us
    pallas_call x3, Pallas kernels, consistency(): pl.pallas_call(body, in_specs=[pl.BlockSpec(memory_space=pltpu.VMEM if di...  11 us
    ppermute x2, starting transfers between devices, per_device(): even = lax.ppermute(combined, 'readout', swaps(readout_parts, 0))  3.62 us
    ppermute x2, starting transfers between devices, per_device(): odd = lax.ppermute(combined, 'readout', swaps(readout_parts, 1))  2.6 us
  transfers between devices with their start and end apart: 22, of which 9 were waited for; matrix products, arithmetic and copies ran while one was open for 0% of the time, Pallas kernels for 18%

profile of v5, /device:TPU:1, one launch (start us, length us, event | category | flops | bytes accessed | tf_op | source)
XLA Modules:
  0.0 78.7 jit_solution(5290356385605880503)
XLA Ops:
  0.1 6.0 %consistency.3 = (bf16[2,288,128]{2,1,0:T(8,128)(2,1)S(1)}, bf16[2,288,128]{2,1,0:T(8,128)(2,1)S(1)}, bf16[2,288,128]{2,1,0:T(8,128)(2,1)S(1)}, bf16[2,288,128]{2,1,0:T(8,128)(2,1)S(1)}) custom-call(bf16[2,4,2,256,128]{4,3,2,1,0:T(8,128)(2,1)} %bitcast.19, bf16[2,4,2,256,128]{4,3,2,1,0:T(8,128)(2,1)} %bitcast.12, bf16[2,4,4,2,256,128]{5,4,3,2,1,0:T(8,128)(2,1)} %bitcast.9, ...), custom_call_target="tpu_custom_call" | custom-call | flops 5368709120 | bytes 4194304 | tf_op jit(solution)/shard_map/consistency/pallas_call | solution.py:220
  6.1 2.2 %collective-permute-start = (bf16[2,288,128]{2,1,0:T(8,128)(2,1)S(1)}, bf16[2,288,128]{2,1,0:T(8,128)(2,1)S(1)}, u32[]{:S(2)}, u32[]{:S(2)}) collective-permute-start(bf16[2,288,128]{2,1,0:T(8,128)(2,1)S(1)} %get-tuple-element.57), channel_id=1, source_target_pairs={{0,4},{4,8},{8,12},{12,0},{1,5},{5,9},{9,13},{13,1},{2,6},{6,10},{... | collective-permute-start | bytes 442376 | tf_op jit(solution)/shard_map/ppermute | solution.py:485
  8.3 2.3 %collective-permute-start.1 = (bf16[2,288,128]{2,1,0:T(8,128)(2,1)S(1)}, bf16[2,288,128]{2,1,0:T(8,128)(2,1)S(1)}, u32[]{:S(2)}, u32[]{:S(2)}) collective-permute-start(bf16[2,288,128]{2,1,0:T(8,128)(2,1)S(1)} %get-tuple-element.58), channel_id=1, source_target_pairs={{0,8},{4,12},{8,0},{12,4},{1,9},{5,13},{9,1},{13,5},{2,10},{6,14},... | collective-permute-start | bytes 442376 | tf_op jit(solution)/shard_map/ppermute | solution.py:485
  11.8 1.3 %collective-permute-start.3 = (bf16[320,64]{1,0:T(8,128)(2,1)S(1)}, bf16[320,64]{1,0:T(8,128)(2,1)S(1)}, u32[]{:S(2)}, u32[]{:S(2)}) collective-permute-start(bf16[320,64]{1,0:T(8,128)(2,1)S(1)} %fusion.4.refs_0_), channel_id=1, source_target_pairs={{0,16},{16,0},{1,17},{17,1},{2,18},{18,2},{3,19},{19,3},{4,20},{20... | collective-permute-start | bytes 122888 | tf_op jit(solution)/shard_map/ppermute | solution.py:485
  13.1 2.3 %collective-permute-done.3.refs_1_ = bf16[320,64]{1,0:T(8,128)(2,1)S(1)} collective-permute-done((bf16[320,64]{1,0:T(8,128)(2,1)S(1)}, bf16[320,64]{1,0:T(8,128)(2,1)S(1)}, u32[]{:S(2)}, u32[]{:S(2)}) %collective-permute-start.3) | collective-permute-done | bytes 40992 | tf_op jit(solution)/shard_map/ppermute | solution.py:485
  16.7 4.2 %collective-permute-done.1 = bf16[2,288,128]{2,1,0:T(8,128)(2,1)S(1)} collective-permute-done((bf16[2,288,128]{2,1,0:T(8,128)(2,1)S(1)}, bf16[2,288,128]{2,1,0:T(8,128)(2,1)S(1)}, u32[]{:S(2)}, u32[]{:S(2)}) %collective-permute-start.1) | collective-permute-done | bytes 147488 | tf_op jit(solution)/shard_map/ppermute | solution.py:485
  23.0 3.8 %denoise_near.2.refs_5_ = f32[3,2,288,128]{3,2,1,0:T(8,128)S(1)} custom-call(bf16[2,288,128]{2,1,0:T(8,128)(2,1)S(1)} %add_convert_fusion.refs_0_, bf16[2,288,128]{2,1,0:T(8,128)(2,1)S(1)} %collective-permute-done.5.refs_1_, bf16[2,256,240]{2,1,0:T(8,128)(2,1)S(1)} %get-tuple-element.70.refs_1_.refs_2_, ...), custom_call_target="tpu_custom_call" | custom-call | flops 3623878656 | bytes 2097152 | tf_op jit(solution)/shard_map/denoise_near/pallas_call | solution.py:457
  27.2 4.4 %denoise_far.2 = (bf16[4,2,64,128]{3,2,1,0:T(8,128)(2,1)S(1)}, bf16[4,1,64,128]{3,2,1,0:T(8,128)(2,1)S(1)}, bf16[4,1,64,128]{3,2,1,0:T(8,128)(2,1)S(1)}) custom-call(bf16[2,288,128]{2,1,0:T(8,128)(2,1)S(1)} %add_convert_fusion.refs_0_, bf16[2,288,128]{2,1,0:T(8,128)(2,1)S(1)} %collective-permute-done.4.refs_1_, ...), custom_call_target="tpu_custom_call" | custom-call | flops 3623878656 | bytes 2097152 | tf_op jit(solution)/shard_map/denoise_far/pallas_call | solution.py:457
  31.7 3.4 %collective-permute-start.12 = (bf16[4,1,64,128]{3,2,1,0:T(8,128)(2,1)S(1)}, bf16[4,1,64,128]{3,2,1,0:T(8,128)(2,1)S(1)}, u32[]{:S(2)}, u32[]{:S(2)}) collective-permute-start(bf16[4,1,64,128]{3,2,1,0:T(8,128)(2,1)S(1)} %get-tuple-element.78.refs_0_), channel_id=1, source_target_pairs={{0,4},{4,8},{8,12},{12,0},{1,5},{5,9},{9,13},{13,1},{2,6},{6,10},{... | collective-permute-start | bytes 196616 | tf_op jit(solution)/shard_map/ppermute | solution.py:485
  35.1 1.3 %collective-permute-start.13 = (bf16[4,1,64,128]{3,2,1,0:T(8,128)(2,1)S(1)}, bf16[4,1,64,128]{3,2,1,0:T(8,128)(2,1)S(1)}, u32[]{:S(2)}, u32[]{:S(2)}) collective-permute-start(bf16[4,1,64,128]{3,2,1,0:T(8,128)(2,1)S(1)} %get-tuple-element.78.refs_0_), channel_id=1, source_target_pairs={{0,8},{4,12},{8,0},{12,4},{1,9},{5,13},{9,1},{13,5},{2,10},{6,14},... | collective-permute-start | bytes 196616 | tf_op jit(solution)/shard_map/ppermute | solution.py:485
  38.9 1.6 %collective-permute-start.8 = (bf16[4,1,64,128]{3,2,1,0:T(8,128)(2,1)S(1)}, bf16[4,1,64,128]{3,2,1,0:T(8,128)(2,1)S(1)}, u32[]{:S(2)}, u32[]{:S(2)}) collective-permute-start(bf16[4,1,64,128]{3,2,1,0:T(8,128)(2,1)S(1)} %get-tuple-element.73.refs_0_), channel_id=1, source_target_pairs={{0,12},{4,0},{8,4},{12,8},{1,13},{5,1},{9,5},{13,9},{2,14},{6,2},{... | collective-permute-start | bytes 196616 | tf_op jit(solution)/shard_map/ppermute | solution.py:485
  40.6 2.0 %collective-permute-done.14.refs_3_ = bf16[4,1,64,128]{3,2,1,0:T(8,128)(2,1)S(1)} collective-permute-done((bf16[4,1,64,128]{3,2,1,0:T(8,128)(2,1)S(1)}, bf16[4,1,64,128]{3,2,1,0:T(8,128)(2,1)S(1)}, u32[]{:S(2)}, u32[]{:S(2)}) %collective-permute-start.14) | collective-permute-done | bytes 65568 | tf_op jit(solution)/shard_map/ppermute | solution.py:485
  42.6 2.5 %consistency.5 = (bf16[1,288,128]{2,1,0:T(8,128)(2,1)S(1)}, bf16[1,288,128]{2,1,0:T(8,128)(2,1)S(1)}, bf16[1,288,128]{2,1,0:T(8,128)(2,1)S(1)}, bf16[1,288,128]{2,1,0:T(8,128)(2,1)S(1)}) custom-call(bf16[4,1,64,128]{3,2,1,0:T(8,128)(2,1)S(1)} %get-tuple-element.78.refs_0_, bf16[4,1,64,128]{3,2,1,0:T(8,128)(2,1)S(1)} %collective-permute-done.12.refs_1_, ...), custom_call_target="tpu_custom_call" | custom-call | flops 2684354560 | bytes 4194304 | tf_op jit(solution)/shard_map/consistency/pallas_call | solution.py:220
  45.1 1.3 %collective-permute-start.18 = (bf16[4,2,64,128]{3,2,1,0:T(8,128)(2,1)S(1)}, bf16[4,2,64,128]{3,2,1,0:T(8,128)(2,1)S(1)}, u32[]{:S(2)}, u32[]{:S(2)}) collective-permute-start(bf16[4,2,64,128]{3,2,1,0:T(8,128)(2,1)S(1)} %get-tuple-element.97), channel_id=1, source_target_pairs={{0,16},{16,0},{1,17},{17,1},{2,18},{18,2},{3,19},{19,3},{4,20},{20... | collective-permute-start | bytes 393224 | tf_op jit(solution)/shard_map/ppermute | solution.py:485
  46.4 2.6 %collective-permute-start.15 = (bf16[1,288,128]{2,1,0:T(8,128)(2,1)S(1)}, bf16[1,288,128]{2,1,0:T(8,128)(2,1)S(1)}, u32[]{:S(2)}, u32[]{:S(2)}) collective-permute-start(bf16[1,288,128]{2,1,0:T(8,128)(2,1)S(1)} %get-tuple-element.85), channel_id=1, source_target_pairs={{0,4},{4,8},{8,12},{12,0},{1,5},{5,9},{9,13},{13,1},{2,6},{6,10},{... | collective-permute-start | bytes 221192 | tf_op jit(solution)/shard_map/ppermute | solution.py:485
  49.0 2.1 %collective-permute-start.17 = (bf16[1,288,128]{2,1,0:T(8,128)(2,1)S(1)}, bf16[1,288,128]{2,1,0:T(8,128)(2,1)S(1)}, u32[]{:S(2)}, u32[]{:S(2)}) collective-permute-start(bf16[1,288,128]{2,1,0:T(8,128)(2,1)S(1)} %get-tuple-element.87), channel_id=1, source_target_pairs={{0,12},{4,0},{8,4},{12,8},{1,13},{5,1},{9,5},{13,9},{2,14},{6,2},{... | collective-permute-start | bytes 221192 | tf_op jit(solution)/shard_map/ppermute | solution.py:485
  51.0 2.5 %consistency.4 = (bf16[1,288,128]{2,1,0:T(8,128)(2,1)S(1)}, bf16[1,288,128]{2,1,0:T(8,128)(2,1)S(1)}, bf16[1,288,128]{2,1,0:T(8,128)(2,1)S(1)}, bf16[1,288,128]{2,1,0:T(8,128)(2,1)S(1)}) custom-call(bf16[4,1,64,128]{3,2,1,0:T(8,128)(2,1)S(1)} %get-tuple-element.73.refs_0_, bf16[4,1,64,128]{3,2,1,0:T(8,128)(2,1)S(1)} %collective-permute-done.6.refs_1_, ...), custom_call_target="tpu_custom_call" | custom-call | flops 2684354560 | bytes 4194304 | tf_op jit(solution)/shard_map/consistency/pallas_call | solution.py:220
  53.9 1.3 %collective-permute-start.11 = (bf16[1,288,128]{2,1,0:T(8,128)(2,1)S(1)}, bf16[1,288,128]{2,1,0:T(8,128)(2,1)S(1)}, u32[]{:S(2)}, u32[]{:S(2)}) collective-permute-start(bf16[1,288,128]{2,1,0:T(8,128)(2,1)S(1)} %get-tuple-element.77), channel_id=1, source_target_pairs={{0,12},{4,0},{8,4},{12,8},{1,13},{5,1},{9,5},{13,9},{2,14},{6,2},{... | collective-permute-start | bytes 221192 | tf_op jit(solution)/shard_map/ppermute | solution.py:485
  55.5 4.1 %collective-permute-done.10 = bf16[1,288,128]{2,1,0:T(8,128)(2,1)S(1)} collective-permute-done((bf16[1,288,128]{2,1,0:T(8,128)(2,1)S(1)}, bf16[1,288,128]{2,1,0:T(8,128)(2,1)S(1)}, u32[]{:S(2)}, u32[]{:S(2)}) %collective-permute-start.10) | collective-permute-done | bytes 73760 | tf_op jit(solution)/shard_map/ppermute | solution.py:485
  60.5 3.0 %collective-permute-start.20 = (bf16[2,288,128]{2,1,0:T(8,128)(2,1)S(1)}, bf16[2,288,128]{2,1,0:T(8,128)(2,1)S(1)}, u32[]{:S(2)}, u32[]{:S(2)}) collective-permute-start(bf16[2,288,128]{2,1,0:T(8,128)(2,1)S(1)} %pad_maximum_fusion.1.refs_0_), channel_id=1, source_target_pairs={{0,1},{2,3},{1,0},{3,2},{4,5},{6,7},{5,4},{7,6},{8,9},{10,11},{9,8... | collective-permute-start | bytes 442376 | tf_op jit(solution)/shard_map/ppermute | solution.py:542
  63.4 1.4 %collective-permute-start.19 = (bf16[2,288,128]{2,1,0:T(8,128)(2,1)S(1)}, bf16[2,288,128]{2,1,0:T(8,128)(2,1)S(1)}, u32[]{:S(2)}, u32[]{:S(2)}) collective-permute-start(bf16[2,288,128]{2,1,0:T(8,128)(2,1)S(1)} %pad_maximum_fusion.1.refs_0_), channel_id=1, source_target_pairs={{1,2},{3,0},{2,1},{0,3},{5,6},{7,4},{6,5},{4,7},{9,10},{11,8},{10,... | collective-permute-start | bytes 442376 | tf_op jit(solution)/shard_map/ppermute | solution.py:543
  65.2 3.8 %denoise_near.3.refs_5_ = f32[3,2,288,128]{3,2,1,0:T(8,128)S(1)} custom-call(bf16[2,288,128]{2,1,0:T(8,128)(2,1)S(1)} %pad_maximum_fusion.1.refs_0_, bf16[2,288,128]{2,1,0:T(8,128)(2,1)S(1)} %collective-permute-done.20.refs_1_, bf16[2,256,240]{2,1,0:T(8,128)(2,1)S(1)} %get-tuple-element.70.refs_1_.refs_2_, ...), custom_call_target="tpu_custom_call" | custom-call | flops 3623878656 | bytes 2097152 | tf_op jit(solution)/shard_map/denoise_near/pallas_call | solution.py:457
  69.0 4.2 %denoise_far.3 = bf16[4,2,64,128]{3,2,1,0:T(8,128)(2,1)S(1)} custom-call(bf16[2,288,128]{2,1,0:T(8,128)(2,1)S(1)} %pad_maximum_fusion.1.refs_0_, bf16[2,288,128]{2,1,0:T(8,128)(2,1)S(1)} %collective-permute-done.19.refs_1_, bf16[2,256,240]{2,1,0:T(8,128)(2,1)S(1)} %get-tuple-element.70.refs_1_.refs_2_, ...), custom_call_target="tpu_custom_call" | custom-call | flops 3623878656 | bytes 2097152 | tf_op jit(solution)/shard_map/denoise_far/pallas_call | solution.py:457
  73.5 4.1 %collective-permute-done.21 = bf16[4,2,64,128]{3,2,1,0:T(8,128)(2,1)S(1)} collective-permute-done((bf16[4,2,64,128]{3,2,1,0:T(8,128)(2,1)S(1)}, bf16[4,2,64,128]{3,2,1,0:T(8,128)(2,1)S(1)}, u32[]{:S(2)}, u32[]{:S(2)}) %collective-permute-start.21) | collective-permute-done | bytes 131104 | tf_op jit(solution)/shard_map/ppermute | solution.py:485
  (69 shorter events, 10.8 us)
Async XLA Ops:
  6.1 10.6 %collective-permute-start = (bf16[2,288,128]{2,1,0:T(8,128)(2,1)S(1)}, bf16[2,288,128]{2,1,0:T(8,128)(2,1)S(1)}, u32[]{:S(2)}, u32[]{:S(2)}) collective-permute-start(bf16[2,288,128]{2,1,0:T(8,128)(2,1)S(1)} %get-tuple-element.57), channel_id=1, source_target_pairs={{0,4},{4,8},{8,12},{12,0},{1,5},{5,9},{9,13},{13,1},{2,6},{6,10},{... | collective-permute-start | bytes 442376 | tf_op jit(solution)/shard_map/ppermute | solution.py:485
  8.3 12.7 %collective-permute-start.1 = (bf16[2,288,128]{2,1,0:T(8,128)(2,1)S(1)}, bf16[2,288,128]{2,1,0:T(8,128)(2,1)S(1)}, u32[]{:S(2)}, u32[]{:S(2)}) collective-permute-start(bf16[2,288,128]{2,1,0:T(8,128)(2,1)S(1)} %get-tuple-element.58), channel_id=1, source_target_pairs={{0,8},{4,12},{8,0},{12,4},{1,9},{5,13},{9,1},{13,5},{2,10},{6,14},... | collective-permute-start | bytes 442376 | tf_op jit(solution)/shard_map/ppermute | solution.py:485
  10.6 10.3 %collective-permute-start.2 = (bf16[2,288,128]{2,1,0:T(8,128)(2,1)S(1)}, bf16[2,288,128]{2,1,0:T(8,128)(2,1)S(1)}, u32[]{:S(2)}, u32[]{:S(2)}) collective-permute-start(bf16[2,288,128]{2,1,0:T(8,128)(2,1)S(1)} %get-tuple-element.59), channel_id=1, source_target_pairs={{0,12},{4,0},{8,4},{12,8},{1,13},{5,1},{9,5},{13,9},{2,14},{6,2},{... | collective-permute-start | bytes 442376 | tf_op jit(solution)/shard_map/ppermute | solution.py:485
  11.8 3.7 %collective-permute-start.3 = (bf16[320,64]{1,0:T(8,128)(2,1)S(1)}, bf16[320,64]{1,0:T(8,128)(2,1)S(1)}, u32[]{:S(2)}, u32[]{:S(2)}) collective-permute-start(bf16[320,64]{1,0:T(8,128)(2,1)S(1)} %fusion.4.refs_0_), channel_id=1, source_target_pairs={{0,16},{16,0},{1,17},{17,1},{2,18},{18,2},{3,19},{19,3},{4,20},{20... | collective-permute-start | bytes 122888 | tf_op jit(solution)/shard_map/ppermute | solution.py:485
  21.1 1.9 %collective-permute-start.5 = (bf16[2,288,128]{2,1,0:T(8,128)(2,1)S(1)}, bf16[2,288,128]{2,1,0:T(8,128)(2,1)S(1)}, u32[]{:S(2)}, u32[]{:S(2)}) collective-permute-start(bf16[2,288,128]{2,1,0:T(8,128)(2,1)S(1)} %add_convert_fusion.refs_0_), channel_id=1, source_target_pairs={{0,1},{2,3},{1,0},{3,2},{4,5},{6,7},{5,4},{7,6},{8,9},{10,11},{9,8... | collective-permute-start | bytes 442376 | tf_op jit(solution)/shard_map/ppermute | solution.py:542
  21.7 5.5 %collective-permute-start.4 = (bf16[2,288,128]{2,1,0:T(8,128)(2,1)S(1)}, bf16[2,288,128]{2,1,0:T(8,128)(2,1)S(1)}, u32[]{:S(2)}, u32[]{:S(2)}) collective-permute-start(bf16[2,288,128]{2,1,0:T(8,128)(2,1)S(1)} %add_convert_fusion.refs_0_), channel_id=1, source_target_pairs={{1,2},{3,0},{2,1},{0,3},{5,6},{7,4},{6,5},{4,7},{9,10},{11,8},{10,... | collective-permute-start | bytes 442376 | tf_op jit(solution)/shard_map/ppermute | solution.py:543
  26.7 15.8 %copy-start.7 = (bf16[2,4,4,2,128,2,128]{6,5,4,3,2,1,0:T(2,128)(2,1)S(1)}, bf16[2,4,4,2,128,2,128]{6,5,4,3,2,1,0:T(2,128)(2,1)}, u32[]{:S(2)}) copy-start(bf16[2,4,4,2,128,2,128]{6,5,4,3,2,1,0:T(2,128)(2,1)} %param.21) | copy-start | bytes 12582916
  26.7 15.8 %copy-start.8 = (bf16[2,4,2,128,2,128]{5,4,3,2,1,0:T(2,128)(2,1)S(1)}, bf16[2,4,2,128,2,128]{5,4,3,2,1,0:T(2,128)(2,1)}, u32[]{:S(2)}) copy-start(bf16[2,4,2,128,2,128]{5,4,3,2,1,0:T(2,128)(2,1)} %param.20) | copy-start | bytes 3145732
  31.7 7.2 %collective-permute-start.12 = (bf16[4,1,64,128]{3,2,1,0:T(8,128)(2,1)S(1)}, bf16[4,1,64,128]{3,2,1,0:T(8,128)(2,1)S(1)}, u32[]{:S(2)}, u32[]{:S(2)}) collective-permute-start(bf16[4,1,64,128]{3,2,1,0:T(8,128)(2,1)S(1)} %get-tuple-element.78.refs_0_), channel_id=1, source_target_pairs={{0,4},{4,8},{8,12},{12,0},{1,5},{5,9},{9,13},{13,1},{2,6},{6,10},{... | collective-permute-start | bytes 196616 | tf_op jit(solution)/shard_map/ppermute | solution.py:485
  35.1 5.5 %collective-permute-start.13 = (bf16[4,1,64,128]{3,2,1,0:T(8,128)(2,1)S(1)}, bf16[4,1,64,128]{3,2,1,0:T(8,128)(2,1)S(1)}, u32[]{:S(2)}, u32[]{:S(2)}) collective-permute-start(bf16[4,1,64,128]{3,2,1,0:T(8,128)(2,1)S(1)} %get-tuple-element.78.refs_0_), channel_id=1, source_target_pairs={{0,8},{4,12},{8,0},{12,4},{1,9},{5,13},{9,1},{13,5},{2,10},{6,14},... | collective-permute-start | bytes 196616 | tf_op jit(solution)/shard_map/ppermute | solution.py:485
  36.4 6.2 %collective-permute-start.14 = (bf16[4,1,64,128]{3,2,1,0:T(8,128)(2,1)S(1)}, bf16[4,1,64,128]{3,2,1,0:T(8,128)(2,1)S(1)}, u32[]{:S(2)}, u32[]{:S(2)}) collective-permute-start(bf16[4,1,64,128]{3,2,1,0:T(8,128)(2,1)S(1)} %get-tuple-element.78.refs_0_), channel_id=1, source_target_pairs={{0,12},{4,0},{8,4},{12,8},{1,13},{5,1},{9,5},{13,9},{2,14},{6,2},{... | collective-permute-start | bytes 196616 | tf_op jit(solution)/shard_map/ppermute | solution.py:485
  37.2 11.7 %collective-permute-start.6 = (bf16[4,1,64,128]{3,2,1,0:T(8,128)(2,1)S(1)}, bf16[4,1,64,128]{3,2,1,0:T(8,128)(2,1)S(1)}, u32[]{:S(2)}, u32[]{:S(2)}) collective-permute-start(bf16[4,1,64,128]{3,2,1,0:T(8,128)(2,1)S(1)} %get-tuple-element.73.refs_0_), channel_id=1, source_target_pairs={{0,4},{4,8},{8,12},{12,0},{1,5},{5,9},{9,13},{13,1},{2,6},{6,10},{... | collective-permute-start | bytes 196616 | tf_op jit(solution)/shard_map/ppermute | solution.py:485
  37.9 11.1 %collective-permute-start.7 = (bf16[4,1,64,128]{3,2,1,0:T(8,128)(2,1)S(1)}, bf16[4,1,64,128]{3,2,1,0:T(8,128)(2,1)S(1)}, u32[]{:S(2)}, u32[]{:S(2)}) collective-permute-start(bf16[4,1,64,128]{3,2,1,0:T(8,128)(2,1)S(1)} %get-tuple-element.73.refs_0_), channel_id=1, source_target_pairs={{0,8},{4,12},{8,0},{12,4},{1,9},{5,13},{9,1},{13,5},{2,10},{6,14},... | collective-permute-start | bytes 196616 | tf_op jit(solution)/shard_map/ppermute | solution.py:485
  38.9 12.1 %collective-permute-start.8 = (bf16[4,1,64,128]{3,2,1,0:T(8,128)(2,1)S(1)}, bf16[4,1,64,128]{3,2,1,0:T(8,128)(2,1)S(1)}, u32[]{:S(2)}, u32[]{:S(2)}) collective-permute-start(bf16[4,1,64,128]{3,2,1,0:T(8,128)(2,1)S(1)} %get-tuple-element.73.refs_0_), channel_id=1, source_target_pairs={{0,12},{4,0},{8,4},{12,8},{1,13},{5,1},{9,5},{13,9},{2,14},{6,2},{... | collective-permute-start | bytes 196616 | tf_op jit(solution)/shard_map/ppermute | solution.py:485
  45.1 15.3 %collective-permute-start.18 = (bf16[4,2,64,128]{3,2,1,0:T(8,128)(2,1)S(1)}, bf16[4,2,64,128]{3,2,1,0:T(8,128)(2,1)S(1)}, u32[]{:S(2)}, u32[]{:S(2)}) collective-permute-start(bf16[4,2,64,128]{3,2,1,0:T(8,128)(2,1)S(1)} %get-tuple-element.97), channel_id=1, source_target_pairs={{0,16},{16,0},{1,17},{17,1},{2,18},{18,2},{3,19},{19,3},{4,20},{20... | collective-permute-start | bytes 393224 | tf_op jit(solution)/shard_map/ppermute | solution.py:485
  46.4 7.5 %collective-permute-start.15 = (bf16[1,288,128]{2,1,0:T(8,128)(2,1)S(1)}, bf16[1,288,128]{2,1,0:T(8,128)(2,1)S(1)}, u32[]{:S(2)}, u32[]{:S(2)}) collective-permute-start(bf16[1,288,128]{2,1,0:T(8,128)(2,1)S(1)} %get-tuple-element.85), channel_id=1, source_target_pairs={{0,4},{4,8},{8,12},{12,0},{1,5},{5,9},{9,13},{13,1},{2,6},{6,10},{... | collective-permute-start | bytes 221192 | tf_op jit(solution)/shard_map/ppermute | solution.py:485
  49.0 6.2 %collective-permute-start.16 = (bf16[1,288,128]{2,1,0:T(8,128)(2,1)S(1)}, bf16[1,288,128]{2,1,0:T(8,128)(2,1)S(1)}, u32[]{:S(2)}, u32[]{:S(2)}) collective-permute-start(bf16[1,288,128]{2,1,0:T(8,128)(2,1)S(1)} %get-tuple-element.86), channel_id=1, source_target_pairs={{0,8},{4,12},{8,0},{12,4},{1,9},{5,13},{9,1},{13,5},{2,10},{6,14},... | collective-permute-start | bytes 221192 | tf_op jit(solution)/shard_map/ppermute | solution.py:485
  49.0 6.5 %collective-permute-start.17 = (bf16[1,288,128]{2,1,0:T(8,128)(2,1)S(1)}, bf16[1,288,128]{2,1,0:T(8,128)(2,1)S(1)}, u32[]{:S(2)}, u32[]{:S(2)}) collective-permute-start(bf16[1,288,128]{2,1,0:T(8,128)(2,1)S(1)} %get-tuple-element.87), channel_id=1, source_target_pairs={{0,12},{4,0},{8,4},{12,8},{1,13},{5,1},{9,5},{13,9},{2,14},{6,2},{... | collective-permute-start | bytes 221192 | tf_op jit(solution)/shard_map/ppermute | solution.py:485
  53.6 6.0 %collective-permute-start.10 = (bf16[1,288,128]{2,1,0:T(8,128)(2,1)S(1)}, bf16[1,288,128]{2,1,0:T(8,128)(2,1)S(1)}, u32[]{:S(2)}, u32[]{:S(2)}) collective-permute-start(bf16[1,288,128]{2,1,0:T(8,128)(2,1)S(1)} %get-tuple-element.76), channel_id=1, source_target_pairs={{0,8},{4,12},{8,0},{12,4},{1,9},{5,13},{9,1},{13,5},{2,10},{6,14},... | collective-permute-start | bytes 221192 | tf_op jit(solution)/shard_map/ppermute | solution.py:485
  53.9 5.6 %collective-permute-start.11 = (bf16[1,288,128]{2,1,0:T(8,128)(2,1)S(1)}, bf16[1,288,128]{2,1,0:T(8,128)(2,1)S(1)}, u32[]{:S(2)}, u32[]{:S(2)}) collective-permute-start(bf16[1,288,128]{2,1,0:T(8,128)(2,1)S(1)} %get-tuple-element.77), channel_id=1, source_target_pairs={{0,12},{4,0},{8,4},{12,8},{1,13},{5,1},{9,5},{13,9},{2,14},{6,2},{... | collective-permute-start | bytes 221192 | tf_op jit(solution)/shard_map/ppermute | solution.py:485
  55.2 5.2 %collective-permute-start.9 = (bf16[1,288,128]{2,1,0:T(8,128)(2,1)S(1)}, bf16[1,288,128]{2,1,0:T(8,128)(2,1)S(1)}, u32[]{:S(2)}, u32[]{:S(2)}) collective-permute-start(bf16[1,288,128]{2,1,0:T(8,128)(2,1)S(1)} %get-tuple-element.75), channel_id=1, source_target_pairs={{0,4},{4,8},{8,12},{12,0},{1,5},{5,9},{9,13},{13,1},{2,6},{6,10},{... | collective-permute-start | bytes 221192 | tf_op jit(solution)/shard_map/ppermute | solution.py:485
  60.5 4.7 %collective-permute-start.20 = (bf16[2,288,128]{2,1,0:T(8,128)(2,1)S(1)}, bf16[2,288,128]{2,1,0:T(8,128)(2,1)S(1)}, u32[]{:S(2)}, u32[]{:S(2)}) collective-permute-start(bf16[2,288,128]{2,1,0:T(8,128)(2,1)S(1)} %pad_maximum_fusion.1.refs_0_), channel_id=1, source_target_pairs={{0,1},{2,3},{1,0},{3,2},{4,5},{6,7},{5,4},{7,6},{8,9},{10,11},{9,8... | collective-permute-start | bytes 442376 | tf_op jit(solution)/shard_map/ppermute | solution.py:542
  63.4 5.6 %collective-permute-start.19 = (bf16[2,288,128]{2,1,0:T(8,128)(2,1)S(1)}, bf16[2,288,128]{2,1,0:T(8,128)(2,1)S(1)}, u32[]{:S(2)}, u32[]{:S(2)}) collective-permute-start(bf16[2,288,128]{2,1,0:T(8,128)(2,1)S(1)} %pad_maximum_fusion.1.refs_0_), channel_id=1, source_target_pairs={{1,2},{3,0},{2,1},{0,3},{5,6},{7,4},{6,5},{4,7},{9,10},{11,8},{10,... | collective-permute-start | bytes 442376 | tf_op jit(solution)/shard_map/ppermute | solution.py:543
  73.2 4.3 %collective-permute-start.21 = (bf16[4,2,64,128]{3,2,1,0:T(8,128)(2,1)S(1)}, bf16[4,2,64,128]{3,2,1,0:T(8,128)(2,1)S(1)}, u32[]{:S(2)}, u32[]{:S(2)}) collective-permute-start(bf16[4,2,64,128]{3,2,1,0:T(8,128)(2,1)S(1)} %denoise_far.3), channel_id=1, source_target_pairs={{0,16},{16,0},{1,17},{17,1},{2,18},{18,2},{3,19},{19,3},{4,20},{20... | collective-permute-start | bytes 393224 | tf_op jit(solution)/shard_map/ppermute | solution.py:485
  (13 other events, 179.0 us)

commit v6 on v5

--- a/solution.py
+++ b/solution.py
@@ -67,13 +67,31 @@
     return jnp.dot(left, right, preferred_element_type=F32)
 
 
-def consistency_kernel(*refs, pieces, shares, edge, batch, direct, chosen):
+def far_is_up():
+    return lax.rem(lax.axis_index("readout"), 2) == 1
+
+
+def side_count(side, readouts):
+    return {"all": readouts, "near": readouts - 1, "far": 1}[side]
+
+
+def side_rows(side, readouts):
+    if side == "all":
+        return list(range(readouts))
+    up = far_is_up().astype(jnp.int32)
+    if side == "far":
+        return [up * (readouts - 1)]
+    return [1 - up + k for k in range(readouts - 1)]
+
+
+def consistency_kernel(*refs, pieces, shares, edge, batch, direct, side):
     images, refs = refs[:pieces], refs[pieces:]
     maps, samples, mask, tables = refs[:4]
     outs = refs[4 : 4 + shares]
     window, joined, refs = refs[4 + shares], refs[5 + shares], refs[6 + shares :]
     block, me = lax.axis_index("cascade"), lax.axis_index("coil")
-    coils, phases, _, rows, part = samples.shape[1:]
+    coils, phases, every, rows, part = samples.shape[1:]
+    chosen = side_rows(side, every)
     readouts = len(chosen)
     count = rows // 2
     share = count // shares
@@ -195,9 +213,9 @@
         outs[k][...] = window[:, pl.ds(begin, width + 2 * edge)]
 
 
-def consistency(images, maps, samples, mask, shares, chosen):
+def consistency(images, maps, samples, mask, shares, side):
     blocks, coils, phases, every, rows, part = samples.shape
-    readouts = len(chosen)
+    readouts = side_count(side, every)
     lines = rows // 2
     share_rows = rows // shares
     edge = HALO * phases * 2
@@ -206,7 +224,7 @@
     direct = pieces > 1
     width = phases * share_rows + 2 * edge
     body = functools.partial(
-        consistency_kernel, pieces=pieces, shares=shares, edge=edge, batch=BATCH, direct=direct, chosen=chosen
+        consistency_kernel, pieces=pieces, shares=shares, edge=edge, batch=BATCH, direct=direct, side=side
     )
     image_shape = (phases, readouts, rows, part)
     buffers = [
@@ -335,7 +353,11 @@
     refs = refs[3:]
     before = None if stage == "alone" else refs.pop(0)
     if stage == "far":
-        apart, *outs, taps, sums = refs
+        apart, out, rest, taps, sums = refs
+    elif stage == "last":
+        apart, done, out, joint, taps, sums = refs
+    elif stage == "end":
+        apart, out, taps, sums = refs
     else:
         sums, taps = refs
     readouts, span, part = own.shape
@@ -344,23 +366,24 @@
     group = taps.shape[2]
     used = 9 * cell
     readout_no, coil_no = lax.axis_index("readout"), lax.axis_index("coil")
-    upward = lax.rem(readout_no, 2) == (0 if stage == "near" else 1)
+    upward = jnp.logical_not(far_is_up()) if stage == "near" else far_is_up()
     there = jnp.where(upward, readout_no < lax.axis_size("readout") - 1, readout_no > 0)
     first_line = (coil_no > 0).astype(F32).astype(BF16)
     last_line = (coil_no < lax.axis_size("coil") - 1).astype(F32).astype(BF16)
-    own_at = jnp.where(upward, 0, HALO)
-    beside_at = jnp.where(upward, readouts, 0)
-
-    def fill_taps():
-        slabs = [(own_at + k, own[k].astype(F32)) for k in range(readouts)]
-        for k in range(HALO):
-            value = jnp.zeros((span, part), F32)
-            if beside is not None:
-                low = beside[readouts - HALO + k].astype(F32)
-                value = jnp.where(there, jnp.where(upward, beside[k].astype(F32), low), value)
-            slabs.append((beside_at + k, value))
+
+    def neighbour(k):
+        if beside is None:
+            return jnp.zeros((span, part), F32)
+        low = beside[readouts - 1 - k].astype(F32)
+        return jnp.where(there, jnp.where(upward, beside[k].astype(F32), low), 0.0)
+
+    def inwards(k):
+        return jnp.where(upward, own[readouts - 1 - k].astype(F32), own[k].astype(F32))
+
+    def fill_taps(slabs):
         filler = [jnp.zeros((group - used, part), F32)] if group > used else []
-        for index, slab in slabs:
+        for k, slab in enumerate(slabs):
+            index = jnp.where(upward, k, len(slabs) - 1 - k)
             views = [shifted(slab, 1), slab, shifted(slab, -1)]
             for line in range(1, lines - 1):
                 around = [
@@ -370,8 +393,7 @@
                 ]
                 taps[index, line - 1] = jnp.concatenate(around + filler, 0).astype(BF16)
 
-    def add_row(row, begun, count):
-        start = row - 1 + own_at
+    def add_row(start, begun, count, target):
         block = range(1, lines - 1)
         near = jnp.concatenate(
             [taps[pl.ds(start, 3), line - 1].reshape(3 * group, part) for line in block], 1
@@ -385,7 +407,6 @@
         chosen = pl.ds(pl.multiple_of(begun * group, 16), count * group)
         result = dot(last[section, chosen], mixed)
         for a in range(count):
-            target = row + 1 - begun - a
             for e in range(3):
                 for line in range(lines):
                     terms = []
@@ -396,64 +417,96 @@
                             terms.append(
                                 result[at : at + cell, source * part : (source + 1) * part]
                             )
-                    sums[e, target, line * cell : (line + 1) * cell] += sum(terms[1:], terms[0])
-
-    def add_outer():
-        add_row(jnp.where(upward, readouts, -1), jnp.where(upward, 2, 0), 1)
-
-    def add_inner():
-        add_row(jnp.where(upward, readouts - 1, 0), jnp.where(upward, 1, 0), 2)
+                    sums[e, target - a, line * cell : (line + 1) * cell] += sum(
+                        terms[1:], terms[0]
+                    )
+
+    def add_outer(start, target):
+        add_row(start, jnp.where(upward, 2, 0), 1, target)
+
+    def add_inner(start):
+        add_row(start, jnp.where(upward, 1, 0), 2, jnp.where(upward, readouts - 1, 1))
+
+    def finished(rows):
+        body = slice(HALO * cell, span - HALO * cell)
+        finals = []
+        for r, at in rows:
+            left, here, right = [sums[e, at, body] for e in range(3)]
+            value = own[r, body].astype(F32) + here + shifted(left, 1) + shifted(right, -1)
+            finals.append(value.astype(BF16))
+        ordered = dot(apart[...], jnp.concatenate(finals, 1)).astype(BF16)
+        height = out.shape[2]
+        for p in range(phases):
+            for k in range(len(rows)):
+                out[p, k] = ordered[p * height : (p + 1) * height, k * part : (k + 1) * part]
 
     sums[...] = jnp.zeros_like(sums) if before is None else before[...]
     if stage == "near":
-        fill_taps()
-        pl.when(there)(add_outer)
-        add_inner()
+        fill_taps([inwards(k) for k in reversed(range(readouts))] + [neighbour(0), neighbour(1)])
+        pl.when(there)(lambda: add_outer(jnp.where(upward, readouts - 1, 0), jnp.where(upward, readouts - 1, 0)))
+        add_inner(jnp.where(upward, readouts - 2, 1))
         for row in range(1, readouts - 1):
-            add_row(row, 0, 3)
-        return
-
-    @pl.when(there if stage == "far" else jnp.logical_not(there))
-    def _():
-        fill_taps()
+            add_row(row - 1 + jnp.where(upward, 0, HALO), 0, 3, row + 1)
+    elif stage == "end":
+
+        @pl.when(there)
+        def _():
+            fill_taps([inwards(1), inwards(0), neighbour(0), neighbour(1)])
+            add_outer(jnp.where(upward, 1, 0), jnp.where(upward, readouts - 1, 0))
+            add_inner(jnp.where(upward, 0, 1))
+
+        finished([(row, row) for row in range(readouts)])
+    elif stage == "last":
+
+        @pl.when(there)
+        def _():
+            fill_taps([inwards(0), neighbour(0), neighbour(1)])
+            add_outer(0, 0)
+
+        (row,) = side_rows("far", readouts)
+        finished([(row, 0)])
+        joint[:, row] = out[:, 0]
+        for k, near_row in enumerate(side_rows("near", readouts)):
+            joint[:, near_row] = done[:, k]
+    else:
+
+        @pl.when(there if stage == "far" else jnp.logical_not(there))
+        def _():
+            fill_taps([inwards(1), inwards(0), neighbour(0)])
+            add_inner(0)
+
         if stage == "far":
-            add_outer()
-        add_inner()
-
-    if stage == "alone":
-        return
-    body = slice(HALO * cell, span - HALO * cell)
-    finals = []
-    for r in range(readouts):
-        left, here, right = [sums[e, r, body] for e in range(3)]
-        value = own[r, body].astype(F32) + here + shifted(left, 1) + shifted(right, -1)
-        finals.append(value.astype(BF16))
-    ordered = dot(apart[...], jnp.concatenate(finals, 1)).astype(BF16)
-    height = outs[0].shape[2]
-    for p in range(phases):
-        for r in range(readouts):
-            piece = ordered[p * height : (p + 1) * height, r * part : (r + 1) * part]
-            outs[0][p, r] = piece
-            if len(outs) > 1:
-                outs[1 + r][p, 0] = piece
-
-
-def denoise(stage, own, matrices, section, phases, beside=None, before=None, split=False):
+            finished([(row, row) for row in side_rows("near", readouts)])
+            (row,) = side_rows("far", readouts)
+            rest[:, 0] = sums[:, row]
+
+
+def denoise(stage, own, matrices, section, phases, beside=None, before=None, done=None):
     readouts, span, part = own.shape
     cell = 2 * phases
     lines = span // cell
     share = lines - 2 * HALO
     group = matrices[0].shape[2] // 3
     operands = [own] + [beside] * (stage != "alone") + list(matrices) + [before] * (stage != "alone")
-    sums_shape = (3, readouts, span, part)
-    scratch = [pltpu.VMEM((readouts + HALO, lines - 2, group, part), BF16)]
-    result = [jax.ShapeDtypeStruct(sums_shape, F32)]
-    if stage == "far":
+    sums_shape = (3, 1 if stage == "last" else readouts, span, part)
+    depth = {"near": readouts + HALO, "end": 4}.get(stage, 3)
+    scratch = [pltpu.VMEM((depth, lines - 2, group, part), BF16)]
+
+    def image(count):
+        return jax.ShapeDtypeStruct((phases, count, 2 * share, part), BF16)
+
+    if stage in ("far", "last", "end"):
         operands.append(bf16(phase_inside(phases, share).T))
         scratch.append(pltpu.VMEM(sums_shape, F32))
-        result = [jax.ShapeDtypeStruct((phases, readouts, 2 * share, part), BF16)]
-        if split:
-            result += [jax.ShapeDtypeStruct((phases, 1, 2 * share, part), BF16)] * readouts
+    if stage == "far":
+        result = [image(readouts - 1), jax.ShapeDtypeStruct((3, 1, span, part), F32)]
+    elif stage == "last":
+        operands.append(done)
+        result = [image(1), image(readouts)]
+    elif stage == "end":
+        result = [image(readouts)]
+    else:
+        result = [jax.ShapeDtypeStruct(sums_shape, F32)]
     return pl.pallas_call(
         functools.partial(denoise_kernel, phases=phases, section=section, stage=stage),
         in_specs=[pl.BlockSpec(memory_space=pltpu.VMEM)] * len(operands),
@@ -462,7 +515,8 @@
         out_shape=result,
         compiler_params=pltpu.CompilerParams(vmem_limit_bytes=VMEM_LIMIT),
         cost_estimate=pl.CostEstimate(
-            flops=(1 if stage == "alone" else 6) * readouts * lines * part * 256 * 256,
+            flops={"alone": 1, "near": 6, "far": 3, "last": 3, "end": 6}[stage]
+            * (readouts * lines * part * 256 * 256),
             bytes_accessed=2 * 1024 * 1024,
             transcendentals=0,
         ),
@@ -502,26 +556,26 @@
         return jnp.pad(block, ((0, -block.shape[0] % 64), (0, 0)))
 
     initial, coil_maps, kspace = rows_of(initial), rows_of(coil_maps), rows_of(kspace)
-    readouts = kspace.shape[3]
-    images = [[initial]]
+    images = {"all": [initial]}
     matrices = None
-    sent = []
+    joints = []
+
+    def in_order(near, far, axis):
+        return jnp.where(
+            far_is_up(),
+            jnp.concatenate([near, far], axis),
+            jnp.concatenate([far, near], axis),
+        )
+
     for section in range(sections):
-        if section == 0:
-            choices = [tuple(range(readouts))]
-        else:
-            choices = [(r,) for r in range(readouts)]
-        parts = []
-        for image, chosen in zip(images, choices):
-            partial = consistency(image, coil_maps, kspace, sampled, shares, chosen)
+        parts = {}
+        for side, image in images.items():
+            partial = consistency(image, coil_maps, kspace, sampled, shares, side)
             if matrices is None:
                 partial, (first_w, time_w, last_w) = lax.optimization_barrier(
                     (partial, (first_w, time_w, last_w))
                 )
-            if section > 0 and chosen[-1] == readouts - 1:
-                partial, waiting = lax.optimization_barrier((partial, waiting))
-                sent.append(exchanged([waiting] * sections, "cascade", sections))
-            parts.append(exchanged(partial, "coil", shares))
+            parts[side] = exchanged(partial, "coil", shares)
         if matrices is None:
             pack = jnp.concatenate(
                 [
@@ -534,30 +588,42 @@
             packs = exchanged([pack] * sections, "cascade", sections)
             matrices = weight_matrices(packs, phases)
             parts, matrices = lax.optimization_barrier((parts, matrices))
-        else:
-            parts, sent[-1] = lax.optimization_barrier((parts, sent[-1]))
-        combined = jnp.concatenate(
-            [sum(p.astype(F32) for p in pieces).astype(BF16) for pieces in parts], 0
-        )
+        added = {
+            side: sum(p.astype(F32) for p in pieces).astype(BF16) for side, pieces in parts.items()
+        }
+        combined = added["all"] if section == 0 else in_order(added["near"], added["far"], 0)
         even = lax.ppermute(combined, "readout", swaps(readout_parts, 0))
         odd = lax.ppermute(combined, "readout", swaps(readout_parts, 1))
         (sums,) = denoise("alone", combined, matrices, section, phases)
         (sums,) = denoise("near", combined, matrices, section, phases, even, sums)
-        more = section < sections - 1
-        output, *split = denoise("far", combined, matrices, section, phases, odd, sums, more)
-        images = [exchanged([value] * shares, "coil", shares) for value in split]
-        if more:
-            waiting = output
+        if section < sections - 1:
+            near, rest = denoise("far", combined, matrices, section, phases, odd, sums)
+            far, joint = denoise("last", combined, matrices, section, phases, odd, rest, near)
+            images = {
+                side: exchanged([value] * shares, "coil", shares)
+                for side, value in (("near", near), ("far", far))
+            }
+
         else:
-            sent.append(exchanged([output] * sections, "cascade", sections))
-
+            (joint,) = denoise("end", combined, matrices, section, phases, odd, sums)
+        joints.append(joint)
+
+    def of_section(values, wanted):
+        value = values[0]
+        for section in range(1, sections):
+            value = jnp.where(wanted == section, values[section], value)
+        return value
+
+    pieces = exchanged(
+        [of_section(joints, (section_no + k) % sections) for k in range(sections)],
+        "cascade",
+        sections,
+    )
     arrived = []
     for block in range(sections):
-        value = None
-        for section in range(sections):
-            k = (section - block) % sections
-            piece = sent[section][k]
-            value = piece if value is None else jnp.where(section_no == section, piece, value)
+        value = pieces[0]
+        for k in range(1, sections):
+            value = jnp.where((section_no - block) % sections == k, pieces[k], value)
         arrived.append(value)
     result = jnp.stack(arrived)[None]
     return result.reshape(result.shape[:-2] + (result.shape[-2] // 2, 2, part))

time: 78.8 us -> 75.3 us (0.956)
  waiting for transfers between devices: 18.2 us -> 15.8 us
  starting transfers between devices: 30 us -> 28.4 us
    ppermute x18 -> x17, waiting for transfers between devices: 17.6 us -> 15.2 us  [exchanged(): arrived[k] = lax.ppermute(values[k], axis, rotation(count, k))]
    ppermute x2, starting transfers between devices: 3.62 us -> 1.82 us  [per_device(): even = lax.ppermute(combined, 'readout', swaps(readout_parts, 0))]
    pallas_call x6 -> x7, Pallas kernels: 16.5 us -> 17 us  [denoise(): pl.pallas_call(functools.partial(denoise_kernel, phases=phases, section=s...]
    ppermute x18 -> x17, starting transfers between devices: 23.8 us -> 23.4 us  [exchanged(): arrived[k] = lax.ppermute(values[k], axis, rotation(count, k))]
  transfers between devices with their start and end apart: 22 -> 21, of which waited for: 9 -> 7; matrix products, arithmetic and copies ran while one was open for 0% -> 0% of each run, Pallas kernels for 18% -> 22%
where the time goes in v6:
time: 75.3 us; the launch traced here: 75.2 us
  Pallas kernels  29.2 us (39%)
  starting transfers between devices  28.4 us (38%)
  waiting for transfers between devices  15.8 us (21%)
  other arithmetic  1.33 us (2%)
    ppermute x17, starting transfers between devices, exchanged(): arrived[k] = lax.ppermute(values[k], axis, rotation(count, k))  23.4 us
    pallas_call x7, Pallas kernels, denoise(): pl.pallas_call(functools.partial(denoise_kernel, phases=phases, section=s...  17 us
    ppermute x17, waiting for transfers between devices, exchanged(): arrived[k] = lax.ppermute(values[k], axis, rotation(count, k))  15.2 us
    pallas_call x3, Pallas kernels, consistency(): pl.pallas_call(body, in_specs=[pl.BlockSpec(memory_space=pltpu.VMEM if di...  11 us
    ppermute x2, starting transfers between devices, per_device(): odd = lax.ppermute(combined, 'readout', swaps(readout_parts, 1))  3.15 us
    ppermute x2, starting transfers between devices, per_device(): even = lax.ppermute(combined, 'readout', swaps(readout_parts, 0))  1.82 us
  transfers between devices with their start and end apart: 21, of which 7 were waited for; matrix products, arithmetic and copies ran while one was open for 0% of the time, Pallas kernels for 22%

profile of v6, /device:TPU:1, one launch (start us, length us, event | category | flops | bytes accessed | tf_op | source)
XLA Modules:
  0.0 75.2 jit_solution(17032043350929318707)
XLA Ops:
  0.1 6.0 %consistency.3 = (bf16[2,288,128]{2,1,0:T(8,128)(2,1)S(1)}, bf16[2,288,128]{2,1,0:T(8,128)(2,1)S(1)}, bf16[2,288,128]{2,1,0:T(8,128)(2,1)S(1)}, bf16[2,288,128]{2,1,0:T(8,128)(2,1)S(1)}) custom-call(bf16[2,4,2,256,128]{4,3,2,1,0:T(8,128)(2,1)} %bitcast.19, bf16[2,4,2,256,128]{4,3,2,1,0:T(8,128)(2,1)} %bitcast.12, bf16[2,4,4,2,256,128]{5,4,3,2,1,0:T(8,128)(2,1)} %bitcast.9, ...), custom_call_target="tpu_custom_call" | custom-call | flops 5368709120 | bytes 4194304 | tf_op jit(solution)/shard_map/consistency/pallas_call | solution.py:238
  6.1 2.2 %collective-permute-start = (bf16[2,288,128]{2,1,0:T(8,128)(2,1)S(1)}, bf16[2,288,128]{2,1,0:T(8,128)(2,1)S(1)}, u32[]{:S(2)}, u32[]{:S(2)}) collective-permute-start(bf16[2,288,128]{2,1,0:T(8,128)(2,1)S(1)} %get-tuple-element.43), channel_id=1, source_target_pairs={{0,4},{4,8},{8,12},{12,0},{1,5},{5,9},{9,13},{13,1},{2,6},{6,10},{... | collective-permute-start | bytes 442376 | tf_op jit(solution)/shard_map/ppermute | solution.py:539
  8.3 2.3 %collective-permute-start.1 = (bf16[2,288,128]{2,1,0:T(8,128)(2,1)S(1)}, bf16[2,288,128]{2,1,0:T(8,128)(2,1)S(1)}, u32[]{:S(2)}, u32[]{:S(2)}) collective-permute-start(bf16[2,288,128]{2,1,0:T(8,128)(2,1)S(1)} %get-tuple-element.44), channel_id=1, source_target_pairs={{0,8},{4,12},{8,0},{12,4},{1,9},{5,13},{9,1},{13,5},{2,10},{6,14},... | collective-permute-start | bytes 442376 | tf_op jit(solution)/shard_map/ppermute | solution.py:539
  11.8 1.3 %collective-permute-start.3 = (bf16[320,64]{1,0:T(8,128)(2,1)S(1)}, bf16[320,64]{1,0:T(8,128)(2,1)S(1)}, u32[]{:S(2)}, u32[]{:S(2)}) collective-permute-start(bf16[320,64]{1,0:T(8,128)(2,1)S(1)} %fusion.4.refs_0_), channel_id=1, source_target_pairs={{0,16},{16,0},{1,17},{17,1},{2,18},{18,2},{3,19},{19,3},{4,20},{20... | collective-permute-start | bytes 122888 | tf_op jit(solution)/shard_map/ppermute | solution.py:539
  13.1 2.3 %collective-permute-done.3.refs_1_ = bf16[320,64]{1,0:T(8,128)(2,1)S(1)} collective-permute-done((bf16[320,64]{1,0:T(8,128)(2,1)S(1)}, bf16[320,64]{1,0:T(8,128)(2,1)S(1)}, u32[]{:S(2)}, u32[]{:S(2)}) %collective-permute-start.3) | collective-permute-done | bytes 40992 | tf_op jit(solution)/shard_map/ppermute | solution.py:539
  15.5 1.2 %weights.1 = (bf16[2,256,240]{2,1,0:T(8,128)(2,1)S(1)}, bf16[2,256,256]{2,1,0:T(8,128)(2,1)S(1)}, bf16[2,240,256]{2,1,0:T(8,128)(2,1)S(1)}) custom-call(bf16[320,64]{1,0:T(8,128)(2,1)S(1)} %fusion.4.refs_0_, bf16[320,64]{1,0:T(8,128)(2,1)S(1)} %collective-permute-done.3.refs_1_, bf16[240,64]{1,0:T(8,128)(2,1)S(1)} %copy-done.4, ...), custom_call_target="tpu_custom_call" | custom-call | flops 131072000 | bytes 2097152 | tf_op jit(solution)/shard_map/weights/pallas_call | solution.py:327
  16.7 4.2 %collective-permute-done.1 = bf16[2,288,128]{2,1,0:T(8,128)(2,1)S(1)} collective-permute-done((bf16[2,288,128]{2,1,0:T(8,128)(2,1)S(1)}, bf16[2,288,128]{2,1,0:T(8,128)(2,1)S(1)}, u32[]{:S(2)}, u32[]{:S(2)}) %collective-permute-start.1) | collective-permute-done | bytes 147488 | tf_op jit(solution)/shard_map/ppermute | solution.py:539
  23.0 3.8 %denoise_near.2.refs_5_ = f32[3,2,288,128]{3,2,1,0:T(8,128)S(1)} custom-call(bf16[2,288,128]{2,1,0:T(8,128)(2,1)S(1)} %add_convert_fusion.refs_0_, bf16[2,288,128]{2,1,0:T(8,128)(2,1)S(1)} %collective-permute-done.5.refs_1_, bf16[2,256,240]{2,1,0:T(8,128)(2,1)S(1)} %get-tuple-element.56.refs_1_.refs_2_, ...), custom_call_target="tpu_custom_call" | custom-call | flops 3623878656 | bytes 2097152 | tf_op jit(solution)/shard_map/denoise_near/pallas_call | solution.py:510
  27.3 2.6 %denoise_far.1 = (bf16[4,1,64,128]{3,2,1,0:T(8,128)(2,1)S(1)}, f32[3,1,288,128]{3,2,1,0:T(8,128)S(1)}) custom-call(bf16[2,288,128]{2,1,0:T(8,128)(2,1)S(1)} %add_convert_fusion.refs_0_, bf16[2,288,128]{2,1,0:T(8,128)(2,1)S(1)} %collective-permute-done.4.refs_1_, bf16[2,256,240]{2,1,0:T(8,128)(2,1)S(1)} %get-tuple-element.56.refs_1_.refs_2_, ...), custom_call_target="tpu_custom_call" | custom-call | flops 1811939328 | bytes 2097152 | tf_op jit(solution)/shard_map/denoise_far/pallas_call | solution.py:510
  29.9 3.4 %collective-permute-start.6 = (bf16[4,1,64,128]{3,2,1,0:T(8,128)(2,1)S(1)}, bf16[4,1,64,128]{3,2,1,0:T(8,128)(2,1)S(1)}, u32[]{:S(2)}, u32[]{:S(2)}) collective-permute-start(bf16[4,1,64,128]{3,2,1,0:T(8,128)(2,1)S(1)} %get-tuple-element.59.refs_0_.refs_7_), channel_id=1, source_target_pairs={{0,4},{4,8},{8,12},{12,0},{1,5},{5,9},{9,13},{13,1},{2,6},{6,10},{... | collective-permute-start | bytes 196616 | tf_op jit(solution)/shard_map/ppermute | solution.py:539
  33.3 1.3 %collective-permute-start.7 = (bf16[4,1,64,128]{3,2,1,0:T(8,128)(2,1)S(1)}, bf16[4,1,64,128]{3,2,1,0:T(8,128)(2,1)S(1)}, u32[]{:S(2)}, u32[]{:S(2)}) collective-permute-start(bf16[4,1,64,128]{3,2,1,0:T(8,128)(2,1)S(1)} %get-tuple-element.59.refs_0_.refs_7_), channel_id=1, source_target_pairs={{0,8},{4,12},{8,0},{12,4},{1,9},{5,13},{9,1},{13,5},{2,10},{6,14},... | collective-permute-start | bytes 196616 | tf_op jit(solution)/shard_map/ppermute | solution.py:539
  35.4 2.3 %denoise_last.1 = (bf16[4,1,64,128]{3,2,1,0:T(8,128)(2,1)S(1)}, bf16[4,2,64,128]{3,2,1,0:T(8,128)(2,1)S(1)}) custom-call(bf16[2,288,128]{2,1,0:T(8,128)(2,1)S(1)} %add_convert_fusion.refs_0_, bf16[2,288,128]{2,1,0:T(8,128)(2,1)S(1)} %collective-permute-done.4.refs_1_, bf16[2,256,240]{2,1,0:T(8,128)(2,1)S(1)} %get-tuple-element.56.refs_1_.refs_2_, ...), custom_call_target="tpu_custom_call" | custom-call | flops 1811939328 | bytes 2097152 | tf_op jit(solution)/shard_map/denoise_last/pallas_call | solution.py:510
  39.5 1.6 %collective-permute-start.14 = (bf16[4,1,64,128]{3,2,1,0:T(8,128)(2,1)S(1)}, bf16[4,1,64,128]{3,2,1,0:T(8,128)(2,1)S(1)}, u32[]{:S(2)}, u32[]{:S(2)}) collective-permute-start(bf16[4,1,64,128]{3,2,1,0:T(8,128)(2,1)S(1)} %get-tuple-element.65.refs_0_), channel_id=1, source_target_pairs={{0,12},{4,0},{8,4},{12,8},{1,13},{5,1},{9,5},{13,9},{2,14},{6,2},{... | collective-permute-start | bytes 196616 | tf_op jit(solution)/shard_map/ppermute | solution.py:539
  41.1 2.5 %consistency.4 = (bf16[1,288,128]{2,1,0:T(8,128)(2,1)S(1)}, bf16[1,288,128]{2,1,0:T(8,128)(2,1)S(1)}, bf16[1,288,128]{2,1,0:T(8,128)(2,1)S(1)}, bf16[1,288,128]{2,1,0:T(8,128)(2,1)S(1)}) custom-call(bf16[4,1,64,128]{3,2,1,0:T(8,128)(2,1)S(1)} %get-tuple-element.59.refs_0_.refs_7_, bf16[4,1,64,128]{3,2,1,0:T(8,128)(2,1)S(1)} %collective-permute-done.6.refs_1_, ...), custom_call_target="tpu_custom_call" | custom-call | flops 2684354560 | bytes 4194304 | tf_op jit(solution)/shard_map/consistency/pallas_call | solution.py:238
  43.6 1.5 %collective-permute-start.10 = (bf16[1,288,128]{2,1,0:T(8,128)(2,1)S(1)}, bf16[1,288,128]{2,1,0:T(8,128)(2,1)S(1)}, u32[]{:S(2)}, u32[]{:S(2)}) collective-permute-start(bf16[1,288,128]{2,1,0:T(8,128)(2,1)S(1)} %get-tuple-element.62), channel_id=1, source_target_pairs={{0,8},{4,12},{8,0},{12,4},{1,9},{5,13},{9,1},{13,5},{2,10},{6,14},... | collective-permute-start | bytes 221192 | tf_op jit(solution)/shard_map/ppermute | solution.py:539
  46.6 2.5 %consistency.5 = (bf16[1,288,128]{2,1,0:T(8,128)(2,1)S(1)}, bf16[1,288,128]{2,1,0:T(8,128)(2,1)S(1)}, bf16[1,288,128]{2,1,0:T(8,128)(2,1)S(1)}, bf16[1,288,128]{2,1,0:T(8,128)(2,1)S(1)}) custom-call(bf16[4,1,64,128]{3,2,1,0:T(8,128)(2,1)S(1)} %get-tuple-element.65.refs_0_, bf16[4,1,64,128]{3,2,1,0:T(8,128)(2,1)S(1)} %collective-permute-done.12.refs_1_, ...), custom_call_target="tpu_custom_call" | custom-call | flops 2684354560 | bytes 4194304 | tf_op jit(solution)/shard_map/consistency/pallas_call | solution.py:238
  49.8 2.6 %collective-permute-start.16 = (bf16[1,288,128]{2,1,0:T(8,128)(2,1)S(1)}, bf16[1,288,128]{2,1,0:T(8,128)(2,1)S(1)}, u32[]{:S(2)}, u32[]{:S(2)}) collective-permute-start(bf16[1,288,128]{2,1,0:T(8,128)(2,1)S(1)} %get-tuple-element.68), channel_id=1, source_target_pairs={{0,8},{4,12},{8,0},{12,4},{1,9},{5,13},{9,1},{13,5},{2,10},{6,14},... | collective-permute-start | bytes 221192 | tf_op jit(solution)/shard_map/ppermute | solution.py:539
  52.5 1.8 %collective-permute-done.15 = bf16[1,288,128]{2,1,0:T(8,128)(2,1)S(1)} collective-permute-done((bf16[1,288,128]{2,1,0:T(8,128)(2,1)S(1)}, bf16[1,288,128]{2,1,0:T(8,128)(2,1)S(1)}, u32[]{:S(2)}, u32[]{:S(2)}) %collective-permute-start.15) | collective-permute-done | bytes 73760 | tf_op jit(solution)/shard_map/ppermute | solution.py:539
  54.3 3.8 %collective-permute-done.16 = bf16[1,288,128]{2,1,0:T(8,128)(2,1)S(1)} collective-permute-done((bf16[1,288,128]{2,1,0:T(8,128)(2,1)S(1)}, bf16[1,288,128]{2,1,0:T(8,128)(2,1)S(1)}, u32[]{:S(2)}, u32[]{:S(2)}) %collective-permute-start.16) | collective-permute-done | bytes 73760 | tf_op jit(solution)/shard_map/ppermute | solution.py:539
  59.4 2.0 %collective-permute-start.18 = (bf16[2,288,128]{2,1,0:T(8,128)(2,1)S(1)}, bf16[2,288,128]{2,1,0:T(8,128)(2,1)S(1)}, u32[]{:S(2)}, u32[]{:S(2)}) collective-permute-start(bf16[2,288,128]{2,1,0:T(8,128)(2,1)S(1)} %maximum_select_fusion.refs_0_), channel_id=1, source_target_pairs={{1,2},{3,0},{2,1},{0,3},{5,6},{7,4},{6,5},{4,7},{9,10},{11,8},{10,... | collective-permute-start | bytes 442376 | tf_op jit(solution)/shard_map/ppermute | solution.py:596
  61.7 3.8 %denoise_near.3.refs_5_ = f32[3,2,288,128]{3,2,1,0:T(8,128)S(1)} custom-call(bf16[2,288,128]{2,1,0:T(8,128)(2,1)S(1)} %maximum_select_fusion.refs_0_, bf16[2,288,128]{2,1,0:T(8,128)(2,1)S(1)} %collective-permute-done.19.refs_1_, bf16[2,256,240]{2,1,0:T(8,128)(2,1)S(1)} %get-tuple-element.56.refs_1_.refs_2_, ...), custom_call_target="tpu_custom_call" | custom-call | flops 3623878656 | bytes 2097152 | tf_op jit(solution)/shard_map/denoise_near/pallas_call | solution.py:510
  65.5 4.2 %denoise_end.1 = bf16[4,2,64,128]{3,2,1,0:T(8,128)(2,1)S(1)} custom-call(bf16[2,288,128]{2,1,0:T(8,128)(2,1)S(1)} %maximum_select_fusion.refs_0_, bf16[2,288,128]{2,1,0:T(8,128)(2,1)S(1)} %collective-permute-done.18.refs_1_, bf16[2,256,240]{2,1,0:T(8,128)(2,1)S(1)} %get-tuple-element.56.refs_1_.refs_2_, ...), custom_call_target="tpu_custom_call" | custom-call | flops 3623878656 | bytes 2097152 | tf_op jit(solution)/shard_map/denoise_end/pallas_call | solution.py:510
  69.8 1.3 %collective-permute-start.20 = (bf16[4,2,64,128]{3,2,1,0:T(8,128)(2,1)S(1)}, bf16[4,2,64,128]{3,2,1,0:T(8,128)(2,1)S(1)}, u32[]{:S(2)}, u32[]{:S(2)}) collective-permute-start(bf16[4,2,64,128]{3,2,1,0:T(8,128)(2,1)S(1)} %broadcast_select_fusion.1), channel_id=1, source_target_pairs={{0,16},{16,0},{1,17},{17,1},{2,18},{18,2},{3,19},{19,3},{4,20},{20... | collective-permute-start | bytes 393224 | tf_op jit(solution)/shard_map/ppermute | solution.py:539
  71.1 3.0 %collective-permute-done.20 = bf16[4,2,64,128]{3,2,1,0:T(8,128)(2,1)S(1)} collective-permute-done((bf16[4,2,64,128]{3,2,1,0:T(8,128)(2,1)S(1)}, bf16[4,2,64,128]{3,2,1,0:T(8,128)(2,1)S(1)}, u32[]{:S(2)}, u32[]{:S(2)}) %collective-permute-start.20) | collective-permute-done | bytes 131104 | tf_op jit(solution)/shard_map/ppermute | solution.py:539
  (69 shorter events, 11.2 us)
Async XLA Ops:
  0.0 15.4 %copy-start = (bf16[3,256,256]{2,1,0:T(8,128)(2,1)S(1)}, bf16[3,256,256]{2,1,0:T(8,128)(2,1)}, u32[]{:S(2)}) copy-start(bf16[3,256,256]{2,1,0:T(8,128)(2,1)} %constant.66.clone.refs_8_) | copy-start | bytes 1179652
  0.0 15.4 %copy-start.1 = (bf16[256,240]{1,0:T(8,128)(2,1)S(1)}, bf16[256,240]{1,0:T(8,128)(2,1)}, u32[]{:S(2)}) copy-start(bf16[256,240]{1,0:T(8,128)(2,1)} %constant.63.clone.refs_5_) | copy-start | bytes 368644
  0.0 15.4 %copy-start.2 = (bf16[240,256]{1,0:T(8,128)(2,1)S(1)}, bf16[240,256]{1,0:T(8,128)(2,1)}, u32[]{:S(2)}) copy-start(bf16[240,256]{1,0:T(8,128)(2,1)} %constant.62.clone.refs_4_) | copy-start | bytes 368644
  6.1 10.6 %collective-permute-start = (bf16[2,288,128]{2,1,0:T(8,128)(2,1)S(1)}, bf16[2,288,128]{2,1,0:T(8,128)(2,1)S(1)}, u32[]{:S(2)}, u32[]{:S(2)}) collective-permute-start(bf16[2,288,128]{2,1,0:T(8,128)(2,1)S(1)} %get-tuple-element.43), channel_id=1, source_target_pairs={{0,4},{4,8},{8,12},{12,0},{1,5},{5,9},{9,13},{13,1},{2,6},{6,10},{... | collective-permute-start | bytes 442376 | tf_op jit(solution)/shard_map/ppermute | solution.py:539
  8.3 12.7 %collective-permute-start.1 = (bf16[2,288,128]{2,1,0:T(8,128)(2,1)S(1)}, bf16[2,288,128]{2,1,0:T(8,128)(2,1)S(1)}, u32[]{:S(2)}, u32[]{:S(2)}) collective-permute-start(bf16[2,288,128]{2,1,0:T(8,128)(2,1)S(1)} %get-tuple-element.44), channel_id=1, source_target_pairs={{0,8},{4,12},{8,0},{12,4},{1,9},{5,13},{9,1},{13,5},{2,10},{6,14},... | collective-permute-start | bytes 442376 | tf_op jit(solution)/shard_map/ppermute | solution.py:539
  10.6 10.3 %collective-permute-start.2 = (bf16[2,288,128]{2,1,0:T(8,128)(2,1)S(1)}, bf16[2,288,128]{2,1,0:T(8,128)(2,1)S(1)}, u32[]{:S(2)}, u32[]{:S(2)}) collective-permute-start(bf16[2,288,128]{2,1,0:T(8,128)(2,1)S(1)} %get-tuple-element.45), channel_id=1, source_target_pairs={{0,12},{4,0},{8,4},{12,8},{1,13},{5,1},{9,5},{13,9},{2,14},{6,2},{... | collective-permute-start | bytes 442376 | tf_op jit(solution)/shard_map/ppermute | solution.py:539
  11.8 3.7 %collective-permute-start.3 = (bf16[320,64]{1,0:T(8,128)(2,1)S(1)}, bf16[320,64]{1,0:T(8,128)(2,1)S(1)}, u32[]{:S(2)}, u32[]{:S(2)}) collective-permute-start(bf16[320,64]{1,0:T(8,128)(2,1)S(1)} %fusion.4.refs_0_), channel_id=1, source_target_pairs={{0,16},{16,0},{1,17},{17,1},{2,18},{18,2},{3,19},{19,3},{4,20},{20... | collective-permute-start | bytes 122888 | tf_op jit(solution)/shard_map/ppermute | solution.py:539
  21.1 1.9 %collective-permute-start.5 = (bf16[2,288,128]{2,1,0:T(8,128)(2,1)S(1)}, bf16[2,288,128]{2,1,0:T(8,128)(2,1)S(1)}, u32[]{:S(2)}, u32[]{:S(2)}) collective-permute-start(bf16[2,288,128]{2,1,0:T(8,128)(2,1)S(1)} %add_convert_fusion.refs_0_), channel_id=1, source_target_pairs={{0,1},{2,3},{1,0},{3,2},{4,5},{6,7},{5,4},{7,6},{8,9},{10,11},{9,8... | collective-permute-start | bytes 442376 | tf_op jit(solution)/shard_map/ppermute | solution.py:595
  21.7 5.5 %collective-permute-start.4 = (bf16[2,288,128]{2,1,0:T(8,128)(2,1)S(1)}, bf16[2,288,128]{2,1,0:T(8,128)(2,1)S(1)}, u32[]{:S(2)}, u32[]{:S(2)}) collective-permute-start(bf16[2,288,128]{2,1,0:T(8,128)(2,1)S(1)} %add_convert_fusion.refs_0_), channel_id=1, source_target_pairs={{1,2},{3,0},{2,1},{0,3},{5,6},{7,4},{6,5},{4,7},{9,10},{11,8},{10,... | collective-permute-start | bytes 442376 | tf_op jit(solution)/shard_map/ppermute | solution.py:596
  29.9 9.6 %collective-permute-start.6 = (bf16[4,1,64,128]{3,2,1,0:T(8,128)(2,1)S(1)}, bf16[4,1,64,128]{3,2,1,0:T(8,128)(2,1)S(1)}, u32[]{:S(2)}, u32[]{:S(2)}) collective-permute-start(bf16[4,1,64,128]{3,2,1,0:T(8,128)(2,1)S(1)} %get-tuple-element.59.refs_0_.refs_7_), channel_id=1, source_target_pairs={{0,4},{4,8},{8,12},{12,0},{1,5},{5,9},{9,13},{13,1},{2,6},{6,10},{... | collective-permute-start | bytes 196616 | tf_op jit(solution)/shard_map/ppermute | solution.py:539
  33.3 7.8 %collective-permute-start.7 = (bf16[4,1,64,128]{3,2,1,0:T(8,128)(2,1)S(1)}, bf16[4,1,64,128]{3,2,1,0:T(8,128)(2,1)S(1)}, u32[]{:S(2)}, u32[]{:S(2)}) collective-permute-start(bf16[4,1,64,128]{3,2,1,0:T(8,128)(2,1)S(1)} %get-tuple-element.59.refs_0_.refs_7_), channel_id=1, source_target_pairs={{0,8},{4,12},{8,0},{12,4},{1,9},{5,13},{9,1},{13,5},{2,10},{6,14},... | collective-permute-start | bytes 196616 | tf_op jit(solution)/shard_map/ppermute | solution.py:539
  34.6 6.4 %collective-permute-start.8 = (bf16[4,1,64,128]{3,2,1,0:T(8,128)(2,1)S(1)}, bf16[4,1,64,128]{3,2,1,0:T(8,128)(2,1)S(1)}, u32[]{:S(2)}, u32[]{:S(2)}) collective-permute-start(bf16[4,1,64,128]{3,2,1,0:T(8,128)(2,1)S(1)} %get-tuple-element.59.refs_0_.refs_7_), channel_id=1, source_target_pairs={{0,12},{4,0},{8,4},{12,8},{1,13},{5,1},{9,5},{13,9},{2,14},{6,2},{... | collective-permute-start | bytes 196616 | tf_op jit(solution)/shard_map/ppermute | solution.py:539
  37.7 8.4 %collective-permute-start.12 = (bf16[4,1,64,128]{3,2,1,0:T(8,128)(2,1)S(1)}, bf16[4,1,64,128]{3,2,1,0:T(8,128)(2,1)S(1)}, u32[]{:S(2)}, u32[]{:S(2)}) collective-permute-start(bf16[4,1,64,128]{3,2,1,0:T(8,128)(2,1)S(1)} %get-tuple-element.65.refs_0_), channel_id=1, source_target_pairs={{0,4},{4,8},{8,12},{12,0},{1,5},{5,9},{9,13},{13,1},{2,6},{6,10},{... | collective-permute-start | bytes 196616 | tf_op jit(solution)/shard_map/ppermute | solution.py:539
  38.4 8.2 %collective-permute-start.13 = (bf16[4,1,64,128]{3,2,1,0:T(8,128)(2,1)S(1)}, bf16[4,1,64,128]{3,2,1,0:T(8,128)(2,1)S(1)}, u32[]{:S(2)}, u32[]{:S(2)}) collective-permute-start(bf16[4,1,64,128]{3,2,1,0:T(8,128)(2,1)S(1)} %get-tuple-element.65.refs_0_), channel_id=1, source_target_pairs={{0,8},{4,12},{8,0},{12,4},{1,9},{5,13},{9,1},{13,5},{2,10},{6,14},... | collective-permute-start | bytes 196616 | tf_op jit(solution)/shard_map/ppermute | solution.py:539
  39.5 7.2 %collective-permute-start.14 = (bf16[4,1,64,128]{3,2,1,0:T(8,128)(2,1)S(1)}, bf16[4,1,64,128]{3,2,1,0:T(8,128)(2,1)S(1)}, u32[]{:S(2)}, u32[]{:S(2)}) collective-permute-start(bf16[4,1,64,128]{3,2,1,0:T(8,128)(2,1)S(1)} %get-tuple-element.65.refs_0_), channel_id=1, source_target_pairs={{0,12},{4,0},{8,4},{12,8},{1,13},{5,1},{9,5},{13,9},{2,14},{6,2},{... | collective-permute-start | bytes 196616 | tf_op jit(solution)/shard_map/ppermute | solution.py:539
  43.6 8.7 %collective-permute-start.10 = (bf16[1,288,128]{2,1,0:T(8,128)(2,1)S(1)}, bf16[1,288,128]{2,1,0:T(8,128)(2,1)S(1)}, u32[]{:S(2)}, u32[]{:S(2)}) collective-permute-start(bf16[1,288,128]{2,1,0:T(8,128)(2,1)S(1)} %get-tuple-element.62), channel_id=1, source_target_pairs={{0,8},{4,12},{8,0},{12,4},{1,9},{5,13},{9,1},{13,5},{2,10},{6,14},... | collective-permute-start | bytes 221192 | tf_op jit(solution)/shard_map/ppermute | solution.py:539
  45.2 7.3 %collective-permute-start.11 = (bf16[1,288,128]{2,1,0:T(8,128)(2,1)S(1)}, bf16[1,288,128]{2,1,0:T(8,128)(2,1)S(1)}, u32[]{:S(2)}, u32[]{:S(2)}) collective-permute-start(bf16[1,288,128]{2,1,0:T(8,128)(2,1)S(1)} %get-tuple-element.63), channel_id=1, source_target_pairs={{0,12},{4,0},{8,4},{12,8},{1,13},{5,1},{9,5},{13,9},{2,14},{6,2},{... | collective-permute-start | bytes 221192 | tf_op jit(solution)/shard_map/ppermute | solution.py:539
  46.2 6.3 %collective-permute-start.9 = (bf16[1,288,128]{2,1,0:T(8,128)(2,1)S(1)}, bf16[1,288,128]{2,1,0:T(8,128)(2,1)S(1)}, u32[]{:S(2)}, u32[]{:S(2)}) collective-permute-start(bf16[1,288,128]{2,1,0:T(8,128)(2,1)S(1)} %get-tuple-element.61), channel_id=1, source_target_pairs={{0,4},{4,8},{8,12},{12,0},{1,5},{5,9},{9,13},{13,1},{2,6},{6,10},{... | collective-permute-start | bytes 221192 | tf_op jit(solution)/shard_map/ppermute | solution.py:539
  49.2 5.2 %collective-permute-start.15 = (bf16[1,288,128]{2,1,0:T(8,128)(2,1)S(1)}, bf16[1,288,128]{2,1,0:T(8,128)(2,1)S(1)}, u32[]{:S(2)}, u32[]{:S(2)}) collective-permute-start(bf16[1,288,128]{2,1,0:T(8,128)(2,1)S(1)} %get-tuple-element.67), channel_id=1, source_target_pairs={{0,4},{4,8},{8,12},{12,0},{1,5},{5,9},{9,13},{13,1},{2,6},{6,10},{... | collective-permute-start | bytes 221192 | tf_op jit(solution)/shard_map/ppermute | solution.py:539
  49.8 8.4 %collective-permute-start.16 = (bf16[1,288,128]{2,1,0:T(8,128)(2,1)S(1)}, bf16[1,288,128]{2,1,0:T(8,128)(2,1)S(1)}, u32[]{:S(2)}, u32[]{:S(2)}) collective-permute-start(bf16[1,288,128]{2,1,0:T(8,128)(2,1)S(1)} %get-tuple-element.68), channel_id=1, source_target_pairs={{0,8},{4,12},{8,0},{12,4},{1,9},{5,13},{9,1},{13,5},{2,10},{6,14},... | collective-permute-start | bytes 221192 | tf_op jit(solution)/shard_map/ppermute | solution.py:539
  52.3 5.8 %collective-permute-start.17 = (bf16[1,288,128]{2,1,0:T(8,128)(2,1)S(1)}, bf16[1,288,128]{2,1,0:T(8,128)(2,1)S(1)}, u32[]{:S(2)}, u32[]{:S(2)}) collective-permute-start(bf16[1,288,128]{2,1,0:T(8,128)(2,1)S(1)} %get-tuple-element.69), channel_id=1, source_target_pairs={{0,12},{4,0},{8,4},{12,8},{1,13},{5,1},{9,5},{13,9},{2,14},{6,2},{... | collective-permute-start | bytes 221192 | tf_op jit(solution)/shard_map/ppermute | solution.py:539
  58.2 3.4 %collective-permute-start.19 = (bf16[2,288,128]{2,1,0:T(8,128)(2,1)S(1)}, bf16[2,288,128]{2,1,0:T(8,128)(2,1)S(1)}, u32[]{:S(2)}, u32[]{:S(2)}) collective-permute-start(bf16[2,288,128]{2,1,0:T(8,128)(2,1)S(1)} %maximum_select_fusion.refs_0_), channel_id=1, source_target_pairs={{0,1},{2,3},{1,0},{3,2},{4,5},{6,7},{5,4},{7,6},{8,9},{10,11},{9,8... | collective-permute-start | bytes 442376 | tf_op jit(solution)/shard_map/ppermute | solution.py:595
  59.4 6.1 %collective-permute-start.18 = (bf16[2,288,128]{2,1,0:T(8,128)(2,1)S(1)}, bf16[2,288,128]{2,1,0:T(8,128)(2,1)S(1)}, u32[]{:S(2)}, u32[]{:S(2)}) collective-permute-start(bf16[2,288,128]{2,1,0:T(8,128)(2,1)S(1)} %maximum_select_fusion.refs_0_), channel_id=1, source_target_pairs={{1,2},{3,0},{2,1},{0,3},{5,6},{7,4},{6,5},{4,7},{9,10},{11,8},{10,... | collective-permute-start | bytes 442376 | tf_op jit(solution)/shard_map/ppermute | solution.py:596
  69.8 4.3 %collective-permute-start.20 = (bf16[4,2,64,128]{3,2,1,0:T(8,128)(2,1)S(1)}, bf16[4,2,64,128]{3,2,1,0:T(8,128)(2,1)S(1)}, u32[]{:S(2)}, u32[]{:S(2)}) collective-permute-start(bf16[4,2,64,128]{3,2,1,0:T(8,128)(2,1)S(1)} %broadcast_select_fusion.1), channel_id=1, source_target_pairs={{0,16},{16,0},{1,17},{17,1},{2,18},{18,2},{3,19},{19,3},{4,20},{20... | collective-permute-start | bytes 393224 | tf_op jit(solution)/shard_map/ppermute | solution.py:539
  (12 other events, 148.5 us)

commit v7 on v6

--- a/solution.py
+++ b/solution.py
@@ -619,13 +619,11 @@
         "cascade",
         sections,
     )
-    arrived = []
-    for block in range(sections):
-        value = pieces[0]
-        for k in range(1, sections):
-            value = jnp.where((section_no - block) % sections == k, pieces[k], value)
-        arrived.append(value)
-    result = jnp.stack(arrived)[None]
+    result = jnp.zeros((sections,) + joints[0].shape, BF16)
+    for k in range(sections):
+        place = lax.rem(section_no - k + sections, sections)
+        result = lax.dynamic_update_slice_in_dim(result, pieces[k][None], place, 0)
+    result = result[None]
     return result.reshape(result.shape[:-2] + (result.shape[-2] // 2, 2, part))
 
 

time: 75.3 us -> 75 us (level)
  other arithmetic: 1.33 us -> 0.28 us
  local copies, waits for them, and re-layouts: 0.15 us -> 0.91 us
    another operation x1 -> x0, other arithmetic: 1.08 us -> none  [per_device(): result = jnp.stack(arrived)[None]]
  transfers between devices with their start and end apart: 21 -> 21, of which waited for: 7 -> 6; matrix products, arithmetic and copies ran while one was open for 0% -> 0% of each run, Pallas kernels for 22% -> 22%
where the time goes in v7:
time: 75 us; the launch traced here: 74.8 us
  Pallas kernels  29.2 us (39%)
  starting transfers between devices  28.4 us (38%)
  waiting for transfers between devices  15.7 us (21%)
  local copies, waits for them, and re-layouts  0.91 us (1%)
    ppermute x17, starting transfers between devices, exchanged(): arrived[k] = lax.ppermute(values[k], axis, rotation(count, k))  23.4 us
    pallas_call x7, Pallas kernels, denoise(): pl.pallas_call(functools.partial(denoise_kernel, phases=phases, section=s...  17 us
    ppermute x17, waiting for transfers between devices, exchanged(): arrived[k] = lax.ppermute(values[k], axis, rotation(count, k))  15.1 us
    pallas_call x3, Pallas kernels, consistency(): pl.pallas_call(body, in_specs=[pl.BlockSpec(memory_space=pltpu.VMEM if di...  11 us
    ppermute x2, starting transfers between devices, per_device(): odd = lax.ppermute(combined, 'readout', swaps(readout_parts, 1))  3.17 us
    ppermute x2, starting transfers between devices, per_device(): even = lax.ppermute(combined, 'readout', swaps(readout_parts, 0))  1.82 us
  transfers between devices with their start and end apart: 21, of which 6 were waited for; matrix products, arithmetic and copies ran while one was open for 0% of the time, Pallas kernels for 22%

profile of v7, /device:TPU:1, one launch (start us, length us, event | category | flops | bytes accessed | tf_op | source)
XLA Modules:
  0.0 74.8 jit_solution(5550711732420595423)
XLA Ops:
  0.1 6.0 %consistency.3 = (bf16[2,288,128]{2,1,0:T(8,128)(2,1)S(1)}, bf16[2,288,128]{2,1,0:T(8,128)(2,1)S(1)}, bf16[2,288,128]{2,1,0:T(8,128)(2,1)S(1)}, bf16[2,288,128]{2,1,0:T(8,128)(2,1)S(1)}) custom-call(bf16[2,4,2,256,128]{4,3,2,1,0:T(8,128)(2,1)} %bitcast.20, bf16[2,4,2,256,128]{4,3,2,1,0:T(8,128)(2,1)} %bitcast.15, bf16[2,4,4,2,256,128]{5,4,3,2,1,0:T(8,128)(2,1)} %bitcast.12, ...), custom_call_target="tpu_custom_call" | custom-call | flops 5368709120 | bytes 4194304 | tf_op jit(solution)/shard_map/consistency/pallas_call | solution.py:238
  6.1 2.2 %collective-permute-start = (bf16[2,288,128]{2,1,0:T(8,128)(2,1)S(1)}, bf16[2,288,128]{2,1,0:T(8,128)(2,1)S(1)}, u32[]{:S(2)}, u32[]{:S(2)}) collective-permute-start(bf16[2,288,128]{2,1,0:T(8,128)(2,1)S(1)} %get-tuple-element.43), channel_id=1, source_target_pairs={{0,4},{4,8},{8,12},{12,0},{1,5},{5,9},{9,13},{13,1},{2,6},{6,10},{... | collective-permute-start | bytes 442376 | tf_op jit(solution)/shard_map/ppermute | solution.py:539
  8.3 2.3 %collective-permute-start.1 = (bf16[2,288,128]{2,1,0:T(8,128)(2,1)S(1)}, bf16[2,288,128]{2,1,0:T(8,128)(2,1)S(1)}, u32[]{:S(2)}, u32[]{:S(2)}) collective-permute-start(bf16[2,288,128]{2,1,0:T(8,128)(2,1)S(1)} %get-tuple-element.44), channel_id=1, source_target_pairs={{0,8},{4,12},{8,0},{12,4},{1,9},{5,13},{9,1},{13,5},{2,10},{6,14},... | collective-permute-start | bytes 442376 | tf_op jit(solution)/shard_map/ppermute | solution.py:539
  11.8 1.3 %collective-permute-start.3 = (bf16[320,64]{1,0:T(8,128)(2,1)S(1)}, bf16[320,64]{1,0:T(8,128)(2,1)S(1)}, u32[]{:S(2)}, u32[]{:S(2)}) collective-permute-start(bf16[320,64]{1,0:T(8,128)(2,1)S(1)} %fusion.4.refs_0_), channel_id=1, source_target_pairs={{0,16},{16,0},{1,17},{17,1},{2,18},{18,2},{3,19},{19,3},{4,20},{20... | collective-permute-start | bytes 122888 | tf_op jit(solution)/shard_map/ppermute | solution.py:539
  13.1 2.3 %collective-permute-done.3.refs_1_ = bf16[320,64]{1,0:T(8,128)(2,1)S(1)} collective-permute-done((bf16[320,64]{1,0:T(8,128)(2,1)S(1)}, bf16[320,64]{1,0:T(8,128)(2,1)S(1)}, u32[]{:S(2)}, u32[]{:S(2)}) %collective-permute-start.3) | collective-permute-done | bytes 40992 | tf_op jit(solution)/shard_map/ppermute | solution.py:539
  15.5 1.2 %weights.1 = (bf16[2,256,240]{2,1,0:T(8,128)(2,1)S(1)}, bf16[2,256,256]{2,1,0:T(8,128)(2,1)S(1)}, bf16[2,240,256]{2,1,0:T(8,128)(2,1)S(1)}) custom-call(bf16[320,64]{1,0:T(8,128)(2,1)S(1)} %fusion.4.refs_0_, bf16[320,64]{1,0:T(8,128)(2,1)S(1)} %collective-permute-done.3.refs_1_, bf16[240,64]{1,0:T(8,128)(2,1)S(1)} %copy-done.4, ...), custom_call_target="tpu_custom_call" | custom-call | flops 131072000 | bytes 2097152 | tf_op jit(solution)/shard_map/weights/pallas_call | solution.py:327
  16.7 4.2 %collective-permute-done.1 = bf16[2,288,128]{2,1,0:T(8,128)(2,1)S(1)} collective-permute-done((bf16[2,288,128]{2,1,0:T(8,128)(2,1)S(1)}, bf16[2,288,128]{2,1,0:T(8,128)(2,1)S(1)}, u32[]{:S(2)}, u32[]{:S(2)}) %collective-permute-start.1) | collective-permute-done | bytes 147488 | tf_op jit(solution)/shard_map/ppermute | solution.py:539
  23.0 3.8 %denoise_near.2.refs_5_ = f32[3,2,288,128]{3,2,1,0:T(8,128)S(1)} custom-call(bf16[2,288,128]{2,1,0:T(8,128)(2,1)S(1)} %add_convert_fusion.refs_0_, bf16[2,288,128]{2,1,0:T(8,128)(2,1)S(1)} %collective-permute-done.5.refs_1_, bf16[2,256,240]{2,1,0:T(8,128)(2,1)S(1)} %get-tuple-element.56.refs_1_.refs_2_, ...), custom_call_target="tpu_custom_call" | custom-call | flops 3623878656 | bytes 2097152 | tf_op jit(solution)/shard_map/denoise_near/pallas_call | solution.py:510
  27.3 2.6 %denoise_far.1 = (bf16[4,1,64,128]{3,2,1,0:T(8,128)(2,1)S(1)}, f32[3,1,288,128]{3,2,1,0:T(8,128)S(1)}) custom-call(bf16[2,288,128]{2,1,0:T(8,128)(2,1)S(1)} %add_convert_fusion.refs_0_, bf16[2,288,128]{2,1,0:T(8,128)(2,1)S(1)} %collective-permute-done.4.refs_1_, bf16[2,256,240]{2,1,0:T(8,128)(2,1)S(1)} %get-tuple-element.56.refs_1_.refs_2_, ...), custom_call_target="tpu_custom_call" | custom-call | flops 1811939328 | bytes 2097152 | tf_op jit(solution)/shard_map/denoise_far/pallas_call | solution.py:510
  29.9 3.4 %collective-permute-start.6 = (bf16[4,1,64,128]{3,2,1,0:T(8,128)(2,1)S(1)}, bf16[4,1,64,128]{3,2,1,0:T(8,128)(2,1)S(1)}, u32[]{:S(2)}, u32[]{:S(2)}) collective-permute-start(bf16[4,1,64,128]{3,2,1,0:T(8,128)(2,1)S(1)} %get-tuple-element.59.refs_0_.refs_7_), channel_id=1, source_target_pairs={{0,4},{4,8},{8,12},{12,0},{1,5},{5,9},{9,13},{13,1},{2,6},{6,10},{... | collective-permute-start | bytes 196616 | tf_op jit(solution)/shard_map/ppermute | solution.py:539
  33.3 1.3 %collective-permute-start.7 = (bf16[4,1,64,128]{3,2,1,0:T(8,128)(2,1)S(1)}, bf16[4,1,64,128]{3,2,1,0:T(8,128)(2,1)S(1)}, u32[]{:S(2)}, u32[]{:S(2)}) collective-permute-start(bf16[4,1,64,128]{3,2,1,0:T(8,128)(2,1)S(1)} %get-tuple-element.59.refs_0_.refs_7_), channel_id=1, source_target_pairs={{0,8},{4,12},{8,0},{12,4},{1,9},{5,13},{9,1},{13,5},{2,10},{6,14},... | collective-permute-start | bytes 196616 | tf_op jit(solution)/shard_map/ppermute | solution.py:539
  35.4 2.3 %denoise_last.1 = (bf16[4,1,64,128]{3,2,1,0:T(8,128)(2,1)S(1)}, bf16[4,2,64,128]{3,2,1,0:T(8,128)(2,1)S(1)}) custom-call(bf16[2,288,128]{2,1,0:T(8,128)(2,1)S(1)} %add_convert_fusion.refs_0_, bf16[2,288,128]{2,1,0:T(8,128)(2,1)S(1)} %collective-permute-done.4.refs_1_, bf16[2,256,240]{2,1,0:T(8,128)(2,1)S(1)} %get-tuple-element.56.refs_1_.refs_2_, ...), custom_call_target="tpu_custom_call" | custom-call | flops 1811939328 | bytes 2097152 | tf_op jit(solution)/shard_map/denoise_last/pallas_call | solution.py:510
  39.5 1.6 %collective-permute-start.14 = (bf16[4,1,64,128]{3,2,1,0:T(8,128)(2,1)S(1)}, bf16[4,1,64,128]{3,2,1,0:T(8,128)(2,1)S(1)}, u32[]{:S(2)}, u32[]{:S(2)}) collective-permute-start(bf16[4,1,64,128]{3,2,1,0:T(8,128)(2,1)S(1)} %get-tuple-element.65.refs_0_), channel_id=1, source_target_pairs={{0,12},{4,0},{8,4},{12,8},{1,13},{5,1},{9,5},{13,9},{2,14},{6,2},{... | collective-permute-start | bytes 196616 | tf_op jit(solution)/shard_map/ppermute | solution.py:539
  41.1 2.5 %consistency.4 = (bf16[1,288,128]{2,1,0:T(8,128)(2,1)S(1)}, bf16[1,288,128]{2,1,0:T(8,128)(2,1)S(1)}, bf16[1,288,128]{2,1,0:T(8,128)(2,1)S(1)}, bf16[1,288,128]{2,1,0:T(8,128)(2,1)S(1)}) custom-call(bf16[4,1,64,128]{3,2,1,0:T(8,128)(2,1)S(1)} %get-tuple-element.59.refs_0_.refs_7_, bf16[4,1,64,128]{3,2,1,0:T(8,128)(2,1)S(1)} %collective-permute-done.6.refs_1_, ...), custom_call_target="tpu_custom_call" | custom-call | flops 2684354560 | bytes 4194304 | tf_op jit(solution)/shard_map/consistency/pallas_call | solution.py:238
  43.6 1.5 %collective-permute-start.10 = (bf16[1,288,128]{2,1,0:T(8,128)(2,1)S(1)}, bf16[1,288,128]{2,1,0:T(8,128)(2,1)S(1)}, u32[]{:S(2)}, u32[]{:S(2)}) collective-permute-start(bf16[1,288,128]{2,1,0:T(8,128)(2,1)S(1)} %get-tuple-element.62), channel_id=1, source_target_pairs={{0,8},{4,12},{8,0},{12,4},{1,9},{5,13},{9,1},{13,5},{2,10},{6,14},... | collective-permute-start | bytes 221192 | tf_op jit(solution)/shard_map/ppermute | solution.py:539
  46.6 2.5 %consistency.5 = (bf16[1,288,128]{2,1,0:T(8,128)(2,1)S(1)}, bf16[1,288,128]{2,1,0:T(8,128)(2,1)S(1)}, bf16[1,288,128]{2,1,0:T(8,128)(2,1)S(1)}, bf16[1,288,128]{2,1,0:T(8,128)(2,1)S(1)}) custom-call(bf16[4,1,64,128]{3,2,1,0:T(8,128)(2,1)S(1)} %get-tuple-element.65.refs_0_, bf16[4,1,64,128]{3,2,1,0:T(8,128)(2,1)S(1)} %collective-permute-done.12.refs_1_, ...), custom_call_target="tpu_custom_call" | custom-call | flops 2684354560 | bytes 4194304 | tf_op jit(solution)/shard_map/consistency/pallas_call | solution.py:238
  49.8 2.6 %collective-permute-start.16 = (bf16[1,288,128]{2,1,0:T(8,128)(2,1)S(1)}, bf16[1,288,128]{2,1,0:T(8,128)(2,1)S(1)}, u32[]{:S(2)}, u32[]{:S(2)}) collective-permute-start(bf16[1,288,128]{2,1,0:T(8,128)(2,1)S(1)} %get-tuple-element.68), channel_id=1, source_target_pairs={{0,8},{4,12},{8,0},{12,4},{1,9},{5,13},{9,1},{13,5},{2,10},{6,14},... | collective-permute-start | bytes 221192 | tf_op jit(solution)/shard_map/ppermute | solution.py:539
  52.5 1.8 %collective-permute-done.15 = bf16[1,288,128]{2,1,0:T(8,128)(2,1)S(1)} collective-permute-done((bf16[1,288,128]{2,1,0:T(8,128)(2,1)S(1)}, bf16[1,288,128]{2,1,0:T(8,128)(2,1)S(1)}, u32[]{:S(2)}, u32[]{:S(2)}) %collective-permute-start.15) | collective-permute-done | bytes 73760 | tf_op jit(solution)/shard_map/ppermute | solution.py:539
  54.3 3.8 %collective-permute-done.16 = bf16[1,288,128]{2,1,0:T(8,128)(2,1)S(1)} collective-permute-done((bf16[1,288,128]{2,1,0:T(8,128)(2,1)S(1)}, bf16[1,288,128]{2,1,0:T(8,128)(2,1)S(1)}, u32[]{:S(2)}, u32[]{:S(2)}) %collective-permute-start.16) | collective-permute-done | bytes 73760 | tf_op jit(solution)/shard_map/ppermute | solution.py:539
  59.4 2.0 %collective-permute-start.18 = (bf16[2,288,128]{2,1,0:T(8,128)(2,1)S(1)}, bf16[2,288,128]{2,1,0:T(8,128)(2,1)S(1)}, u32[]{:S(2)}, u32[]{:S(2)}) collective-permute-start(bf16[2,288,128]{2,1,0:T(8,128)(2,1)S(1)} %maximum_select_fusion.refs_0_), channel_id=1, source_target_pairs={{1,2},{3,0},{2,1},{0,3},{5,6},{7,4},{6,5},{4,7},{9,10},{11,8},{10,... | collective-permute-start | bytes 442376 | tf_op jit(solution)/shard_map/ppermute | solution.py:596
  61.7 3.8 %denoise_near.3.refs_5_ = f32[3,2,288,128]{3,2,1,0:T(8,128)S(1)} custom-call(bf16[2,288,128]{2,1,0:T(8,128)(2,1)S(1)} %maximum_select_fusion.refs_0_, bf16[2,288,128]{2,1,0:T(8,128)(2,1)S(1)} %collective-permute-done.19.refs_1_, bf16[2,256,240]{2,1,0:T(8,128)(2,1)S(1)} %get-tuple-element.56.refs_1_.refs_2_, ...), custom_call_target="tpu_custom_call" | custom-call | flops 3623878656 | bytes 2097152 | tf_op jit(solution)/shard_map/denoise_near/pallas_call | solution.py:510
  65.5 4.2 %denoise_end.1 = bf16[4,2,64,128]{3,2,1,0:T(8,128)(2,1)S(1)} custom-call(bf16[2,288,128]{2,1,0:T(8,128)(2,1)S(1)} %maximum_select_fusion.refs_0_, bf16[2,288,128]{2,1,0:T(8,128)(2,1)S(1)} %collective-permute-done.18.refs_1_, bf16[2,256,240]{2,1,0:T(8,128)(2,1)S(1)} %get-tuple-element.56.refs_1_.refs_2_, ...), custom_call_target="tpu_custom_call" | custom-call | flops 3623878656 | bytes 2097152 | tf_op jit(solution)/shard_map/denoise_end/pallas_call | solution.py:510
  69.7 1.3 %collective-permute-start.20 = (bf16[4,2,64,128]{3,2,1,0:T(8,128)(2,1)S(1)}, bf16[4,2,64,128]{3,2,1,0:T(8,128)(2,1)S(1)}, u32[]{:S(2)}, u32[]{:S(2)}) collective-permute-start(bf16[4,2,64,128]{3,2,1,0:T(8,128)(2,1)S(1)} %broadcast_select_fusion), channel_id=1, source_target_pairs={{0,16},{16,0},{1,17},{17,1},{2,18},{18,2},{3,19},{19,3},{4,20},{20... | collective-permute-start | bytes 393224 | tf_op jit(solution)/shard_map/ppermute | solution.py:539
  71.2 2.9 %collective-permute-done.20 = bf16[4,2,64,128]{3,2,1,0:T(8,128)(2,1)S(1)} collective-permute-done((bf16[4,2,64,128]{3,2,1,0:T(8,128)(2,1)S(1)}, bf16[4,2,64,128]{3,2,1,0:T(8,128)(2,1)S(1)}, u32[]{:S(2)}, u32[]{:S(2)}) %collective-permute-start.20) | collective-permute-done | bytes 131104 | tf_op jit(solution)/shard_map/ppermute | solution.py:539
  (72 shorter events, 10.9 us)
Async XLA Ops:
  0.0 15.4 %copy-start = (bf16[3,256,256]{2,1,0:T(8,128)(2,1)S(1)}, bf16[3,256,256]{2,1,0:T(8,128)(2,1)}, u32[]{:S(2)}) copy-start(bf16[3,256,256]{2,1,0:T(8,128)(2,1)} %constant.65.clone.refs_8_) | copy-start | bytes 1179652
  0.0 15.4 %copy-start.1 = (bf16[256,240]{1,0:T(8,128)(2,1)S(1)}, bf16[256,240]{1,0:T(8,128)(2,1)}, u32[]{:S(2)}) copy-start(bf16[256,240]{1,0:T(8,128)(2,1)} %constant.62.clone.refs_5_) | copy-start | bytes 368644
  0.0 15.4 %copy-start.2 = (bf16[240,256]{1,0:T(8,128)(2,1)S(1)}, bf16[240,256]{1,0:T(8,128)(2,1)}, u32[]{:S(2)}) copy-start(bf16[240,256]{1,0:T(8,128)(2,1)} %constant.61.clone.refs_4_) | copy-start | bytes 368644
  6.1 10.6 %collective-permute-start = (bf16[2,288,128]{2,1,0:T(8,128)(2,1)S(1)}, bf16[2,288,128]{2,1,0:T(8,128)(2,1)S(1)}, u32[]{:S(2)}, u32[]{:S(2)}) collective-permute-start(bf16[2,288,128]{2,1,0:T(8,128)(2,1)S(1)} %get-tuple-element.43), channel_id=1, source_target_pairs={{0,4},{4,8},{8,12},{12,0},{1,5},{5,9},{9,13},{13,1},{2,6},{6,10},{... | collective-permute-start | bytes 442376 | tf_op jit(solution)/shard_map/ppermute | solution.py:539
  8.3 12.7 %collective-permute-start.1 = (bf16[2,288,128]{2,1,0:T(8,128)(2,1)S(1)}, bf16[2,288,128]{2,1,0:T(8,128)(2,1)S(1)}, u32[]{:S(2)}, u32[]{:S(2)}) collective-permute-start(bf16[2,288,128]{2,1,0:T(8,128)(2,1)S(1)} %get-tuple-element.44), channel_id=1, source_target_pairs={{0,8},{4,12},{8,0},{12,4},{1,9},{5,13},{9,1},{13,5},{2,10},{6,14},... | collective-permute-start | bytes 442376 | tf_op jit(solution)/shard_map/ppermute | solution.py:539
  10.6 10.3 %collective-permute-start.2 = (bf16[2,288,128]{2,1,0:T(8,128)(2,1)S(1)}, bf16[2,288,128]{2,1,0:T(8,128)(2,1)S(1)}, u32[]{:S(2)}, u32[]{:S(2)}) collective-permute-start(bf16[2,288,128]{2,1,0:T(8,128)(2,1)S(1)} %get-tuple-element.45), channel_id=1, source_target_pairs={{0,12},{4,0},{8,4},{12,8},{1,13},{5,1},{9,5},{13,9},{2,14},{6,2},{... | collective-permute-start | bytes 442376 | tf_op jit(solution)/shard_map/ppermute | solution.py:539
  11.8 3.7 %collective-permute-start.3 = (bf16[320,64]{1,0:T(8,128)(2,1)S(1)}, bf16[320,64]{1,0:T(8,128)(2,1)S(1)}, u32[]{:S(2)}, u32[]{:S(2)}) collective-permute-start(bf16[320,64]{1,0:T(8,128)(2,1)S(1)} %fusion.4.refs_0_), channel_id=1, source_target_pairs={{0,16},{16,0},{1,17},{17,1},{2,18},{18,2},{3,19},{19,3},{4,20},{20... | collective-permute-start | bytes 122888 | tf_op jit(solution)/shard_map/ppermute | solution.py:539
  21.1 1.9 %collective-permute-start.5 = (bf16[2,288,128]{2,1,0:T(8,128)(2,1)S(1)}, bf16[2,288,128]{2,1,0:T(8,128)(2,1)S(1)}, u32[]{:S(2)}, u32[]{:S(2)}) collective-permute-start(bf16[2,288,128]{2,1,0:T(8,128)(2,1)S(1)} %add_convert_fusion.refs_0_), channel_id=1, source_target_pairs={{0,1},{2,3},{1,0},{3,2},{4,5},{6,7},{5,4},{7,6},{8,9},{10,11},{9,8... | collective-permute-start | bytes 442376 | tf_op jit(solution)/shard_map/ppermute | solution.py:595
  21.7 5.5 %collective-permute-start.4 = (bf16[2,288,128]{2,1,0:T(8,128)(2,1)S(1)}, bf16[2,288,128]{2,1,0:T(8,128)(2,1)S(1)}, u32[]{:S(2)}, u32[]{:S(2)}) collective-permute-start(bf16[2,288,128]{2,1,0:T(8,128)(2,1)S(1)} %add_convert_fusion.refs_0_), channel_id=1, source_target_pairs={{1,2},{3,0},{2,1},{0,3},{5,6},{7,4},{6,5},{4,7},{9,10},{11,8},{10,... | collective-permute-start | bytes 442376 | tf_op jit(solution)/shard_map/ppermute | solution.py:596
  29.9 9.6 %collective-permute-start.6 = (bf16[4,1,64,128]{3,2,1,0:T(8,128)(2,1)S(1)}, bf16[4,1,64,128]{3,2,1,0:T(8,128)(2,1)S(1)}, u32[]{:S(2)}, u32[]{:S(2)}) collective-permute-start(bf16[4,1,64,128]{3,2,1,0:T(8,128)(2,1)S(1)} %get-tuple-element.59.refs_0_.refs_7_), channel_id=1, source_target_pairs={{0,4},{4,8},{8,12},{12,0},{1,5},{5,9},{9,13},{13,1},{2,6},{6,10},{... | collective-permute-start | bytes 196616 | tf_op jit(solution)/shard_map/ppermute | solution.py:539
  33.3 7.8 %collective-permute-start.7 = (bf16[4,1,64,128]{3,2,1,0:T(8,128)(2,1)S(1)}, bf16[4,1,64,128]{3,2,1,0:T(8,128)(2,1)S(1)}, u32[]{:S(2)}, u32[]{:S(2)}) collective-permute-start(bf16[4,1,64,128]{3,2,1,0:T(8,128)(2,1)S(1)} %get-tuple-element.59.refs_0_.refs_7_), channel_id=1, source_target_pairs={{0,8},{4,12},{8,0},{12,4},{1,9},{5,13},{9,1},{13,5},{2,10},{6,14},... | collective-permute-start | bytes 196616 | tf_op jit(solution)/shard_map/ppermute | solution.py:539
  34.6 6.4 %collective-permute-start.8 = (bf16[4,1,64,128]{3,2,1,0:T(8,128)(2,1)S(1)}, bf16[4,1,64,128]{3,2,1,0:T(8,128)(2,1)S(1)}, u32[]{:S(2)}, u32[]{:S(2)}) collective-permute-start(bf16[4,1,64,128]{3,2,1,0:T(8,128)(2,1)S(1)} %get-tuple-element.59.refs_0_.refs_7_), channel_id=1, source_target_pairs={{0,12},{4,0},{8,4},{12,8},{1,13},{5,1},{9,5},{13,9},{2,14},{6,2},{... | collective-permute-start | bytes 196616 | tf_op jit(solution)/shard_map/ppermute | solution.py:539
  37.7 8.4 %collective-permute-start.12 = (bf16[4,1,64,128]{3,2,1,0:T(8,128)(2,1)S(1)}, bf16[4,1,64,128]{3,2,1,0:T(8,128)(2,1)S(1)}, u32[]{:S(2)}, u32[]{:S(2)}) collective-permute-start(bf16[4,1,64,128]{3,2,1,0:T(8,128)(2,1)S(1)} %get-tuple-element.65.refs_0_), channel_id=1, source_target_pairs={{0,4},{4,8},{8,12},{12,0},{1,5},{5,9},{9,13},{13,1},{2,6},{6,10},{... | collective-permute-start | bytes 196616 | tf_op jit(solution)/shard_map/ppermute | solution.py:539
  38.4 8.2 %collective-permute-start.13 = (bf16[4,1,64,128]{3,2,1,0:T(8,128)(2,1)S(1)}, bf16[4,1,64,128]{3,2,1,0:T(8,128)(2,1)S(1)}, u32[]{:S(2)}, u32[]{:S(2)}) collective-permute-start(bf16[4,1,64,128]{3,2,1,0:T(8,128)(2,1)S(1)} %get-tuple-element.65.refs_0_), channel_id=1, source_target_pairs={{0,8},{4,12},{8,0},{12,4},{1,9},{5,13},{9,1},{13,5},{2,10},{6,14},... | collective-permute-start | bytes 196616 | tf_op jit(solution)/shard_map/ppermute | solution.py:539
  39.5 7.2 %collective-permute-start.14 = (bf16[4,1,64,128]{3,2,1,0:T(8,128)(2,1)S(1)}, bf16[4,1,64,128]{3,2,1,0:T(8,128)(2,1)S(1)}, u32[]{:S(2)}, u32[]{:S(2)}) collective-permute-start(bf16[4,1,64,128]{3,2,1,0:T(8,128)(2,1)S(1)} %get-tuple-element.65.refs_0_), channel_id=1, source_target_pairs={{0,12},{4,0},{8,4},{12,8},{1,13},{5,1},{9,5},{13,9},{2,14},{6,2},{... | collective-permute-start | bytes 196616 | tf_op jit(solution)/shard_map/ppermute | solution.py:539
  43.6 8.7 %collective-permute-start.10 = (bf16[1,288,128]{2,1,0:T(8,128)(2,1)S(1)}, bf16[1,288,128]{2,1,0:T(8,128)(2,1)S(1)}, u32[]{:S(2)}, u32[]{:S(2)}) collective-permute-start(bf16[1,288,128]{2,1,0:T(8,128)(2,1)S(1)} %get-tuple-element.62), channel_id=1, source_target_pairs={{0,8},{4,12},{8,0},{12,4},{1,9},{5,13},{9,1},{13,5},{2,10},{6,14},... | collective-permute-start | bytes 221192 | tf_op jit(solution)/shard_map/ppermute | solution.py:539
  45.2 7.3 %collective-permute-start.11 = (bf16[1,288,128]{2,1,0:T(8,128)(2,1)S(1)}, bf16[1,288,128]{2,1,0:T(8,128)(2,1)S(1)}, u32[]{:S(2)}, u32[]{:S(2)}) collective-permute-start(bf16[1,288,128]{2,1,0:T(8,128)(2,1)S(1)} %get-tuple-element.63), channel_id=1, source_target_pairs={{0,12},{4,0},{8,4},{12,8},{1,13},{5,1},{9,5},{13,9},{2,14},{6,2},{... | collective-permute-start | bytes 221192 | tf_op jit(solution)/shard_map/ppermute | solution.py:539
  46.2 6.3 %collective-permute-start.9 = (bf16[1,288,128]{2,1,0:T(8,128)(2,1)S(1)}, bf16[1,288,128]{2,1,0:T(8,128)(2,1)S(1)}, u32[]{:S(2)}, u32[]{:S(2)}) collective-permute-start(bf16[1,288,128]{2,1,0:T(8,128)(2,1)S(1)} %get-tuple-element.61), channel_id=1, source_target_pairs={{0,4},{4,8},{8,12},{12,0},{1,5},{5,9},{9,13},{13,1},{2,6},{6,10},{... | collective-permute-start | bytes 221192 | tf_op jit(solution)/shard_map/ppermute | solution.py:539
  49.2 5.2 %collective-permute-start.15 = (bf16[1,288,128]{2,1,0:T(8,128)(2,1)S(1)}, bf16[1,288,128]{2,1,0:T(8,128)(2,1)S(1)}, u32[]{:S(2)}, u32[]{:S(2)}) collective-permute-start(bf16[1,288,128]{2,1,0:T(8,128)(2,1)S(1)} %get-tuple-element.67), channel_id=1, source_target_pairs={{0,4},{4,8},{8,12},{12,0},{1,5},{5,9},{9,13},{13,1},{2,6},{6,10},{... | collective-permute-start | bytes 221192 | tf_op jit(solution)/shard_map/ppermute | solution.py:539
  49.8 8.4 %collective-permute-start.16 = (bf16[1,288,128]{2,1,0:T(8,128)(2,1)S(1)}, bf16[1,288,128]{2,1,0:T(8,128)(2,1)S(1)}, u32[]{:S(2)}, u32[]{:S(2)}) collective-permute-start(bf16[1,288,128]{2,1,0:T(8,128)(2,1)S(1)} %get-tuple-element.68), channel_id=1, source_target_pairs={{0,8},{4,12},{8,0},{12,4},{1,9},{5,13},{9,1},{13,5},{2,10},{6,14},... | collective-permute-start | bytes 221192 | tf_op jit(solution)/shard_map/ppermute | solution.py:539
  52.3 5.8 %collective-permute-start.17 = (bf16[1,288,128]{2,1,0:T(8,128)(2,1)S(1)}, bf16[1,288,128]{2,1,0:T(8,128)(2,1)S(1)}, u32[]{:S(2)}, u32[]{:S(2)}) collective-permute-start(bf16[1,288,128]{2,1,0:T(8,128)(2,1)S(1)} %get-tuple-element.69), channel_id=1, source_target_pairs={{0,12},{4,0},{8,4},{12,8},{1,13},{5,1},{9,5},{13,9},{2,14},{6,2},{... | collective-permute-start | bytes 221192 | tf_op jit(solution)/shard_map/ppermute | solution.py:539
  58.2 3.4 %collective-permute-start.19 = (bf16[2,288,128]{2,1,0:T(8,128)(2,1)S(1)}, bf16[2,288,128]{2,1,0:T(8,128)(2,1)S(1)}, u32[]{:S(2)}, u32[]{:S(2)}) collective-permute-start(bf16[2,288,128]{2,1,0:T(8,128)(2,1)S(1)} %maximum_select_fusion.refs_0_), channel_id=1, source_target_pairs={{0,1},{2,3},{1,0},{3,2},{4,5},{6,7},{5,4},{7,6},{8,9},{10,11},{9,8... | collective-permute-start | bytes 442376 | tf_op jit(solution)/shard_map/ppermute | solution.py:595
  59.4 6.1 %collective-permute-start.18 = (bf16[2,288,128]{2,1,0:T(8,128)(2,1)S(1)}, bf16[2,288,128]{2,1,0:T(8,128)(2,1)S(1)}, u32[]{:S(2)}, u32[]{:S(2)}) collective-permute-start(bf16[2,288,128]{2,1,0:T(8,128)(2,1)S(1)} %maximum_select_fusion.refs_0_), channel_id=1, source_target_pairs={{1,2},{3,0},{2,1},{0,3},{5,6},{7,4},{6,5},{4,7},{9,10},{11,8},{10,... | collective-permute-start | bytes 442376 | tf_op jit(solution)/shard_map/ppermute | solution.py:596
  69.7 4.3 %collective-permute-start.20 = (bf16[4,2,64,128]{3,2,1,0:T(8,128)(2,1)S(1)}, bf16[4,2,64,128]{3,2,1,0:T(8,128)(2,1)S(1)}, u32[]{:S(2)}, u32[]{:S(2)}) collective-permute-start(bf16[4,2,64,128]{3,2,1,0:T(8,128)(2,1)S(1)} %broadcast_select_fusion), channel_id=1, source_target_pairs={{0,16},{16,0},{1,17},{17,1},{2,18},{18,2},{3,19},{19,3},{4,20},{20... | collective-permute-start | bytes 393224 | tf_op jit(solution)/shard_map/ppermute | solution.py:539
  (13 other events, 149.2 us)

commit v8 on v7

--- a/solution.py
+++ b/solution.py
@@ -47,10 +47,15 @@
         line_major(phases, share),
     ]
     size = max(max(t.shape) for t in tables)
-    stacked = np.zeros((len(tables), size, size))
-    for index, table in enumerate(tables):
-        stacked[index, : table.shape[0], : table.shape[1]] = table
-    return stacked
+    kept, places = [], []
+    for table in tables:
+        padded = np.zeros((size, size))
+        padded[: table.shape[0], : table.shape[1]] = table
+        same = [k for k, other in enumerate(kept) if np.array_equal(other, padded)]
+        places.append(same[0] if same else len(kept))
+        if not same:
+            kept.append(padded)
+    return np.stack(kept), tuple(places)
 
 
 def line_major(phases, share):
@@ -84,7 +89,7 @@
     return [1 - up + k for k in range(readouts - 1)]
 
 
-def consistency_kernel(*refs, pieces, shares, edge, batch, direct, side):
+def consistency_kernel(*refs, pieces, shares, edge, batch, direct, side, table_at):
     images, refs = refs[:pieces], refs[pieces:]
     maps, samples, mask, tables = refs[:4]
     outs = refs[4 : 4 + shares]
@@ -123,7 +128,7 @@
             joined[:, :, pl.ds(to, 2 * share)] = images[k][...]
 
     def apart(values):
-        return dot(tables[4, :rows, :rows], values)
+        return dot(tables[table_at[4], :rows, :rows], values)
 
     def lane(n):
         return slice(n * part, (n + 1) * part)
@@ -162,11 +167,11 @@
                     1,
                 )
             )
-        half = dot(jnp.concatenate(fields, 0), tables[0, : 2 * part, : 2 * part]).astype(BF16)
+        half = dot(jnp.concatenate(fields, 0), tables[table_at[0], : 2 * part, : 2 * part]).astype(BF16)
         stacked = jnp.concatenate(
             [jnp.concatenate([half[band(n), :part], half[band(n), part:]], 0) for n in every], 1
         )
-        spectrum = dot(tables[1, :rows, :rows], stacked)
+        spectrum = dot(tables[table_at[1], :rows, :rows], stacked)
         wait("mask")
         wait("samples")
         measured = apart(
@@ -180,11 +185,11 @@
             ],
             0,
         )
-        back = dot(tables[2, :rows, :rows], mixed).astype(BF16)
+        back = dot(tables[table_at[2], :rows, :rows], mixed).astype(BF16)
         paired = jnp.concatenate(
             [jnp.concatenate([back[:count, lane(n)], back[count:, lane(n)]], 1) for n in every], 0
         )
-        restored = dot(paired, tables[3, : 2 * part, : 2 * part])
+        restored = dot(paired, tables[table_at[3], : 2 * part, : 2 * part])
         for n, (r, coil, p) in enumerate(group):
             map_real, map_imag = map_parts(r, coil)
             real, imag = restored[band(n), :part], restored[band(n), part:]
@@ -201,7 +206,7 @@
             for k in range(shares)
         ]
     width = phases * 2 * share
-    ordered = dot(tables[5, :width, :width], jnp.concatenate(blocks, 1)).astype(BF16)
+    ordered = dot(tables[table_at[5], :width, :width], jnp.concatenate(blocks, 1)).astype(BF16)
     border = jnp.zeros((edge, part), BF16)
     for r in range(readouts):
         window[r, 0:edge] = border
@@ -219,12 +224,14 @@
     lines = rows // 2
     share_rows = rows // shares
     edge = HALO * phases * 2
-    tables = bf16(consistency_tables(lines, part, phases, lines // shares))
+    tables, places = consistency_tables(lines, part, phases, lines // shares)
+    tables = bf16(tables)
     pieces = len(images)
     direct = pieces > 1
     width = phases * share_rows + 2 * edge
     body = functools.partial(
-        consistency_kernel, pieces=pieces, shares=shares, edge=edge, batch=BATCH, direct=direct, side=side
+        consistency_kernel, pieces=pieces, shares=shares, edge=edge, batch=BATCH, direct=direct, side=side,
+        table_at=places
     )
     image_shape = (phases, readouts, rows, part)
     buffers = [
@@ -440,7 +447,21 @@
             for k in range(len(rows)):
                 out[p, k] = ordered[p * height : (p + 1) * height, k * part : (k + 1) * part]
 
-    sums[...] = jnp.zeros_like(sums) if before is None else before[...]
+    if stage == "near":
+        alone = jnp.where(
+            far_is_up(), readout_no == lax.axis_size("readout") - 1, readout_no == 0
+        )
+
+        @pl.when(alone)
+        def _():
+            sums[...] = before[...]
+
+        @pl.when(jnp.logical_not(alone))
+        def _():
+            sums[...] = jnp.zeros_like(sums)
+
+    elif stage != "alone":
+        sums[...] = before[...]
     if stage == "near":
         fill_taps([inwards(k) for k in reversed(range(readouts))] + [neighbour(0), neighbour(1)])
         pl.when(there)(lambda: add_outer(jnp.where(upward, readouts - 1, 0), jnp.where(upward, readouts - 1, 0)))
@@ -472,6 +493,8 @@
 
         @pl.when(there if stage == "far" else jnp.logical_not(there))
         def _():
+            if stage == "alone":
+                sums[...] = jnp.zeros_like(sums)
             fill_taps([inwards(1), inwards(0), neighbour(0)])
             add_inner(0)
 

time: 75 us -> 74.5 us (level)
  transfers between devices with their start and end apart: 21 -> 21, of which waited for: 6 -> 7; matrix products, arithmetic and copies ran while one was open for 0% -> 0% of each run, Pallas kernels for 22% -> 22%
where the time goes in v8:
time: 74.5 us; the launch traced here: 74.4 us
  Pallas kernels  28.7 us (39%)
  starting transfers between devices  28.4 us (38%)
  waiting for transfers between devices  15.8 us (21%)
  local copies, waits for them, and re-layouts  0.9 us (1%)
    ppermute x17, starting transfers between devices, exchanged(): arrived[k] = lax.ppermute(values[k], axis, rotation(count, k))  23.4 us
    pallas_call x7, Pallas kernels, denoise(): pl.pallas_call(functools.partial(denoise_kernel, phases=phases, section=s...  16.6 us
    ppermute x17, waiting for transfers between devices, exchanged(): arrived[k] = lax.ppermute(values[k], axis, rotation(count, k))  14.9 us
    pallas_call x3, Pallas kernels, consistency(): pl.pallas_call(body, in_specs=[pl.BlockSpec(memory_space=pltpu.VMEM if di...  10.9 us
    ppermute x2, starting transfers between devices, per_device(): odd = lax.ppermute(combined, 'readout', swaps(readout_parts, 1))  3.14 us
    ppermute x2, starting transfers between devices, per_device(): even = lax.ppermute(combined, 'readout', swaps(readout_parts, 0))  1.83 us
  transfers between devices with their start and end apart: 21, of which 7 were waited for; matrix products, arithmetic and copies ran while one was open for 0% of the time, Pallas kernels for 22%

profile of v8, /device:TPU:1, one launch (start us, length us, event | category | flops | bytes accessed | tf_op | source)
XLA Modules:
  0.0 74.4 jit_solution(8535955108380955818)
XLA Ops:
  0.1 5.9 %consistency.3 = (bf16[2,288,128]{2,1,0:T(8,128)(2,1)S(1)}, bf16[2,288,128]{2,1,0:T(8,128)(2,1)S(1)}, bf16[2,288,128]{2,1,0:T(8,128)(2,1)S(1)}, bf16[2,288,128]{2,1,0:T(8,128)(2,1)S(1)}) custom-call(bf16[2,4,2,256,128]{4,3,2,1,0:T(8,128)(2,1)} %bitcast.20, bf16[2,4,2,256,128]{4,3,2,1,0:T(8,128)(2,1)} %bitcast.15, bf16[2,4,4,2,256,128]{5,4,3,2,1,0:T(8,128)(2,1)} %bitcast.12, ...), custom_call_target="tpu_custom_call" | custom-call | flops 5368709120 | bytes 4194304 | tf_op jit(solution)/shard_map/consistency/pallas_call | solution.py:245
  6.0 2.2 %collective-permute-start = (bf16[2,288,128]{2,1,0:T(8,128)(2,1)S(1)}, bf16[2,288,128]{2,1,0:T(8,128)(2,1)S(1)}, u32[]{:S(2)}, u32[]{:S(2)}) collective-permute-start(bf16[2,288,128]{2,1,0:T(8,128)(2,1)S(1)} %get-tuple-element.43), channel_id=1, source_target_pairs={{0,4},{4,8},{8,12},{12,0},{1,5},{5,9},{9,13},{13,1},{2,6},{6,10},{... | collective-permute-start | bytes 442376 | tf_op jit(solution)/shard_map/ppermute | solution.py:562
  8.2 2.3 %collective-permute-start.1 = (bf16[2,288,128]{2,1,0:T(8,128)(2,1)S(1)}, bf16[2,288,128]{2,1,0:T(8,128)(2,1)S(1)}, u32[]{:S(2)}, u32[]{:S(2)}) collective-permute-start(bf16[2,288,128]{2,1,0:T(8,128)(2,1)S(1)} %get-tuple-element.44), channel_id=1, source_target_pairs={{0,8},{4,12},{8,0},{12,4},{1,9},{5,13},{9,1},{13,5},{2,10},{6,14},... | collective-permute-start | bytes 442376 | tf_op jit(solution)/shard_map/ppermute | solution.py:562
  11.7 1.3 %collective-permute-start.3 = (bf16[320,64]{1,0:T(8,128)(2,1)S(1)}, bf16[320,64]{1,0:T(8,128)(2,1)S(1)}, u32[]{:S(2)}, u32[]{:S(2)}) collective-permute-start(bf16[320,64]{1,0:T(8,128)(2,1)S(1)} %fusion.4.refs_0_), channel_id=1, source_target_pairs={{0,16},{16,0},{1,17},{17,1},{2,18},{18,2},{3,19},{19,3},{4,20},{20... | collective-permute-start | bytes 122888 | tf_op jit(solution)/shard_map/ppermute | solution.py:562
  13.0 2.4 %collective-permute-done.3.refs_1_ = bf16[320,64]{1,0:T(8,128)(2,1)S(1)} collective-permute-done((bf16[320,64]{1,0:T(8,128)(2,1)S(1)}, bf16[320,64]{1,0:T(8,128)(2,1)S(1)}, u32[]{:S(2)}, u32[]{:S(2)}) %collective-permute-start.3) | collective-permute-done | bytes 40992 | tf_op jit(solution)/shard_map/ppermute | solution.py:562
  15.4 1.2 %weights.1 = (bf16[2,256,240]{2,1,0:T(8,128)(2,1)S(1)}, bf16[2,256,256]{2,1,0:T(8,128)(2,1)S(1)}, bf16[2,240,256]{2,1,0:T(8,128)(2,1)S(1)}) custom-call(bf16[320,64]{1,0:T(8,128)(2,1)S(1)} %fusion.4.refs_0_, bf16[320,64]{1,0:T(8,128)(2,1)S(1)} %collective-permute-done.3.refs_1_, bf16[240,64]{1,0:T(8,128)(2,1)S(1)} %copy-done.4, ...), custom_call_target="tpu_custom_call" | custom-call | flops 131072000 | bytes 2097152 | tf_op jit(solution)/shard_map/weights/pallas_call | solution.py:334
  16.6 4.3 %collective-permute-done.1 = bf16[2,288,128]{2,1,0:T(8,128)(2,1)S(1)} collective-permute-done((bf16[2,288,128]{2,1,0:T(8,128)(2,1)S(1)}, bf16[2,288,128]{2,1,0:T(8,128)(2,1)S(1)}, u32[]{:S(2)}, u32[]{:S(2)}) %collective-permute-start.1) | collective-permute-done | bytes 147488 | tf_op jit(solution)/shard_map/ppermute | solution.py:562
  22.8 3.8 %denoise_near.2.refs_5_ = f32[3,2,288,128]{3,2,1,0:T(8,128)S(1)} custom-call(bf16[2,288,128]{2,1,0:T(8,128)(2,1)S(1)} %add_convert_fusion.refs_0_, bf16[2,288,128]{2,1,0:T(8,128)(2,1)S(1)} %collective-permute-done.5.refs_1_, bf16[2,256,240]{2,1,0:T(8,128)(2,1)S(1)} %get-tuple-element.56.refs_1_.refs_2_, ...), custom_call_target="tpu_custom_call" | custom-call | flops 3623878656 | bytes 2097152 | tf_op jit(solution)/shard_map/denoise_near/pallas_call | solution.py:533
  27.2 2.6 %denoise_far.1 = (bf16[4,1,64,128]{3,2,1,0:T(8,128)(2,1)S(1)}, f32[3,1,288,128]{3,2,1,0:T(8,128)S(1)}) custom-call(bf16[2,288,128]{2,1,0:T(8,128)(2,1)S(1)} %add_convert_fusion.refs_0_, bf16[2,288,128]{2,1,0:T(8,128)(2,1)S(1)} %collective-permute-done.4.refs_1_, bf16[2,256,240]{2,1,0:T(8,128)(2,1)S(1)} %get-tuple-element.56.refs_1_.refs_2_, ...), custom_call_target="tpu_custom_call" | custom-call | flops 1811939328 | bytes 2097152 | tf_op jit(solution)/shard_map/denoise_far/pallas_call | solution.py:533
  29.8 3.4 %collective-permute-start.6 = (bf16[4,1,64,128]{3,2,1,0:T(8,128)(2,1)S(1)}, bf16[4,1,64,128]{3,2,1,0:T(8,128)(2,1)S(1)}, u32[]{:S(2)}, u32[]{:S(2)}) collective-permute-start(bf16[4,1,64,128]{3,2,1,0:T(8,128)(2,1)S(1)} %get-tuple-element.59.refs_0_.refs_7_), channel_id=1, source_target_pairs={{0,4},{4,8},{8,12},{12,0},{1,5},{5,9},{9,13},{13,1},{2,6},{6,10},{... | collective-permute-start | bytes 196616 | tf_op jit(solution)/shard_map/ppermute | solution.py:562
  33.2 1.3 %collective-permute-start.7 = (bf16[4,1,64,128]{3,2,1,0:T(8,128)(2,1)S(1)}, bf16[4,1,64,128]{3,2,1,0:T(8,128)(2,1)S(1)}, u32[]{:S(2)}, u32[]{:S(2)}) collective-permute-start(bf16[4,1,64,128]{3,2,1,0:T(8,128)(2,1)S(1)} %get-tuple-element.59.refs_0_.refs_7_), channel_id=1, source_target_pairs={{0,8},{4,12},{8,0},{12,4},{1,9},{5,13},{9,1},{13,5},{2,10},{6,14},... | collective-permute-start | bytes 196616 | tf_op jit(solution)/shard_map/ppermute | solution.py:562
  35.4 2.3 %denoise_last.1 = (bf16[4,1,64,128]{3,2,1,0:T(8,128)(2,1)S(1)}, bf16[4,2,64,128]{3,2,1,0:T(8,128)(2,1)S(1)}) custom-call(bf16[2,288,128]{2,1,0:T(8,128)(2,1)S(1)} %add_convert_fusion.refs_0_, bf16[2,288,128]{2,1,0:T(8,128)(2,1)S(1)} %collective-permute-done.4.refs_1_, bf16[2,256,240]{2,1,0:T(8,128)(2,1)S(1)} %get-tuple-element.56.refs_1_.refs_2_, ...), custom_call_target="tpu_custom_call" | custom-call | flops 1811939328 | bytes 2097152 | tf_op jit(solution)/shard_map/denoise_last/pallas_call | solution.py:533
  39.4 1.6 %collective-permute-start.14 = (bf16[4,1,64,128]{3,2,1,0:T(8,128)(2,1)S(1)}, bf16[4,1,64,128]{3,2,1,0:T(8,128)(2,1)S(1)}, u32[]{:S(2)}, u32[]{:S(2)}) collective-permute-start(bf16[4,1,64,128]{3,2,1,0:T(8,128)(2,1)S(1)} %get-tuple-element.65.refs_0_), channel_id=1, source_target_pairs={{0,12},{4,0},{8,4},{12,8},{1,13},{5,1},{9,5},{13,9},{2,14},{6,2},{... | collective-permute-start | bytes 196616 | tf_op jit(solution)/shard_map/ppermute | solution.py:562
  41.0 2.5 %consistency.4 = (bf16[1,288,128]{2,1,0:T(8,128)(2,1)S(1)}, bf16[1,288,128]{2,1,0:T(8,128)(2,1)S(1)}, bf16[1,288,128]{2,1,0:T(8,128)(2,1)S(1)}, bf16[1,288,128]{2,1,0:T(8,128)(2,1)S(1)}) custom-call(bf16[4,1,64,128]{3,2,1,0:T(8,128)(2,1)S(1)} %get-tuple-element.59.refs_0_.refs_7_, bf16[4,1,64,128]{3,2,1,0:T(8,128)(2,1)S(1)} %collective-permute-done.6.refs_1_, ...), custom_call_target="tpu_custom_call" | custom-call | flops 2684354560 | bytes 4194304 | tf_op jit(solution)/shard_map/consistency/pallas_call | solution.py:245
  43.5 1.5 %collective-permute-start.10 = (bf16[1,288,128]{2,1,0:T(8,128)(2,1)S(1)}, bf16[1,288,128]{2,1,0:T(8,128)(2,1)S(1)}, u32[]{:S(2)}, u32[]{:S(2)}) collective-permute-start(bf16[1,288,128]{2,1,0:T(8,128)(2,1)S(1)} %get-tuple-element.62), channel_id=1, source_target_pairs={{0,8},{4,12},{8,0},{12,4},{1,9},{5,13},{9,1},{13,5},{2,10},{6,14},... | collective-permute-start | bytes 221192 | tf_op jit(solution)/shard_map/ppermute | solution.py:562
  46.6 2.5 %consistency.5 = (bf16[1,288,128]{2,1,0:T(8,128)(2,1)S(1)}, bf16[1,288,128]{2,1,0:T(8,128)(2,1)S(1)}, bf16[1,288,128]{2,1,0:T(8,128)(2,1)S(1)}, bf16[1,288,128]{2,1,0:T(8,128)(2,1)S(1)}) custom-call(bf16[4,1,64,128]{3,2,1,0:T(8,128)(2,1)S(1)} %get-tuple-element.65.refs_0_, bf16[4,1,64,128]{3,2,1,0:T(8,128)(2,1)S(1)} %collective-permute-done.12.refs_1_, ...), custom_call_target="tpu_custom_call" | custom-call | flops 2684354560 | bytes 4194304 | tf_op jit(solution)/shard_map/consistency/pallas_call | solution.py:245
  49.6 2.7 %collective-permute-start.16 = (bf16[1,288,128]{2,1,0:T(8,128)(2,1)S(1)}, bf16[1,288,128]{2,1,0:T(8,128)(2,1)S(1)}, u32[]{:S(2)}, u32[]{:S(2)}) collective-permute-start(bf16[1,288,128]{2,1,0:T(8,128)(2,1)S(1)} %get-tuple-element.68), channel_id=1, source_target_pairs={{0,8},{4,12},{8,0},{12,4},{1,9},{5,13},{9,1},{13,5},{2,10},{6,14},... | collective-permute-start | bytes 221192 | tf_op jit(solution)/shard_map/ppermute | solution.py:562
  52.5 1.8 %collective-permute-done.15 = bf16[1,288,128]{2,1,0:T(8,128)(2,1)S(1)} collective-permute-done((bf16[1,288,128]{2,1,0:T(8,128)(2,1)S(1)}, bf16[1,288,128]{2,1,0:T(8,128)(2,1)S(1)}, u32[]{:S(2)}, u32[]{:S(2)}) %collective-permute-start.15) | collective-permute-done | bytes 73760 | tf_op jit(solution)/shard_map/ppermute | solution.py:562
  54.2 3.8 %collective-permute-done.16 = bf16[1,288,128]{2,1,0:T(8,128)(2,1)S(1)} collective-permute-done((bf16[1,288,128]{2,1,0:T(8,128)(2,1)S(1)}, bf16[1,288,128]{2,1,0:T(8,128)(2,1)S(1)}, u32[]{:S(2)}, u32[]{:S(2)}) %collective-permute-start.16) | collective-permute-done | bytes 73760 | tf_op jit(solution)/shard_map/ppermute | solution.py:562
  59.3 2.0 %collective-permute-start.18 = (bf16[2,288,128]{2,1,0:T(8,128)(2,1)S(1)}, bf16[2,288,128]{2,1,0:T(8,128)(2,1)S(1)}, u32[]{:S(2)}, u32[]{:S(2)}) collective-permute-start(bf16[2,288,128]{2,1,0:T(8,128)(2,1)S(1)} %maximum_select_fusion.refs_0_), channel_id=1, source_target_pairs={{1,2},{3,0},{2,1},{0,3},{5,6},{7,4},{6,5},{4,7},{9,10},{11,8},{10,... | collective-permute-start | bytes 442376 | tf_op jit(solution)/shard_map/ppermute | solution.py:619
  61.3 3.8 %denoise_near.3.refs_5_ = f32[3,2,288,128]{3,2,1,0:T(8,128)S(1)} custom-call(bf16[2,288,128]{2,1,0:T(8,128)(2,1)S(1)} %maximum_select_fusion.refs_0_, bf16[2,288,128]{2,1,0:T(8,128)(2,1)S(1)} %collective-permute-done.19.refs_1_, bf16[2,256,240]{2,1,0:T(8,128)(2,1)S(1)} %get-tuple-element.56.refs_1_.refs_2_, ...), custom_call_target="tpu_custom_call" | custom-call | flops 3623878656 | bytes 2097152 | tf_op jit(solution)/shard_map/denoise_near/pallas_call | solution.py:533
  65.4 4.2 %denoise_end.1 = bf16[4,2,64,128]{3,2,1,0:T(8,128)(2,1)S(1)} custom-call(bf16[2,288,128]{2,1,0:T(8,128)(2,1)S(1)} %maximum_select_fusion.refs_0_, bf16[2,288,128]{2,1,0:T(8,128)(2,1)S(1)} %collective-permute-done.18.refs_1_, bf16[2,256,240]{2,1,0:T(8,128)(2,1)S(1)} %get-tuple-element.56.refs_1_.refs_2_, ...), custom_call_target="tpu_custom_call" | custom-call | flops 3623878656 | bytes 2097152 | tf_op jit(solution)/shard_map/denoise_end/pallas_call | solution.py:533
  69.6 1.3 %collective-permute-start.20 = (bf16[4,2,64,128]{3,2,1,0:T(8,128)(2,1)S(1)}, bf16[4,2,64,128]{3,2,1,0:T(8,128)(2,1)S(1)}, u32[]{:S(2)}, u32[]{:S(2)}) collective-permute-start(bf16[4,2,64,128]{3,2,1,0:T(8,128)(2,1)S(1)} %broadcast_select_fusion), channel_id=1, source_target_pairs={{0,16},{16,0},{1,17},{17,1},{2,18},{18,2},{3,19},{19,3},{4,20},{20... | collective-permute-start | bytes 393224 | tf_op jit(solution)/shard_map/ppermute | solution.py:562
  71.1 2.6 %collective-permute-done.20 = bf16[4,2,64,128]{3,2,1,0:T(8,128)(2,1)S(1)} collective-permute-done((bf16[4,2,64,128]{3,2,1,0:T(8,128)(2,1)S(1)}, bf16[4,2,64,128]{3,2,1,0:T(8,128)(2,1)S(1)}, u32[]{:S(2)}, u32[]{:S(2)}) %collective-permute-start.20) | collective-permute-done | bytes 131104 | tf_op jit(solution)/shard_map/ppermute | solution.py:562
  (72 shorter events, 10.9 us)
Async XLA Ops:
  0.0 15.4 %copy-start = (bf16[3,256,256]{2,1,0:T(8,128)(2,1)S(1)}, bf16[3,256,256]{2,1,0:T(8,128)(2,1)}, u32[]{:S(2)}) copy-start(bf16[3,256,256]{2,1,0:T(8,128)(2,1)} %constant.65.clone.refs_8_) | copy-start | bytes 1179652
  0.0 15.3 %copy-start.1 = (bf16[256,240]{1,0:T(8,128)(2,1)S(1)}, bf16[256,240]{1,0:T(8,128)(2,1)}, u32[]{:S(2)}) copy-start(bf16[256,240]{1,0:T(8,128)(2,1)} %constant.62.clone.refs_5_) | copy-start | bytes 368644
  0.0 15.3 %copy-start.2 = (bf16[240,256]{1,0:T(8,128)(2,1)S(1)}, bf16[240,256]{1,0:T(8,128)(2,1)}, u32[]{:S(2)}) copy-start(bf16[240,256]{1,0:T(8,128)(2,1)} %constant.61.clone.refs_4_) | copy-start | bytes 368644
  6.0 10.6 %collective-permute-start = (bf16[2,288,128]{2,1,0:T(8,128)(2,1)S(1)}, bf16[2,288,128]{2,1,0:T(8,128)(2,1)S(1)}, u32[]{:S(2)}, u32[]{:S(2)}) collective-permute-start(bf16[2,288,128]{2,1,0:T(8,128)(2,1)S(1)} %get-tuple-element.43), channel_id=1, source_target_pairs={{0,4},{4,8},{8,12},{12,0},{1,5},{5,9},{9,13},{13,1},{2,6},{6,10},{... | collective-permute-start | bytes 442376 | tf_op jit(solution)/shard_map/ppermute | solution.py:562
  8.2 12.7 %collective-permute-start.1 = (bf16[2,288,128]{2,1,0:T(8,128)(2,1)S(1)}, bf16[2,288,128]{2,1,0:T(8,128)(2,1)S(1)}, u32[]{:S(2)}, u32[]{:S(2)}) collective-permute-start(bf16[2,288,128]{2,1,0:T(8,128)(2,1)S(1)} %get-tuple-element.44), channel_id=1, source_target_pairs={{0,8},{4,12},{8,0},{12,4},{1,9},{5,13},{9,1},{13,5},{2,10},{6,14},... | collective-permute-start | bytes 442376 | tf_op jit(solution)/shard_map/ppermute | solution.py:562
  10.5 10.3 %collective-permute-start.2 = (bf16[2,288,128]{2,1,0:T(8,128)(2,1)S(1)}, bf16[2,288,128]{2,1,0:T(8,128)(2,1)S(1)}, u32[]{:S(2)}, u32[]{:S(2)}) collective-permute-start(bf16[2,288,128]{2,1,0:T(8,128)(2,1)S(1)} %get-tuple-element.45), channel_id=1, source_target_pairs={{0,12},{4,0},{8,4},{12,8},{1,13},{5,1},{9,5},{13,9},{2,14},{6,2},{... | collective-permute-start | bytes 442376 | tf_op jit(solution)/shard_map/ppermute | solution.py:562
  11.7 3.7 %collective-permute-start.3 = (bf16[320,64]{1,0:T(8,128)(2,1)S(1)}, bf16[320,64]{1,0:T(8,128)(2,1)S(1)}, u32[]{:S(2)}, u32[]{:S(2)}) collective-permute-start(bf16[320,64]{1,0:T(8,128)(2,1)S(1)} %fusion.4.refs_0_), channel_id=1, source_target_pairs={{0,16},{16,0},{1,17},{17,1},{2,18},{18,2},{3,19},{19,3},{4,20},{20... | collective-permute-start | bytes 122888 | tf_op jit(solution)/shard_map/ppermute | solution.py:562
  21.0 1.8 %collective-permute-start.5 = (bf16[2,288,128]{2,1,0:T(8,128)(2,1)S(1)}, bf16[2,288,128]{2,1,0:T(8,128)(2,1)S(1)}, u32[]{:S(2)}, u32[]{:S(2)}) collective-permute-start(bf16[2,288,128]{2,1,0:T(8,128)(2,1)S(1)} %add_convert_fusion.refs_0_), channel_id=1, source_target_pairs={{0,1},{2,3},{1,0},{3,2},{4,5},{6,7},{5,4},{7,6},{8,9},{10,11},{9,8... | collective-permute-start | bytes 442376 | tf_op jit(solution)/shard_map/ppermute | solution.py:618
  21.6 5.5 %collective-permute-start.4 = (bf16[2,288,128]{2,1,0:T(8,128)(2,1)S(1)}, bf16[2,288,128]{2,1,0:T(8,128)(2,1)S(1)}, u32[]{:S(2)}, u32[]{:S(2)}) collective-permute-start(bf16[2,288,128]{2,1,0:T(8,128)(2,1)S(1)} %add_convert_fusion.refs_0_), channel_id=1, source_target_pairs={{1,2},{3,0},{2,1},{0,3},{5,6},{7,4},{6,5},{4,7},{9,10},{11,8},{10,... | collective-permute-start | bytes 442376 | tf_op jit(solution)/shard_map/ppermute | solution.py:619
  29.8 9.6 %collective-permute-start.6 = (bf16[4,1,64,128]{3,2,1,0:T(8,128)(2,1)S(1)}, bf16[4,1,64,128]{3,2,1,0:T(8,128)(2,1)S(1)}, u32[]{:S(2)}, u32[]{:S(2)}) collective-permute-start(bf16[4,1,64,128]{3,2,1,0:T(8,128)(2,1)S(1)} %get-tuple-element.59.refs_0_.refs_7_), channel_id=1, source_target_pairs={{0,4},{4,8},{8,12},{12,0},{1,5},{5,9},{9,13},{13,1},{2,6},{6,10},{... | collective-permute-start | bytes 196616 | tf_op jit(solution)/shard_map/ppermute | solution.py:562
  33.2 7.8 %collective-permute-start.7 = (bf16[4,1,64,128]{3,2,1,0:T(8,128)(2,1)S(1)}, bf16[4,1,64,128]{3,2,1,0:T(8,128)(2,1)S(1)}, u32[]{:S(2)}, u32[]{:S(2)}) collective-permute-start(bf16[4,1,64,128]{3,2,1,0:T(8,128)(2,1)S(1)} %get-tuple-element.59.refs_0_.refs_7_), channel_id=1, source_target_pairs={{0,8},{4,12},{8,0},{12,4},{1,9},{5,13},{9,1},{13,5},{2,10},{6,14},... | collective-permute-start | bytes 196616 | tf_op jit(solution)/shard_map/ppermute | solution.py:562
  34.5 6.4 %collective-permute-start.8 = (bf16[4,1,64,128]{3,2,1,0:T(8,128)(2,1)S(1)}, bf16[4,1,64,128]{3,2,1,0:T(8,128)(2,1)S(1)}, u32[]{:S(2)}, u32[]{:S(2)}) collective-permute-start(bf16[4,1,64,128]{3,2,1,0:T(8,128)(2,1)S(1)} %get-tuple-element.59.refs_0_.refs_7_), channel_id=1, source_target_pairs={{0,12},{4,0},{8,4},{12,8},{1,13},{5,1},{9,5},{13,9},{2,14},{6,2},{... | collective-permute-start | bytes 196616 | tf_op jit(solution)/shard_map/ppermute | solution.py:562
  37.6 8.5 %collective-permute-start.12 = (bf16[4,1,64,128]{3,2,1,0:T(8,128)(2,1)S(1)}, bf16[4,1,64,128]{3,2,1,0:T(8,128)(2,1)S(1)}, u32[]{:S(2)}, u32[]{:S(2)}) collective-permute-start(bf16[4,1,64,128]{3,2,1,0:T(8,128)(2,1)S(1)} %get-tuple-element.65.refs_0_), channel_id=1, source_target_pairs={{0,4},{4,8},{8,12},{12,0},{1,5},{5,9},{9,13},{13,1},{2,6},{6,10},{... | collective-permute-start | bytes 196616 | tf_op jit(solution)/shard_map/ppermute | solution.py:562
  38.4 8.2 %collective-permute-start.13 = (bf16[4,1,64,128]{3,2,1,0:T(8,128)(2,1)S(1)}, bf16[4,1,64,128]{3,2,1,0:T(8,128)(2,1)S(1)}, u32[]{:S(2)}, u32[]{:S(2)}) collective-permute-start(bf16[4,1,64,128]{3,2,1,0:T(8,128)(2,1)S(1)} %get-tuple-element.65.refs_0_), channel_id=1, source_target_pairs={{0,8},{4,12},{8,0},{12,4},{1,9},{5,13},{9,1},{13,5},{2,10},{6,14},... | collective-permute-start | bytes 196616 | tf_op jit(solution)/shard_map/ppermute | solution.py:562
  39.4 7.2 %collective-permute-start.14 = (bf16[4,1,64,128]{3,2,1,0:T(8,128)(2,1)S(1)}, bf16[4,1,64,128]{3,2,1,0:T(8,128)(2,1)S(1)}, u32[]{:S(2)}, u32[]{:S(2)}) collective-permute-start(bf16[4,1,64,128]{3,2,1,0:T(8,128)(2,1)S(1)} %get-tuple-element.65.refs_0_), channel_id=1, source_target_pairs={{0,12},{4,0},{8,4},{12,8},{1,13},{5,1},{9,5},{13,9},{2,14},{6,2},{... | collective-permute-start | bytes 196616 | tf_op jit(solution)/shard_map/ppermute | solution.py:562
  43.5 8.7 %collective-permute-start.10 = (bf16[1,288,128]{2,1,0:T(8,128)(2,1)S(1)}, bf16[1,288,128]{2,1,0:T(8,128)(2,1)S(1)}, u32[]{:S(2)}, u32[]{:S(2)}) collective-permute-start(bf16[1,288,128]{2,1,0:T(8,128)(2,1)S(1)} %get-tuple-element.62), channel_id=1, source_target_pairs={{0,8},{4,12},{8,0},{12,4},{1,9},{5,13},{9,1},{13,5},{2,10},{6,14},... | collective-permute-start | bytes 221192 | tf_op jit(solution)/shard_map/ppermute | solution.py:562
  45.1 7.3 %collective-permute-start.11 = (bf16[1,288,128]{2,1,0:T(8,128)(2,1)S(1)}, bf16[1,288,128]{2,1,0:T(8,128)(2,1)S(1)}, u32[]{:S(2)}, u32[]{:S(2)}) collective-permute-start(bf16[1,288,128]{2,1,0:T(8,128)(2,1)S(1)} %get-tuple-element.63), channel_id=1, source_target_pairs={{0,12},{4,0},{8,4},{12,8},{1,13},{5,1},{9,5},{13,9},{2,14},{6,2},{... | collective-permute-start | bytes 221192 | tf_op jit(solution)/shard_map/ppermute | solution.py:562
  46.1 6.3 %collective-permute-start.9 = (bf16[1,288,128]{2,1,0:T(8,128)(2,1)S(1)}, bf16[1,288,128]{2,1,0:T(8,128)(2,1)S(1)}, u32[]{:S(2)}, u32[]{:S(2)}) collective-permute-start(bf16[1,288,128]{2,1,0:T(8,128)(2,1)S(1)} %get-tuple-element.61), channel_id=1, source_target_pairs={{0,4},{4,8},{8,12},{12,0},{1,5},{5,9},{9,13},{13,1},{2,6},{6,10},{... | collective-permute-start | bytes 221192 | tf_op jit(solution)/shard_map/ppermute | solution.py:562
  49.1 5.2 %collective-permute-start.15 = (bf16[1,288,128]{2,1,0:T(8,128)(2,1)S(1)}, bf16[1,288,128]{2,1,0:T(8,128)(2,1)S(1)}, u32[]{:S(2)}, u32[]{:S(2)}) collective-permute-start(bf16[1,288,128]{2,1,0:T(8,128)(2,1)S(1)} %get-tuple-element.67), channel_id=1, source_target_pairs={{0,4},{4,8},{8,12},{12,0},{1,5},{5,9},{9,13},{13,1},{2,6},{6,10},{... | collective-permute-start | bytes 221192 | tf_op jit(solution)/shard_map/ppermute | solution.py:562
  49.6 8.4 %collective-permute-start.16 = (bf16[1,288,128]{2,1,0:T(8,128)(2,1)S(1)}, bf16[1,288,128]{2,1,0:T(8,128)(2,1)S(1)}, u32[]{:S(2)}, u32[]{:S(2)}) collective-permute-start(bf16[1,288,128]{2,1,0:T(8,128)(2,1)S(1)} %get-tuple-element.68), channel_id=1, source_target_pairs={{0,8},{4,12},{8,0},{12,4},{1,9},{5,13},{9,1},{13,5},{2,10},{6,14},... | collective-permute-start | bytes 221192 | tf_op jit(solution)/shard_map/ppermute | solution.py:562
  52.3 5.8 %collective-permute-start.17 = (bf16[1,288,128]{2,1,0:T(8,128)(2,1)S(1)}, bf16[1,288,128]{2,1,0:T(8,128)(2,1)S(1)}, u32[]{:S(2)}, u32[]{:S(2)}) collective-permute-start(bf16[1,288,128]{2,1,0:T(8,128)(2,1)S(1)} %get-tuple-element.69), channel_id=1, source_target_pairs={{0,12},{4,0},{8,4},{12,8},{1,13},{5,1},{9,5},{13,9},{2,14},{6,2},{... | collective-permute-start | bytes 221192 | tf_op jit(solution)/shard_map/ppermute | solution.py:562
  58.1 3.1 %collective-permute-start.19 = (bf16[2,288,128]{2,1,0:T(8,128)(2,1)S(1)}, bf16[2,288,128]{2,1,0:T(8,128)(2,1)S(1)}, u32[]{:S(2)}, u32[]{:S(2)}) collective-permute-start(bf16[2,288,128]{2,1,0:T(8,128)(2,1)S(1)} %maximum_select_fusion.refs_0_), channel_id=1, source_target_pairs={{0,1},{2,3},{1,0},{3,2},{4,5},{6,7},{5,4},{7,6},{8,9},{10,11},{9,8... | collective-permute-start | bytes 442376 | tf_op jit(solution)/shard_map/ppermute | solution.py:618
  59.3 6.1 %collective-permute-start.18 = (bf16[2,288,128]{2,1,0:T(8,128)(2,1)S(1)}, bf16[2,288,128]{2,1,0:T(8,128)(2,1)S(1)}, u32[]{:S(2)}, u32[]{:S(2)}) collective-permute-start(bf16[2,288,128]{2,1,0:T(8,128)(2,1)S(1)} %maximum_select_fusion.refs_0_), channel_id=1, source_target_pairs={{1,2},{3,0},{2,1},{0,3},{5,6},{7,4},{6,5},{4,7},{9,10},{11,8},{10,... | collective-permute-start | bytes 442376 | tf_op jit(solution)/shard_map/ppermute | solution.py:619
  69.6 4.0 %collective-permute-start.20 = (bf16[4,2,64,128]{3,2,1,0:T(8,128)(2,1)S(1)}, bf16[4,2,64,128]{3,2,1,0:T(8,128)(2,1)S(1)}, u32[]{:S(2)}, u32[]{:S(2)}) collective-permute-start(bf16[4,2,64,128]{3,2,1,0:T(8,128)(2,1)S(1)} %broadcast_select_fusion), channel_id=1, source_target_pairs={{0,16},{16,0},{1,17},{17,1},{2,18},{18,2},{3,19},{19,3},{4,20},{20... | collective-permute-start | bytes 393224 | tf_op jit(solution)/shard_map/ppermute | solution.py:562
  (13 other events, 148.7 us)
